TPU v7x, 256 devices: a whole 4x4x8 slice. The times are simulated.
256 devices in a mesh: member: 8 (over x_lo, y), grid: 32 (over x_hi, z, core).
Axes of the slice: x: 4 (x_hi: 2, x_lo: 2; x = x_hi * 2 + x_lo), y: 4, z: 8, core: 2. Of those that a mesh axis runs over, the one named last changes fastest.
Arguments:
- latent: bfloat16 [8, 8192, 1024], P('member', 'grid'), may hold values from -6 to 6
- grid_latent_skip: bfloat16 [8, 16384, 1024], P('member', 'grid'), may hold values from -6 to 6
- initial_member_state: float32 [8, 100, 16384], P('member', None, 'grid'), may hold values from -6 to 6
- target: float32 [100, 16384], P(None, 'grid'), may hold values from -6 to 6
- neighbours: int32 [3, 16384], P(None, 'grid'), may hold values from 0 to 511, as said below
- edge_weight: float32 [3, 16384], P(None, 'grid'), may hold values from 0.2 to 1
- area_weight: float32 [16384], P('grid'), may hold values from 0.3 to 27, as said below
- variable_weight: float32 [100], replicated, may hold values from 0.3 to 3
- output_projection: bfloat16 [100, 1024], replicated, may hold values from -0.1875 to 0.1875
- layer_norm_gain: float32 [1024], replicated, may hold values from 0.1 to 1.9
Outputs:
- fair_crps: float32 [], replicated
- latent_grad: bfloat16 [8, 8192, 1024], P('member', 'grid')
- out_weight_grad: float32 [100, 1024], replicated
- norm_gain_grad: float32 [1024], replicated
Inputs may be any that keep to these rules, and one draw needn't show every extreme that they name: neighbours[k, p] indexes 256 + 2 * 128 rows ordered by latitude: the 128 last mesh rows of the slab below the point's slab, the slab's own 256 rows, then the 128 first rows of the slab above. `area_weight`: positive.
All inputs are finite; a program needn't handle non-finite values.
Results may differ from a plain program's by a relative error of at most 0.0067.
Values may be sent and summed in bfloat16 or wider, within the bound.
No kernel may reach another device: no remote copies, remote signals or barrier semaphores. Data moves between devices by JAX's collectives and lax.ppermute only.
A program may use at most 64 MiB of HBM per device.

v0:
```python
import jax
import jax.numpy as jnp
from jax import lax
from jax.sharding import PartitionSpec as P

SMOOTHING = 0.25
FAIRNESS = 0.95
norm_eps = 1e-05


def with_halo(array, sides, width):
    for axis, dim in sides:
        size, length = (lax.axis_size(axis), array.shape[dim])
        up = [(i, (i + 1) % size) for i in range(size - 1)]
        down = [(j, i) for i, j in up]
        last = lax.slice_in_dim(array, length - width, length, axis=dim)
        initial = lax.slice_in_dim(array, 0, width, axis=dim)
        before = lax.ppermute(last, axis, up)
        after = lax.ppermute(initial, axis, down)
        array = jnp.concatenate([before, array, after], axis=dim)
    return array


def from_behind(block, axis, distance):
    devices = range(lax.axis_size(axis))
    route = [(i - distance, i) for i in devices if i - distance in devices]
    return lax.ppermute(block, axis, route)


def smooth_abs(value):
    return jnp.sqrt(value * value + SMOOTHING * SMOOTHING)


def per_device(
    latent,
    grid_latent_skip,
    initial_member_state,
    target,
    neighbours,
    edge_weight,
    area_weight,
    variable_weight,
    output_projection,
    layer_norm_gain,
):
    mesh_count = latent.shape[1]
    rim = mesh_count // 2
    points = grid_latent_skip.shape[1]
    slots = neighbours.shape[0]
    variables = output_projection.shape[0]
    member_list = lax.axis_size("member")
    extended = with_halo(latent, (("grid", 1),), rim)[0]
    weight_arrays = edge_weight / jnp.sum(edge_weight, axis=0, keepdims=True)
    mixed = grid_latent_skip[0].astype(jnp.float32)
    for slot in range(slots):
        mixed = mixed + weight_arrays[slot][:, None] * jnp.take(
            extended, neighbours[slot], axis=0
        ).astype(jnp.float32)
    centred = mixed - jnp.mean(mixed, axis=1, keepdims=True)
    rscale = lax.rsqrt(jnp.mean(centred * centred, axis=1, keepdims=True) + norm_eps)
    normed = centred * rscale
    scaled = (normed * layer_norm_gain[None, :]).astype(jnp.bfloat16)
    predicted_field = initial_member_state[0] + lax.dot_general(
        output_projection, scaled, (((1,), (1,)), ((), ())), preferred_element_type=jnp.float32
    )
    weight_map = variable_weight[:, None] * area_weight[None, :]
    pair_distance = predicted_field - target
    spread = smooth_abs(pair_distance)
    eps_fair = (1.0 - FAIRNESS) / member_list
    coef_pair = (1.0 - eps_fair) / (member_list * (member_list - 1))
    every_member_set = lax.all_gather(predicted_field[None], "member", axis=0, tiled=True)
    member_difference = predicted_field[None] - every_member_set
    dist = smooth_abs(member_difference)
    pair_total = jnp.sum(dist, axis=0) - SMOOTHING
    pair_slope = jnp.sum(member_difference / dist, axis=0)
    pair_loss = jnp.sum(weight_map * pair_total)
    local_loss = jnp.sum(weight_map * spread) / member_list - 0.5 * coef_pair * pair_loss
    fore_grad = (
        weight_map * (pair_distance / spread / member_list - coef_pair * pair_slope)
    ).astype(jnp.bfloat16)
    wout_part = jnp.dot(fore_grad, scaled, preferred_element_type=jnp.float32)
    scaled_grad = lax.dot_general(
        fore_grad, output_projection, (((0,), (0,)), ((), ())), preferred_element_type=jnp.float32
    )
    gain_part = jnp.sum(scaled_grad * normed, axis=0)
    norm_grad = scaled_grad * layer_norm_gain[None, :]
    mixed_grad = rscale * (
        norm_grad
        - jnp.mean(norm_grad, axis=1, keepdims=True)
        - normed * jnp.mean(norm_grad * normed, axis=1, keepdims=True)
    )
    collect = jnp.zeros((extended.shape[0], extended.shape[1]), jnp.float32)
    for slot in range(slots):
        collect = collect.at[neighbours[slot]].add(weight_arrays[slot][:, None] * mixed_grad)
    from_above = from_behind(collect[:rim].astype(jnp.bfloat16), "grid", -1).astype(jnp.float32)
    from_below = from_behind(collect[rim + mesh_count :].astype(jnp.bfloat16), "grid", 1).astype(
        jnp.float32
    )
    owned = collect[rim : rim + mesh_count] + jnp.concatenate([from_below, from_above], axis=0)
    sums = lax.psum((wout_part, gain_part, local_loss), ("member", "grid"))
    fair_crps = sums[2] / (points * lax.axis_size("grid") * variables)
    return (fair_crps, owned[None].astype(jnp.bfloat16), sums[0], sums[1])


def solution(mesh):
    placed = (
        P("member", "grid", None),
        P("member", "grid", None),
        P("member", None, "grid"),
        P(None, "grid"),
        P(None, "grid"),
        P(None, "grid"),
        P("grid"),
        P(),
        P(),
        P(),
    )
    return jax.shard_map(
        per_device,
        mesh=mesh,
        in_specs=placed,
        out_specs=(P(), P("member", "grid", None), P(), P()),
        check_vma=False,
    )
```

profile of v0, /device:TPU:1, one launch (start us, length us, event | category | flops | bytes accessed | tf_op | source)
XLA Modules:
  0.0 377.7 jit_solution(10001090698908370508)
XLA Ops:
  7.2 1.1 fusion.24
  8.3 4.9 %collective-permute-start = (bf16[1,128,1024]{2,1,0:T(8,128)(2,1)S(1)}, bf16[1,128,1024]{2,1,0:T(8,128)(2,1)S(1)}, u32[]{:S(2)}, u32[]{:S(2)}) collective-permute-start(bf16[1,128,1024]{2,1,0:T(8,128)(2,1)S(1)} %get-tuple-element.18), channel_id=1, source_target_pairs={{0,1},{1,2},{2,3},{3,4},{4,5},{5,6},{6,7},{7,8},{8,9},{9,10},{10,1... | collective-permute-start | bytes 786440 | tf_op jit(solution)/shard_map/ppermute | solution.py:18
  13.3 1.9 collective-permute-start.1
  15.2 0.8 fusion.26
  16.1 0.7 reduce_sum.90
  16.8 0.7 broadcast_divide_fusion
  17.6 3.4 collective-permute-done.1
  21.0 1.1 maximum_bitcast_fusion
  22.1 2.1 gather_fusion.2
  24.2 2.8 gather_fusion.1
  26.9 2.8 gather_fusion
  29.7 2.8 fusion.21
  32.6 0.3 multiply_reduce_fusion.2
  33.3 0.3 multiply_convert_fusion
  33.9 1.1 fusion.11
  35.1 40.4 %all-gather.4.cloned.1.call-done = f32[8,100,512]{2,1,0:T(8,128)} async-done(((f32[1,100,512]{2,1,0:T(8,128)}), f32[8,100,512]{2,1,0:T(8,128)}) %all-gather.4.cloned.1.call-update) | async-done | bytes 1638416 | tf_op jit(solution)/shard_map/all_gather | solution.py:71
  75.5 2.5 fusion.10
  78.0 0.8 fusion.19
  78.9 0.9 multiply_reduce_fusion
  79.8 1.9 subtract_multiply_fusion
  81.7 7.4 %scatter_custom_fusion = f32[512,1024]{1,0:T(8,128)} fusion(s32[512]{0:T(512)S(1)} %bitcast.51, f32[512,1024]{1,0:T(8,128)} %subtract_multiply_fusion, f32[]{:T(128)} %constant.19.clone.1, f32[512]{0:T(512)S(1)} %bitcast.42), kind=kCustom, calls=%fused_computation.14 | custom fusion | flops 1048576 | bytes 4196356 | tf_op jit(solution)/shard_map/scatter-add | solution.py:94
  89.1 7.7 %scatter_custom_fusion.1 = f32[512,1024]{1,0:T(8,128)} fusion(f32[512,1024]{1,0:T(8,128)} %scatter_custom_fusion, s32[512]{0:T(512)S(1)} %bitcast.50, f32[512,1024]{1,0:T(8,128)S(1)} %copy-done.1, f32[512]{0:T(512)S(1)} %bitcast.40), kind=kCustom, calls=%fused_computation.12 | custom fusion | flops 1048576 | bytes 4196352 | tf_op jit(solution)/shard_map/scatter-add | solution.py:94
  96.9 7.7 %scatter_custom_fusion.2 = f32[512,1024]{1,0:T(8,128)} fusion(f32[512,1024]{1,0:T(8,128)} %scatter_custom_fusion.1, s32[512]{0:T(512)S(1)} %bitcast.49, f32[512,1024]{1,0:T(8,128)S(1)} %copy-done.1, f32[512]{0:T(512)S(1)} %bitcast.38), kind=kCustom, calls=%fused_computation.10 | custom fusion | flops 1048576 | bytes 4196352 | tf_op jit(solution)/shard_map/scatter-add | solution.py:94
  104.6 1.7 convert.6
  106.4 0.8 fusion.23
  107.2 9.1 %collective-permute-start.2 = (bf16[128,1024]{1,0:T(8,128)(2,1)}, bf16[128,1024]{1,0:T(8,128)(2,1)}, u32[]{:S(2)}, u32[]{:S(2)}) collective-permute-start(bf16[128,1024]{1,0:T(8,128)(2,1)} %get-tuple-element.16), channel_id=1, source_target_pairs={{0,1},{1,2},{2,3},{3,4},{4,5},{5,6},{6,7},{7,8},{8,9},{9,10},{10,1... | collective-permute-start | bytes 786440 | tf_op jit(solution)/shard_map/ppermute | solution.py:27
  116.3 1.9 collective-permute-start.3
  118.3 1.1 fusion.27
  120.6 77.3 %all-reduce = (f32[]{:T(128)}, f32[1024]{0:T(1024)}) all-reduce(f32[]{:T(128)S(6)} %sub.46, f32[1024]{0:T(1024)S(1)} %get-tuple-element.5), channel_id=1, replica_groups=mesh['member'=8,'grid'=32] {'member','grid'}, use_global_device_ids=true, to_apply=%region_6.8 | all-reduce | flops 1025 | bytes 8200 | tf_op jit(solution)/shard_map/psum | solution.py:100
  198.6 2.0 fusion.17
  200.6 167.3 %all-reduce.3.cloned.1.call-done = f32[100,1024]{1,0:T(8,128)} async-done(((f32[100,1024]{1,0:T(8,128)}), f32[100,1024]{1,0:T(8,128)}) %all-reduce.3.cloned.1.call-update) | async-done | bytes 409616 | tf_op jit(solution)/shard_map/psum | solution.py:100
  367.9 1.8 copy.19
  (41 shorter events, 0.8 us)
Async XLA Ops:
  7.2 26.4 %copy-start = (bf16[100,1024]{1,0:T(8,128)(2,1)S(1)}, bf16[100,1024]{1,0:T(8,128)(2,1)}, u32[]{:S(2)}) copy-start(bf16[100,1024]{1,0:T(8,128)(2,1)} %param.20) | copy-start | bytes 614404
  7.2 68.3 %all-gather.4.cloned.1.call-start = ((), (), s32[]{:S(2)}) async-start(), calls=%async_computation.1 | async-start | bytes 1916928 | tf_op jit(solution)/shard_map/all_gather | solution.py:71
  8.3 9.2 %collective-permute-start = (bf16[1,128,1024]{2,1,0:T(8,128)(2,1)S(1)}, bf16[1,128,1024]{2,1,0:T(8,128)(2,1)S(1)}, u32[]{:S(2)}, u32[]{:S(2)}) collective-permute-start(bf16[1,128,1024]{2,1,0:T(8,128)(2,1)S(1)} %get-tuple-element.18), channel_id=1, source_target_pairs={{0,1},{1,2},{2,3},{3,4},{4,5},{5,6},{6,7},{7,8},{8,9},{9,10},{10,1... | collective-permute-start | bytes 786440 | tf_op jit(solution)/shard_map/ppermute | solution.py:18
  13.3 7.7 %collective-permute-start.1 = (bf16[1,128,1024]{2,1,0:T(8,128)(2,1)S(1)}, bf16[1,128,1024]{2,1,0:T(8,128)(2,1)S(1)}, u32[]{:S(2)}, u32[]{:S(2)}) collective-permute-start(bf16[1,128,1024]{2,1,0:T(8,128)(2,1)S(1)} %get-tuple-element.19), channel_id=1, source_target_pairs={{1,0},{2,1},{3,2},{4,3},{5,4},{6,5},{7,6},{8,7},{9,8},{10,9},{11,1... | collective-permute-start | bytes 786440 | tf_op jit(solution)/shard_map/ppermute | solution.py:19
  32.6 0.7 copy-start.6
  32.9 0.9 copy-start.4
  33.3 1.8 copy-start.7
  33.9 44.1 %copy-start.8 = (f32[512]{0:T(512)S(1)}, f32[512]{0:T(512)}, u32[]{:S(2)}) copy-start(f32[512]{0:T(512)} %param.18) | copy-start | bytes 6148
  33.9 44.1 %copy-start.9 = (f32[100]{0:T(128)S(1)}, f32[100]{0:T(128)}, u32[]{:S(2)}) copy-start(f32[100]{0:T(128)} %param.19) | copy-start | bytes 1204
  35.1 332.8 %all-reduce.3.cloned.1.call-start = ((), (), s32[]{:S(2)}) async-start(), calls=%async_computation | async-start | bytes 851968 | tf_op jit(solution)/shard_map/psum | solution.py:100
  75.5 2.5 copy-start.3
  75.5 2.5 copy-start.5
  81.7 7.5 %copy-start.1 = (f32[512,1024]{1,0:T(8,128)S(1)}, f32[512,1024]{1,0:T(8,128)}, u32[]{:S(2)}) copy-start(f32[512,1024]{1,0:T(8,128)} %subtract_multiply_fusion) | copy-start | bytes 6291460
  106.4 92.2 %copy-start.2 = (f32[512,1024]{1,0:T(8,128)S(1)}, f32[512,1024]{1,0:T(8,128)}, u32[]{:S(2)}) copy-start(f32[512,1024]{1,0:T(8,128)} %scatter_custom_fusion.2) | copy-start | bytes 6291460
  107.2 91.3 %collective-permute-start.2 = (bf16[128,1024]{1,0:T(8,128)(2,1)}, bf16[128,1024]{1,0:T(8,128)(2,1)}, u32[]{:S(2)}, u32[]{:S(2)}) collective-permute-start(bf16[128,1024]{1,0:T(8,128)(2,1)} %get-tuple-element.16), channel_id=1, source_target_pairs={{0,1},{1,2},{2,3},{3,4},{4,5},{5,6},{6,7},{7,8},{8,9},{9,10},{10,1... | collective-permute-start | bytes 786440 | tf_op jit(solution)/shard_map/ppermute | solution.py:27
  116.3 82.2 %collective-permute-start.3 = (bf16[128,1024]{1,0:T(8,128)(2,1)}, bf16[128,1024]{1,0:T(8,128)(2,1)}, u32[]{:S(2)}, u32[]{:S(2)}) collective-permute-start(bf16[128,1024]{1,0:T(8,128)(2,1)} %get-tuple-element.17), channel_id=1, source_target_pairs={{1,0},{2,1},{3,2},{4,3},{5,4},{6,5},{7,6},{8,7},{9,8},{10,9},{11,1... | collective-permute-start | bytes 786440 | tf_op jit(solution)/shard_map/ppermute | solution.py:27
Sparse Core Ops, SparseCore 0:
  35.2 40.2 all-gather.3
  119.5 248.3 all-reduce.2
where the time goes:
time: 379 us; the launch traced here: 378 us
  waiting for transfers between devices  211 us (56%)
  blocking collectives  77.3 us (20%)
  other arithmetic  38 us (10%)
  starting transfers between devices  17.9 us (5%)
  between operations  17.4 us (5%)
  local copies, waits for them, and re-layouts  12.8 us (3%)
    psum x1, waiting for transfers between devices, per_device(): sums = lax.psum((wout_part, gain_part, local_loss), ('member', 'grid'))  167 us
    psum x1, blocking collectives, per_device(): sums = lax.psum((wout_part, gain_part, local_loss), ('member', 'grid'))  77.3 us
    all_gather x1, waiting for transfers between devices, per_device(): lax.all_gather(predicted_field[None], 'member', axis=0, tiled=True)  40.4 us
    scatter-add x3, other arithmetic, per_device(): collect.at[neighbours[slot]].add(weight_arrays[slot][:, None] * mixed_grad)  22.9 us
    ppermute x2, starting transfers between devices, from_behind(): return lax.ppermute(block, axis, route)  11 us
    gather x3, local copies, waits for them, and re-layouts, per_device(): jnp.take(extended, neighbours[slot], axis=0).astype(jnp.float32)  7.64 us
  transfers between devices with their start and end apart: 6, of which 3 were waited for; matrix products, arithmetic and copies ran while one was open for 1% of the time, Pallas kernels for 0%

commit v1 on v0

v1 whole, which is shorter than its diff:
```python
import jax
import jax.numpy as jnp
from jax import lax
from jax.experimental import pallas as pl
from jax.experimental.pallas import tpu as pltpu
from jax.sharding import Mesh
from jax.sharding import PartitionSpec as P

SMOOTHING = 0.25
FAIRNESS = 0.95
NORM_EPS = 1e-05
MEMBER = ("xl", "y")
GRID = ("xh", "z", "c")
PLANE = ("xl", "y", "xh")
ROWS = 128
BF16 = jnp.bfloat16
F32 = jnp.float32
VMEM_LIMIT = 48 * 1024 * 1024


def dot(a, b, dims):
    return lax.dot_general(a, b, (dims, ((), ())), preferred_element_type=F32)


def call(kernel, outs, flops=0, moved=0, smem=0):
    def run(*operands):
        specs = [
            pl.BlockSpec(memory_space=pltpu.SMEM if i < smem else pltpu.VMEM)
            for i in range(len(operands))
        ]
        return pl.pallas_call(
            kernel,
            out_shape=[jax.ShapeDtypeStruct(s, d) for s, d in outs],
            in_specs=specs,
            out_specs=[pl.BlockSpec(memory_space=pltpu.VMEM) for _ in outs],
            compiler_params=pltpu.CompilerParams(vmem_limit_bytes=VMEM_LIMIT),
            cost_estimate=pl.CostEstimate(flops=flops, bytes_accessed=moved, transcendentals=0),
        )(*operands)

    return run


def prepare_kernel(nb, ew, vw, area, latent, skip, et_out, halo_out, part_out, wm_out):
    slots, points = nb.shape
    mesh_count = latent.shape[0]
    rim = mesh_count // 2
    extent = mesh_count + 2 * rim
    weights = ew[...]
    weights = weights / jnp.sum(weights, axis=0, keepdims=True)
    rows = nb[...]
    row_id = lax.broadcasted_iota(jnp.int32, (extent, points), 0)
    et = jnp.zeros((extent, points), F32)
    for k in range(slots):
        et = et + jnp.where(row_id == rows[k : k + 1, :], weights[k : k + 1, :], 0.0)
    et_out[...] = et.astype(BF16)
    both = jnp.concatenate(
        [rows.astype(F32), weights, jnp.zeros((8 - 2 * slots, points), F32)], axis=0
    )
    columns = jnp.transpose(both)
    lane_id = lax.broadcasted_iota(jnp.int32, (points, extent), 1).astype(F32)
    edges = jnp.zeros((points, extent), F32)
    for k in range(slots):
        edges = edges + jnp.where(
            lane_id == columns[:, k : k + 1], columns[:, slots + k : slots + k + 1], 0.0
        )
    edges = edges.astype(BF16)
    halo_out[:, :rim] = edges[:, :rim]
    halo_out[:, rim:] = edges[:, rim + mesh_count :]
    part_out[...] = skip[...].astype(F32) + dot(
        edges[:, rim : rim + mesh_count], latent[...], ((1,), (0,))
    )
    variables = vw.shape[1]
    diagonal = lax.broadcasted_iota(jnp.int32, (variables, variables), 0) == (
        lax.broadcasted_iota(jnp.int32, (variables, variables), 1)
    )
    vw_column = jnp.sum(jnp.where(diagonal, vw[...], 0.0), axis=1, keepdims=True)
    wm_out[...] = vw_column * area[...]


def forward_kernel(part, edges, before, after, gain, proj, state, f_out, fb_out, sc_out, rs_out):
    rim = before.shape[0]
    mixed = (
        part[...]
        + dot(edges[:, :rim], before[...], ((1,), (0,)))
        + dot(edges[:, rim:], after[...], ((1,), (0,)))
    )
    centred = mixed - jnp.mean(mixed, axis=1, keepdims=True)
    rscale = lax.rsqrt(jnp.mean(centred * centred, axis=1, keepdims=True) + NORM_EPS)
    scaled = (centred * rscale * gain[...]).astype(BF16)
    sc_out[...] = scaled
    rs_out[...] = rscale
    field = state[...] + dot(proj[...], scaled, ((1,), (1,)))
    f_out[...] = field
    low = field.astype(BF16)
    for m in range(fb_out.shape[0]):
        fb_out[m] = low


def loss_kernel(me, every, field, target, wm, proj, scaled, gain, fg_out, keep_out, send_out):
    members, variables, _ = every.shape
    eps_fair = (1.0 - FAIRNESS) / members
    coef_pair = (1.0 - eps_fair) / (members * (members - 1))
    smooth = SMOOTHING * SMOOTHING
    f = field[...]
    weight_map = wm[...]
    d = f - target[...]
    s = d * d + smooth
    r = lax.rsqrt(s)
    spread, slope = s * r, d * r
    pair_total = jnp.full_like(f, -SMOOTHING)
    pair_slope = jnp.zeros_like(f)
    for k in range(members):
        other = jnp.where(me[0] == k, f, every[k].astype(F32))
        d = f - other
        s = d * d + smooth
        r = lax.rsqrt(s)
        pair_total = pair_total + s * r
        pair_slope = pair_slope + d * r
    terms = weight_map * (spread / members - 0.5 * coef_pair * pair_total)
    loss = jnp.sum(jnp.sum(terms, axis=0, keepdims=True), axis=1, keepdims=True)
    fore_grad = (weight_map * (slope / members - coef_pair * pair_slope)).astype(BF16)
    fg_out[...] = fore_grad
    values = scaled[...]
    wout = dot(fore_grad, values, ((1,), (0,)))
    scaled_grad = dot(fore_grad, proj[...], ((0,), (0,)))
    product = jnp.sum(scaled_grad * values.astype(F32), axis=0, keepdims=True) / gain[...]
    half = wout.shape[1] // 2
    upper = me[1] == 1

    def store(out, left):
        out[:variables, :] = jnp.where(left, wout[:, :half], wout[:, half:])
        out[variables : variables + 1, :] = jnp.where(left, product[:, :half], product[:, half:])
        out[variables + 1 : variables + 2, :] = jnp.broadcast_to(loss, (1, half))
        out[variables + 2 :, :] = jnp.zeros((ROWS - variables - 2, half), F32)

    store(keep_out, jnp.logical_not(upper))
    store(send_out, upper)


def back_kernel(fore_grad, proj, scaled, gain, rscale, et, own_out, up_out, down_out):
    channels = scaled.shape[1]
    rim = up_out.shape[0]
    mesh_count = own_out.shape[0]
    scaled_grad = dot(fore_grad[...], proj[...], ((0,), (0,)))
    values = scaled[...].astype(F32)
    norm_grad = scaled_grad * gain[...]
    first = jnp.sum(norm_grad, axis=1, keepdims=True) / channels
    second = jnp.sum(scaled_grad * values, axis=1, keepdims=True) / channels
    mixed_grad = rscale[...] * (norm_grad - first - values * (1.0 / gain[...]) * second)
    mixed_grad = mixed_grad.astype(BF16)
    down_out[...] = dot(et[:rim], mixed_grad, ((1,), (0,))).astype(BF16)
    up_out[...] = dot(et[rim + mesh_count :], mixed_grad, ((1,), (0,))).astype(BF16)
    own_out[...] = dot(et[rim : rim + mesh_count], mixed_grad, ((1,), (0,)))


def finish_latent_kernel(own, below, above, out):
    rim = below.shape[0]
    out[0, :rim] = (own[:rim] + below[...].astype(F32)).astype(BF16)
    out[0, rim:] = (own[rim:] + above[...].astype(F32)).astype(BF16)


def fold_kernel(parts, out):
    total = jnp.sum(parts[...], axis=0)
    for i in range(out.shape[0]):
        out[i] = total


def finish_weights_kernel(me, mine, other, wout_out, gain_out, loss_out):
    variables, channels = wout_out.shape
    half = channels // 2
    left = me[1] == 0
    a, b = mine[...], other[...]
    first = jnp.where(left, a, b)
    second = jnp.where(left, b, a)
    wout_out[:, :half] = first[:variables]
    wout_out[:, half:] = second[:variables]
    gain_out[:, :half] = first[variables : variables + 1]
    gain_out[:, half:] = second[variables : variables + 1]
    loss_out[...] = first[variables + 1 : variables + 2, :1]


def per_device(
    latent,
    grid_latent_skip,
    initial_member_state,
    target,
    neighbours,
    edge_weight,
    area_weight,
    variable_weight,
    output_projection,
    layer_norm_gain,
):
    latent, skip, state = latent[0], grid_latent_skip[0], initial_member_state[0]
    mesh_count, channels = latent.shape
    points = skip.shape[0]
    rim = mesh_count // 2
    extent = mesh_count + 2 * rim
    variables = output_projection.shape[0]
    members = lax.axis_size(MEMBER)
    slabs = lax.axis_size(GRID)
    plane = lax.axis_size(PLANE)
    half = channels // 2
    gain = layer_norm_gain[None]
    up = [(i, i + 1) for i in range(slabs - 1)]
    down = [(i + 1, i) for i in range(slabs - 1)]
    swap = [(0, 1), (1, 0)]
    me = jnp.stack([lax.axis_index(MEMBER), lax.axis_index("c")]).astype(jnp.int32)

    before = lax.ppermute(latent[mesh_count - rim :], GRID, up)
    after = lax.ppermute(latent[:rim], GRID, down)
    et, edges, part, weight_map = call(
        prepare_kernel,
        [
            ((extent, points), BF16),
            ((points, 2 * rim), BF16),
            ((points, channels), F32),
            ((variables, points), F32),
        ],
        flops=2 * points * mesh_count * channels,
        moved=8_000_000,
    )(neighbours, edge_weight, variable_weight[None], area_weight[None], latent, skip)
    field, copies, scaled, rscale = call(
        forward_kernel,
        [
            ((variables, points), F32),
            ((members, variables, points), BF16),
            ((points, channels), BF16),
            ((points, 1), F32),
        ],
        flops=2 * points * channels * (2 * rim + variables),
        moved=5_000_000,
    )(part, edges, before, after, gain, output_projection, state)
    every = lax.all_to_all(copies, MEMBER, 0, 0, tiled=True)
    fore_grad, keep, send = call(
        loss_kernel,
        [((variables, points), BF16), ((ROWS, half), F32), ((ROWS, half), F32)],
        flops=4 * points * channels * variables,
        moved=4_000_000,
        smem=1,
    )(me, every, field, target, weight_map, output_projection, scaled, gain)

    met = keep + lax.ppermute(send, "c", swap)
    parts = lax.all_to_all(met.reshape(plane, ROWS // plane, half), PLANE, 0, 0, tiled=True)
    depth = lax.axis_size("z")
    (spread,) = call(fold_kernel, [((depth, ROWS // plane, half), F32)])(parts)
    parts = lax.all_to_all(spread, "z", 0, 0, tiled=True)
    (spread,) = call(fold_kernel, [((plane, ROWS // plane, half), F32)])(parts)
    mine = lax.all_to_all(spread, PLANE, 0, 0, tiled=True).reshape(ROWS, half)
    other = lax.ppermute(mine, "c", swap)
    wout, gain_grad, loss = call(
        finish_weights_kernel,
        [((variables, channels), F32), ((1, channels), F32), ((1, 1), F32)],
        smem=1,
    )(me, mine, other)

    own, to_above, to_below = call(
        back_kernel,
        [((mesh_count, channels), F32), ((rim, channels), BF16), ((rim, channels), BF16)],
        flops=2 * points * channels * (extent + variables),
        moved=6_000_000,
    )(fore_grad, output_projection, scaled, gain, rscale, et)
    below = lax.ppermute(to_above, GRID, up)
    above = lax.ppermute(to_below, GRID, down)
    (latent_grad,) = call(finish_latent_kernel, [((1, mesh_count, channels), BF16)])(
        own, below, above
    )
    fair_crps = loss[0, 0] / (points * slabs * variables)
    return (fair_crps, latent_grad, wout, gain_grad[0])


def solution(mesh):
    fine = Mesh(mesh.devices.reshape(2, 4, 2, 8, 2), ("xl", "y", "xh", "z", "c"))
    placed = (
        P(MEMBER, GRID, None),
        P(MEMBER, GRID, None),
        P(MEMBER, None, GRID),
        P(None, GRID),
        P(None, GRID),
        P(None, GRID),
        P(GRID),
        P(),
        P(),
        P(),
    )
    return jax.shard_map(
        per_device,
        mesh=fine,
        in_specs=placed,
        out_specs=(P(), P(MEMBER, GRID, None), P(), P()),
        check_vma=False,
    )
```

time: 379 us -> 95.1 us (0.25)
  the two profiles are of different devices: /device:TPU:1 before, /device:TPU:225 now
where the time goes in v1:
time: 95.1 us; the launch traced here: 94.5 us
  starting transfers between devices  27.3 us (29%)
  waiting for transfers between devices  24.2 us (25%)
  blocking collectives  22.1 us (23%)
  Pallas kernels  11.1 us (12%)
  local copies, waits for them, and re-layouts  7.07 us (7%)
  between operations  2.56 us (3%)
    all_to_all x1, waiting for transfers between devices, per_device(): every = lax.all_to_all(copies, MEMBER, 0, 0, tiled=True)  12.3 us
    all_to_all x1, blocking collectives, per_device(): lax.all_to_all(met.reshape(plane, ROWS // plane, half), PLANE, 0, 0, tile...  11.5 us
    pallas_call x8, Pallas kernels, run(): pl.pallas_call(kernel, out_shape=[jax.ShapeDtypeStruct(s, d) for s, d in...  11.1 us
    ppermute x1, starting transfers between devices, per_device(): below = lax.ppermute(to_above, GRID, up)  10.9 us
    all_to_all x1, blocking collectives, per_device(): parts = lax.all_to_all(spread, 'z', 0, 0, tiled=True)  10.6 us
    ppermute x1, waiting for transfers between devices, per_device(): above = lax.ppermute(to_below, GRID, down)  7.9 us
    unnamed x23, local copies, waits for them, and re-layouts  5.96 us
    all_to_all x1, starting transfers between devices, per_device(): every = lax.all_to_all(copies, MEMBER, 0, 0, tiled=True)  5.01 us
  transfers between devices with their start and end apart: 8, of which 5 were waited for; matrix products, arithmetic and copies ran while one was open for 1% of the time, Pallas kernels for 5%

profile of v1, /device:TPU:225, one launch (start us, length us, event | category | flops | bytes accessed | tf_op | source)
XLA Modules:
  0.0 94.5 jit_solution(557065935104363064)
XLA Ops:
  0.7 1.1 %slice_bitcast_fusion = (bf16[128,1024]{1,0:T(8,128)(2,1)S(1)}, bf16[128,1024]{1,0:T(8,128)(2,1)S(1)}) fusion(bf16[1,256,1024]{2,1,0:T(8,128)(2,1)} %param.10), kind=kLoop, calls=%fused_computation.1 | loop fusion | bytes 1048576 | tf_op jit(solution)/shard_map/slice | solution.py:211
  1.8 2.0 %collective-permute-start = (bf16[128,1024]{1,0:T(8,128)(2,1)S(1)}, bf16[128,1024]{1,0:T(8,128)(2,1)S(1)}, u32[]{:S(2)}, u32[]{:S(2)}) collective-permute-start(bf16[128,1024]{1,0:T(8,128)(2,1)S(1)} %get-tuple-element.39), channel_id=1, source_target_pairs={{0,1},{1,2},{2,3},{3,4},{4,5},{5,6},{6,7},{7,8},{8,9},{9,10},{10,1... | collective-permute-start | bytes 786440 | tf_op jit(solution)/shard_map/ppermute | solution.py:210
  3.8 2.5 %collective-permute-start.1 = (bf16[128,1024]{1,0:T(8,128)(2,1)S(1)}, bf16[128,1024]{1,0:T(8,128)(2,1)S(1)}, u32[]{:S(2)}, u32[]{:S(2)}) collective-permute-start(bf16[128,1024]{1,0:T(8,128)(2,1)S(1)} %get-tuple-element.38), channel_id=1, source_target_pairs={{1,0},{2,1},{3,2},{4,3},{5,4},{6,5},{7,6},{8,7},{9,8},{10,9},{11,1... | collective-permute-start | bytes 786440 | tf_op jit(solution)/shard_map/ppermute | solution.py:211
  6.3 0.9 %copy.16 = f32[1,100,512]{2,1,0:T(8,128)S(1)} copy(f32[1,100,512]{2,0,1:T(1,128)} %param.12) | data formatting | bytes 409600
  7.2 0.0 copy-start
  7.2 1.0 %copy-done = bf16[1,256,1024]{2,1,0:T(8,128)(2,1)S(1)} copy-done((bf16[1,256,1024]{2,1,0:T(8,128)(2,1)S(1)}, bf16[1,256,1024]{2,1,0:T(8,128)(2,1)}, u32[]{:S(2)}) %copy-start) | copy-done | bytes 524312
  8.3 1.2 %copy-done.1 = bf16[1,512,1024]{2,1,0:T(8,128)(2,1)S(1)} copy-done((bf16[1,512,1024]{2,1,0:T(8,128)(2,1)S(1)}, bf16[1,512,1024]{2,1,0:T(8,128)(2,1)}, u32[]{:S(2)}) %copy-start.1) | copy-done | bytes 1048600
  9.5 0.7 copy-done.5
  10.2 0.7 copy-done.6
  10.9 0.7 copy-done.7
  11.6 0.7 copy-done.8
  12.2 1.6 %shard_map.129 = (bf16[512,512]{1,0:T(8,128)(2,1)S(1)}, bf16[512,256]{1,0:T(8,128)(2,1)S(1)}, f32[512,1024]{1,0:T(8,128)S(1)}, f32[100,512]{1,0:T(8,128)S(1)}) custom-call(s32[3,512]{1,0:T(4,128)S(1)} %copy-done.5, f32[3,512]{1,0:T(4,128)S(1)} %copy-done.6, f32[1,100]{1,0:T(1,128)S(1)} %bitcast.28, f32[1,512]{1,0:T(1,128)S(1)} %bitcast.27, ...), custom_call_target="tpu_custom_call" | custom-call | flops 268435456 | bytes 8000000 | tf_op jit(solution)/shard_map/pallas_call | solution.py:31
  13.8 1.3 %collective-permute-done.1.after = bf16[128,1024]{1,0:T(8,128)(2,1)S(1)} collective-permute-done((bf16[128,1024]{1,0:T(8,128)(2,1)S(1)}, bf16[128,1024]{1,0:T(8,128)(2,1)S(1)}, u32[]{:S(2)}, u32[]{:S(2)}) %collective-permute-start.1) | collective-permute-done | bytes 262176 | tf_op jit(solution)/shard_map/ppermute | solution.py:211
  15.1 2.5 %shard_map.130 = (f32[100,512]{1,0:T(8,128)S(1)}, bf16[8,100,512]{2,1,0:T(8,128)(2,1)}, bf16[512,1024]{1,0:T(8,128)(2,1)S(1)}, f32[512,1]{1,0:T(8,128)S(1)}) custom-call(f32[512,1024]{1,0:T(8,128)S(1)} %get-tuple-element.21.part, bf16[512,256]{1,0:T(8,128)(2,1)S(1)} %get-tuple-element.22.edges, bf16[128,1024]{1,0:T(8,128)(2,1)S(1)} %collective-permute-done.before, ...), custom_call_target="tpu_custom_call" | custom-call | flops 373293056 | bytes 5000000 | tf_op jit(solution)/shard_map/pallas_call | solution.py:31
  17.6 5.0 %all-to-all-start = ((bf16[8,100,512]{2,1,0:T(8,128)(2,1)}), bf16[8,100,512]{2,1,0:T(8,128)(2,1)S(1)}, u32[]{:S(2)}, u32[]{:S(2)}) async-start(bf16[8,100,512]{2,1,0:T(8,128)(2,1)} %get-tuple-element.23), calls=%async_computation | async-start | bytes 1703936 | tf_op jit(solution)/shard_map/all_to_all | solution.py:234
  22.6 0.1 pad_add_fusion.me
  22.7 12.3 %all-to-all-done.every = bf16[8,100,512]{2,1,0:T(8,128)(2,1)S(1)} async-done(((bf16[8,100,512]{2,1,0:T(8,128)(2,1)}), bf16[8,100,512]{2,1,0:T(8,128)(2,1)S(1)}, u32[]{:S(2)}, u32[]{:S(2)}) %all-to-all-start) | async-done | bytes 819232 | tf_op jit(solution)/shard_map/all_to_all | solution.py:234
  35.0 1.7 %shard_map.131 = (bf16[100,512]{1,0:T(8,128)(2,1)S(1)}, f32[128,512]{1,0:T(8,128)S(1)}, f32[128,512]{1,0:T(8,128)S(1)}) custom-call(s32[2]{0:T(128)S(1)} %pad_add_fusion.me, bf16[8,100,512]{2,1,0:T(8,128)(2,1)S(1)} %all-to-all-done.every, f32[100,512]{1,0:T(8,128)S(1)} %get-tuple-element.24.field, f32[100,512]{1,0:T(8,128)S(1)} %copy-done.3, ...), custom_call_target="tpu_custom_call" | custom-call | flops 209715200 | bytes 4000000 | tf_op jit(solution)/shard_map/pallas_call | solution.py:31
  36.7 1.4 %collective-permute-start.2 = (f32[128,512]{1,0:T(8,128)S(1)}, f32[128,512]{1,0:T(8,128)S(1)}, u32[]{:S(2)}, u32[]{:S(2)}) collective-permute-start(f32[128,512]{1,0:T(8,128)S(1)} %get-tuple-element.28), channel_id=1, source_target_pairs={{0,1},{1,0},{2,3},{3,2},{4,5},{5,4},{6,7},{7,6},{8,9},{9,8},{10,11... | collective-permute-start | bytes 786440 | tf_op jit(solution)/shard_map/ppermute | solution.py:243
  38.1 1.2 %collective-permute-done.2 = f32[128,512]{1,0:T(8,128)S(1)} collective-permute-done((f32[128,512]{1,0:T(8,128)S(1)}, f32[128,512]{1,0:T(8,128)S(1)}, u32[]{:S(2)}, u32[]{:S(2)}) %collective-permute-start.2) | collective-permute-done | bytes 262176 | tf_op jit(solution)/shard_map/ppermute | solution.py:243
  39.3 11.5 %all_to_all.20.parts = f32[16,8,512]{2,1,0:T(8,128)S(1)} all-to-all(f32[16,8,512]{2,1,0:T(8,128)S(1)} %add_bitcast_fusion), channel_id=1, replica_groups=mesh['xl'=2,'y'=4,'xh'=2,'z'=8,'c'=2] {'xl','y','xh'}, dimensions={0} | all-to-all | bytes 524288 | tf_op jit(solution)/shard_map/all_to_all | solution.py:244
  50.9 10.6 %all_to_all.21.parts = f32[8,8,512]{2,1,0:T(8,128)S(1)} all-to-all(f32[8,8,512]{2,1,0:T(8,128)S(1)} %shard_map.132), channel_id=1, replica_groups=mesh['xl'=2,'y'=4,'xh'=2,'z'=8,'c'=2] {'z'}, dimensions={0} | all-to-all | bytes 262144 | tf_op jit(solution)/shard_map/all_to_all | solution.py:247
  61.5 0.7 shard_map.133
  62.2 3.5 %all-to-all-start.3 = ((f32[16,8,512]{2,1,0:T(8,128)}), f32[16,8,512]{2,1,0:T(8,128)S(1)}, u32[]{:S(2)}, u32[]{:S(2)}) async-start(f32[16,8,512]{2,1,0:T(8,128)} %shard_map.133), calls=%async_computation.3 | async-start | bytes 524288 | tf_op jit(solution)/shard_map/all_to_all | solution.py:249
  65.8 2.3 %shard_map.135 = (f32[256,1024]{1,0:T(8,128)S(1)}, bf16[128,1024]{1,0:T(8,128)(2,1)}, bf16[128,1024]{1,0:T(8,128)(2,1)}) custom-call(bf16[100,512]{1,0:T(8,128)(2,1)S(1)} %get-tuple-element.30.fore_grad, bf16[100,1024]{1,0:T(8,128)(2,1)S(1)} %copy-done.2, bf16[512,1024]{1,0:T(8,128)(2,1)S(1)} %get-tuple-element.26.scaled, f32[1,1024]{1,0:T(1,128)S(1)} %bitcast.26, ...), custom_call_target="tpu_custom_call" | custom-call | flops 641728512 | bytes 6000000 | tf_op jit(solution)/shard_map/pallas_call | solution.py:31
  68.0 10.9 %collective-permute-start.4 = (bf16[128,1024]{1,0:T(8,128)(2,1)}, bf16[128,1024]{1,0:T(8,128)(2,1)S(1)}, u32[]{:S(2)}, u32[]{:S(2)}) collective-permute-start(bf16[128,1024]{1,0:T(8,128)(2,1)} %get-tuple-element.34), channel_id=1, source_target_pairs={{0,1},{1,2},{2,3},{3,4},{4,5},{5,6},{6,7},{7,8},{8,9},{9,10},{10,1... | collective-permute-start | bytes 786440 | tf_op jit(solution)/shard_map/ppermute | solution.py:263
  78.9 1.9 %collective-permute-start.5 = (bf16[128,1024]{1,0:T(8,128)(2,1)}, bf16[128,1024]{1,0:T(8,128)(2,1)S(1)}, u32[]{:S(2)}, u32[]{:S(2)}) collective-permute-start(bf16[128,1024]{1,0:T(8,128)(2,1)} %get-tuple-element.35), channel_id=1, source_target_pairs={{1,0},{2,1},{3,2},{4,3},{5,4},{6,5},{7,6},{8,7},{9,8},{10,9},{11,1... | collective-permute-start | bytes 786440 | tf_op jit(solution)/shard_map/ppermute | solution.py:264
  80.9 0.1 collective-permute-start.3
  81.0 1.6 %collective-permute-done.4.below = bf16[128,1024]{1,0:T(8,128)(2,1)S(1)} collective-permute-done((bf16[128,1024]{1,0:T(8,128)(2,1)}, bf16[128,1024]{1,0:T(8,128)(2,1)S(1)}, u32[]{:S(2)}, u32[]{:S(2)}) %collective-permute-start.4) | collective-permute-done | bytes 262176 | tf_op jit(solution)/shard_map/ppermute | solution.py:263
  82.5 7.9 %collective-permute-done.5.above = bf16[128,1024]{1,0:T(8,128)(2,1)S(1)} collective-permute-done((bf16[128,1024]{1,0:T(8,128)(2,1)}, bf16[128,1024]{1,0:T(8,128)(2,1)S(1)}, u32[]{:S(2)}, u32[]{:S(2)}) %collective-permute-start.5) | collective-permute-done | bytes 262176 | tf_op jit(solution)/shard_map/ppermute | solution.py:264
  90.4 0.9 shard_map.136
  91.3 1.4 %shard_map.134 = (f32[100,1024]{1,0:T(8,128)}, f32[1,1024]{1,0:T(1,128)}, f32[1,1]{1,0:T(1,128)}) custom-call(s32[2]{0:T(128)S(1)} %pad_add_fusion.me, f32[128,512]{1,0:T(8,128)S(1)} %bitcast.21, f32[128,512]{1,0:T(8,128)S(1)} %collective-permute-done.3.other), custom_call_target="tpu_custom_call" | custom-call | tf_op jit(solution)/shard_map/pallas_call | solution.py:31
  (20 shorter events, 0.1 us)
Async XLA Ops:
  0.6 14.5 %copy-start.4 = (f32[1024]{0:T(1024)S(1)}, f32[1024]{0:T(1024)}, u32[]{:S(2)}) copy-start(f32[1024]{0:T(1024)} %param.19) | copy-start | bytes 12292
  0.6 14.5 %copy-start.2 = (bf16[100,1024]{1,0:T(8,128)(2,1)S(1)}, bf16[100,1024]{1,0:T(8,128)(2,1)}, u32[]{:S(2)}) copy-start(bf16[100,1024]{1,0:T(8,128)(2,1)} %proj.5) | copy-start | bytes 614404
  1.8 12.1 %collective-permute-start = (bf16[128,1024]{1,0:T(8,128)(2,1)S(1)}, bf16[128,1024]{1,0:T(8,128)(2,1)S(1)}, u32[]{:S(2)}, u32[]{:S(2)}) collective-permute-start(bf16[128,1024]{1,0:T(8,128)(2,1)S(1)} %get-tuple-element.39), channel_id=1, source_target_pairs={{0,1},{1,2},{2,3},{3,4},{4,5},{5,6},{6,7},{7,8},{8,9},{9,10},{10,1... | collective-permute-start | bytes 786440 | tf_op jit(solution)/shard_map/ppermute | solution.py:210
  3.8 11.3 %collective-permute-start.1 = (bf16[128,1024]{1,0:T(8,128)(2,1)S(1)}, bf16[128,1024]{1,0:T(8,128)(2,1)S(1)}, u32[]{:S(2)}, u32[]{:S(2)}) collective-permute-start(bf16[128,1024]{1,0:T(8,128)(2,1)S(1)} %get-tuple-element.38), channel_id=1, source_target_pairs={{1,0},{2,1},{3,2},{4,3},{5,4},{6,5},{7,6},{8,7},{9,8},{10,9},{11,1... | collective-permute-start | bytes 786440 | tf_op jit(solution)/shard_map/ppermute | solution.py:211
  7.2 1.0 %copy-start = (bf16[1,256,1024]{2,1,0:T(8,128)(2,1)S(1)}, bf16[1,256,1024]{2,1,0:T(8,128)(2,1)}, u32[]{:S(2)}) copy-start(bf16[1,256,1024]{2,1,0:T(8,128)(2,1)} %param.10) | copy-start | bytes 1572868
  8.3 1.2 %copy-start.1 = (bf16[1,512,1024]{2,1,0:T(8,128)(2,1)S(1)}, bf16[1,512,1024]{2,1,0:T(8,128)(2,1)}, u32[]{:S(2)}) copy-start(bf16[1,512,1024]{2,1,0:T(8,128)(2,1)} %param.11) | copy-start | bytes 3145732
  9.5 0.7 copy-start.5
  10.2 0.7 copy-start.6
  10.9 0.7 copy-start.7
  11.6 0.7 copy-start.8
  13.8 3.8 %copy-start.9 = (bf16[512,512]{1,0:T(8,128)(2,1)}, bf16[512,512]{1,0:T(8,128)(2,1)S(1)}, u32[]{:S(2)}) copy-start(bf16[512,512]{1,0:T(8,128)(2,1)S(1)} %get-tuple-element.32.et) | copy-start | bytes 1572868
  15.1 19.9 %copy-start.3 = (f32[100,512]{1,0:T(8,128)S(1)}, f32[100,512]{1,0:T(8,128)}, u32[]{:S(2)}) copy-start(f32[100,512]{1,0:T(8,128)} %target.1) | copy-start | bytes 614404
  17.6 17.3 %all-to-all-start = ((bf16[8,100,512]{2,1,0:T(8,128)(2,1)}), bf16[8,100,512]{2,1,0:T(8,128)(2,1)S(1)}, u32[]{:S(2)}, u32[]{:S(2)}) async-start(bf16[8,100,512]{2,1,0:T(8,128)(2,1)} %get-tuple-element.23), calls=%async_computation | async-start | bytes 1703936 | tf_op jit(solution)/shard_map/all_to_all | solution.py:234
  36.7 29.0 %copy-start.10 = (bf16[512,512]{1,0:T(8,128)(2,1)S(1)}, bf16[512,512]{1,0:T(8,128)(2,1)}, u32[]{:S(2)}) copy-start(bf16[512,512]{1,0:T(8,128)(2,1)} %copy-done.9) | copy-start | bytes 1572868
  36.7 2.6 %collective-permute-start.2 = (f32[128,512]{1,0:T(8,128)S(1)}, f32[128,512]{1,0:T(8,128)S(1)}, u32[]{:S(2)}, u32[]{:S(2)}) collective-permute-start(f32[128,512]{1,0:T(8,128)S(1)} %get-tuple-element.28), channel_id=1, source_target_pairs={{0,1},{1,0},{2,3},{3,2},{4,5},{5,4},{6,7},{7,6},{8,9},{9,8},{10,11... | collective-permute-start | bytes 786440 | tf_op jit(solution)/shard_map/ppermute | solution.py:243
  62.2 18.6 %all-to-all-start.3 = ((f32[16,8,512]{2,1,0:T(8,128)}), f32[16,8,512]{2,1,0:T(8,128)S(1)}, u32[]{:S(2)}, u32[]{:S(2)}) async-start(f32[16,8,512]{2,1,0:T(8,128)} %shard_map.133), calls=%async_computation.3 | async-start | bytes 524288 | tf_op jit(solution)/shard_map/all_to_all | solution.py:249
  68.0 14.5 %collective-permute-start.4 = (bf16[128,1024]{1,0:T(8,128)(2,1)}, bf16[128,1024]{1,0:T(8,128)(2,1)S(1)}, u32[]{:S(2)}, u32[]{:S(2)}) collective-permute-start(bf16[128,1024]{1,0:T(8,128)(2,1)} %get-tuple-element.34), channel_id=1, source_target_pairs={{0,1},{1,2},{2,3},{3,4},{4,5},{5,6},{6,7},{7,8},{8,9},{9,10},{10,1... | collective-permute-start | bytes 786440 | tf_op jit(solution)/shard_map/ppermute | solution.py:263
  78.9 11.5 %collective-permute-start.5 = (bf16[128,1024]{1,0:T(8,128)(2,1)}, bf16[128,1024]{1,0:T(8,128)(2,1)S(1)}, u32[]{:S(2)}, u32[]{:S(2)}) collective-permute-start(bf16[128,1024]{1,0:T(8,128)(2,1)} %get-tuple-element.35), channel_id=1, source_target_pairs={{1,0},{2,1},{3,2},{4,3},{5,4},{6,5},{7,6},{8,7},{9,8},{10,9},{11,1... | collective-permute-start | bytes 786440 | tf_op jit(solution)/shard_map/ppermute | solution.py:264
  80.9 10.5 %collective-permute-start.3 = (f32[128,512]{1,0:T(8,128)S(1)}, f32[128,512]{1,0:T(8,128)S(1)}, u32[]{:S(2)}, u32[]{:S(2)}) collective-permute-start(f32[128,512]{1,0:T(8,128)S(1)} %bitcast.20), channel_id=1, source_target_pairs={{0,1},{1,0},{2,3},{3,2},{4,5},{5,4},{6,7},{7,6},{8,9},{9,8},{10,11... | collective-permute-start | bytes 786440 | tf_op jit(solution)/shard_map/ppermute | solution.py:250

commit v2 on v1

--- a/solution.py
+++ b/solution.py
@@ -15,24 +15,28 @@
 ROWS = 128
 BF16 = jnp.bfloat16
 F32 = jnp.float32
-VMEM_LIMIT = 48 * 1024 * 1024
+VMEM_LIMIT = 24 * 1024 * 1024
 
 
 def dot(a, b, dims):
     return lax.dot_general(a, b, (dims, ((), ())), preferred_element_type=F32)
 
 
-def call(kernel, outs, flops=0, moved=0, smem=0):
+def call(kernel, outs, spaces="", scratch=(), flops=0, moved=0):
+    places = {"s": pltpu.SMEM, "h": pltpu.HBM, "a": pl.ANY, "v": pltpu.VMEM}
+
     def run(*operands):
-        specs = [
-            pl.BlockSpec(memory_space=pltpu.SMEM if i < smem else pltpu.VMEM)
-            for i in range(len(operands))
+        letters = spaces.ljust(len(operands), "v")
+        operands = [
+            pltpu.with_memory_space_constraint(x, pltpu.HBM) if c == "h" else x
+            for x, c in zip(operands, letters)
         ]
         return pl.pallas_call(
             kernel,
             out_shape=[jax.ShapeDtypeStruct(s, d) for s, d in outs],
-            in_specs=specs,
+            in_specs=[pl.BlockSpec(memory_space=places[c]) for c in letters],
             out_specs=[pl.BlockSpec(memory_space=pltpu.VMEM) for _ in outs],
+            scratch_shapes=list(scratch),
             compiler_params=pltpu.CompilerParams(vmem_limit_bytes=VMEM_LIMIT),
             cost_estimate=pl.CostEstimate(flops=flops, bytes_accessed=moved, transcendentals=0),
         )(*operands)
@@ -40,49 +44,102 @@
     return run
 
 
-def prepare_kernel(nb, ew, vw, area, latent, skip, et_out, halo_out, part_out, wm_out):
+def cut_kernel(me, latent, first_out, second_out, sems):
+    rim = first_out.shape[0]
+    start = pl.multiple_of((1 - me[1]) * rim, rim)
+    other = pl.multiple_of(me[1] * rim, rim)
+    one = pltpu.make_async_copy(latent.at[pl.ds(start, rim)], first_out, sems.at[0])
+    two = pltpu.make_async_copy(latent.at[pl.ds(other, rim)], second_out, sems.at[1])
+    one.start()
+    two.start()
+    one.wait()
+    two.wait()
+
+
+def prepare_kernel(
+    me, nb_in, ew_in, vw_in, area_in, latent_in, skip_in, state_in, near,
+    et_out, far_out, part_out, wm_out, state_out,
+    nb, ew, vw, area, latent, skip, state, sems,
+):
+    pairs = (
+        (nb_in, nb), (ew_in, ew), (vw_in, vw), (area_in, area),
+        (latent_in, latent), (skip_in, skip), (state_in, state),
+    )
+    copies = [pltpu.make_async_copy(a, b, sems.at[i]) for i, (a, b) in enumerate(pairs)]
+    for copy in copies:
+        copy.start()
+    for copy in copies[:4]:
+        copy.wait()
     slots, points = nb.shape
     mesh_count = latent.shape[0]
     rim = mesh_count // 2
-    extent = mesh_count + 2 * rim
+    near_start = (1 - me[1]) * (rim + mesh_count)
+    far_start = me[1] * (rim + mesh_count)
+    far_there = me[2] == 1
     weights = ew[...]
     weights = weights / jnp.sum(weights, axis=0, keepdims=True)
     rows = nb[...]
-    row_id = lax.broadcasted_iota(jnp.int32, (extent, points), 0)
-    et = jnp.zeros((extent, points), F32)
-    for k in range(slots):
-        et = et + jnp.where(row_id == rows[k : k + 1, :], weights[k : k + 1, :], 0.0)
-    et_out[...] = et.astype(BF16)
     both = jnp.concatenate(
         [rows.astype(F32), weights, jnp.zeros((8 - 2 * slots, points), F32)], axis=0
     )
     columns = jnp.transpose(both)
-    lane_id = lax.broadcasted_iota(jnp.int32, (points, extent), 1).astype(F32)
-    edges = jnp.zeros((points, extent), F32)
-    for k in range(slots):
-        edges = edges + jnp.where(
-            lane_id == columns[:, k : k + 1], columns[:, slots + k : slots + k + 1], 0.0
-        )
-    edges = edges.astype(BF16)
-    halo_out[:, :rim] = edges[:, :rim]
-    halo_out[:, rim:] = edges[:, rim + mesh_count :]
-    part_out[...] = skip[...].astype(F32) + dot(
-        edges[:, rim : rim + mesh_count], latent[...], ((1,), (0,))
-    )
+    ids = columns.astype(jnp.int32)
+
+    def edges(start, count):
+        lane = lax.broadcasted_iota(jnp.int32, (points, count), 1) + start
+        total = jnp.zeros((points, count), F32)
+        for k in range(slots):
+            total = total + jnp.where(
+                lane == ids[:, k : k + 1], columns[:, slots + k : slots + k + 1], 0.0
+            )
+        return total
+
+    def edges_turned(start, count):
+        sublane = lax.broadcasted_iota(jnp.int32, (count, points), 0) + start
+        total = jnp.zeros((count, points), F32)
+        for k in range(slots):
+            total = total + jnp.where(sublane == rows[k : k + 1], weights[k : k + 1], 0.0)
+        return total
+
+    def parts(value):
+        high = value.astype(BF16)
+        return high, (value - high.astype(F32)).astype(BF16)
+
+    near_high, near_low = parts(edges(near_start, rim))
+    own_high, own_low = parts(edges(rim, mesh_count))
+    far_high, far_low = parts(jnp.where(far_there, edges(far_start, rim), 0.0))
+    far_out[:, :rim] = far_high
+    far_out[:, rim:] = far_low
+    copies[4].wait()
+    borrowed, own = near[...], latent[...]
+    mix = (
+        dot(near_high, borrowed, ((1,), (0,)))
+        + dot(near_low, borrowed, ((1,), (0,)))
+        + dot(own_high, own, ((1,), (0,)))
+        + dot(own_low, own, ((1,), (0,)))
+    )
+    copies[5].wait()
+    part_out[...] = skip[...].astype(F32) + mix
+    et_out[:rim] = edges_turned(near_start, rim).astype(BF16)
+    et_out[rim : rim + mesh_count] = edges_turned(rim, mesh_count).astype(BF16)
+    et_out[rim + mesh_count :] = jnp.where(far_there, edges_turned(far_start, rim), 0.0).astype(BF16)
     variables = vw.shape[1]
     diagonal = lax.broadcasted_iota(jnp.int32, (variables, variables), 0) == (
         lax.broadcasted_iota(jnp.int32, (variables, variables), 1)
     )
     vw_column = jnp.sum(jnp.where(diagonal, vw[...], 0.0), axis=1, keepdims=True)
     wm_out[...] = vw_column * area[...]
-
-
-def forward_kernel(part, edges, before, after, gain, proj, state, f_out, fb_out, sc_out, rs_out):
-    rim = before.shape[0]
+    copies[6].wait()
+    state_out[...] = state[:, 0, :]
+
+
+def forward_kernel(part, edges, far, gain, proj, state, f_out, fb_out, sc_out, rs_out):
+    rim = far.shape[0]
+    borrowed = far[...]
     mixed = (
         part[...]
-        + dot(edges[:, :rim], before[...], ((1,), (0,)))
-        + dot(edges[:, rim:], after[...], ((1,), (0,)))
+        + dot(edges[:, :rim], borrowed, ((1,), (0,)))
+        + dot(edges[:, rim:], borrowed, ((1,), (0,)))
     )
     centred = mixed - jnp.mean(mixed, axis=1, keepdims=True)
     rscale = lax.rsqrt(jnp.mean(centred * centred, axis=1, keepdims=True) + NORM_EPS)
@@ -137,9 +194,9 @@
     store(send_out, upper)
 
 
-def back_kernel(fore_grad, proj, scaled, gain, rscale, et, own_out, up_out, down_out):
+def back_kernel(fore_grad, proj, scaled, gain, rscale, et, own_out, near_out, far_out):
     channels = scaled.shape[1]
-    rim = up_out.shape[0]
+    rim = near_out.shape[0]
     mesh_count = own_out.shape[0]
     scaled_grad = dot(fore_grad[...], proj[...], ((0,), (0,)))
     values = scaled[...].astype(F32)
@@ -148,18 +205,20 @@
     second = jnp.sum(scaled_grad * values, axis=1, keepdims=True) / channels
     mixed_grad = rscale[...] * (norm_grad - first - values * (1.0 / gain[...]) * second)
     mixed_grad = mixed_grad.astype(BF16)
-    down_out[...] = dot(et[:rim], mixed_grad, ((1,), (0,))).astype(BF16)
-    up_out[...] = dot(et[rim + mesh_count :], mixed_grad, ((1,), (0,))).astype(BF16)
+    near_out[...] = dot(et[:rim], mixed_grad, ((1,), (0,))).astype(BF16)
+    far_out[...] = dot(et[rim + mesh_count :], mixed_grad, ((1,), (0,))).astype(BF16)
     own_out[...] = dot(et[rim : rim + mesh_count], mixed_grad, ((1,), (0,)))
 
 
-def finish_latent_kernel(own, below, above, out):
-    rim = below.shape[0]
-    out[0, :rim] = (own[:rim] + below[...].astype(F32)).astype(BF16)
-    out[0, rim:] = (own[rim:] + above[...].astype(F32)).astype(BF16)
-
-
-def fold_kernel(parts, out):
+def finish_latent_kernel(me, own, near, far, out):
+    rim = near.shape[0]
+    a, b = near[...].astype(F32), far[...].astype(F32)
+    second = me[1] == 1
+    out[0, :rim] = (own[:rim] + jnp.where(second, a, b)).astype(BF16)
+    out[0, rim:] = (own[rim:] + jnp.where(second, b, a)).astype(BF16)
+
+
+def fold_kernel(parts, earlier, out):
     total = jnp.sum(parts[...], axis=0)
     for i in range(out.shape[0]):
         out[i] = total
@@ -202,24 +261,47 @@
     plane = lax.axis_size(PLANE)
     half = channels // 2
     gain = layer_norm_gain[None]
-    up = [(i, i + 1) for i in range(slabs - 1)]
-    down = [(i + 1, i) for i in range(slabs - 1)]
     swap = [(0, 1), (1, 0)]
-    me = jnp.stack([lax.axis_index(MEMBER), lax.axis_index("c")]).astype(jnp.int32)
-
-    before = lax.ppermute(latent[mesh_count - rim :], GRID, up)
-    after = lax.ppermute(latent[:rim], GRID, down)
-    et, edges, part, weight_map = call(
+    links = [((i + 1) % slabs, (i + 2) % slabs) for i in range(0, slabs, 2)]
+    links = links + [(j, i) for i, j in links]
+    core, slab = lax.axis_index("c"), lax.axis_index(GRID)
+    far_there = jnp.logical_and(slab > 0, slab < slabs - 1)
+    me = jnp.stack([lax.axis_index(MEMBER), core, far_there]).astype(jnp.int32)
+
+    near_send, far_send = call(
+        cut_kernel,
+        [((rim, channels), BF16), ((rim, channels), BF16)],
+        "sh",
+        [pltpu.SemaphoreType.DMA((2,))],
+    )(me, latent)
+    far = lax.ppermute(far_send, GRID, links)
+    near = lax.ppermute(near_send, "c", swap)
+    et, edges, part, weight_map, state = call(
         prepare_kernel,
         [
             ((extent, points), BF16),
             ((points, 2 * rim), BF16),
             ((points, channels), F32),
             ((variables, points), F32),
+            ((variables, points), F32),
         ],
-        flops=2 * points * mesh_count * channels,
+        "shhhhhhhv",
+        [
+            pltpu.VMEM(neighbours.shape, jnp.int32),
+            pltpu.VMEM(edge_weight.shape, F32),
+            pltpu.VMEM((1, variables), F32),
+            pltpu.VMEM((1, points), F32),
+            pltpu.VMEM((mesh_count, channels), BF16),
+            pltpu.VMEM((points, channels), BF16),
+            pltpu.VMEM((variables, 1, points), F32),
+            pltpu.SemaphoreType.DMA((7,)),
+        ],
+        flops=6 * points * mesh_count * channels,
         moved=8_000_000,
-    )(neighbours, edge_weight, variable_weight[None], area_weight[None], latent, skip)
+    )(
+        me, neighbours, edge_weight, variable_weight[None], area_weight[None], latent, skip,
+        state.reshape(variables, 1, points), near,
+    )
     field, copies, scaled, rscale = call(
         forward_kernel,
         [
@@ -230,41 +312,40 @@
         ],
         flops=2 * points * channels * (2 * rim + variables),
         moved=5_000_000,
-    )(part, edges, before, after, gain, output_projection, state)
+    )(part, edges, far, gain, output_projection, state)
     every = lax.all_to_all(copies, MEMBER, 0, 0, tiled=True)
     fore_grad, keep, send = call(
         loss_kernel,
         [((variables, points), BF16), ((ROWS, half), F32), ((ROWS, half), F32)],
+        "s",
         flops=4 * points * channels * variables,
         moved=4_000_000,
-        smem=1,
     )(me, every, field, target, weight_map, output_projection, scaled, gain)
 
     met = keep + lax.ppermute(send, "c", swap)
-    parts = lax.all_to_all(met.reshape(plane, ROWS // plane, half), PLANE, 0, 0, tiled=True)
-    depth = lax.axis_size("z")
-    (spread,) = call(fold_kernel, [((depth, ROWS // plane, half), F32)])(parts)
-    parts = lax.all_to_all(spread, "z", 0, 0, tiled=True)
-    (spread,) = call(fold_kernel, [((plane, ROWS // plane, half), F32)])(parts)
-    mine = lax.all_to_all(spread, PLANE, 0, 0, tiled=True).reshape(ROWS, half)
-    other = lax.ppermute(mine, "c", swap)
-    wout, gain_grad, loss = call(
-        finish_weights_kernel,
-        [((variables, channels), F32), ((1, channels), F32), ((1, 1), F32)],
-        smem=1,
-    )(me, mine, other)
-
-    own, to_above, to_below = call(
+    own, near_grad, far_grad = call(
         back_kernel,
         [((mesh_count, channels), F32), ((rim, channels), BF16), ((rim, channels), BF16)],
         flops=2 * points * channels * (extent + variables),
         moved=6_000_000,
     )(fore_grad, output_projection, scaled, gain, rscale, et)
-    below = lax.ppermute(to_above, GRID, up)
-    above = lax.ppermute(to_below, GRID, down)
-    (latent_grad,) = call(finish_latent_kernel, [((1, mesh_count, channels), BF16)])(
-        own, below, above
-    )
+    far_grad = lax.ppermute(far_grad, GRID, links)
+    near_grad = lax.ppermute(near_grad, "c", swap)
+    (latent_grad,) = call(finish_latent_kernel, [((1, mesh_count, channels), BF16)], "s")(
+        me, own, near_grad, far_grad
+    )
+    depth, rows = lax.axis_size("z"), ROWS // plane
+    parts = lax.all_to_all(met.reshape(plane, rows, half), PLANE, 0, 0, tiled=True)
+    (parts,) = call(fold_kernel, [((depth, rows, half), F32)], "va")(parts, own)
+    parts = lax.all_to_all(parts, "z", 0, 0, tiled=True)
+    (parts,) = call(fold_kernel, [((plane, rows, half), F32)], "vh")(parts, latent_grad)
+    mine = lax.all_to_all(parts, PLANE, 0, 0, tiled=True).reshape(ROWS, half)
+    other = lax.ppermute(mine, "c", swap)
+    wout, gain_grad, loss = call(
+        finish_weights_kernel,
+        [((variables, channels), F32), ((1, channels), F32), ((1, 1), F32)],
+        "s",
+    )(me, mine, other)
     fair_crps = loss[0, 0] / (points * slabs * variables)
     return (fair_crps, latent_grad, wout, gain_grad[0])
 

time: 95.1 us -> 84 us (0.88)
  the two profiles are of different devices: /device:TPU:225 before, /device:TPU:1 now
where the time goes in v2:
time: 84 us; the launch traced here: 83.5 us
  starting transfers between devices  25.9 us (31%)
  blocking collectives  23.9 us (28%)
  Pallas kernels  14.6 us (17%)
  waiting for transfers between devices  13.9 us (17%)
  between operations  2.54 us (3%)
  local copies, waits for them, and re-layouts  1.84 us (2%)
    pallas_call x9, Pallas kernels, run(): pl.pallas_call(kernel, out_shape=[jax.ShapeDtypeStruct(s, d) for s, d in...  14.6 us
    all_to_all x1, blocking collectives, per_device(): every = lax.all_to_all(copies, MEMBER, 0, 0, tiled=True)  13.1 us
    all_to_all x1, blocking collectives, per_device(): mine = lax.all_to_all(parts, PLANE, 0, 0, tiled=True).reshape(ROWS, half)  10.8 us
    ppermute x1, starting transfers between devices, per_device(): met = keep + lax.ppermute(send, 'c', swap)  7.43 us
    all_to_all x1, waiting for transfers between devices, per_device(): parts = lax.all_to_all(parts, 'z', 0, 0, tiled=True)  6.51 us
    all_to_all x1, starting transfers between devices, per_device(): parts = lax.all_to_all(parts, 'z', 0, 0, tiled=True)  6.4 us
    ppermute x1, starting transfers between devices, per_device(): other = lax.ppermute(mine, 'c', swap)  4.09 us
    all_to_all x1, waiting for transfers between devices, per_device(): lax.all_to_all(met.reshape(plane, rows, half), PLANE, 0, 0, tiled=True)  3.89 us
  transfers between devices with their start and end apart: 8, of which 5 were waited for; matrix products, arithmetic and copies ran while one was open for 0% of the time, Pallas kernels for 10%

profile of v2, /device:TPU:1, one launch (start us, length us, event | category | flops | bytes accessed | tf_op | source)
XLA Modules:
  0.0 83.5 jit_solution(10422216478067448143)
XLA Ops:
  0.7 0.1 pad_add_fusion.me
  0.7 1.6 %shard_map.129 = (bf16[128,1024]{1,0:T(8,128)(2,1)S(1)}, bf16[128,1024]{1,0:T(8,128)(2,1)S(1)}) custom-call(s32[3]{0:T(128)S(1)} %pad_add_fusion.me, bf16[256,1024]{1,0:T(8,128)(2,1)} %bitcast.19), custom_call_target="tpu_custom_call" | custom-call | tf_op jit(solution)/shard_map/pallas_call | solution.py:34
  2.3 3.3 %collective-permute-start = (bf16[128,1024]{1,0:T(8,128)(2,1)S(1)}, bf16[128,1024]{1,0:T(8,128)(2,1)S(1)}, u32[]{:S(2)}, u32[]{:S(2)}) collective-permute-start(bf16[128,1024]{1,0:T(8,128)(2,1)S(1)} %get-tuple-element.24), channel_id=1, source_target_pairs={{0,1},{1,0},{2,3},{3,2},{4,5},{5,4},{6,7},{7,6},{8,9},{9,8},{10,11... | collective-permute-start | bytes 786440 | tf_op jit(solution)/shard_map/ppermute | solution.py:278
  5.7 0.0 collective-permute-start.1
  5.7 1.2 %collective-permute-done.near = bf16[128,1024]{1,0:T(8,128)(2,1)S(1)} collective-permute-done((bf16[128,1024]{1,0:T(8,128)(2,1)S(1)}, bf16[128,1024]{1,0:T(8,128)(2,1)S(1)}, u32[]{:S(2)}, u32[]{:S(2)}) %collective-permute-start) | collective-permute-done | bytes 262176 | tf_op jit(solution)/shard_map/ppermute | solution.py:278
  6.8 4.3 %shard_map.130 = (bf16[512,512]{1,0:T(8,128)(2,1)S(1)}, bf16[512,256]{1,0:T(8,128)(2,1)S(1)}, f32[512,1024]{1,0:T(8,128)S(1)}, f32[100,512]{1,0:T(8,128)S(1)}, f32[100,512]{1,0:T(8,128)S(1)}) custom-call(s32[3]{0:T(128)S(1)} %pad_add_fusion.me, s32[3,512]{1,0:T(4,128)} %nb_in.1, f32[3,512]{1,0:T(4,128)} %ew_in.1, f32[1,100]{1,0:T(1,128)} %bitcast.25, ...), custom_call_target="tpu_custom_call" | custom-call | flops 805306368 | bytes 8000000 | tf_op jit(solution)/shard_map/pallas_call | solution.py:34
  11.1 0.0 copy-start.3
  11.1 0.8 copy-done.3
  11.9 0.0 copy-start.1
  11.9 1.6 %shard_map.131 = (f32[100,512]{1,0:T(8,128)S(1)}, bf16[8,100,512]{2,1,0:T(8,128)(2,1)S(1)}, bf16[512,1024]{1,0:T(8,128)(2,1)S(1)}, f32[512,1]{1,0:T(8,128)S(1)}) custom-call(f32[512,1024]{1,0:T(8,128)S(1)} %get-tuple-element.25.part, bf16[512,256]{1,0:T(8,128)(2,1)S(1)} %get-tuple-element.26.edges, bf16[128,1024]{1,0:T(8,128)(2,1)S(1)} %collective-permute-done.1.far, ...), custom_call_target="tpu_custom_call" | custom-call | flops 373293056 | bytes 5000000 | tf_op jit(solution)/shard_map/pallas_call | solution.py:34
  13.5 13.1 %all_to_all.20.every = bf16[8,100,512]{2,1,0:T(8,128)(2,1)S(1)} all-to-all(bf16[8,100,512]{2,1,0:T(8,128)(2,1)S(1)} %get-tuple-element.29), channel_id=1, replica_groups=mesh['xl'=2,'y'=4,'xh'=2,'z'=8,'c'=2] {'xl','y'}, dimensions={0} | all-to-all | bytes 1638400 | tf_op jit(solution)/shard_map/all_to_all | solution.py:316
  26.6 1.8 %shard_map.132 = (bf16[100,512]{1,0:T(8,128)(2,1)S(1)}, f32[128,512]{1,0:T(8,128)S(1)}, f32[128,512]{1,0:T(8,128)S(1)}) custom-call(s32[3]{0:T(128)S(1)} %pad_add_fusion.me, bf16[8,100,512]{2,1,0:T(8,128)(2,1)S(1)} %all_to_all.20.every, f32[100,512]{1,0:T(8,128)S(1)} %get-tuple-element.30.field, f32[100,512]{1,0:T(8,128)S(1)} %copy-done.1, ...), custom_call_target="tpu_custom_call" | custom-call | flops 209715200 | bytes 4000000 | tf_op jit(solution)/shard_map/pallas_call | solution.py:34
  28.4 7.4 %collective-permute-start.2 = (f32[128,512]{1,0:T(8,128)S(1)}, f32[128,512]{1,0:T(8,128)S(1)}, u32[]{:S(2)}, u32[]{:S(2)}) collective-permute-start(f32[128,512]{1,0:T(8,128)S(1)} %get-tuple-element.34), channel_id=1, source_target_pairs={{0,1},{1,0},{2,3},{3,2},{4,5},{5,4},{6,7},{7,6},{8,9},{9,8},{10,11... | collective-permute-start | bytes 786440 | tf_op jit(solution)/shard_map/ppermute | solution.py:325
  35.8 1.2 %collective-permute-done.2 = f32[128,512]{1,0:T(8,128)S(1)} collective-permute-done((f32[128,512]{1,0:T(8,128)S(1)}, f32[128,512]{1,0:T(8,128)S(1)}, u32[]{:S(2)}, u32[]{:S(2)}) %collective-permute-start.2) | collective-permute-done | bytes 262176 | tf_op jit(solution)/shard_map/ppermute | solution.py:325
  36.9 0.7 add_bitcast_fusion
  37.7 3.7 %all-to-all-start.1 = ((f32[16,8,512]{2,1,0:T(8,128)}), f32[16,8,512]{2,1,0:T(8,128)S(1)}, u32[]{:S(2)}, u32[]{:S(2)}) async-start(f32[16,8,512]{2,1,0:T(8,128)} %add_bitcast_fusion), calls=%async_computation.1 | async-start | bytes 524288 | tf_op jit(solution)/shard_map/all_to_all | solution.py:338
  41.4 0.0 copy-start.4
  41.4 1.0 %copy-done.4 = bf16[512,512]{1,0:T(8,128)(2,1)S(1)} copy-done((bf16[512,512]{1,0:T(8,128)(2,1)S(1)}, bf16[512,512]{1,0:T(8,128)(2,1)}, u32[]{:S(2)}) %copy-start.4) | copy-done | bytes 524312
  42.5 1.8 %shard_map.133 = (f32[256,1024]{1,0:T(8,128)S(1)}, bf16[128,1024]{1,0:T(8,128)(2,1)S(1)}, bf16[128,1024]{1,0:T(8,128)(2,1)S(1)}) custom-call(bf16[100,512]{1,0:T(8,128)(2,1)S(1)} %get-tuple-element.35.fore_grad, bf16[100,1024]{1,0:T(8,128)(2,1)S(1)} %copy-done, bf16[512,1024]{1,0:T(8,128)(2,1)S(1)} %get-tuple-element.32.scaled, f32[1,1024]{1,0:T(1,128)S(1)} %bitcast.18, ...), custom_call_target="tpu_custom_call" | custom-call | flops 641728512 | bytes 6000000 | tf_op jit(solution)/shard_map/pallas_call | solution.py:34
  44.3 0.7 collective-permute-start.3
  45.0 0.2 collective-permute-start.4
  45.3 3.9 %all-to-all-done.1.parts = f32[16,8,512]{2,1,0:T(8,128)S(1)} async-done(((f32[16,8,512]{2,1,0:T(8,128)}), f32[16,8,512]{2,1,0:T(8,128)S(1)}, u32[]{:S(2)}, u32[]{:S(2)}) %all-to-all-start.1) | async-done | bytes 262176 | tf_op jit(solution)/shard_map/all_to_all | solution.py:338
  49.1 0.7 shard_map.134
  49.8 6.4 %all-to-all-start.2 = ((f32[8,8,512]{2,1,0:T(8,128)}), f32[8,8,512]{2,1,0:T(8,128)S(1)}, u32[]{:S(2)}, u32[]{:S(2)}) async-start(f32[8,8,512]{2,1,0:T(8,128)} %shard_map.134), calls=%async_computation.2 | async-start | bytes 262144 | tf_op jit(solution)/shard_map/all_to_all | solution.py:340
  56.2 0.0 collective-permute-done.3.near
  56.2 0.0 collective-permute-done.4.far
  56.2 1.5 %shard_map.135.earlier = bf16[1,256,1024]{2,1,0:T(8,128)(2,1)} custom-call(s32[3]{0:T(128)S(1)} %pad_add_fusion.me, f32[256,1024]{1,0:T(8,128)S(1)} %get-tuple-element.38.earlier.own, bf16[128,1024]{1,0:T(8,128)(2,1)S(1)} %collective-permute-done.3.near, bf16[128,1024]{1,0:T(8,128)(2,1)S(1)} %collective-permute-done.4.far), custom_call_target="tpu_custom_call" | custom-call | tf_op jit(solution)/shard_map/pallas_call | solution.py:34
  57.7 6.5 %all-to-all-done.2.parts = f32[8,8,512]{2,1,0:T(8,128)S(1)} async-done(((f32[8,8,512]{2,1,0:T(8,128)}), f32[8,8,512]{2,1,0:T(8,128)S(1)}, u32[]{:S(2)}, u32[]{:S(2)}) %all-to-all-start.2) | async-done | bytes 131104 | tf_op jit(solution)/shard_map/all_to_all | solution.py:340
  64.3 10.8 %all_to_all.21 = f32[16,8,512]{2,1,0:T(8,128)S(1)} all-to-all(f32[16,8,512]{2,1,0:T(8,128)S(1)} %shard_map.136), channel_id=1, replica_groups=mesh['xl'=2,'y'=4,'xh'=2,'z'=8,'c'=2] {'xl','y','xh'}, dimensions={0} | all-to-all | bytes 524288 | tf_op jit(solution)/shard_map/all_to_all | solution.py:342
  75.1 4.1 %collective-permute-start.5 = (f32[128,512]{1,0:T(8,128)S(1)}, f32[128,512]{1,0:T(8,128)S(1)}, u32[]{:S(2)}, u32[]{:S(2)}) collective-permute-start(f32[128,512]{1,0:T(8,128)S(1)} %bitcast.14), channel_id=1, source_target_pairs={{0,1},{1,0},{2,3},{3,2},{4,5},{5,4},{6,7},{7,6},{8,9},{9,8},{10,11... | collective-permute-start | bytes 786440 | tf_op jit(solution)/shard_map/ppermute | solution.py:343
  79.2 1.2 %collective-permute-done.5.other = f32[128,512]{1,0:T(8,128)S(1)} collective-permute-done((f32[128,512]{1,0:T(8,128)S(1)}, f32[128,512]{1,0:T(8,128)S(1)}, u32[]{:S(2)}, u32[]{:S(2)}) %collective-permute-start.5) | collective-permute-done | bytes 262176 | tf_op jit(solution)/shard_map/ppermute | solution.py:343
  80.4 1.3 %shard_map.137 = (f32[100,1024]{1,0:T(8,128)}, f32[1,1024]{1,0:T(1,128)}, f32[1,1]{1,0:T(1,128)}) custom-call(s32[3]{0:T(128)S(1)} %pad_add_fusion.me, f32[128,512]{1,0:T(8,128)S(1)} %bitcast.15, f32[128,512]{1,0:T(8,128)S(1)} %collective-permute-done.5.other), custom_call_target="tpu_custom_call" | custom-call | tf_op jit(solution)/shard_map/pallas_call | solution.py:34
  (7 shorter events, 0.0 us)
Async XLA Ops:
  0.6 11.3 %copy-start = (bf16[100,1024]{1,0:T(8,128)(2,1)S(1)}, bf16[100,1024]{1,0:T(8,128)(2,1)}, u32[]{:S(2)}) copy-start(bf16[100,1024]{1,0:T(8,128)(2,1)} %proj.5) | copy-start | bytes 614404
  0.6 11.3 %copy-start.2 = (f32[1024]{0:T(1024)S(1)}, f32[1024]{0:T(1024)}, u32[]{:S(2)}) copy-start(f32[1024]{0:T(1024)} %param.19) | copy-start | bytes 12292
  2.3 4.5 %collective-permute-start = (bf16[128,1024]{1,0:T(8,128)(2,1)S(1)}, bf16[128,1024]{1,0:T(8,128)(2,1)S(1)}, u32[]{:S(2)}, u32[]{:S(2)}) collective-permute-start(bf16[128,1024]{1,0:T(8,128)(2,1)S(1)} %get-tuple-element.24), channel_id=1, source_target_pairs={{0,1},{1,0},{2,3},{3,2},{4,5},{5,4},{6,7},{7,6},{8,9},{9,8},{10,11... | collective-permute-start | bytes 786440 | tf_op jit(solution)/shard_map/ppermute | solution.py:278
  5.7 6.2 %collective-permute-start.1 = (bf16[128,1024]{1,0:T(8,128)(2,1)S(1)}, bf16[128,1024]{1,0:T(8,128)(2,1)S(1)}, u32[]{:S(2)}, u32[]{:S(2)}) collective-permute-start(bf16[128,1024]{1,0:T(8,128)(2,1)S(1)} %get-tuple-element.27), channel_id=1, source_target_pairs={{1,2},{3,4},{5,6},{7,8},{9,10},{11,12},{13,14},{15,16},{17,18},{19... | collective-permute-start | bytes 786440 | tf_op jit(solution)/shard_map/ppermute | solution.py:277
  11.1 0.8 copy-start.3
  11.9 14.7 %copy-start.1 = (f32[100,512]{1,0:T(8,128)S(1)}, f32[100,512]{1,0:T(8,128)}, u32[]{:S(2)}) copy-start(f32[100,512]{1,0:T(8,128)} %target.1) | copy-start | bytes 614404
  28.4 8.6 %collective-permute-start.2 = (f32[128,512]{1,0:T(8,128)S(1)}, f32[128,512]{1,0:T(8,128)S(1)}, u32[]{:S(2)}, u32[]{:S(2)}) collective-permute-start(f32[128,512]{1,0:T(8,128)S(1)} %get-tuple-element.34), channel_id=1, source_target_pairs={{0,1},{1,0},{2,3},{3,2},{4,5},{5,4},{6,7},{7,6},{8,9},{9,8},{10,11... | collective-permute-start | bytes 786440 | tf_op jit(solution)/shard_map/ppermute | solution.py:325
  37.7 11.5 %all-to-all-start.1 = ((f32[16,8,512]{2,1,0:T(8,128)}), f32[16,8,512]{2,1,0:T(8,128)S(1)}, u32[]{:S(2)}, u32[]{:S(2)}) async-start(f32[16,8,512]{2,1,0:T(8,128)} %add_bitcast_fusion), calls=%async_computation.1 | async-start | bytes 524288 | tf_op jit(solution)/shard_map/all_to_all | solution.py:338
  41.4 1.0 %copy-start.4 = (bf16[512,512]{1,0:T(8,128)(2,1)S(1)}, bf16[512,512]{1,0:T(8,128)(2,1)}, u32[]{:S(2)}) copy-start(bf16[512,512]{1,0:T(8,128)(2,1)} %copy-done.3) | copy-start | bytes 1572868
  44.3 12.0 %collective-permute-start.3 = (bf16[128,1024]{1,0:T(8,128)(2,1)S(1)}, bf16[128,1024]{1,0:T(8,128)(2,1)S(1)}, u32[]{:S(2)}, u32[]{:S(2)}) collective-permute-start(bf16[128,1024]{1,0:T(8,128)(2,1)S(1)} %get-tuple-element.39), channel_id=1, source_target_pairs={{0,1},{1,0},{2,3},{3,2},{4,5},{5,4},{6,7},{7,6},{8,9},{9,8},{10,11... | collective-permute-start | bytes 786440 | tf_op jit(solution)/shard_map/ppermute | solution.py:333
  45.0 11.2 %collective-permute-start.4 = (bf16[128,1024]{1,0:T(8,128)(2,1)S(1)}, bf16[128,1024]{1,0:T(8,128)(2,1)S(1)}, u32[]{:S(2)}, u32[]{:S(2)}) collective-permute-start(bf16[128,1024]{1,0:T(8,128)(2,1)S(1)} %get-tuple-element.40), channel_id=1, source_target_pairs={{1,2},{3,4},{5,6},{7,8},{9,10},{11,12},{13,14},{15,16},{17,18},{19... | collective-permute-start | bytes 786440 | tf_op jit(solution)/shard_map/ppermute | solution.py:332
  49.8 14.4 %all-to-all-start.2 = ((f32[8,8,512]{2,1,0:T(8,128)}), f32[8,8,512]{2,1,0:T(8,128)S(1)}, u32[]{:S(2)}, u32[]{:S(2)}) async-start(f32[8,8,512]{2,1,0:T(8,128)} %shard_map.134), calls=%async_computation.2 | async-start | bytes 262144 | tf_op jit(solution)/shard_map/all_to_all | solution.py:340
  75.1 5.2 %collective-permute-start.5 = (f32[128,512]{1,0:T(8,128)S(1)}, f32[128,512]{1,0:T(8,128)S(1)}, u32[]{:S(2)}, u32[]{:S(2)}) collective-permute-start(f32[128,512]{1,0:T(8,128)S(1)} %bitcast.14), channel_id=1, source_target_pairs={{0,1},{1,0},{2,3},{3,2},{4,5},{5,4},{6,7},{7,6},{8,9},{9,8},{10,11... | collective-permute-start | bytes 786440 | tf_op jit(solution)/shard_map/ppermute | solution.py:343

commit v3 on v2

--- a/solution.py
+++ b/solution.py
@@ -44,10 +44,11 @@
     return run
 
 
-def cut_kernel(me, latent, first_out, second_out, sems):
+def cut_kernel(latent, first_out, second_out, sems):
     rim = first_out.shape[0]
-    start = pl.multiple_of((1 - me[1]) * rim, rim)
-    other = pl.multiple_of(me[1] * rim, rim)
+    core = lax.axis_index("c")
+    start = pl.multiple_of((1 - core) * rim, rim)
+    other = pl.multiple_of(core * rim, rim)
     one = pltpu.make_async_copy(latent.at[pl.ds(start, rim)], first_out, sems.at[0])
     two = pltpu.make_async_copy(latent.at[pl.ds(other, rim)], second_out, sems.at[1])
     one.start()
@@ -56,9 +57,15 @@
     two.wait()
 
 
+def borrowed_rows(distance):
+    core, slab = lax.axis_index("c"), lax.axis_index(GRID)
+    inner = jnp.logical_and(slab > 0, slab < lax.axis_size(GRID) - 1)
+    return (1 - core) * distance, core * distance, inner
+
+
 def prepare_kernel(
-    me, nb_in, ew_in, vw_in, area_in, latent_in, skip_in, state_in, near,
-    et_out, far_out, part_out, wm_out, state_out,
+    nb_in, ew_in, vw_in, area_in, latent_in, skip_in, state_in, near,
+    far_out, part_out, wm_out, state_out,
     nb, ew, vw, area, latent, skip, state, sems,
 ):
     pairs = (
@@ -73,9 +80,7 @@
     slots, points = nb.shape
     mesh_count = latent.shape[0]
     rim = mesh_count // 2
-    near_start = (1 - me[1]) * (rim + mesh_count)
-    far_start = me[1] * (rim + mesh_count)
-    far_there = me[2] == 1
+    near_start, far_start, far_there = borrowed_rows(rim + mesh_count)
     weights = ew[...]
     weights = weights / jnp.sum(weights, axis=0, keepdims=True)
     rows = nb[...]
@@ -92,13 +97,6 @@
             total = total + jnp.where(
                 lane == ids[:, k : k + 1], columns[:, slots + k : slots + k + 1], 0.0
             )
-        return total
-
-    def edges_turned(start, count):
-        sublane = lax.broadcasted_iota(jnp.int32, (count, points), 0) + start
-        total = jnp.zeros((count, points), F32)
-        for k in range(slots):
-            total = total + jnp.where(sublane == rows[k : k + 1], weights[k : k + 1], 0.0)
         return total
 
     def parts(value):
@@ -120,9 +118,6 @@
     )
     copies[5].wait()
     part_out[...] = skip[...].astype(F32) + mix
-    et_out[:rim] = edges_turned(near_start, rim).astype(BF16)
-    et_out[rim : rim + mesh_count] = edges_turned(rim, mesh_count).astype(BF16)
-    et_out[rim + mesh_count :] = jnp.where(far_there, edges_turned(far_start, rim), 0.0).astype(BF16)
     variables = vw.shape[1]
     diagonal = lax.broadcasted_iota(jnp.int32, (variables, variables), 0) == (
         lax.broadcasted_iota(jnp.int32, (variables, variables), 1)
@@ -153,11 +148,12 @@
         fb_out[m] = low
 
 
-def loss_kernel(me, every, field, target, wm, proj, scaled, gain, fg_out, keep_out, send_out):
+def loss_kernel(every, field, target, wm, proj, scaled, gain, fg_out, keep_out, send_out):
     members, variables, _ = every.shape
     eps_fair = (1.0 - FAIRNESS) / members
     coef_pair = (1.0 - eps_fair) / (members * (members - 1))
     smooth = SMOOTHING * SMOOTHING
+    member = lax.axis_index(MEMBER)
     f = field[...]
     weight_map = wm[...]
     d = f - target[...]
@@ -167,7 +163,7 @@
     pair_total = jnp.full_like(f, -SMOOTHING)
     pair_slope = jnp.zeros_like(f)
     for k in range(members):
-        other = jnp.where(me[0] == k, f, every[k].astype(F32))
+        other = jnp.where(member == k, f, every[k].astype(F32))
         d = f - other
         s = d * d + smooth
         r = lax.rsqrt(s)
@@ -182,7 +178,7 @@
     scaled_grad = dot(fore_grad, proj[...], ((0,), (0,)))
     product = jnp.sum(scaled_grad * values.astype(F32), axis=0, keepdims=True) / gain[...]
     half = wout.shape[1] // 2
-    upper = me[1] == 1
+    upper = lax.axis_index("c") == 1
 
     def store(out, left):
         out[:variables, :] = jnp.where(left, wout[:, :half], wout[:, half:])
@@ -194,7 +190,7 @@
     store(send_out, upper)
 
 
-def back_kernel(fore_grad, proj, scaled, gain, rscale, et, own_out, near_out, far_out):
+def back_kernel(nb, ew, fore_grad, proj, scaled, gain, rscale, own_out, near_out, far_out):
     channels = scaled.shape[1]
     rim = near_out.shape[0]
     mesh_count = own_out.shape[0]
@@ -205,29 +201,44 @@
     second = jnp.sum(scaled_grad * values, axis=1, keepdims=True) / channels
     mixed_grad = rscale[...] * (norm_grad - first - values * (1.0 / gain[...]) * second)
     mixed_grad = mixed_grad.astype(BF16)
-    near_out[...] = dot(et[:rim], mixed_grad, ((1,), (0,))).astype(BF16)
-    far_out[...] = dot(et[rim + mesh_count :], mixed_grad, ((1,), (0,))).astype(BF16)
-    own_out[...] = dot(et[rim : rim + mesh_count], mixed_grad, ((1,), (0,)))
-
-
-def finish_latent_kernel(me, own, near, far, out):
+    weights = ew[...]
+    weights = weights / jnp.sum(weights, axis=0, keepdims=True)
+    rows = nb[...]
+    near_start, far_start, far_there = borrowed_rows(rim + mesh_count)
+
+    def back(start, count, there=None):
+        row = lax.broadcasted_iota(jnp.int32, (count, nb.shape[1]), 0) + start
+        edges = jnp.zeros(row.shape, F32)
+        for k in range(nb.shape[0]):
+            edges = edges + jnp.where(row == rows[k : k + 1], weights[k : k + 1], 0.0)
+        if there is not None:
+            edges = jnp.where(there, edges, 0.0)
+        return dot(edges.astype(BF16), mixed_grad, ((1,), (0,)))
+
+    far_out[...] = back(far_start, rim, far_there).astype(BF16)
+    near_out[...] = back(near_start, rim).astype(BF16)
+    own_out[...] = back(rim, mesh_count)
+
+
+def finish_latent_kernel(own, near, far, earlier, out):
     rim = near.shape[0]
     a, b = near[...].astype(F32), far[...].astype(F32)
-    second = me[1] == 1
+    second = lax.axis_index("c") == 1
     out[0, :rim] = (own[:rim] + jnp.where(second, a, b)).astype(BF16)
     out[0, rim:] = (own[rim:] + jnp.where(second, b, a)).astype(BF16)
 
 
-def fold_kernel(parts, earlier, out):
+def fold_kernel(parts, *rest):
+    out = rest[-1]
     total = jnp.sum(parts[...], axis=0)
     for i in range(out.shape[0]):
         out[i] = total
 
 
-def finish_weights_kernel(me, mine, other, wout_out, gain_out, loss_out):
+def finish_weights_kernel(mine, other, earlier, wout_out, gain_out, loss_out):
     variables, channels = wout_out.shape
     half = channels // 2
-    left = me[1] == 0
+    left = lax.axis_index("c") == 0
     a, b = mine[...], other[...]
     first = jnp.where(left, a, b)
     second = jnp.where(left, b, a)
@@ -264,28 +275,24 @@
     swap = [(0, 1), (1, 0)]
     links = [((i + 1) % slabs, (i + 2) % slabs) for i in range(0, slabs, 2)]
     links = links + [(j, i) for i, j in links]
-    core, slab = lax.axis_index("c"), lax.axis_index(GRID)
-    far_there = jnp.logical_and(slab > 0, slab < slabs - 1)
-    me = jnp.stack([lax.axis_index(MEMBER), core, far_there]).astype(jnp.int32)
 
     near_send, far_send = call(
         cut_kernel,
         [((rim, channels), BF16), ((rim, channels), BF16)],
-        "sh",
+        "h",
         [pltpu.SemaphoreType.DMA((2,))],
-    )(me, latent)
+    )(latent)
     far = lax.ppermute(far_send, GRID, links)
     near = lax.ppermute(near_send, "c", swap)
-    et, edges, part, weight_map, state = call(
+    edges, part, weight_map, state = call(
         prepare_kernel,
         [
-            ((extent, points), BF16),
             ((points, 2 * rim), BF16),
             ((points, channels), F32),
             ((variables, points), F32),
             ((variables, points), F32),
         ],
-        "shhhhhhhv",
+        "hhhhhhhv",
         [
             pltpu.VMEM(neighbours.shape, jnp.int32),
             pltpu.VMEM(edge_weight.shape, F32),
@@ -299,7 +306,7 @@
         flops=6 * points * mesh_count * channels,
         moved=8_000_000,
     )(
-        me, neighbours, edge_weight, variable_weight[None], area_weight[None], latent, skip,
+        neighbours, edge_weight, variable_weight[None], area_weight[None], latent, skip,
         state.reshape(variables, 1, points), near,
     )
     field, copies, scaled, rscale = call(
@@ -317,10 +324,9 @@
     fore_grad, keep, send = call(
         loss_kernel,
         [((variables, points), BF16), ((ROWS, half), F32), ((ROWS, half), F32)],
-        "s",
         flops=4 * points * channels * variables,
         moved=4_000_000,
-    )(me, every, field, target, weight_map, output_projection, scaled, gain)
+    )(every, field, target, weight_map, output_projection, scaled, gain)
 
     met = keep + lax.ppermute(send, "c", swap)
     own, near_grad, far_grad = call(
@@ -328,24 +334,26 @@
         [((mesh_count, channels), F32), ((rim, channels), BF16), ((rim, channels), BF16)],
         flops=2 * points * channels * (extent + variables),
         moved=6_000_000,
-    )(fore_grad, output_projection, scaled, gain, rscale, et)
+    )(neighbours, edge_weight, fore_grad, output_projection, scaled, gain, rscale)
     far_grad = lax.ppermute(far_grad, GRID, links)
     near_grad = lax.ppermute(near_grad, "c", swap)
-    (latent_grad,) = call(finish_latent_kernel, [((1, mesh_count, channels), BF16)], "s")(
-        me, own, near_grad, far_grad
-    )
     depth, rows = lax.axis_size("z"), ROWS // plane
     parts = lax.all_to_all(met.reshape(plane, rows, half), PLANE, 0, 0, tiled=True)
-    (parts,) = call(fold_kernel, [((depth, rows, half), F32)], "va")(parts, own)
+    (parts,) = call(fold_kernel, [((depth, rows, half), F32)], "vaa")(
+        parts, near_grad, far_grad
+    )
     parts = lax.all_to_all(parts, "z", 0, 0, tiled=True)
-    (parts,) = call(fold_kernel, [((plane, rows, half), F32)], "vh")(parts, latent_grad)
+    (parts,) = call(fold_kernel, [((plane, rows, half), F32)])(parts)
     mine = lax.all_to_all(parts, PLANE, 0, 0, tiled=True).reshape(ROWS, half)
     other = lax.ppermute(mine, "c", swap)
+    (latent_grad,) = call(finish_latent_kernel, [((1, mesh_count, channels), BF16)], "vvva")(
+        own, near_grad, far_grad, mine
+    )
     wout, gain_grad, loss = call(
         finish_weights_kernel,
         [((variables, channels), F32), ((1, channels), F32), ((1, 1), F32)],
-        "s",
-    )(me, mine, other)
+        "vvh",
+    )(mine, other, latent_grad)
     fair_crps = loss[0, 0] / (points * slabs * variables)
     return (fair_crps, latent_grad, wout, gain_grad[0])
 

time: 84 us -> 82.9 us (0.987)
  blocking collectives: 23.9 us -> 39.2 us
  starting transfers between devices: 25.9 us -> 18.9 us
  waiting for transfers between devices: 13.9 us -> 10.2 us
  Pallas kernels: 14.6 us -> 10.9 us
  local copies, waits for them, and re-layouts: 1.84 us -> 0.02 us
    all_to_all x0 -> x1, blocking collectives: none -> 15.7 us  [per_device(): parts = lax.all_to_all(parts, 'z', 0, 0, tiled=True)]
    all_to_all x1 -> x0, waiting for transfers between devices: 6.51 us -> none  [per_device(): parts = lax.all_to_all(parts, 'z', 0, 0, tiled=True)]
    all_to_all x1 -> x0, starting transfers between devices: 6.4 us -> none  [per_device(): parts = lax.all_to_all(parts, 'z', 0, 0, tiled=True)]
    pallas_call x9, Pallas kernels: 14.6 us -> 10.9 us  [run(): pl.pallas_call(kernel, out_shape=[jax.ShapeDtypeStruct(s, d) for s, d in...]
    all_to_all x1, waiting for transfers between devices: 3.89 us -> 6.83 us  [per_device(): lax.all_to_all(met.reshape(plane, rows, half), PLANE, 0, 0, tiled=True)]
    unnamed x10, local copies, waits for them, and re-layouts: 1.84 us -> 0.02 us
    ppermute x1, waiting for transfers between devices: 0.01 us -> 1.33 us  [per_device(): far = lax.ppermute(far_send, GRID, links)]
    ppermute x1, waiting for transfers between devices: 1.16 us -> 0.01 us  [per_device(): met = keep + lax.ppermute(send, 'c', swap)]
  transfers between devices with their start and end apart: 8 -> 7, of which waited for: 5 -> 5; matrix products, arithmetic and copies ran while one was open for 0% -> 1% of each run, Pallas kernels for 10% -> 7%
where the time goes in v3:
time: 82.9 us; the launch traced here: 82.5 us
  blocking collectives  39.2 us (47%)
  starting transfers between devices  18.9 us (23%)
  Pallas kernels  10.9 us (13%)
  waiting for transfers between devices  10.2 us (12%)
  between operations  2.53 us (3%)
    all_to_all x1, blocking collectives, per_device(): parts = lax.all_to_all(parts, 'z', 0, 0, tiled=True)  15.7 us
    all_to_all x1, blocking collectives, per_device(): every = lax.all_to_all(copies, MEMBER, 0, 0, tiled=True)  12.6 us
    all_to_all x1, blocking collectives, per_device(): mine = lax.all_to_all(parts, PLANE, 0, 0, tiled=True).reshape(ROWS, half)  11 us
    pallas_call x9, Pallas kernels, run(): pl.pallas_call(kernel, out_shape=[jax.ShapeDtypeStruct(s, d) for s, d in...  10.9 us
    ppermute x1, starting transfers between devices, per_device(): met = keep + lax.ppermute(send, 'c', swap)  7.31 us
    all_to_all x1, waiting for transfers between devices, per_device(): lax.all_to_all(met.reshape(plane, rows, half), PLANE, 0, 0, tiled=True)  6.83 us
    all_to_all x1, starting transfers between devices, per_device(): lax.all_to_all(met.reshape(plane, rows, half), PLANE, 0, 0, tiled=True)  4.38 us
    ppermute x1, starting transfers between devices, per_device(): other = lax.ppermute(mine, 'c', swap)  3.67 us
  transfers between devices with their start and end apart: 7, of which 5 were waited for; matrix products, arithmetic and copies ran while one was open for 1% of the time, Pallas kernels for 7%

profile of v3, /device:TPU:1, one launch (start us, length us, event | category | flops | bytes accessed | tf_op | source)
XLA Modules:
  0.0 82.5 jit_solution(12305912110046041845)
XLA Ops:
  0.6 0.0 copy-start
  0.6 0.0 copy-start.2
  0.7 1.1 %shard_map.129 = (bf16[128,1024]{1,0:T(8,128)(2,1)S(1)}, bf16[128,1024]{1,0:T(8,128)(2,1)S(1)}) custom-call(bf16[256,1024]{1,0:T(8,128)(2,1)} %bitcast.17), custom_call_target="tpu_custom_call" | custom-call | tf_op jit(solution)/shard_map/pallas_call | solution.py:34
  1.8 3.3 %collective-permute-start = (bf16[128,1024]{1,0:T(8,128)(2,1)S(1)}, bf16[128,1024]{1,0:T(8,128)(2,1)S(1)}, u32[]{:S(2)}, u32[]{:S(2)}) collective-permute-start(bf16[128,1024]{1,0:T(8,128)(2,1)S(1)} %get-tuple-element.23), channel_id=1, source_target_pairs={{0,1},{1,0},{2,3},{3,2},{4,5},{5,4},{6,7},{7,6},{8,9},{9,8},{10,11... | collective-permute-start | bytes 786440 | tf_op jit(solution)/shard_map/ppermute | solution.py:286
  5.1 0.0 collective-permute-start.1
  5.1 1.2 %collective-permute-done.near = bf16[128,1024]{1,0:T(8,128)(2,1)S(1)} collective-permute-done((bf16[128,1024]{1,0:T(8,128)(2,1)S(1)}, bf16[128,1024]{1,0:T(8,128)(2,1)S(1)}, u32[]{:S(2)}, u32[]{:S(2)}) %collective-permute-start) | collective-permute-done | bytes 262176 | tf_op jit(solution)/shard_map/ppermute | solution.py:286
  6.2 3.3 %shard_map.130 = (bf16[512,256]{1,0:T(8,128)(2,1)S(1)}, f32[512,1024]{1,0:T(8,128)S(1)}, f32[100,512]{1,0:T(8,128)S(1)}, f32[100,512]{1,0:T(8,128)S(1)}) custom-call(s32[3,512]{1,0:T(4,128)} %nb.1, f32[3,512]{1,0:T(4,128)} %ew.1, f32[1,100]{1,0:T(1,128)} %bitcast.23, f32[1,512]{1,0:T(1,128)} %bitcast.22, bf16[256,1024]{1,0:T(8,128)(2,1)} %bitcast.18, ...), custom_call_target="tpu_custom_call" | custom-call | flops 805306368 | bytes 8000000 | tf_op jit(solution)/shard_map/pallas_call | solution.py:34
  9.5 1.3 %collective-permute-done.1.far = bf16[128,1024]{1,0:T(8,128)(2,1)S(1)} collective-permute-done((bf16[128,1024]{1,0:T(8,128)(2,1)S(1)}, bf16[128,1024]{1,0:T(8,128)(2,1)S(1)}, u32[]{:S(2)}, u32[]{:S(2)}) %collective-permute-start.1) | collective-permute-done | bytes 262176 | tf_op jit(solution)/shard_map/ppermute | solution.py:285
  10.9 0.0 copy-done
  10.9 0.0 copy-done.2
  10.9 1.6 %shard_map.131 = (f32[100,512]{1,0:T(8,128)S(1)}, bf16[8,100,512]{2,1,0:T(8,128)(2,1)S(1)}, bf16[512,1024]{1,0:T(8,128)(2,1)S(1)}, f32[512,1]{1,0:T(8,128)S(1)}) custom-call(f32[512,1024]{1,0:T(8,128)S(1)} %get-tuple-element.24.part, bf16[512,256]{1,0:T(8,128)(2,1)S(1)} %get-tuple-element.25.edges, bf16[128,1024]{1,0:T(8,128)(2,1)S(1)} %collective-permute-done.1.far, ...), custom_call_target="tpu_custom_call" | custom-call | flops 373293056 | bytes 5000000 | tf_op jit(solution)/shard_map/pallas_call | solution.py:34
  12.5 0.0 copy-start.3
  12.5 0.0 copy-start.4
  12.5 12.6 %all_to_all.20.every = bf16[8,100,512]{2,1,0:T(8,128)(2,1)S(1)} all-to-all(bf16[8,100,512]{2,1,0:T(8,128)(2,1)S(1)} %get-tuple-element.28), channel_id=1, replica_groups=mesh['xl'=2,'y'=4,'xh'=2,'z'=8,'c'=2] {'xl','y'}, dimensions={0} | all-to-all | bytes 1638400 | tf_op jit(solution)/shard_map/all_to_all | solution.py:323
  25.1 0.0 copy-done.1
  25.1 1.2 %shard_map.132 = (bf16[100,512]{1,0:T(8,128)(2,1)S(1)}, f32[128,512]{1,0:T(8,128)S(1)}, f32[128,512]{1,0:T(8,128)S(1)}) custom-call(bf16[8,100,512]{2,1,0:T(8,128)(2,1)S(1)} %all_to_all.20.every, f32[100,512]{1,0:T(8,128)S(1)} %get-tuple-element.29.field, f32[100,512]{1,0:T(8,128)S(1)} %copy-done.1, f32[100,512]{1,0:T(8,128)S(1)} %get-tuple-element.30.wm, ...), custom_call_target="tpu_custom_call" | custom-call | flops 209715200 | bytes 4000000 | tf_op jit(solution)/shard_map/pallas_call | solution.py:34
  26.3 7.3 %collective-permute-start.2 = (f32[128,512]{1,0:T(8,128)S(1)}, f32[128,512]{1,0:T(8,128)S(1)}, u32[]{:S(2)}, u32[]{:S(2)}) collective-permute-start(f32[128,512]{1,0:T(8,128)S(1)} %get-tuple-element.33), channel_id=1, source_target_pairs={{0,1},{1,0},{2,3},{3,2},{4,5},{5,4},{6,7},{7,6},{8,9},{9,8},{10,11... | collective-permute-start | bytes 786440 | tf_op jit(solution)/shard_map/ppermute | solution.py:331
  33.6 1.9 %shard_map.133 = (f32[256,1024]{1,0:T(8,128)S(1)}, bf16[128,1024]{1,0:T(8,128)(2,1)S(1)}, bf16[128,1024]{1,0:T(8,128)(2,1)S(1)}) custom-call(s32[3,512]{1,0:T(4,128)S(1)} %copy-done.3, f32[3,512]{1,0:T(4,128)S(1)} %copy-done.4, bf16[100,512]{1,0:T(8,128)(2,1)S(1)} %get-tuple-element.34.fore_grad, bf16[100,1024]{1,0:T(8,128)(2,1)S(1)} %copy-done, ...), custom_call_target="tpu_custom_call" | custom-call | flops 641728512 | bytes 6000000 | tf_op jit(solution)/shard_map/pallas_call | solution.py:34
  35.5 0.1 collective-permute-start.3
  35.7 0.1 collective-permute-start.4
  35.7 0.0 collective-permute-done.2
  35.8 0.7 add_bitcast_fusion
  36.5 4.4 %all-to-all-start.1 = ((f32[16,8,512]{2,1,0:T(8,128)}), f32[16,8,512]{2,1,0:T(8,128)S(1)}, u32[]{:S(2)}, u32[]{:S(2)}) async-start(f32[16,8,512]{2,1,0:T(8,128)} %add_bitcast_fusion), calls=%async_computation.1 | async-start | bytes 524288 | tf_op jit(solution)/shard_map/all_to_all | solution.py:341
  40.9 0.0 collective-permute-done.3.rest_0_.near
  40.9 0.6 collective-permute-done.4.rest_1_.far
  41.5 6.8 %all-to-all-done.1.parts = f32[16,8,512]{2,1,0:T(8,128)S(1)} async-done(((f32[16,8,512]{2,1,0:T(8,128)}), f32[16,8,512]{2,1,0:T(8,128)S(1)}, u32[]{:S(2)}, u32[]{:S(2)}) %all-to-all-start.1) | async-done | bytes 262176 | tf_op jit(solution)/shard_map/all_to_all | solution.py:341
  48.4 15.7 %all_to_all.21.parts = f32[8,8,512]{2,1,0:T(8,128)S(1)} all-to-all(f32[8,8,512]{2,1,0:T(8,128)S(1)} %shard_map.134), channel_id=1, replica_groups=mesh['xl'=2,'y'=4,'xh'=2,'z'=8,'c'=2] {'z'}, dimensions={0} | all-to-all | bytes 262144 | tf_op jit(solution)/shard_map/all_to_all | solution.py:345
  64.1 11.0 %all_to_all.22 = f32[16,8,512]{2,1,0:T(8,128)S(1)} all-to-all(f32[16,8,512]{2,1,0:T(8,128)S(1)} %shard_map.135), channel_id=1, replica_groups=mesh['xl'=2,'y'=4,'xh'=2,'z'=8,'c'=2] {'xl','y','xh'}, dimensions={0} | all-to-all | bytes 524288 | tf_op jit(solution)/shard_map/all_to_all | solution.py:347
  75.1 3.7 %collective-permute-start.5 = (f32[128,512]{1,0:T(8,128)S(1)}, f32[128,512]{1,0:T(8,128)S(1)}, u32[]{:S(2)}, u32[]{:S(2)}) collective-permute-start(f32[128,512]{1,0:T(8,128)S(1)} %bitcast.11), channel_id=1, source_target_pairs={{0,1},{1,0},{2,3},{3,2},{4,5},{5,4},{6,7},{7,6},{8,9},{9,8},{10,11... | collective-permute-start | bytes 786440 | tf_op jit(solution)/shard_map/ppermute | solution.py:348
  78.8 1.0 %shard_map.136.earlier = bf16[1,256,1024]{2,1,0:T(8,128)(2,1)} custom-call(f32[256,1024]{1,0:T(8,128)S(1)} %get-tuple-element.38.own, bf16[128,1024]{1,0:T(8,128)(2,1)S(1)} %collective-permute-done.3.rest_0_.near, bf16[128,1024]{1,0:T(8,128)(2,1)S(1)} %collective-permute-done.4.rest_1_.far, f32[128,512]{1,0:T(8,128)S(1)} %bitcast.12), custom_call_target="tpu_custom_call" | custom-call | tf_op jit(solution)/shard_map/pallas_call | solution.py:34
  79.7 0.2 collective-permute-done.5.other
  79.9 0.8 shard_map.137
  (5 shorter events, 0.1 us)
Async XLA Ops:
  0.6 10.3 %copy-start = (bf16[100,1024]{1,0:T(8,128)(2,1)S(1)}, bf16[100,1024]{1,0:T(8,128)(2,1)}, u32[]{:S(2)}) copy-start(bf16[100,1024]{1,0:T(8,128)(2,1)} %proj.5) | copy-start | bytes 614404
  0.6 10.2 %copy-start.2 = (f32[1024]{0:T(1024)S(1)}, f32[1024]{0:T(1024)}, u32[]{:S(2)}) copy-start(f32[1024]{0:T(1024)} %param.19) | copy-start | bytes 12292
  1.8 4.5 %collective-permute-start = (bf16[128,1024]{1,0:T(8,128)(2,1)S(1)}, bf16[128,1024]{1,0:T(8,128)(2,1)S(1)}, u32[]{:S(2)}, u32[]{:S(2)}) collective-permute-start(bf16[128,1024]{1,0:T(8,128)(2,1)S(1)} %get-tuple-element.23), channel_id=1, source_target_pairs={{0,1},{1,0},{2,3},{3,2},{4,5},{5,4},{6,7},{7,6},{8,9},{9,8},{10,11... | collective-permute-start | bytes 786440 | tf_op jit(solution)/shard_map/ppermute | solution.py:286
  5.1 5.8 %collective-permute-start.1 = (bf16[128,1024]{1,0:T(8,128)(2,1)S(1)}, bf16[128,1024]{1,0:T(8,128)(2,1)S(1)}, u32[]{:S(2)}, u32[]{:S(2)}) collective-permute-start(bf16[128,1024]{1,0:T(8,128)(2,1)S(1)} %get-tuple-element.26), channel_id=1, source_target_pairs={{1,2},{3,4},{5,6},{7,8},{9,10},{11,12},{13,14},{15,16},{17,18},{19... | collective-permute-start | bytes 786440 | tf_op jit(solution)/shard_map/ppermute | solution.py:285
  10.9 14.2 %copy-start.1 = (f32[100,512]{1,0:T(8,128)S(1)}, f32[100,512]{1,0:T(8,128)}, u32[]{:S(2)}) copy-start(f32[100,512]{1,0:T(8,128)} %target.1) | copy-start | bytes 614404
  12.5 21.1 %copy-start.3 = (s32[3,512]{1,0:T(4,128)S(1)}, s32[3,512]{1,0:T(4,128)}, u32[]{:S(2)}) copy-start(s32[3,512]{1,0:T(4,128)} %nb.1) | copy-start | bytes 18436
  12.5 21.1 %copy-start.4 = (f32[3,512]{1,0:T(4,128)S(1)}, f32[3,512]{1,0:T(4,128)}, u32[]{:S(2)}) copy-start(f32[3,512]{1,0:T(4,128)} %ew.1) | copy-start | bytes 18436
  26.3 9.4 %collective-permute-start.2 = (f32[128,512]{1,0:T(8,128)S(1)}, f32[128,512]{1,0:T(8,128)S(1)}, u32[]{:S(2)}, u32[]{:S(2)}) collective-permute-start(f32[128,512]{1,0:T(8,128)S(1)} %get-tuple-element.33), channel_id=1, source_target_pairs={{0,1},{1,0},{2,3},{3,2},{4,5},{5,4},{6,7},{7,6},{8,9},{9,8},{10,11... | collective-permute-start | bytes 786440 | tf_op jit(solution)/shard_map/ppermute | solution.py:331
  35.5 5.3 %collective-permute-start.3 = (bf16[128,1024]{1,0:T(8,128)(2,1)S(1)}, bf16[128,1024]{1,0:T(8,128)(2,1)S(1)}, u32[]{:S(2)}, u32[]{:S(2)}) collective-permute-start(bf16[128,1024]{1,0:T(8,128)(2,1)S(1)} %get-tuple-element.36), channel_id=1, source_target_pairs={{0,1},{1,0},{2,3},{3,2},{4,5},{5,4},{6,7},{7,6},{8,9},{9,8},{10,11... | collective-permute-start | bytes 786440 | tf_op jit(solution)/shard_map/ppermute | solution.py:339
  35.7 5.9 %collective-permute-start.4 = (bf16[128,1024]{1,0:T(8,128)(2,1)S(1)}, bf16[128,1024]{1,0:T(8,128)(2,1)S(1)}, u32[]{:S(2)}, u32[]{:S(2)}) collective-permute-start(bf16[128,1024]{1,0:T(8,128)(2,1)S(1)} %get-tuple-element.37), channel_id=1, source_target_pairs={{1,2},{3,4},{5,6},{7,8},{9,10},{11,12},{13,14},{15,16},{17,18},{19... | collective-permute-start | bytes 786440 | tf_op jit(solution)/shard_map/ppermute | solution.py:338
  36.5 11.9 %all-to-all-start.1 = ((f32[16,8,512]{2,1,0:T(8,128)}), f32[16,8,512]{2,1,0:T(8,128)S(1)}, u32[]{:S(2)}, u32[]{:S(2)}) async-start(f32[16,8,512]{2,1,0:T(8,128)} %add_bitcast_fusion), calls=%async_computation.1 | async-start | bytes 524288 | tf_op jit(solution)/shard_map/all_to_all | solution.py:341
  75.1 4.8 %collective-permute-start.5 = (f32[128,512]{1,0:T(8,128)S(1)}, f32[128,512]{1,0:T(8,128)S(1)}, u32[]{:S(2)}, u32[]{:S(2)}) collective-permute-start(f32[128,512]{1,0:T(8,128)S(1)} %bitcast.11), channel_id=1, source_target_pairs={{0,1},{1,0},{2,3},{3,2},{4,5},{5,4},{6,7},{7,6},{8,9},{9,8},{10,11... | collective-permute-start | bytes 786440 | tf_op jit(solution)/shard_map/ppermute | solution.py:348

commit v4 on v3

--- a/solution.py
+++ b/solution.py
@@ -128,7 +128,7 @@
     state_out[...] = state[:, 0, :]
 
 
-def forward_kernel(part, edges, far, gain, proj, state, f_out, fb_out, sc_out, rs_out):
+def forward_kernel(part, edges, far, gain, proj, state, f_out, sc_out, rs_out):
     rim = far.shape[0]
     borrowed = far[...]
     mixed = (
@@ -141,11 +141,7 @@
     scaled = (centred * rscale * gain[...]).astype(BF16)
     sc_out[...] = scaled
     rs_out[...] = rscale
-    field = state[...] + dot(proj[...], scaled, ((1,), (1,)))
-    f_out[...] = field
-    low = field.astype(BF16)
-    for m in range(fb_out.shape[0]):
-        fb_out[m] = low
+    f_out[...] = state[...] + dot(proj[...], scaled, ((1,), (1,)))
 
 
 def loss_kernel(every, field, target, wm, proj, scaled, gain, fg_out, keep_out, send_out):
@@ -163,7 +159,7 @@
     pair_total = jnp.full_like(f, -SMOOTHING)
     pair_slope = jnp.zeros_like(f)
     for k in range(members):
-        other = jnp.where(member == k, f, every[k].astype(F32))
+        other = jnp.where(member == k, f, every[k])
         d = f - other
         s = d * d + smooth
         r = lax.rsqrt(s)
@@ -190,7 +186,7 @@
     store(send_out, upper)
 
 
-def back_kernel(nb, ew, fore_grad, proj, scaled, gain, rscale, own_out, near_out, far_out):
+def back_kernel(earlier, nb, ew, fore_grad, proj, scaled, gain, rscale, own_out, near_out, far_out):
     channels = scaled.shape[1]
     rim = near_out.shape[0]
     mesh_count = own_out.shape[0]
@@ -220,7 +216,7 @@
     own_out[...] = back(rim, mesh_count)
 
 
-def finish_latent_kernel(own, near, far, earlier, out):
+def finish_latent_kernel(own, near, far, out):
     rim = near.shape[0]
     a, b = near[...].astype(F32), far[...].astype(F32)
     second = lax.axis_index("c") == 1
@@ -235,7 +231,7 @@
         out[i] = total
 
 
-def finish_weights_kernel(mine, other, earlier, wout_out, gain_out, loss_out):
+def finish_weights_kernel(mine, other, wout_out, gain_out, loss_out):
     variables, channels = wout_out.shape
     half = channels // 2
     left = lax.axis_index("c") == 0
@@ -309,18 +305,18 @@
         neighbours, edge_weight, variable_weight[None], area_weight[None], latent, skip,
         state.reshape(variables, 1, points), near,
     )
-    field, copies, scaled, rscale = call(
+    field, scaled, rscale = call(
         forward_kernel,
         [
             ((variables, points), F32),
-            ((members, variables, points), BF16),
             ((points, channels), BF16),
             ((points, 1), F32),
         ],
         flops=2 * points * channels * (2 * rim + variables),
         moved=5_000_000,
     )(part, edges, far, gain, output_projection, state)
-    every = lax.all_to_all(copies, MEMBER, 0, 0, tiled=True)
+    sent = jnp.broadcast_to(field.astype(jnp.float16)[None], (members, variables, points))
+    every = lax.all_to_all(sent, MEMBER, 0, 0, tiled=True).astype(F32)
     fore_grad, keep, send = call(
         loss_kernel,
         [((variables, points), BF16), ((ROWS, half), F32), ((ROWS, half), F32)],
@@ -334,26 +330,24 @@
         [((mesh_count, channels), F32), ((rim, channels), BF16), ((rim, channels), BF16)],
         flops=2 * points * channels * (extent + variables),
         moved=6_000_000,
-    )(neighbours, edge_weight, fore_grad, output_projection, scaled, gain, rscale)
+        spaces="a",
+    )(met, neighbours, edge_weight, fore_grad, output_projection, scaled, gain, rscale)
     far_grad = lax.ppermute(far_grad, GRID, links)
     near_grad = lax.ppermute(near_grad, "c", swap)
+    (latent_grad,) = call(finish_latent_kernel, [((1, mesh_count, channels), BF16)])(
+        own, near_grad, far_grad
+    )
     depth, rows = lax.axis_size("z"), ROWS // plane
     parts = lax.all_to_all(met.reshape(plane, rows, half), PLANE, 0, 0, tiled=True)
-    (parts,) = call(fold_kernel, [((depth, rows, half), F32)], "vaa")(
-        parts, near_grad, far_grad
-    )
+    (parts,) = call(fold_kernel, [((depth, rows, half), F32)], "va")(parts, own)
     parts = lax.all_to_all(parts, "z", 0, 0, tiled=True)
-    (parts,) = call(fold_kernel, [((plane, rows, half), F32)])(parts)
+    (parts,) = call(fold_kernel, [((plane, rows, half), F32)], "vh")(parts, latent_grad)
     mine = lax.all_to_all(parts, PLANE, 0, 0, tiled=True).reshape(ROWS, half)
     other = lax.ppermute(mine, "c", swap)
-    (latent_grad,) = call(finish_latent_kernel, [((1, mesh_count, channels), BF16)], "vvva")(
-        own, near_grad, far_grad, mine
-    )
     wout, gain_grad, loss = call(
         finish_weights_kernel,
         [((variables, channels), F32), ((1, channels), F32), ((1, 1), F32)],
-        "vvh",
-    )(mine, other, latent_grad)
+    )(mine, other)
     fair_crps = loss[0, 0] / (points * slabs * variables)
     return (fair_crps, latent_grad, wout, gain_grad[0])
 

time: 82.9 us -> 82.6 us (level)
  blocking collectives: 39.2 us -> 23 us
  starting transfers between devices: 18.9 us -> 27.4 us
  waiting for transfers between devices: 10.2 us -> 16.5 us
    all_to_all x2 -> x1, blocking collectives: 28.2 us -> 12.7 us  [per_device(): every = lax.all_to_all(sent, MEMBER, 0, 0, tiled=True).astype(F32)]
    all_to_all x0 -> x1, starting transfers between devices: none -> 7.27 us  [per_device(): parts = lax.all_to_all(parts, 'z', 0, 0, tiled=True)]
    all_to_all x0 -> x1, waiting for transfers between devices: none -> 7.04 us  [per_device(): parts = lax.all_to_all(parts, 'z', 0, 0, tiled=True)]
    all_to_all x1, waiting for transfers between devices: 6.83 us -> 4.68 us  [per_device(): lax.all_to_all(met.reshape(plane, rows, half), PLANE, 0, 0, tiled=True)]
    ppermute x1, waiting for transfers between devices: 0.01 us -> 1.16 us  [per_device(): met = keep + lax.ppermute(send, 'c', swap)]
    ppermute x1, waiting for transfers between devices: 0.2 us -> 1.16 us  [per_device(): other = lax.ppermute(mine, 'c', swap)]
    ppermute x1, starting transfers between devices: 3.67 us -> 4.62 us  [per_device(): other = lax.ppermute(mine, 'c', swap)]
  transfers between devices with their start and end apart: 7 -> 8, of which waited for: 5 -> 6; matrix products, arithmetic and copies ran while one was open for 1% -> 0% of each run, Pallas kernels for 7% -> 8%
where the time goes in v4:
time: 82.6 us; the launch traced here: 82.1 us
  starting transfers between devices  27.4 us (33%)
  blocking collectives  23 us (28%)
  waiting for transfers between devices  16.5 us (20%)
  Pallas kernels  11.5 us (14%)
  between operations  2.57 us (3%)
  other arithmetic  0.98 us (1%)
    all_to_all x1, blocking collectives, per_device(): every = lax.all_to_all(sent, MEMBER, 0, 0, tiled=True).astype(F32)  12.7 us
    pallas_call x9, Pallas kernels, run(): pl.pallas_call(kernel, out_shape=[jax.ShapeDtypeStruct(s, d) for s, d in...  11.5 us
    all_to_all x1, blocking collectives, per_device(): mine = lax.all_to_all(parts, PLANE, 0, 0, tiled=True).reshape(ROWS, half)  10.3 us
    ppermute x1, starting transfers between devices, per_device(): met = keep + lax.ppermute(send, 'c', swap)  7.31 us
    all_to_all x1, starting transfers between devices, per_device(): parts = lax.all_to_all(parts, 'z', 0, 0, tiled=True)  7.27 us
    all_to_all x1, waiting for transfers between devices, per_device(): parts = lax.all_to_all(parts, 'z', 0, 0, tiled=True)  7.04 us
    all_to_all x1, waiting for transfers between devices, per_device(): lax.all_to_all(met.reshape(plane, rows, half), PLANE, 0, 0, tiled=True)  4.68 us
    ppermute x1, starting transfers between devices, per_device(): other = lax.ppermute(mine, 'c', swap)  4.62 us
  transfers between devices with their start and end apart: 8, of which 6 were waited for; matrix products, arithmetic and copies ran while one was open for 0% of the time, Pallas kernels for 8%

profile of v4, /device:TPU:1, one launch (start us, length us, event | category | flops | bytes accessed | tf_op | source)
XLA Modules:
  0.0 82.1 jit_solution(17145247728202619569)
XLA Ops:
  0.7 1.1 %shard_map.129 = (bf16[128,1024]{1,0:T(8,128)(2,1)S(1)}, bf16[128,1024]{1,0:T(8,128)(2,1)S(1)}) custom-call(bf16[256,1024]{1,0:T(8,128)(2,1)} %bitcast.15), custom_call_target="tpu_custom_call" | custom-call | tf_op jit(solution)/shard_map/pallas_call | solution.py:34
  1.8 3.3 %collective-permute-start = (bf16[128,1024]{1,0:T(8,128)(2,1)S(1)}, bf16[128,1024]{1,0:T(8,128)(2,1)S(1)}, u32[]{:S(2)}, u32[]{:S(2)}) collective-permute-start(bf16[128,1024]{1,0:T(8,128)(2,1)S(1)} %get-tuple-element.22), channel_id=1, source_target_pairs={{0,1},{1,0},{2,3},{3,2},{4,5},{5,4},{6,7},{7,6},{8,9},{9,8},{10,11... | collective-permute-start | bytes 786440 | tf_op jit(solution)/shard_map/ppermute | solution.py:282
  5.1 0.0 collective-permute-start.1
  5.1 1.2 %collective-permute-done.near = bf16[128,1024]{1,0:T(8,128)(2,1)S(1)} collective-permute-done((bf16[128,1024]{1,0:T(8,128)(2,1)S(1)}, bf16[128,1024]{1,0:T(8,128)(2,1)S(1)}, u32[]{:S(2)}, u32[]{:S(2)}) %collective-permute-start) | collective-permute-done | bytes 262176 | tf_op jit(solution)/shard_map/ppermute | solution.py:282
  6.2 3.3 %shard_map.130 = (bf16[512,256]{1,0:T(8,128)(2,1)S(1)}, f32[512,1024]{1,0:T(8,128)S(1)}, f32[100,512]{1,0:T(8,128)S(1)}, f32[100,512]{1,0:T(8,128)S(1)}) custom-call(s32[3,512]{1,0:T(4,128)} %nb.1, f32[3,512]{1,0:T(4,128)} %ew.1, f32[1,100]{1,0:T(1,128)} %bitcast.21, f32[1,512]{1,0:T(1,128)} %bitcast.20, bf16[256,1024]{1,0:T(8,128)(2,1)} %bitcast.16, ...), custom_call_target="tpu_custom_call" | custom-call | flops 805306368 | bytes 8000000 | tf_op jit(solution)/shard_map/pallas_call | solution.py:34
  9.5 1.3 %collective-permute-done.1.far = bf16[128,1024]{1,0:T(8,128)(2,1)S(1)} collective-permute-done((bf16[128,1024]{1,0:T(8,128)(2,1)S(1)}, bf16[128,1024]{1,0:T(8,128)(2,1)S(1)}, u32[]{:S(2)}, u32[]{:S(2)}) %collective-permute-start.1) | collective-permute-done | bytes 262176 | tf_op jit(solution)/shard_map/ppermute | solution.py:281
  10.9 1.6 %shard_map.131 = (f32[100,512]{1,0:T(8,128)S(1)}, bf16[512,1024]{1,0:T(8,128)(2,1)S(1)}, f32[512,1]{1,0:T(8,128)S(1)}) custom-call(f32[512,1024]{1,0:T(8,128)S(1)} %get-tuple-element.23.part, bf16[512,256]{1,0:T(8,128)(2,1)S(1)} %get-tuple-element.24.edges, bf16[128,1024]{1,0:T(8,128)(2,1)S(1)} %collective-permute-done.1.far, f32[1,1024]{1,0:T(1,128)S(1)} %bitcast.12, ...), custom_call_target="tpu_custom_call" | custom-call | flops 373293056 | bytes 5000000 | tf_op jit(solution)/shard_map/pallas_call | solution.py:34
  12.5 0.1 broadcast_in_dim.18
  12.5 0.0 copy-start.1
  12.6 12.7 %all_to_all.20 = f16[8,100,512]{2,1,0:T(8,128)(2,1)S(1)} all-to-all(f16[8,100,512]{2,1,0:T(8,128)(2,1)S(1)} %broadcast_in_dim.18), channel_id=1, replica_groups=mesh['xl'=2,'y'=4,'xh'=2,'z'=8,'c'=2] {'xl','y'}, dimensions={0} | all-to-all | bytes 1638400 | tf_op jit(solution)/shard_map/all_to_all | solution.py:319
  25.3 0.2 convert_element_type.7.every
  25.5 0.0 copy-start.3
  25.5 0.0 copy-start.4
  25.5 1.2 %shard_map.132 = (bf16[100,512]{1,0:T(8,128)(2,1)S(1)}, f32[128,512]{1,0:T(8,128)S(1)}, f32[128,512]{1,0:T(8,128)S(1)}) custom-call(f32[8,100,512]{2,1,0:T(8,128)S(1)} %convert_element_type.7.every, f32[100,512]{1,0:T(8,128)S(1)} %get-tuple-element.27.field, f32[100,512]{1,0:T(8,128)S(1)} %copy-done.1, f32[100,512]{1,0:T(8,128)S(1)} %get-tuple-element.28.wm, ...), custom_call_target="tpu_custom_call" | custom-call | flops 209715200 | bytes 4000000 | tf_op jit(solution)/shard_map/pallas_call | solution.py:34
  26.7 7.3 %collective-permute-start.2 = (f32[128,512]{1,0:T(8,128)S(1)}, f32[128,512]{1,0:T(8,128)S(1)}, u32[]{:S(2)}, u32[]{:S(2)}) collective-permute-start(f32[128,512]{1,0:T(8,128)S(1)} %get-tuple-element.31), channel_id=1, source_target_pairs={{0,1},{1,0},{2,3},{3,2},{4,5},{5,4},{6,7},{7,6},{8,9},{9,8},{10,11... | collective-permute-start | bytes 786440 | tf_op jit(solution)/shard_map/ppermute | solution.py:327
  34.0 1.2 %collective-permute-done.2 = f32[128,512]{1,0:T(8,128)S(1)} collective-permute-done((f32[128,512]{1,0:T(8,128)S(1)}, f32[128,512]{1,0:T(8,128)S(1)}, u32[]{:S(2)}, u32[]{:S(2)}) %collective-permute-start.2) | collective-permute-done | bytes 262176 | tf_op jit(solution)/shard_map/ppermute | solution.py:327
  35.2 0.7 add.3.earlier
  35.9 3.7 %all-to-all-start.1 = ((f32[16,8,512]{2,1,0:T(8,128)}), f32[16,8,512]{2,1,0:T(8,128)S(1)}, u32[]{:S(2)}, u32[]{:S(2)}) async-start(f32[16,8,512]{2,1,0:T(8,128)} %bitcast.6), calls=%async_computation.1 | async-start | bytes 524288 | tf_op jit(solution)/shard_map/all_to_all | solution.py:341
  39.7 1.9 %shard_map.133 = (f32[256,1024]{1,0:T(8,128)S(1)}, bf16[128,1024]{1,0:T(8,128)(2,1)S(1)}, bf16[128,1024]{1,0:T(8,128)(2,1)S(1)}) custom-call(f32[128,512]{1,0:T(8,128)} %add.3.earlier, s32[3,512]{1,0:T(4,128)S(1)} %copy-done.3, f32[3,512]{1,0:T(4,128)S(1)} %copy-done.4, bf16[100,512]{1,0:T(8,128)(2,1)S(1)} %get-tuple-element.32.fore_grad, ...), custom_call_target="tpu_custom_call" | custom-call | flops 641728512 | bytes 6000000 | tf_op jit(solution)/shard_map/pallas_call | solution.py:34
  41.6 0.7 collective-permute-start.3
  42.3 0.4 collective-permute-start.4
  42.7 4.7 %all-to-all-done.1.parts = f32[16,8,512]{2,1,0:T(8,128)S(1)} async-done(((f32[16,8,512]{2,1,0:T(8,128)}), f32[16,8,512]{2,1,0:T(8,128)S(1)}, u32[]{:S(2)}, u32[]{:S(2)}) %all-to-all-start.1) | async-done | bytes 262176 | tf_op jit(solution)/shard_map/all_to_all | solution.py:341
  47.4 0.7 shard_map.134
  48.1 7.3 %all-to-all-start.2 = ((f32[8,8,512]{2,1,0:T(8,128)}), f32[8,8,512]{2,1,0:T(8,128)S(1)}, u32[]{:S(2)}, u32[]{:S(2)}) async-start(f32[8,8,512]{2,1,0:T(8,128)} %shard_map.134), calls=%async_computation.2 | async-start | bytes 262144 | tf_op jit(solution)/shard_map/all_to_all | solution.py:343
  55.3 0.0 collective-permute-done.3.near
  55.4 0.0 collective-permute-done.4.far
  55.4 1.0 %shard_map.135.rest_0_ = bf16[1,256,1024]{2,1,0:T(8,128)(2,1)} custom-call(f32[256,1024]{1,0:T(8,128)S(1)} %get-tuple-element.34.rest_0_.own, bf16[128,1024]{1,0:T(8,128)(2,1)S(1)} %collective-permute-done.3.near, bf16[128,1024]{1,0:T(8,128)(2,1)S(1)} %collective-permute-done.4.far), custom_call_target="tpu_custom_call" | custom-call | tf_op jit(solution)/shard_map/pallas_call | solution.py:34
  56.3 7.0 %all-to-all-done.2.parts = f32[8,8,512]{2,1,0:T(8,128)S(1)} async-done(((f32[8,8,512]{2,1,0:T(8,128)}), f32[8,8,512]{2,1,0:T(8,128)S(1)}, u32[]{:S(2)}, u32[]{:S(2)}) %all-to-all-start.2) | async-done | bytes 131104 | tf_op jit(solution)/shard_map/all_to_all | solution.py:343
  63.4 10.3 %all_to_all.21 = f32[16,8,512]{2,1,0:T(8,128)S(1)} all-to-all(f32[16,8,512]{2,1,0:T(8,128)S(1)} %shard_map.136), channel_id=1, replica_groups=mesh['xl'=2,'y'=4,'xh'=2,'z'=8,'c'=2] {'xl','y','xh'}, dimensions={0} | all-to-all | bytes 524288 | tf_op jit(solution)/shard_map/all_to_all | solution.py:345
  73.7 4.6 %collective-permute-start.5 = (f32[128,512]{1,0:T(8,128)S(1)}, f32[128,512]{1,0:T(8,128)S(1)}, u32[]{:S(2)}, u32[]{:S(2)}) collective-permute-start(f32[128,512]{1,0:T(8,128)S(1)} %bitcast.10), channel_id=1, source_target_pairs={{0,1},{1,0},{2,3},{3,2},{4,5},{5,4},{6,7},{7,6},{8,9},{9,8},{10,11... | collective-permute-start | bytes 786440 | tf_op jit(solution)/shard_map/ppermute | solution.py:346
  78.3 1.2 %collective-permute-done.5.other = f32[128,512]{1,0:T(8,128)S(1)} collective-permute-done((f32[128,512]{1,0:T(8,128)S(1)}, f32[128,512]{1,0:T(8,128)S(1)}, u32[]{:S(2)}, u32[]{:S(2)}) %collective-permute-start.5) | collective-permute-done | bytes 262176 | tf_op jit(solution)/shard_map/ppermute | solution.py:346
  79.5 0.8 shard_map.137
  (9 shorter events, 0.1 us)
Async XLA Ops:
  0.6 10.3 %copy-start = (bf16[100,1024]{1,0:T(8,128)(2,1)S(1)}, bf16[100,1024]{1,0:T(8,128)(2,1)}, u32[]{:S(2)}) copy-start(bf16[100,1024]{1,0:T(8,128)(2,1)} %proj.5) | copy-start | bytes 614404
  0.6 10.2 %copy-start.2 = (f32[1024]{0:T(1024)S(1)}, f32[1024]{0:T(1024)}, u32[]{:S(2)}) copy-start(f32[1024]{0:T(1024)} %param.19) | copy-start | bytes 12292
  1.8 4.5 %collective-permute-start = (bf16[128,1024]{1,0:T(8,128)(2,1)S(1)}, bf16[128,1024]{1,0:T(8,128)(2,1)S(1)}, u32[]{:S(2)}, u32[]{:S(2)}) collective-permute-start(bf16[128,1024]{1,0:T(8,128)(2,1)S(1)} %get-tuple-element.22), channel_id=1, source_target_pairs={{0,1},{1,0},{2,3},{3,2},{4,5},{5,4},{6,7},{7,6},{8,9},{9,8},{10,11... | collective-permute-start | bytes 786440 | tf_op jit(solution)/shard_map/ppermute | solution.py:282
  5.1 5.8 %collective-permute-start.1 = (bf16[128,1024]{1,0:T(8,128)(2,1)S(1)}, bf16[128,1024]{1,0:T(8,128)(2,1)S(1)}, u32[]{:S(2)}, u32[]{:S(2)}) collective-permute-start(bf16[128,1024]{1,0:T(8,128)(2,1)S(1)} %get-tuple-element.25), channel_id=1, source_target_pairs={{1,2},{3,4},{5,6},{7,8},{9,10},{11,12},{13,14},{15,16},{17,18},{19... | collective-permute-start | bytes 786440 | tf_op jit(solution)/shard_map/ppermute | solution.py:281
  12.5 13.0 %copy-start.1 = (f32[100,512]{1,0:T(8,128)S(1)}, f32[100,512]{1,0:T(8,128)}, u32[]{:S(2)}) copy-start(f32[100,512]{1,0:T(8,128)} %target.1) | copy-start | bytes 614404
  25.5 14.1 %copy-start.3 = (s32[3,512]{1,0:T(4,128)S(1)}, s32[3,512]{1,0:T(4,128)}, u32[]{:S(2)}) copy-start(s32[3,512]{1,0:T(4,128)} %nb.1) | copy-start | bytes 18436
  25.5 14.1 %copy-start.4 = (f32[3,512]{1,0:T(4,128)S(1)}, f32[3,512]{1,0:T(4,128)}, u32[]{:S(2)}) copy-start(f32[3,512]{1,0:T(4,128)} %ew.1) | copy-start | bytes 18436
  26.7 8.5 %collective-permute-start.2 = (f32[128,512]{1,0:T(8,128)S(1)}, f32[128,512]{1,0:T(8,128)S(1)}, u32[]{:S(2)}, u32[]{:S(2)}) collective-permute-start(f32[128,512]{1,0:T(8,128)S(1)} %get-tuple-element.31), channel_id=1, source_target_pairs={{0,1},{1,0},{2,3},{3,2},{4,5},{5,4},{6,7},{7,6},{8,9},{9,8},{10,11... | collective-permute-start | bytes 786440 | tf_op jit(solution)/shard_map/ppermute | solution.py:327
  35.9 11.5 %all-to-all-start.1 = ((f32[16,8,512]{2,1,0:T(8,128)}), f32[16,8,512]{2,1,0:T(8,128)S(1)}, u32[]{:S(2)}, u32[]{:S(2)}) async-start(f32[16,8,512]{2,1,0:T(8,128)} %bitcast.6), calls=%async_computation.1 | async-start | bytes 524288 | tf_op jit(solution)/shard_map/all_to_all | solution.py:341
  41.6 13.8 %collective-permute-start.3 = (bf16[128,1024]{1,0:T(8,128)(2,1)S(1)}, bf16[128,1024]{1,0:T(8,128)(2,1)S(1)}, u32[]{:S(2)}, u32[]{:S(2)}) collective-permute-start(bf16[128,1024]{1,0:T(8,128)(2,1)S(1)} %get-tuple-element.35), channel_id=1, source_target_pairs={{0,1},{1,0},{2,3},{3,2},{4,5},{5,4},{6,7},{7,6},{8,9},{9,8},{10,11... | collective-permute-start | bytes 786440 | tf_op jit(solution)/shard_map/ppermute | solution.py:336
  42.3 13.0 %collective-permute-start.4 = (bf16[128,1024]{1,0:T(8,128)(2,1)S(1)}, bf16[128,1024]{1,0:T(8,128)(2,1)S(1)}, u32[]{:S(2)}, u32[]{:S(2)}) collective-permute-start(bf16[128,1024]{1,0:T(8,128)(2,1)S(1)} %get-tuple-element.36), channel_id=1, source_target_pairs={{1,2},{3,4},{5,6},{7,8},{9,10},{11,12},{13,14},{15,16},{17,18},{19... | collective-permute-start | bytes 786440 | tf_op jit(solution)/shard_map/ppermute | solution.py:335
  48.1 15.3 %all-to-all-start.2 = ((f32[8,8,512]{2,1,0:T(8,128)}), f32[8,8,512]{2,1,0:T(8,128)S(1)}, u32[]{:S(2)}, u32[]{:S(2)}) async-start(f32[8,8,512]{2,1,0:T(8,128)} %shard_map.134), calls=%async_computation.2 | async-start | bytes 262144 | tf_op jit(solution)/shard_map/all_to_all | solution.py:343
  73.7 5.8 %collective-permute-start.5 = (f32[128,512]{1,0:T(8,128)S(1)}, f32[128,512]{1,0:T(8,128)S(1)}, u32[]{:S(2)}, u32[]{:S(2)}) collective-permute-start(f32[128,512]{1,0:T(8,128)S(1)} %bitcast.10), channel_id=1, source_target_pairs={{0,1},{1,0},{2,3},{3,2},{4,5},{5,4},{6,7},{7,6},{8,9},{9,8},{10,11... | collective-permute-start | bytes 786440 | tf_op jit(solution)/shard_map/ppermute | solution.py:346

commit v5 on v4

--- a/solution.py
+++ b/solution.py
@@ -1,3 +1,5 @@
+import functools
+
 import jax
 import jax.numpy as jnp
 from jax import lax
@@ -12,7 +14,7 @@
 MEMBER = ("xl", "y")
 GRID = ("xh", "z", "c")
 PLANE = ("xl", "y", "xh")
-ROWS = 128
+CHUNK = 8
 BF16 = jnp.bfloat16
 F32 = jnp.float32
 VMEM_LIMIT = 24 * 1024 * 1024
@@ -144,7 +146,7 @@
     f_out[...] = state[...] + dot(proj[...], scaled, ((1,), (1,)))
 
 
-def loss_kernel(every, field, target, wm, proj, scaled, gain, fg_out, keep_out, send_out):
+def loss_kernel(every, field, target, wm, proj, scaled, gain, fg_out, parts_out):
     members, variables, _ = every.shape
     eps_fair = (1.0 - FAIRNESS) / members
     coef_pair = (1.0 - eps_fair) / (members * (members - 1))
@@ -173,20 +175,27 @@
     wout = dot(fore_grad, values, ((1,), (0,)))
     scaled_grad = dot(fore_grad, proj[...], ((0,), (0,)))
     product = jnp.sum(scaled_grad * values.astype(F32), axis=0, keepdims=True) / gain[...]
-    half = wout.shape[1] // 2
-    upper = lax.axis_index("c") == 1
-
-    def store(out, left):
-        out[:variables, :] = jnp.where(left, wout[:, :half], wout[:, half:])
-        out[variables : variables + 1, :] = jnp.where(left, product[:, :half], product[:, half:])
-        out[variables + 1 : variables + 2, :] = jnp.broadcast_to(loss, (1, half))
-        out[variables + 2 :, :] = jnp.zeros((ROWS - variables - 2, half), F32)
-
-    store(keep_out, jnp.logical_not(upper))
-    store(send_out, upper)
-
-
-def back_kernel(earlier, nb, ew, fore_grad, proj, scaled, gain, rscale, own_out, near_out, far_out):
+    last = variables // CHUNK
+    for i in range(last):
+        parts_out[i] = wout[i * CHUNK : (i + 1) * CHUNK].astype(BF16)
+    channels = wout.shape[1]
+    high = loss.astype(BF16).astype(F32)
+    rest = variables - last * CHUNK
+    parts_out[last] = jnp.concatenate(
+        [
+            wout[last * CHUNK :],
+            product,
+            jnp.broadcast_to(high, (1, channels)),
+            jnp.broadcast_to(loss - high, (1, channels)),
+            jnp.zeros((CHUNK - rest - 3, channels), F32),
+        ],
+        axis=0,
+    ).astype(BF16)
+    for i in range(last + 1, parts_out.shape[0]):
+        parts_out[i] = jnp.zeros((CHUNK, channels), BF16)
+
+
+def back_kernel(nb, ew, fore_grad, proj, scaled, gain, rscale, own_out, near_out, far_out):
     channels = scaled.shape[1]
     rim = near_out.shape[0]
     mesh_count = own_out.shape[0]
@@ -224,25 +233,43 @@
     out[0, rim:] = (own[rim:] + jnp.where(second, b, a)).astype(BF16)
 
 
-def fold_kernel(parts, *rest):
-    out = rest[-1]
-    total = jnp.sum(parts[...], axis=0)
+def narrowed(total, variables):
+    here = lax.axis_index(PLANE) == variables // CHUNK
+    first = variables % CHUNK + 1
+    loss = total[first : first + 1] + total[first + 1 : first + 2]
+    high = loss.astype(BF16).astype(F32)
+    row = lax.broadcasted_iota(jnp.int32, total.shape, 0)
+    split = jnp.where(row == first, high, jnp.where(row == first + 1, loss - high, total))
+    return jnp.where(here, split, total).astype(BF16)
+
+
+def fold_kernel(parts, earlier, out):
+    out[...] = jnp.sum(parts[...].astype(F32), axis=0)
+
+
+def pair_kernel(variables, mine, met, earlier, out):
+    total = narrowed(mine[...] + met[...], variables)
     for i in range(out.shape[0]):
         out[i] = total
 
 
-def finish_weights_kernel(mine, other, wout_out, gain_out, loss_out):
-    variables, channels = wout_out.shape
-    half = channels // 2
-    left = lax.axis_index("c") == 0
-    a, b = mine[...], other[...]
-    first = jnp.where(left, a, b)
-    second = jnp.where(left, b, a)
-    wout_out[:, :half] = first[:variables]
-    wout_out[:, half:] = second[:variables]
-    gain_out[:, :half] = first[variables : variables + 1]
-    gain_out[:, half:] = second[variables : variables + 1]
-    loss_out[...] = first[variables + 1 : variables + 2, :1]
+def spread_kernel(variables, parts, out):
+    total = narrowed(jnp.sum(parts[...].astype(F32), axis=0), variables)
+    for i in range(out.shape[0]):
+        out[i] = total
+
+
+def finish_weights_kernel(count, parts, wout_out, gain_out, loss_out):
+    variables = wout_out.shape[0]
+    last = variables // CHUNK
+    for i in range(last):
+        wout_out[i * CHUNK : (i + 1) * CHUNK] = parts[i].astype(F32)
+    chunk = parts[last].astype(F32)
+    rest = variables - last * CHUNK
+    wout_out[last * CHUNK :] = chunk[:rest]
+    gain_out[...] = chunk[rest : rest + 1]
+    loss = chunk[rest + 1 : rest + 2, :1] + chunk[rest + 2 : rest + 3, :1]
+    loss_out[...] = loss * (1.0 / count)
 
 
 def per_device(
@@ -266,7 +293,6 @@
     members = lax.axis_size(MEMBER)
     slabs = lax.axis_size(GRID)
     plane = lax.axis_size(PLANE)
-    half = channels // 2
     gain = layer_norm_gain[None]
     swap = [(0, 1), (1, 0)]
     links = [((i + 1) % slabs, (i + 2) % slabs) for i in range(0, slabs, 2)]
@@ -317,39 +343,41 @@
     )(part, edges, far, gain, output_projection, state)
     sent = jnp.broadcast_to(field.astype(jnp.float16)[None], (members, variables, points))
     every = lax.all_to_all(sent, MEMBER, 0, 0, tiled=True).astype(F32)
-    fore_grad, keep, send = call(
+    fore_grad, parts = call(
         loss_kernel,
-        [((variables, points), BF16), ((ROWS, half), F32), ((ROWS, half), F32)],
+        [((variables, points), BF16), ((plane, CHUNK, channels), BF16)],
         flops=4 * points * channels * variables,
         moved=4_000_000,
     )(every, field, target, weight_map, output_projection, scaled, gain)
 
-    met = keep + lax.ppermute(send, "c", swap)
     own, near_grad, far_grad = call(
         back_kernel,
         [((mesh_count, channels), F32), ((rim, channels), BF16), ((rim, channels), BF16)],
         flops=2 * points * channels * (extent + variables),
         moved=6_000_000,
-        spaces="a",
-    )(met, neighbours, edge_weight, fore_grad, output_projection, scaled, gain, rscale)
+    )(neighbours, edge_weight, fore_grad, output_projection, scaled, gain, rscale)
     far_grad = lax.ppermute(far_grad, GRID, links)
     near_grad = lax.ppermute(near_grad, "c", swap)
     (latent_grad,) = call(finish_latent_kernel, [((1, mesh_count, channels), BF16)])(
         own, near_grad, far_grad
     )
-    depth, rows = lax.axis_size("z"), ROWS // plane
-    parts = lax.all_to_all(met.reshape(plane, rows, half), PLANE, 0, 0, tiled=True)
-    (parts,) = call(fold_kernel, [((depth, rows, half), F32)], "va")(parts, own)
+    parts = lax.all_to_all(parts, PLANE, 0, 0, tiled=True)
+    (mine,) = call(fold_kernel, [((CHUNK, channels), F32)], "va")(parts, own)
+    met = lax.ppermute(mine, "c", swap)
+    depth = lax.axis_size("z")
+    (parts,) = call(
+        functools.partial(pair_kernel, variables), [((depth, CHUNK, channels), BF16)], "vvh"
+    )(mine, met, latent_grad)
     parts = lax.all_to_all(parts, "z", 0, 0, tiled=True)
-    (parts,) = call(fold_kernel, [((plane, rows, half), F32)], "vh")(parts, latent_grad)
-    mine = lax.all_to_all(parts, PLANE, 0, 0, tiled=True).reshape(ROWS, half)
-    other = lax.ppermute(mine, "c", swap)
-    wout, gain_grad, loss = call(
-        finish_weights_kernel,
+    (parts,) = call(
+        functools.partial(spread_kernel, variables), [((plane, CHUNK, channels), BF16)]
+    )(parts)
+    parts = lax.all_to_all(parts, PLANE, 0, 0, tiled=True)
+    wout, gain_grad, crps = call(
+        functools.partial(finish_weights_kernel, points * slabs * variables),
         [((variables, channels), F32), ((1, channels), F32), ((1, 1), F32)],
-    )(mine, other)
-    fair_crps = loss[0, 0] / (points * slabs * variables)
-    return (fair_crps, latent_grad, wout, gain_grad[0])
+    )(parts)
+    return (crps[0, 0], latent_grad, wout, gain_grad[0])
 
 
 def solution(mesh):

time: 82.6 us -> 81.4 us (0.985)
  blocking collectives: 23 us -> 43.8 us
  waiting for transfers between devices: 16.5 us -> 2.5 us
  starting transfers between devices: 27.4 us -> 22 us
  between operations: 2.57 us -> 0.78 us
    all_to_all x1 -> x2, blocking collectives: 10.3 us -> 31.1 us  [the longest x1 17 us: per_device(): parts = lax.all_to_all(parts, 'z', 0, 0, tiled=True)]
    all_to_all x2 -> x1, waiting for transfers between devices: 11.7 us -> 0.01 us  [per_device(): parts = lax.all_to_all(parts, PLANE, 0, 0, tiled=True)]
    all_to_all x2 -> x1, starting transfers between devices: 11 us -> 4.57 us  [per_device(): parts = lax.all_to_all(parts, PLANE, 0, 0, tiled=True)]
    ppermute x1, starting transfers between devices: 0.73 us -> 6.74 us  [per_device(): near_grad = lax.ppermute(near_grad, 'c', swap)]
    ppermute x2 -> x1, starting transfers between devices: 11.9 us -> 7.02 us  [per_device(): met = lax.ppermute(mine, 'c', swap)]
    ppermute x2 -> x1, waiting for transfers between devices: 2.32 us -> 0.01 us  [per_device(): met = lax.ppermute(mine, 'c', swap)]
    pallas_call x9 -> x10, Pallas kernels: 11.5 us -> 11.6 us  [run(): pl.pallas_call(kernel, out_shape=[jax.ShapeDtypeStruct(s, d) for s, d in...]
  transfers between devices with their start and end apart: 8 -> 6, of which waited for: 6 -> 2; matrix products, arithmetic and copies ran while one was open for 0% -> 0% of each run, Pallas kernels for 8% -> 8%
where the time goes in v5:
time: 81.4 us; the launch traced here: 81.1 us
  blocking collectives  43.8 us (54%)
  starting transfers between devices  22 us (27%)
  Pallas kernels  11.6 us (14%)
  waiting for transfers between devices  2.5 us (3%)
    all_to_all x1, blocking collectives, per_device(): parts = lax.all_to_all(parts, 'z', 0, 0, tiled=True)  17 us
    all_to_all x1, blocking collectives, per_device(): parts = lax.all_to_all(parts, PLANE, 0, 0, tiled=True)  14.1 us
    all_to_all x1, blocking collectives, per_device(): every = lax.all_to_all(sent, MEMBER, 0, 0, tiled=True).astype(F32)  12.7 us
    pallas_call x10, Pallas kernels, run(): pl.pallas_call(kernel, out_shape=[jax.ShapeDtypeStruct(s, d) for s, d in...  11.6 us
    ppermute x1, starting transfers between devices, per_device(): met = lax.ppermute(mine, 'c', swap)  7.02 us
    ppermute x1, starting transfers between devices, per_device(): near_grad = lax.ppermute(near_grad, 'c', swap)  6.74 us
    all_to_all x1, starting transfers between devices, per_device(): parts = lax.all_to_all(parts, PLANE, 0, 0, tiled=True)  4.57 us
    ppermute x1, starting transfers between devices, per_device(): near = lax.ppermute(near_send, 'c', swap)  3.33 us
  transfers between devices with their start and end apart: 6, of which 2 were waited for; matrix products, arithmetic and copies ran while one was open for 0% of the time, Pallas kernels for 8%

profile of v5, /device:TPU:1, one launch (start us, length us, event | category | flops | bytes accessed | tf_op | source)
XLA Modules:
  0.0 81.1 jit_solution(12610637923695077969)
XLA Ops:
  0.6 0.0 copy-start
  0.6 0.0 copy-start.2
  0.7 1.1 %shard_map.129 = (bf16[128,1024]{1,0:T(8,128)(2,1)S(1)}, bf16[128,1024]{1,0:T(8,128)(2,1)S(1)}) custom-call(bf16[256,1024]{1,0:T(8,128)(2,1)} %bitcast.11), custom_call_target="tpu_custom_call" | custom-call | tf_op jit(solution)/shard_map/pallas_call | solution.py:36
  1.8 3.3 %collective-permute-start = (bf16[128,1024]{1,0:T(8,128)(2,1)S(1)}, bf16[128,1024]{1,0:T(8,128)(2,1)S(1)}, u32[]{:S(2)}, u32[]{:S(2)}) collective-permute-start(bf16[128,1024]{1,0:T(8,128)(2,1)S(1)} %get-tuple-element.21), channel_id=1, source_target_pairs={{0,1},{1,0},{2,3},{3,2},{4,5},{5,4},{6,7},{7,6},{8,9},{9,8},{10,11... | collective-permute-start | bytes 786440 | tf_op jit(solution)/shard_map/ppermute | solution.py:308
  5.1 0.0 collective-permute-start.1
  5.1 1.2 %collective-permute-done.near = bf16[128,1024]{1,0:T(8,128)(2,1)S(1)} collective-permute-done((bf16[128,1024]{1,0:T(8,128)(2,1)S(1)}, bf16[128,1024]{1,0:T(8,128)(2,1)S(1)}, u32[]{:S(2)}, u32[]{:S(2)}) %collective-permute-start) | collective-permute-done | bytes 262176 | tf_op jit(solution)/shard_map/ppermute | solution.py:308
  6.2 3.3 %shard_map.130 = (bf16[512,256]{1,0:T(8,128)(2,1)S(1)}, f32[512,1024]{1,0:T(8,128)S(1)}, f32[100,512]{1,0:T(8,128)S(1)}, f32[100,512]{1,0:T(8,128)S(1)}) custom-call(s32[3,512]{1,0:T(4,128)} %nb.1, f32[3,512]{1,0:T(4,128)} %ew.1, f32[1,100]{1,0:T(1,128)} %bitcast.17, f32[1,512]{1,0:T(1,128)} %bitcast.16, bf16[256,1024]{1,0:T(8,128)(2,1)} %bitcast.12, ...), custom_call_target="tpu_custom_call" | custom-call | flops 805306368 | bytes 8000000 | tf_op jit(solution)/shard_map/pallas_call | solution.py:36
  9.5 1.3 %collective-permute-done.1.far = bf16[128,1024]{1,0:T(8,128)(2,1)S(1)} collective-permute-done((bf16[128,1024]{1,0:T(8,128)(2,1)S(1)}, bf16[128,1024]{1,0:T(8,128)(2,1)S(1)}, u32[]{:S(2)}, u32[]{:S(2)}) %collective-permute-start.1) | collective-permute-done | bytes 262176 | tf_op jit(solution)/shard_map/ppermute | solution.py:307
  10.9 0.0 copy-done
  10.9 0.0 copy-done.2
  10.9 1.6 %shard_map.131 = (f32[100,512]{1,0:T(8,128)S(1)}, bf16[512,1024]{1,0:T(8,128)(2,1)S(1)}, f32[512,1]{1,0:T(8,128)S(1)}) custom-call(f32[512,1024]{1,0:T(8,128)S(1)} %get-tuple-element.22.part, bf16[512,256]{1,0:T(8,128)(2,1)S(1)} %get-tuple-element.23.edges, bf16[128,1024]{1,0:T(8,128)(2,1)S(1)} %collective-permute-done.1.far, f32[1,1024]{1,0:T(1,128)S(1)} %bitcast.8, ...), custom_call_target="tpu_custom_call" | custom-call | flops 373293056 | bytes 5000000 | tf_op jit(solution)/shard_map/pallas_call | solution.py:36
  12.5 0.1 broadcast_in_dim.18
  12.5 0.0 copy-start.1
  12.6 12.7 %all_to_all.20 = f16[8,100,512]{2,1,0:T(8,128)(2,1)S(1)} all-to-all(f16[8,100,512]{2,1,0:T(8,128)(2,1)S(1)} %broadcast_in_dim.18), channel_id=1, replica_groups=mesh['xl'=2,'y'=4,'xh'=2,'z'=8,'c'=2] {'xl','y'}, dimensions={0} | all-to-all | bytes 1638400 | tf_op jit(solution)/shard_map/all_to_all | solution.py:345
  25.3 0.2 convert_element_type.7.every
  25.5 0.0 copy-start.3
  25.5 0.0 copy-start.4
  25.5 0.0 copy-done.1
  25.5 1.9 %shard_map.132 = (bf16[100,512]{1,0:T(8,128)(2,1)S(1)}, bf16[16,8,1024]{2,1,0:T(8,128)(2,1)}) custom-call(f32[8,100,512]{2,1,0:T(8,128)S(1)} %convert_element_type.7.every, f32[100,512]{1,0:T(8,128)S(1)} %get-tuple-element.26.field, f32[100,512]{1,0:T(8,128)S(1)} %copy-done.1, f32[100,512]{1,0:T(8,128)S(1)} %get-tuple-element.27.wm, ...), custom_call_target="tpu_custom_call" | custom-call | flops 209715200 | bytes 4000000 | tf_op jit(solution)/shard_map/pallas_call | solution.py:36
  27.4 4.6 %all-to-all-start.1 = ((bf16[16,8,1024]{2,1,0:T(8,128)(2,1)}), bf16[16,8,1024]{2,1,0:T(8,128)(2,1)S(1)}, u32[]{:S(2)}, u32[]{:S(2)}) async-start(bf16[16,8,1024]{2,1,0:T(8,128)(2,1)} %get-tuple-element.29), calls=%async_computation.1 | async-start | bytes 524288 | tf_op jit(solution)/shard_map/all_to_all | solution.py:364
  32.0 1.9 %shard_map.133 = (f32[256,1024]{1,0:T(8,128)S(1)}, bf16[128,1024]{1,0:T(8,128)(2,1)S(1)}, bf16[128,1024]{1,0:T(8,128)(2,1)S(1)}) custom-call(s32[3,512]{1,0:T(4,128)S(1)} %copy-done.3, f32[3,512]{1,0:T(4,128)S(1)} %copy-done.4, bf16[100,512]{1,0:T(8,128)(2,1)S(1)} %get-tuple-element.30.fore_grad, bf16[100,1024]{1,0:T(8,128)(2,1)S(1)} %copy-done, ...), custom_call_target="tpu_custom_call" | custom-call | flops 641728512 | bytes 6000000 | tf_op jit(solution)/shard_map/pallas_call | solution.py:36
  33.9 6.7 %collective-permute-start.3 = (bf16[128,1024]{1,0:T(8,128)(2,1)S(1)}, bf16[128,1024]{1,0:T(8,128)(2,1)S(1)}, u32[]{:S(2)}, u32[]{:S(2)}) collective-permute-start(bf16[128,1024]{1,0:T(8,128)(2,1)S(1)} %get-tuple-element.33), channel_id=1, source_target_pairs={{0,1},{1,0},{2,3},{3,2},{4,5},{5,4},{6,7},{7,6},{8,9},{9,8},{10,11... | collective-permute-start | bytes 786440 | tf_op jit(solution)/shard_map/ppermute | solution.py:360
  40.7 0.4 collective-permute-start.4
  41.0 0.0 all-to-all-done.1.parts
  41.1 7.0 %collective-permute-start.2 = (f32[8,1024]{1,0:T(8,128)S(1)}, f32[8,1024]{1,0:T(8,128)S(1)}, u32[]{:S(2)}, u32[]{:S(2)}) collective-permute-start(f32[8,1024]{1,0:T(8,128)S(1)} %shard_map.134.mine), channel_id=1, source_target_pairs={{0,1},{1,0},{2,3},{3,2},{4,5},{5,4},{6,7},{7,6},{8,9},{9,8},{10,11... | collective-permute-start | bytes 98312 | tf_op jit(solution)/shard_map/ppermute | solution.py:366
  48.1 0.0 collective-permute-done.3.near
  48.1 0.0 collective-permute-done.4.far
  48.1 1.0 %shard_map.135.earlier = bf16[1,256,1024]{2,1,0:T(8,128)(2,1)} custom-call(f32[256,1024]{1,0:T(8,128)S(1)} %get-tuple-element.32.earlier.own, bf16[128,1024]{1,0:T(8,128)(2,1)S(1)} %collective-permute-done.3.near, bf16[128,1024]{1,0:T(8,128)(2,1)S(1)} %collective-permute-done.4.far), custom_call_target="tpu_custom_call" | custom-call | tf_op jit(solution)/shard_map/pallas_call | solution.py:36
  49.1 0.0 collective-permute-done.2.met
  49.1 17.0 %all_to_all.21.parts = bf16[8,8,1024]{2,1,0:T(8,128)(2,1)S(1)} all-to-all(bf16[8,8,1024]{2,1,0:T(8,128)(2,1)S(1)} %shard_map.136), channel_id=1, replica_groups=mesh['xl'=2,'y'=4,'xh'=2,'z'=8,'c'=2] {'z'}, dimensions={0} | all-to-all | bytes 262144 | tf_op jit(solution)/shard_map/all_to_all | solution.py:371
  66.2 14.1 %all_to_all.22.parts = bf16[16,8,1024]{2,1,0:T(8,128)(2,1)S(1)} all-to-all(bf16[16,8,1024]{2,1,0:T(8,128)(2,1)S(1)} %shard_map.137), channel_id=1, replica_groups=mesh['xl'=2,'y'=4,'xh'=2,'z'=8,'c'=2] {'xl','y','xh'}, dimensions={0} | all-to-all | bytes 524288 | tf_op jit(solution)/shard_map/all_to_all | solution.py:375
  80.3 0.8 shard_map.138
  (6 shorter events, 0.1 us)
Async XLA Ops:
  0.6 10.3 %copy-start = (bf16[100,1024]{1,0:T(8,128)(2,1)S(1)}, bf16[100,1024]{1,0:T(8,128)(2,1)}, u32[]{:S(2)}) copy-start(bf16[100,1024]{1,0:T(8,128)(2,1)} %proj.5) | copy-start | bytes 614404
  0.6 10.2 %copy-start.2 = (f32[1024]{0:T(1024)S(1)}, f32[1024]{0:T(1024)}, u32[]{:S(2)}) copy-start(f32[1024]{0:T(1024)} %param.19) | copy-start | bytes 12292
  1.8 4.5 %collective-permute-start = (bf16[128,1024]{1,0:T(8,128)(2,1)S(1)}, bf16[128,1024]{1,0:T(8,128)(2,1)S(1)}, u32[]{:S(2)}, u32[]{:S(2)}) collective-permute-start(bf16[128,1024]{1,0:T(8,128)(2,1)S(1)} %get-tuple-element.21), channel_id=1, source_target_pairs={{0,1},{1,0},{2,3},{3,2},{4,5},{5,4},{6,7},{7,6},{8,9},{9,8},{10,11... | collective-permute-start | bytes 786440 | tf_op jit(solution)/shard_map/ppermute | solution.py:308
  5.1 5.8 %collective-permute-start.1 = (bf16[128,1024]{1,0:T(8,128)(2,1)S(1)}, bf16[128,1024]{1,0:T(8,128)(2,1)S(1)}, u32[]{:S(2)}, u32[]{:S(2)}) collective-permute-start(bf16[128,1024]{1,0:T(8,128)(2,1)S(1)} %get-tuple-element.24), channel_id=1, source_target_pairs={{1,2},{3,4},{5,6},{7,8},{9,10},{11,12},{13,14},{15,16},{17,18},{19... | collective-permute-start | bytes 786440 | tf_op jit(solution)/shard_map/ppermute | solution.py:307
  12.5 13.0 %copy-start.1 = (f32[100,512]{1,0:T(8,128)S(1)}, f32[100,512]{1,0:T(8,128)}, u32[]{:S(2)}) copy-start(f32[100,512]{1,0:T(8,128)} %target.1) | copy-start | bytes 614404
  25.5 6.5 %copy-start.3 = (s32[3,512]{1,0:T(4,128)S(1)}, s32[3,512]{1,0:T(4,128)}, u32[]{:S(2)}) copy-start(s32[3,512]{1,0:T(4,128)} %nb.1) | copy-start | bytes 18436
  25.5 6.5 %copy-start.4 = (f32[3,512]{1,0:T(4,128)S(1)}, f32[3,512]{1,0:T(4,128)}, u32[]{:S(2)}) copy-start(f32[3,512]{1,0:T(4,128)} %ew.1) | copy-start | bytes 18436
  27.4 13.6 %all-to-all-start.1 = ((bf16[16,8,1024]{2,1,0:T(8,128)(2,1)}), bf16[16,8,1024]{2,1,0:T(8,128)(2,1)S(1)}, u32[]{:S(2)}, u32[]{:S(2)}) async-start(bf16[16,8,1024]{2,1,0:T(8,128)(2,1)} %get-tuple-element.29), calls=%async_computation.1 | async-start | bytes 524288 | tf_op jit(solution)/shard_map/all_to_all | solution.py:364
  33.9 14.2 %collective-permute-start.3 = (bf16[128,1024]{1,0:T(8,128)(2,1)S(1)}, bf16[128,1024]{1,0:T(8,128)(2,1)S(1)}, u32[]{:S(2)}, u32[]{:S(2)}) collective-permute-start(bf16[128,1024]{1,0:T(8,128)(2,1)S(1)} %get-tuple-element.33), channel_id=1, source_target_pairs={{0,1},{1,0},{2,3},{3,2},{4,5},{5,4},{6,7},{7,6},{8,9},{9,8},{10,11... | collective-permute-start | bytes 786440 | tf_op jit(solution)/shard_map/ppermute | solution.py:360
  40.7 7.5 %collective-permute-start.4 = (bf16[128,1024]{1,0:T(8,128)(2,1)S(1)}, bf16[128,1024]{1,0:T(8,128)(2,1)S(1)}, u32[]{:S(2)}, u32[]{:S(2)}) collective-permute-start(bf16[128,1024]{1,0:T(8,128)(2,1)S(1)} %get-tuple-element.34), channel_id=1, source_target_pairs={{1,2},{3,4},{5,6},{7,8},{9,10},{11,12},{13,14},{15,16},{17,18},{19... | collective-permute-start | bytes 786440 | tf_op jit(solution)/shard_map/ppermute | solution.py:359
  41.1 8.0 %collective-permute-start.2 = (f32[8,1024]{1,0:T(8,128)S(1)}, f32[8,1024]{1,0:T(8,128)S(1)}, u32[]{:S(2)}, u32[]{:S(2)}) collective-permute-start(f32[8,1024]{1,0:T(8,128)S(1)} %shard_map.134.mine), channel_id=1, source_target_pairs={{0,1},{1,0},{2,3},{3,2},{4,5},{5,4},{6,7},{7,6},{8,9},{9,8},{10,11... | collective-permute-start | bytes 98312 | tf_op jit(solution)/shard_map/ppermute | solution.py:366

commit v6 on v5

--- a/solution.py
+++ b/solution.py
@@ -247,13 +247,13 @@
     out[...] = jnp.sum(parts[...].astype(F32), axis=0)
 
 
-def pair_kernel(variables, mine, met, earlier, out):
+def pair_kernel(variables, mine, met, out):
     total = narrowed(mine[...] + met[...], variables)
     for i in range(out.shape[0]):
         out[i] = total
 
 
-def spread_kernel(variables, parts, out):
+def spread_kernel(variables, parts, earlier, out):
     total = narrowed(jnp.sum(parts[...].astype(F32), axis=0), variables)
     for i in range(out.shape[0]):
         out[i] = total
@@ -366,12 +366,12 @@
     met = lax.ppermute(mine, "c", swap)
     depth = lax.axis_size("z")
     (parts,) = call(
-        functools.partial(pair_kernel, variables), [((depth, CHUNK, channels), BF16)], "vvh"
-    )(mine, met, latent_grad)
+        functools.partial(pair_kernel, variables), [((depth, CHUNK, channels), BF16)]
+    )(mine, met)
     parts = lax.all_to_all(parts, "z", 0, 0, tiled=True)
     (parts,) = call(
-        functools.partial(spread_kernel, variables), [((plane, CHUNK, channels), BF16)]
-    )(parts)
+        functools.partial(spread_kernel, variables), [((plane, CHUNK, channels), BF16)], "vh"
+    )(parts, latent_grad)
     parts = lax.all_to_all(parts, PLANE, 0, 0, tiled=True)
     wout, gain_grad, crps = call(
         functools.partial(finish_weights_kernel, points * slabs * variables),

time: 81.4 us -> 76.9 us (0.945); the launches traced: 81.1 us -> 75.4 us
  blocking collectives: 43.8 us -> 23.1 us
  waiting for transfers between devices: 2.5 us -> 10.3 us
  starting transfers between devices: 22 us -> 28.6 us
    all_to_all x1 -> x0, blocking collectives: 17 us -> none  [per_device(): parts = lax.all_to_all(parts, 'z', 0, 0, tiled=True)]
    all_to_all x0 -> x1, waiting for transfers between devices: none -> 6.95 us  [per_device(): parts = lax.all_to_all(parts, 'z', 0, 0, tiled=True)]
    all_to_all x0 -> x1, starting transfers between devices: none -> 6.57 us  [per_device(): parts = lax.all_to_all(parts, 'z', 0, 0, tiled=True)]
    all_to_all x1, blocking collectives: 14.1 us -> 10.4 us  [per_device(): parts = lax.all_to_all(parts, PLANE, 0, 0, tiled=True)]
    ppermute x1, waiting for transfers between devices: 0.01 us -> 0.86 us  [per_device(): met = lax.ppermute(mine, 'c', swap)]
  transfers between devices with their start and end apart: 6 -> 7, of which waited for: 2 -> 4; matrix products, arithmetic and copies ran while one was open for 0% -> 0% of each run, Pallas kernels for 8% -> 9%
where the time goes in v6:
time: 76.9 us; the launch traced here: 75.4 us
  starting transfers between devices  28.6 us (37%)
  blocking collectives  23.1 us (30%)
  Pallas kernels  12.2 us (16%)
  waiting for transfers between devices  10.3 us (13%)
  between operations  0.78 us (1%)
    all_to_all x1, blocking collectives, per_device(): every = lax.all_to_all(sent, MEMBER, 0, 0, tiled=True).astype(F32)  12.7 us
    pallas_call x10, Pallas kernels, run(): pl.pallas_call(kernel, out_shape=[jax.ShapeDtypeStruct(s, d) for s, d in...  12.2 us
    all_to_all x1, blocking collectives, per_device(): parts = lax.all_to_all(parts, PLANE, 0, 0, tiled=True)  10.4 us
    ppermute x1, starting transfers between devices, per_device(): met = lax.ppermute(mine, 'c', swap)  7.02 us
    all_to_all x1, waiting for transfers between devices, per_device(): parts = lax.all_to_all(parts, 'z', 0, 0, tiled=True)  6.95 us
    ppermute x1, starting transfers between devices, per_device(): near_grad = lax.ppermute(near_grad, 'c', swap)  6.74 us
    all_to_all x1, starting transfers between devices, per_device(): parts = lax.all_to_all(parts, 'z', 0, 0, tiled=True)  6.57 us
    all_to_all x1, starting transfers between devices, per_device(): parts = lax.all_to_all(parts, PLANE, 0, 0, tiled=True)  4.57 us
  transfers between devices with their start and end apart: 7, of which 4 were waited for; matrix products, arithmetic and copies ran while one was open for 0% of the time, Pallas kernels for 9%

profile of v6, /device:TPU:1, one launch (start us, length us, event | category | flops | bytes accessed | tf_op | source)
XLA Modules:
  0.0 75.4 jit_solution(4101416847868064143)
XLA Ops:
  0.6 0.0 copy-start
  0.6 0.0 copy-start.2
  0.7 1.1 %shard_map.129 = (bf16[128,1024]{1,0:T(8,128)(2,1)S(1)}, bf16[128,1024]{1,0:T(8,128)(2,1)S(1)}) custom-call(bf16[256,1024]{1,0:T(8,128)(2,1)} %bitcast.11), custom_call_target="tpu_custom_call" | custom-call | tf_op jit(solution)/shard_map/pallas_call | solution.py:36
  1.8 3.3 %collective-permute-start = (bf16[128,1024]{1,0:T(8,128)(2,1)S(1)}, bf16[128,1024]{1,0:T(8,128)(2,1)S(1)}, u32[]{:S(2)}, u32[]{:S(2)}) collective-permute-start(bf16[128,1024]{1,0:T(8,128)(2,1)S(1)} %get-tuple-element.21), channel_id=1, source_target_pairs={{0,1},{1,0},{2,3},{3,2},{4,5},{5,4},{6,7},{7,6},{8,9},{9,8},{10,11... | collective-permute-start | bytes 786440 | tf_op jit(solution)/shard_map/ppermute | solution.py:308
  5.1 0.0 collective-permute-start.1
  5.1 1.2 %collective-permute-done.near = bf16[128,1024]{1,0:T(8,128)(2,1)S(1)} collective-permute-done((bf16[128,1024]{1,0:T(8,128)(2,1)S(1)}, bf16[128,1024]{1,0:T(8,128)(2,1)S(1)}, u32[]{:S(2)}, u32[]{:S(2)}) %collective-permute-start) | collective-permute-done | bytes 262176 | tf_op jit(solution)/shard_map/ppermute | solution.py:308
  6.2 3.3 %shard_map.130 = (bf16[512,256]{1,0:T(8,128)(2,1)S(1)}, f32[512,1024]{1,0:T(8,128)S(1)}, f32[100,512]{1,0:T(8,128)S(1)}, f32[100,512]{1,0:T(8,128)S(1)}) custom-call(s32[3,512]{1,0:T(4,128)} %nb.1, f32[3,512]{1,0:T(4,128)} %ew.1, f32[1,100]{1,0:T(1,128)} %bitcast.17, f32[1,512]{1,0:T(1,128)} %bitcast.16, bf16[256,1024]{1,0:T(8,128)(2,1)} %bitcast.12, ...), custom_call_target="tpu_custom_call" | custom-call | flops 805306368 | bytes 8000000 | tf_op jit(solution)/shard_map/pallas_call | solution.py:36
  9.5 1.3 %collective-permute-done.1.far = bf16[128,1024]{1,0:T(8,128)(2,1)S(1)} collective-permute-done((bf16[128,1024]{1,0:T(8,128)(2,1)S(1)}, bf16[128,1024]{1,0:T(8,128)(2,1)S(1)}, u32[]{:S(2)}, u32[]{:S(2)}) %collective-permute-start.1) | collective-permute-done | bytes 262176 | tf_op jit(solution)/shard_map/ppermute | solution.py:307
  10.9 1.6 %shard_map.131 = (f32[100,512]{1,0:T(8,128)S(1)}, bf16[512,1024]{1,0:T(8,128)(2,1)S(1)}, f32[512,1]{1,0:T(8,128)S(1)}) custom-call(f32[512,1024]{1,0:T(8,128)S(1)} %get-tuple-element.22.part, bf16[512,256]{1,0:T(8,128)(2,1)S(1)} %get-tuple-element.23.edges, bf16[128,1024]{1,0:T(8,128)(2,1)S(1)} %collective-permute-done.1.far, f32[1,1024]{1,0:T(1,128)S(1)} %bitcast.8, ...), custom_call_target="tpu_custom_call" | custom-call | flops 373293056 | bytes 5000000 | tf_op jit(solution)/shard_map/pallas_call | solution.py:36
  12.5 0.1 broadcast_in_dim.18
  12.5 0.0 copy-start.1
  12.6 12.7 %all_to_all.20 = f16[8,100,512]{2,1,0:T(8,128)(2,1)S(1)} all-to-all(f16[8,100,512]{2,1,0:T(8,128)(2,1)S(1)} %broadcast_in_dim.18), channel_id=1, replica_groups=mesh['xl'=2,'y'=4,'xh'=2,'z'=8,'c'=2] {'xl','y'}, dimensions={0} | all-to-all | bytes 1638400 | tf_op jit(solution)/shard_map/all_to_all | solution.py:345
  25.3 0.2 convert_element_type.7.every
  25.5 0.0 copy-start.3
  25.5 0.0 copy-start.4
  25.5 0.0 copy-done.1
  25.5 1.9 %shard_map.132 = (bf16[100,512]{1,0:T(8,128)(2,1)S(1)}, bf16[16,8,1024]{2,1,0:T(8,128)(2,1)}) custom-call(f32[8,100,512]{2,1,0:T(8,128)S(1)} %convert_element_type.7.every, f32[100,512]{1,0:T(8,128)S(1)} %get-tuple-element.26.field, f32[100,512]{1,0:T(8,128)S(1)} %copy-done.1, f32[100,512]{1,0:T(8,128)S(1)} %get-tuple-element.27.wm, ...), custom_call_target="tpu_custom_call" | custom-call | flops 209715200 | bytes 4000000 | tf_op jit(solution)/shard_map/pallas_call | solution.py:36
  27.4 4.6 %all-to-all-start.1 = ((bf16[16,8,1024]{2,1,0:T(8,128)(2,1)}), bf16[16,8,1024]{2,1,0:T(8,128)(2,1)S(1)}, u32[]{:S(2)}, u32[]{:S(2)}) async-start(bf16[16,8,1024]{2,1,0:T(8,128)(2,1)} %get-tuple-element.29), calls=%async_computation.1 | async-start | bytes 524288 | tf_op jit(solution)/shard_map/all_to_all | solution.py:364
  32.0 1.9 %shard_map.133 = (f32[256,1024]{1,0:T(8,128)S(1)}, bf16[128,1024]{1,0:T(8,128)(2,1)S(1)}, bf16[128,1024]{1,0:T(8,128)(2,1)S(1)}) custom-call(s32[3,512]{1,0:T(4,128)S(1)} %copy-done.3, f32[3,512]{1,0:T(4,128)S(1)} %copy-done.4, bf16[100,512]{1,0:T(8,128)(2,1)S(1)} %get-tuple-element.30.fore_grad, bf16[100,1024]{1,0:T(8,128)(2,1)S(1)} %copy-done, ...), custom_call_target="tpu_custom_call" | custom-call | flops 641728512 | bytes 6000000 | tf_op jit(solution)/shard_map/pallas_call | solution.py:36
  33.9 6.7 %collective-permute-start.3 = (bf16[128,1024]{1,0:T(8,128)(2,1)S(1)}, bf16[128,1024]{1,0:T(8,128)(2,1)S(1)}, u32[]{:S(2)}, u32[]{:S(2)}) collective-permute-start(bf16[128,1024]{1,0:T(8,128)(2,1)S(1)} %get-tuple-element.33), channel_id=1, source_target_pairs={{0,1},{1,0},{2,3},{3,2},{4,5},{5,4},{6,7},{7,6},{8,9},{9,8},{10,11... | collective-permute-start | bytes 786440 | tf_op jit(solution)/shard_map/ppermute | solution.py:360
  40.7 0.4 collective-permute-start.4
  41.0 0.0 all-to-all-done.1.parts
  41.1 7.0 %collective-permute-start.2 = (f32[8,1024]{1,0:T(8,128)S(1)}, f32[8,1024]{1,0:T(8,128)S(1)}, u32[]{:S(2)}, u32[]{:S(2)}) collective-permute-start(f32[8,1024]{1,0:T(8,128)S(1)} %shard_map.134.mine), channel_id=1, source_target_pairs={{0,1},{1,0},{2,3},{3,2},{4,5},{5,4},{6,7},{7,6},{8,9},{9,8},{10,11... | collective-permute-start | bytes 98312 | tf_op jit(solution)/shard_map/ppermute | solution.py:366
  48.1 0.9 %collective-permute-done.2.met = f32[8,1024]{1,0:T(8,128)S(1)} collective-permute-done((f32[8,1024]{1,0:T(8,128)S(1)}, f32[8,1024]{1,0:T(8,128)S(1)}, u32[]{:S(2)}, u32[]{:S(2)}) %collective-permute-start.2) | collective-permute-done | bytes 32800 | tf_op jit(solution)/shard_map/ppermute | solution.py:366
  49.0 0.7 shard_map.135
  49.6 6.6 %all-to-all-start.2 = ((bf16[8,8,1024]{2,1,0:T(8,128)(2,1)}), bf16[8,8,1024]{2,1,0:T(8,128)(2,1)S(1)}, u32[]{:S(2)}, u32[]{:S(2)}) async-start(bf16[8,8,1024]{2,1,0:T(8,128)(2,1)} %shard_map.135), calls=%async_computation.2 | async-start | bytes 262144 | tf_op jit(solution)/shard_map/all_to_all | solution.py:371
  56.2 0.0 collective-permute-done.3.near
  56.2 0.0 collective-permute-done.4.far
  56.2 1.0 %shard_map.136.earlier = bf16[1,256,1024]{2,1,0:T(8,128)(2,1)} custom-call(f32[256,1024]{1,0:T(8,128)S(1)} %get-tuple-element.32.earlier.own, bf16[128,1024]{1,0:T(8,128)(2,1)S(1)} %collective-permute-done.3.near, bf16[128,1024]{1,0:T(8,128)(2,1)S(1)} %collective-permute-done.4.far), custom_call_target="tpu_custom_call" | custom-call | tf_op jit(solution)/shard_map/pallas_call | solution.py:36
  57.2 7.0 %all-to-all-done.2.parts = bf16[8,8,1024]{2,1,0:T(8,128)(2,1)S(1)} async-done(((bf16[8,8,1024]{2,1,0:T(8,128)(2,1)}), bf16[8,8,1024]{2,1,0:T(8,128)(2,1)S(1)}, u32[]{:S(2)}, u32[]{:S(2)}) %all-to-all-start.2) | async-done | bytes 131104 | tf_op jit(solution)/shard_map/all_to_all | solution.py:371
  64.2 10.4 %all_to_all.21.parts = bf16[16,8,1024]{2,1,0:T(8,128)(2,1)S(1)} all-to-all(bf16[16,8,1024]{2,1,0:T(8,128)(2,1)S(1)} %shard_map.137), channel_id=1, replica_groups=mesh['xl'=2,'y'=4,'xh'=2,'z'=8,'c'=2] {'xl','y','xh'}, dimensions={0} | all-to-all | bytes 524288 | tf_op jit(solution)/shard_map/all_to_all | solution.py:375
  74.6 0.8 %shard_map.138 = (f32[100,1024]{1,0:T(8,128)}, f32[1,1024]{1,0:T(1,128)}, f32[1,1]{1,0:T(1,128)}) custom-call(bf16[16,8,1024]{2,1,0:T(8,128)(2,1)S(1)} %all_to_all.21.parts), custom_call_target="tpu_custom_call" | custom-call | tf_op jit(solution)/shard_map/pallas_call | solution.py:36
  (7 shorter events, 0.1 us)
Async XLA Ops:
  0.6 10.3 %copy-start = (bf16[100,1024]{1,0:T(8,128)(2,1)S(1)}, bf16[100,1024]{1,0:T(8,128)(2,1)}, u32[]{:S(2)}) copy-start(bf16[100,1024]{1,0:T(8,128)(2,1)} %proj.5) | copy-start | bytes 614404
  0.6 10.2 %copy-start.2 = (f32[1024]{0:T(1024)S(1)}, f32[1024]{0:T(1024)}, u32[]{:S(2)}) copy-start(f32[1024]{0:T(1024)} %param.19) | copy-start | bytes 12292
  1.8 4.5 %collective-permute-start = (bf16[128,1024]{1,0:T(8,128)(2,1)S(1)}, bf16[128,1024]{1,0:T(8,128)(2,1)S(1)}, u32[]{:S(2)}, u32[]{:S(2)}) collective-permute-start(bf16[128,1024]{1,0:T(8,128)(2,1)S(1)} %get-tuple-element.21), channel_id=1, source_target_pairs={{0,1},{1,0},{2,3},{3,2},{4,5},{5,4},{6,7},{7,6},{8,9},{9,8},{10,11... | collective-permute-start | bytes 786440 | tf_op jit(solution)/shard_map/ppermute | solution.py:308
  5.1 5.8 %collective-permute-start.1 = (bf16[128,1024]{1,0:T(8,128)(2,1)S(1)}, bf16[128,1024]{1,0:T(8,128)(2,1)S(1)}, u32[]{:S(2)}, u32[]{:S(2)}) collective-permute-start(bf16[128,1024]{1,0:T(8,128)(2,1)S(1)} %get-tuple-element.24), channel_id=1, source_target_pairs={{1,2},{3,4},{5,6},{7,8},{9,10},{11,12},{13,14},{15,16},{17,18},{19... | collective-permute-start | bytes 786440 | tf_op jit(solution)/shard_map/ppermute | solution.py:307
  12.5 13.0 %copy-start.1 = (f32[100,512]{1,0:T(8,128)S(1)}, f32[100,512]{1,0:T(8,128)}, u32[]{:S(2)}) copy-start(f32[100,512]{1,0:T(8,128)} %target.1) | copy-start | bytes 614404
  25.5 6.5 %copy-start.3 = (s32[3,512]{1,0:T(4,128)S(1)}, s32[3,512]{1,0:T(4,128)}, u32[]{:S(2)}) copy-start(s32[3,512]{1,0:T(4,128)} %nb.1) | copy-start | bytes 18436
  25.5 6.5 %copy-start.4 = (f32[3,512]{1,0:T(4,128)S(1)}, f32[3,512]{1,0:T(4,128)}, u32[]{:S(2)}) copy-start(f32[3,512]{1,0:T(4,128)} %ew.1) | copy-start | bytes 18436
  27.4 13.6 %all-to-all-start.1 = ((bf16[16,8,1024]{2,1,0:T(8,128)(2,1)}), bf16[16,8,1024]{2,1,0:T(8,128)(2,1)S(1)}, u32[]{:S(2)}, u32[]{:S(2)}) async-start(bf16[16,8,1024]{2,1,0:T(8,128)(2,1)} %get-tuple-element.29), calls=%async_computation.1 | async-start | bytes 524288 | tf_op jit(solution)/shard_map/all_to_all | solution.py:364
  33.9 22.3 %collective-permute-start.3 = (bf16[128,1024]{1,0:T(8,128)(2,1)S(1)}, bf16[128,1024]{1,0:T(8,128)(2,1)S(1)}, u32[]{:S(2)}, u32[]{:S(2)}) collective-permute-start(bf16[128,1024]{1,0:T(8,128)(2,1)S(1)} %get-tuple-element.33), channel_id=1, source_target_pairs={{0,1},{1,0},{2,3},{3,2},{4,5},{5,4},{6,7},{7,6},{8,9},{9,8},{10,11... | collective-permute-start | bytes 786440 | tf_op jit(solution)/shard_map/ppermute | solution.py:360
  40.7 15.6 %collective-permute-start.4 = (bf16[128,1024]{1,0:T(8,128)(2,1)S(1)}, bf16[128,1024]{1,0:T(8,128)(2,1)S(1)}, u32[]{:S(2)}, u32[]{:S(2)}) collective-permute-start(bf16[128,1024]{1,0:T(8,128)(2,1)S(1)} %get-tuple-element.34), channel_id=1, source_target_pairs={{1,2},{3,4},{5,6},{7,8},{9,10},{11,12},{13,14},{15,16},{17,18},{19... | collective-permute-start | bytes 786440 | tf_op jit(solution)/shard_map/ppermute | solution.py:359
  41.1 7.9 %collective-permute-start.2 = (f32[8,1024]{1,0:T(8,128)S(1)}, f32[8,1024]{1,0:T(8,128)S(1)}, u32[]{:S(2)}, u32[]{:S(2)}) collective-permute-start(f32[8,1024]{1,0:T(8,128)S(1)} %shard_map.134.mine), channel_id=1, source_target_pairs={{0,1},{1,0},{2,3},{3,2},{4,5},{5,4},{6,7},{7,6},{8,9},{9,8},{10,11... | collective-permute-start | bytes 98312 | tf_op jit(solution)/shard_map/ppermute | solution.py:366
  49.6 14.5 %all-to-all-start.2 = ((bf16[8,8,1024]{2,1,0:T(8,128)(2,1)}), bf16[8,8,1024]{2,1,0:T(8,128)(2,1)S(1)}, u32[]{:S(2)}, u32[]{:S(2)}) async-start(bf16[8,8,1024]{2,1,0:T(8,128)(2,1)} %shard_map.135), calls=%async_computation.2 | async-start | bytes 262144 | tf_op jit(solution)/shard_map/all_to_all | solution.py:371

commit v7 on v6

--- a/solution.py
+++ b/solution.py
@@ -112,11 +112,10 @@
     far_out[:, rim:] = far_low
     copies[4].wait()
     borrowed, own = near[...], latent[...]
-    mix = (
-        dot(near_high, borrowed, ((1,), (0,)))
-        + dot(near_low, borrowed, ((1,), (0,)))
-        + dot(own_high, own, ((1,), (0,)))
-        + dot(own_low, own, ((1,), (0,)))
+    mix = dot(
+        jnp.concatenate([near_high, near_low, own_high, own_low], axis=1),
+        jnp.concatenate([borrowed, borrowed, own, own], axis=0),
+        ((1,), (0,)),
     )
     copies[5].wait()
     part_out[...] = skip[...].astype(F32) + mix
@@ -131,13 +130,9 @@
 
 
 def forward_kernel(part, edges, far, gain, proj, state, f_out, sc_out, rs_out):
-    rim = far.shape[0]
     borrowed = far[...]
-    mixed = (
-        part[...]
-        + dot(edges[:, :rim], borrowed, ((1,), (0,)))
-        + dot(edges[:, rim:], borrowed, ((1,), (0,)))
-    )
+    twice = jnp.concatenate([borrowed, borrowed], axis=0)
+    mixed = part[...] + dot(edges[...], twice, ((1,), (0,)))
     centred = mixed - jnp.mean(mixed, axis=1, keepdims=True)
     rscale = lax.rsqrt(jnp.mean(centred * centred, axis=1, keepdims=True) + NORM_EPS)
     scaled = (centred * rscale * gain[...]).astype(BF16)
@@ -171,10 +166,8 @@
     loss = jnp.sum(jnp.sum(terms, axis=0, keepdims=True), axis=1, keepdims=True)
     fore_grad = (weight_map * (slope / members - coef_pair * pair_slope)).astype(BF16)
     fg_out[...] = fore_grad
-    values = scaled[...]
-    wout = dot(fore_grad, values, ((1,), (0,)))
-    scaled_grad = dot(fore_grad, proj[...], ((0,), (0,)))
-    product = jnp.sum(scaled_grad * values.astype(F32), axis=0, keepdims=True) / gain[...]
+    wout = dot(fore_grad, scaled[...], ((1,), (0,)))
+    product = jnp.sum(wout * proj[...].astype(F32), axis=0, keepdims=True) / gain[...]
     last = variables // CHUNK
     for i in range(last):
         parts_out[i] = wout[i * CHUNK : (i + 1) * CHUNK].astype(BF16)

time: 76.9 us -> 76.4 us (level)
  no operation moved by 1% of the time
where the time goes in v7:
time: 76.4 us; the launch traced here: 74.9 us
  starting transfers between devices  28.6 us (37%)
  blocking collectives  23.1 us (30%)
  Pallas kernels  11.5 us (15%)
  waiting for transfers between devices  10.6 us (14%)
  between operations  0.78 us (1%)
    all_to_all x1, blocking collectives, per_device(): every = lax.all_to_all(sent, MEMBER, 0, 0, tiled=True).astype(F32)  12.7 us
    pallas_call x10, Pallas kernels, run(): pl.pallas_call(kernel, out_shape=[jax.ShapeDtypeStruct(s, d) for s, d in...  11.5 us
    all_to_all x1, blocking collectives, per_device(): parts = lax.all_to_all(parts, PLANE, 0, 0, tiled=True)  10.4 us
    ppermute x1, starting transfers between devices, per_device(): met = lax.ppermute(mine, 'c', swap)  7.01 us
    all_to_all x1, waiting for transfers between devices, per_device(): parts = lax.all_to_all(parts, 'z', 0, 0, tiled=True)  6.95 us
    ppermute x1, starting transfers between devices, per_device(): near_grad = lax.ppermute(near_grad, 'c', swap)  6.74 us
    all_to_all x1, starting transfers between devices, per_device(): parts = lax.all_to_all(parts, 'z', 0, 0, tiled=True)  6.58 us
    all_to_all x1, starting transfers between devices, per_device(): parts = lax.all_to_all(parts, PLANE, 0, 0, tiled=True)  4.56 us
  transfers between devices with their start and end apart: 7, of which 4 were waited for; matrix products, arithmetic and copies ran while one was open for 0% of the time, Pallas kernels for 9%

profile of v7, /device:TPU:1, one launch (start us, length us, event | category | flops | bytes accessed | tf_op | source)
XLA Modules:
  0.0 74.9 jit_solution(13031362810217718406)
XLA Ops:
  0.6 0.0 copy-start
  0.6 0.0 copy-start.2
  0.7 1.1 %shard_map.129 = (bf16[128,1024]{1,0:T(8,128)(2,1)S(1)}, bf16[128,1024]{1,0:T(8,128)(2,1)S(1)}) custom-call(bf16[256,1024]{1,0:T(8,128)(2,1)} %bitcast.11), custom_call_target="tpu_custom_call" | custom-call | tf_op jit(solution)/shard_map/pallas_call | solution.py:36
  1.8 3.3 %collective-permute-start = (bf16[128,1024]{1,0:T(8,128)(2,1)S(1)}, bf16[128,1024]{1,0:T(8,128)(2,1)S(1)}, u32[]{:S(2)}, u32[]{:S(2)}) collective-permute-start(bf16[128,1024]{1,0:T(8,128)(2,1)S(1)} %get-tuple-element.21), channel_id=1, source_target_pairs={{0,1},{1,0},{2,3},{3,2},{4,5},{5,4},{6,7},{7,6},{8,9},{9,8},{10,11... | collective-permute-start | bytes 786440 | tf_op jit(solution)/shard_map/ppermute | solution.py:301
  5.1 0.0 collective-permute-start.1
  5.1 1.2 %collective-permute-done.near = bf16[128,1024]{1,0:T(8,128)(2,1)S(1)} collective-permute-done((bf16[128,1024]{1,0:T(8,128)(2,1)S(1)}, bf16[128,1024]{1,0:T(8,128)(2,1)S(1)}, u32[]{:S(2)}, u32[]{:S(2)}) %collective-permute-start) | collective-permute-done | bytes 262176 | tf_op jit(solution)/shard_map/ppermute | solution.py:301
  6.2 3.0 %shard_map.130 = (bf16[512,256]{1,0:T(8,128)(2,1)S(1)}, f32[512,1024]{1,0:T(8,128)S(1)}, f32[100,512]{1,0:T(8,128)S(1)}, f32[100,512]{1,0:T(8,128)S(1)}) custom-call(s32[3,512]{1,0:T(4,128)} %nb.1, f32[3,512]{1,0:T(4,128)} %ew.1, f32[1,100]{1,0:T(1,128)} %bitcast.17, f32[1,512]{1,0:T(1,128)} %bitcast.16, bf16[256,1024]{1,0:T(8,128)(2,1)} %bitcast.12, ...), custom_call_target="tpu_custom_call" | custom-call | flops 805306368 | bytes 8000000 | tf_op jit(solution)/shard_map/pallas_call | solution.py:36
  9.3 1.6 %collective-permute-done.1.far = bf16[128,1024]{1,0:T(8,128)(2,1)S(1)} collective-permute-done((bf16[128,1024]{1,0:T(8,128)(2,1)S(1)}, bf16[128,1024]{1,0:T(8,128)(2,1)S(1)}, u32[]{:S(2)}, u32[]{:S(2)}) %collective-permute-start.1) | collective-permute-done | bytes 262176 | tf_op jit(solution)/shard_map/ppermute | solution.py:300
  10.9 0.0 copy-done
  10.9 1.3 %shard_map.131 = (f32[100,512]{1,0:T(8,128)S(1)}, bf16[512,1024]{1,0:T(8,128)(2,1)S(1)}, f32[512,1]{1,0:T(8,128)S(1)}) custom-call(f32[512,1024]{1,0:T(8,128)S(1)} %get-tuple-element.22.part, bf16[512,256]{1,0:T(8,128)(2,1)S(1)} %get-tuple-element.23.edges, bf16[128,1024]{1,0:T(8,128)(2,1)S(1)} %collective-permute-done.1.far, f32[1,1024]{1,0:T(1,128)S(1)} %bitcast.8, ...), custom_call_target="tpu_custom_call" | custom-call | flops 373293056 | bytes 5000000 | tf_op jit(solution)/shard_map/pallas_call | solution.py:36
  12.2 0.1 broadcast_in_dim.18
  12.3 0.0 copy-start.1
  12.3 12.7 %all_to_all.20 = f16[8,100,512]{2,1,0:T(8,128)(2,1)S(1)} all-to-all(f16[8,100,512]{2,1,0:T(8,128)(2,1)S(1)} %broadcast_in_dim.18), channel_id=1, replica_groups=mesh['xl'=2,'y'=4,'xh'=2,'z'=8,'c'=2] {'xl','y'}, dimensions={0} | all-to-all | bytes 1638400 | tf_op jit(solution)/shard_map/all_to_all | solution.py:338
  25.0 0.2 convert_element_type.7.every
  25.3 0.0 copy-start.3
  25.3 0.0 copy-start.4
  25.3 1.6 %shard_map.132 = (bf16[100,512]{1,0:T(8,128)(2,1)S(1)}, bf16[16,8,1024]{2,1,0:T(8,128)(2,1)}) custom-call(f32[8,100,512]{2,1,0:T(8,128)S(1)} %convert_element_type.7.every, f32[100,512]{1,0:T(8,128)S(1)} %get-tuple-element.26.field, f32[100,512]{1,0:T(8,128)S(1)} %copy-done.1, f32[100,512]{1,0:T(8,128)S(1)} %get-tuple-element.27.wm, ...), custom_call_target="tpu_custom_call" | custom-call | flops 209715200 | bytes 4000000 | tf_op jit(solution)/shard_map/pallas_call | solution.py:36
  26.9 4.6 %all-to-all-start.1 = ((bf16[16,8,1024]{2,1,0:T(8,128)(2,1)}), bf16[16,8,1024]{2,1,0:T(8,128)(2,1)S(1)}, u32[]{:S(2)}, u32[]{:S(2)}) async-start(bf16[16,8,1024]{2,1,0:T(8,128)(2,1)} %get-tuple-element.29), calls=%async_computation.1 | async-start | bytes 524288 | tf_op jit(solution)/shard_map/all_to_all | solution.py:357
  31.5 1.9 %shard_map.133 = (f32[256,1024]{1,0:T(8,128)S(1)}, bf16[128,1024]{1,0:T(8,128)(2,1)S(1)}, bf16[128,1024]{1,0:T(8,128)(2,1)S(1)}) custom-call(s32[3,512]{1,0:T(4,128)S(1)} %copy-done.3, f32[3,512]{1,0:T(4,128)S(1)} %copy-done.4, bf16[100,512]{1,0:T(8,128)(2,1)S(1)} %get-tuple-element.30.fore_grad, bf16[100,1024]{1,0:T(8,128)(2,1)S(1)} %copy-done, ...), custom_call_target="tpu_custom_call" | custom-call | flops 641728512 | bytes 6000000 | tf_op jit(solution)/shard_map/pallas_call | solution.py:36
  33.4 6.7 %collective-permute-start.3 = (bf16[128,1024]{1,0:T(8,128)(2,1)S(1)}, bf16[128,1024]{1,0:T(8,128)(2,1)S(1)}, u32[]{:S(2)}, u32[]{:S(2)}) collective-permute-start(bf16[128,1024]{1,0:T(8,128)(2,1)S(1)} %get-tuple-element.33), channel_id=1, source_target_pairs={{0,1},{1,0},{2,3},{3,2},{4,5},{5,4},{6,7},{7,6},{8,9},{9,8},{10,11... | collective-permute-start | bytes 786440 | tf_op jit(solution)/shard_map/ppermute | solution.py:353
  40.1 0.4 collective-permute-start.4
  40.5 0.0 all-to-all-done.1.parts
  40.6 7.0 %collective-permute-start.2 = (f32[8,1024]{1,0:T(8,128)S(1)}, f32[8,1024]{1,0:T(8,128)S(1)}, u32[]{:S(2)}, u32[]{:S(2)}) collective-permute-start(f32[8,1024]{1,0:T(8,128)S(1)} %shard_map.134.mine), channel_id=1, source_target_pairs={{0,1},{1,0},{2,3},{3,2},{4,5},{5,4},{6,7},{7,6},{8,9},{9,8},{10,11... | collective-permute-start | bytes 98312 | tf_op jit(solution)/shard_map/ppermute | solution.py:359
  47.6 0.9 %collective-permute-done.2.met = f32[8,1024]{1,0:T(8,128)S(1)} collective-permute-done((f32[8,1024]{1,0:T(8,128)S(1)}, f32[8,1024]{1,0:T(8,128)S(1)}, u32[]{:S(2)}, u32[]{:S(2)}) %collective-permute-start.2) | collective-permute-done | bytes 32800 | tf_op jit(solution)/shard_map/ppermute | solution.py:359
  48.4 0.7 shard_map.135
  49.1 6.6 %all-to-all-start.2 = ((bf16[8,8,1024]{2,1,0:T(8,128)(2,1)}), bf16[8,8,1024]{2,1,0:T(8,128)(2,1)S(1)}, u32[]{:S(2)}, u32[]{:S(2)}) async-start(bf16[8,8,1024]{2,1,0:T(8,128)(2,1)} %shard_map.135), calls=%async_computation.2 | async-start | bytes 262144 | tf_op jit(solution)/shard_map/all_to_all | solution.py:364
  55.7 0.0 collective-permute-done.3.near
  55.7 0.0 collective-permute-done.4.far
  55.7 1.0 %shard_map.136.earlier = bf16[1,256,1024]{2,1,0:T(8,128)(2,1)} custom-call(f32[256,1024]{1,0:T(8,128)S(1)} %get-tuple-element.32.earlier.own, bf16[128,1024]{1,0:T(8,128)(2,1)S(1)} %collective-permute-done.3.near, bf16[128,1024]{1,0:T(8,128)(2,1)S(1)} %collective-permute-done.4.far), custom_call_target="tpu_custom_call" | custom-call | tf_op jit(solution)/shard_map/pallas_call | solution.py:36
  56.7 7.0 %all-to-all-done.2.parts = bf16[8,8,1024]{2,1,0:T(8,128)(2,1)S(1)} async-done(((bf16[8,8,1024]{2,1,0:T(8,128)(2,1)}), bf16[8,8,1024]{2,1,0:T(8,128)(2,1)S(1)}, u32[]{:S(2)}, u32[]{:S(2)}) %all-to-all-start.2) | async-done | bytes 131104 | tf_op jit(solution)/shard_map/all_to_all | solution.py:364
  63.7 10.4 %all_to_all.21.parts = bf16[16,8,1024]{2,1,0:T(8,128)(2,1)S(1)} all-to-all(bf16[16,8,1024]{2,1,0:T(8,128)(2,1)S(1)} %shard_map.137), channel_id=1, replica_groups=mesh['xl'=2,'y'=4,'xh'=2,'z'=8,'c'=2] {'xl','y','xh'}, dimensions={0} | all-to-all | bytes 524288 | tf_op jit(solution)/shard_map/all_to_all | solution.py:368
  74.1 0.8 %shard_map.138 = (f32[100,1024]{1,0:T(8,128)}, f32[1,1024]{1,0:T(1,128)}, f32[1,1]{1,0:T(1,128)}) custom-call(bf16[16,8,1024]{2,1,0:T(8,128)(2,1)S(1)} %all_to_all.21.parts), custom_call_target="tpu_custom_call" | custom-call | tf_op jit(solution)/shard_map/pallas_call | solution.py:36
  (7 shorter events, 0.1 us)
Async XLA Ops:
  0.6 10.3 %copy-start = (bf16[100,1024]{1,0:T(8,128)(2,1)S(1)}, bf16[100,1024]{1,0:T(8,128)(2,1)}, u32[]{:S(2)}) copy-start(bf16[100,1024]{1,0:T(8,128)(2,1)} %proj.5) | copy-start | bytes 614404
  0.6 10.2 %copy-start.2 = (f32[1024]{0:T(1024)S(1)}, f32[1024]{0:T(1024)}, u32[]{:S(2)}) copy-start(f32[1024]{0:T(1024)} %param.19) | copy-start | bytes 12292
  1.8 4.5 %collective-permute-start = (bf16[128,1024]{1,0:T(8,128)(2,1)S(1)}, bf16[128,1024]{1,0:T(8,128)(2,1)S(1)}, u32[]{:S(2)}, u32[]{:S(2)}) collective-permute-start(bf16[128,1024]{1,0:T(8,128)(2,1)S(1)} %get-tuple-element.21), channel_id=1, source_target_pairs={{0,1},{1,0},{2,3},{3,2},{4,5},{5,4},{6,7},{7,6},{8,9},{9,8},{10,11... | collective-permute-start | bytes 786440 | tf_op jit(solution)/shard_map/ppermute | solution.py:301
  5.1 5.8 %collective-permute-start.1 = (bf16[128,1024]{1,0:T(8,128)(2,1)S(1)}, bf16[128,1024]{1,0:T(8,128)(2,1)S(1)}, u32[]{:S(2)}, u32[]{:S(2)}) collective-permute-start(bf16[128,1024]{1,0:T(8,128)(2,1)S(1)} %get-tuple-element.24), channel_id=1, source_target_pairs={{1,2},{3,4},{5,6},{7,8},{9,10},{11,12},{13,14},{15,16},{17,18},{19... | collective-permute-start | bytes 786440 | tf_op jit(solution)/shard_map/ppermute | solution.py:300
  12.3 13.0 %copy-start.1 = (f32[100,512]{1,0:T(8,128)S(1)}, f32[100,512]{1,0:T(8,128)}, u32[]{:S(2)}) copy-start(f32[100,512]{1,0:T(8,128)} %target.1) | copy-start | bytes 614404
  25.3 6.2 %copy-start.3 = (s32[3,512]{1,0:T(4,128)S(1)}, s32[3,512]{1,0:T(4,128)}, u32[]{:S(2)}) copy-start(s32[3,512]{1,0:T(4,128)} %nb.1) | copy-start | bytes 18436
  25.3 6.2 %copy-start.4 = (f32[3,512]{1,0:T(4,128)S(1)}, f32[3,512]{1,0:T(4,128)}, u32[]{:S(2)}) copy-start(f32[3,512]{1,0:T(4,128)} %ew.1) | copy-start | bytes 18436
  26.9 13.6 %all-to-all-start.1 = ((bf16[16,8,1024]{2,1,0:T(8,128)(2,1)}), bf16[16,8,1024]{2,1,0:T(8,128)(2,1)S(1)}, u32[]{:S(2)}, u32[]{:S(2)}) async-start(bf16[16,8,1024]{2,1,0:T(8,128)(2,1)} %get-tuple-element.29), calls=%async_computation.1 | async-start | bytes 524288 | tf_op jit(solution)/shard_map/all_to_all | solution.py:357
  33.4 22.3 %collective-permute-start.3 = (bf16[128,1024]{1,0:T(8,128)(2,1)S(1)}, bf16[128,1024]{1,0:T(8,128)(2,1)S(1)}, u32[]{:S(2)}, u32[]{:S(2)}) collective-permute-start(bf16[128,1024]{1,0:T(8,128)(2,1)S(1)} %get-tuple-element.33), channel_id=1, source_target_pairs={{0,1},{1,0},{2,3},{3,2},{4,5},{5,4},{6,7},{7,6},{8,9},{9,8},{10,11... | collective-permute-start | bytes 786440 | tf_op jit(solution)/shard_map/ppermute | solution.py:353
  40.1 15.6 %collective-permute-start.4 = (bf16[128,1024]{1,0:T(8,128)(2,1)S(1)}, bf16[128,1024]{1,0:T(8,128)(2,1)S(1)}, u32[]{:S(2)}, u32[]{:S(2)}) collective-permute-start(bf16[128,1024]{1,0:T(8,128)(2,1)S(1)} %get-tuple-element.34), channel_id=1, source_target_pairs={{1,2},{3,4},{5,6},{7,8},{9,10},{11,12},{13,14},{15,16},{17,18},{19... | collective-permute-start | bytes 786440 | tf_op jit(solution)/shard_map/ppermute | solution.py:352
  40.6 7.9 %collective-permute-start.2 = (f32[8,1024]{1,0:T(8,128)S(1)}, f32[8,1024]{1,0:T(8,128)S(1)}, u32[]{:S(2)}, u32[]{:S(2)}) collective-permute-start(f32[8,1024]{1,0:T(8,128)S(1)} %shard_map.134.mine), channel_id=1, source_target_pairs={{0,1},{1,0},{2,3},{3,2},{4,5},{5,4},{6,7},{7,6},{8,9},{9,8},{10,11... | collective-permute-start | bytes 98312 | tf_op jit(solution)/shard_map/ppermute | solution.py:359
  49.1 14.5 %all-to-all-start.2 = ((bf16[8,8,1024]{2,1,0:T(8,128)(2,1)}), bf16[8,8,1024]{2,1,0:T(8,128)(2,1)S(1)}, u32[]{:S(2)}, u32[]{:S(2)}) async-start(bf16[8,8,1024]{2,1,0:T(8,128)(2,1)} %shard_map.135), calls=%async_computation.2 | async-start | bytes 262144 | tf_op jit(solution)/shard_map/all_to_all | solution.py:364

commit v8 on v7

--- a/solution.py
+++ b/solution.py
@@ -46,17 +46,12 @@
     return run
 
 
-def cut_kernel(latent, first_out, second_out, sems):
-    rim = first_out.shape[0]
-    core = lax.axis_index("c")
-    start = pl.multiple_of((1 - core) * rim, rim)
-    other = pl.multiple_of(core * rim, rim)
-    one = pltpu.make_async_copy(latent.at[pl.ds(start, rim)], first_out, sems.at[0])
-    two = pltpu.make_async_copy(latent.at[pl.ds(other, rim)], second_out, sems.at[1])
-    one.start()
-    two.start()
-    one.wait()
-    two.wait()
+def cut_kernel(latent, out, sem):
+    rim = out.shape[0]
+    start = pl.multiple_of(lax.axis_index("c") * rim, rim)
+    copy = pltpu.make_async_copy(latent.at[pl.ds(start, rim)], out, sem)
+    copy.start()
+    copy.wait()
 
 
 def borrowed_rows(distance):
@@ -66,8 +61,8 @@
 
 
 def prepare_kernel(
-    nb_in, ew_in, vw_in, area_in, latent_in, skip_in, state_in, near,
-    far_out, part_out, wm_out, state_out,
+    nb_in, ew_in, vw_in, area_in, latent_in, skip_in, state_in, earlier,
+    near_out, edges_out, part_out, wm_out, state_out,
     nb, ew, vw, area, latent, skip, state, sems,
 ):
     pairs = (
@@ -75,13 +70,15 @@
         (latent_in, latent), (skip_in, skip), (state_in, state),
     )
     copies = [pltpu.make_async_copy(a, b, sems.at[i]) for i, (a, b) in enumerate(pairs)]
+    rim = near_out.shape[0]
+    near_rows = pl.ds(pl.multiple_of((1 - lax.axis_index("c")) * rim, rim), rim)
+    copies.append(pltpu.make_async_copy(latent_in.at[near_rows], near_out, sems.at[len(pairs)]))
     for copy in copies:
         copy.start()
     for copy in copies[:4]:
         copy.wait()
     slots, points = nb.shape
     mesh_count = latent.shape[0]
-    rim = mesh_count // 2
     near_start, far_start, far_there = borrowed_rows(rim + mesh_count)
     weights = ew[...]
     weights = weights / jnp.sum(weights, axis=0, keepdims=True)
@@ -108,14 +105,12 @@
     near_high, near_low = parts(edges(near_start, rim))
     own_high, own_low = parts(edges(rim, mesh_count))
     far_high, far_low = parts(jnp.where(far_there, edges(far_start, rim), 0.0))
-    far_out[:, :rim] = far_high
-    far_out[:, rim:] = far_low
+    for i, value in enumerate((near_high, near_low, far_high, far_low)):
+        edges_out[:, i * rim : (i + 1) * rim] = value
     copies[4].wait()
-    borrowed, own = near[...], latent[...]
+    own = latent[...]
     mix = dot(
-        jnp.concatenate([near_high, near_low, own_high, own_low], axis=1),
-        jnp.concatenate([borrowed, borrowed, own, own], axis=0),
-        ((1,), (0,)),
+        jnp.concatenate([own_high, own_low], axis=1), jnp.concatenate([own, own], axis=0), ((1,), (0,))
     )
     copies[5].wait()
     part_out[...] = skip[...].astype(F32) + mix
@@ -127,11 +122,12 @@
     wm_out[...] = vw_column * area[...]
     copies[6].wait()
     state_out[...] = state[:, 0, :]
-
-
-def forward_kernel(part, edges, far, gain, proj, state, f_out, sc_out, rs_out):
-    borrowed = far[...]
-    twice = jnp.concatenate([borrowed, borrowed], axis=0)
+    copies[7].wait()
+
+
+def forward_kernel(part, edges, near, far, gain, proj, state, f_out, sc_out, rs_out):
+    close, distant = near[...], far[...]
+    twice = jnp.concatenate([close, close, distant, distant], axis=0)
     mixed = part[...] + dot(edges[...], twice, ((1,), (0,)))
     centred = mixed - jnp.mean(mixed, axis=1, keepdims=True)
     rscale = lax.rsqrt(jnp.mean(centred * centred, axis=1, keepdims=True) + NORM_EPS)
@@ -188,7 +184,7 @@
         parts_out[i] = jnp.zeros((CHUNK, channels), BF16)
 
 
-def back_kernel(nb, ew, fore_grad, proj, scaled, gain, rscale, own_out, near_out, far_out):
+def back_kernel(earlier, nb, ew, fore_grad, proj, scaled, gain, rscale, own_out, near_out, far_out):
     channels = scaled.shape[1]
     rim = near_out.shape[0]
     mesh_count = own_out.shape[0]
@@ -236,7 +232,7 @@
     return jnp.where(here, split, total).astype(BF16)
 
 
-def fold_kernel(parts, earlier, out):
+def fold_kernel(parts, out):
     out[...] = jnp.sum(parts[...].astype(F32), axis=0)
 
 
@@ -252,7 +248,7 @@
         out[i] = total
 
 
-def finish_weights_kernel(count, parts, wout_out, gain_out, loss_out):
+def finish_weights_kernel(count, parts, earlier, wout_out, gain_out, loss_out):
     variables = wout_out.shape[0]
     last = variables // CHUNK
     for i in range(last):
@@ -291,23 +287,20 @@
     links = [((i + 1) % slabs, (i + 2) % slabs) for i in range(0, slabs, 2)]
     links = links + [(j, i) for i, j in links]
 
-    near_send, far_send = call(
-        cut_kernel,
-        [((rim, channels), BF16), ((rim, channels), BF16)],
-        "h",
-        [pltpu.SemaphoreType.DMA((2,))],
+    (far_send,) = call(
+        cut_kernel, [((rim, channels), BF16)], "h", [pltpu.SemaphoreType.DMA]
     )(latent)
     far = lax.ppermute(far_send, GRID, links)
-    near = lax.ppermute(near_send, "c", swap)
-    edges, part, weight_map, state = call(
+    near_send, edges, part, weight_map, state = call(
         prepare_kernel,
         [
-            ((points, 2 * rim), BF16),
+            ((rim, channels), BF16),
+            ((points, 4 * rim), BF16),
             ((points, channels), F32),
             ((variables, points), F32),
             ((variables, points), F32),
         ],
-        "hhhhhhhv",
+        "hhhhhhha",
         [
             pltpu.VMEM(neighbours.shape, jnp.int32),
             pltpu.VMEM(edge_weight.shape, F32),
@@ -316,14 +309,15 @@
             pltpu.VMEM((mesh_count, channels), BF16),
             pltpu.VMEM((points, channels), BF16),
             pltpu.VMEM((variables, 1, points), F32),
-            pltpu.SemaphoreType.DMA((7,)),
+            pltpu.SemaphoreType.DMA((8,)),
         ],
         flops=6 * points * mesh_count * channels,
         moved=8_000_000,
     )(
         neighbours, edge_weight, variable_weight[None], area_weight[None], latent, skip,
-        state.reshape(variables, 1, points), near,
-    )
+        state.reshape(variables, 1, points), far_send,
+    )
+    near = lax.ppermute(near_send, "c", swap)
     field, scaled, rscale = call(
         forward_kernel,
         [
@@ -333,7 +327,7 @@
         ],
         flops=2 * points * channels * (2 * rim + variables),
         moved=5_000_000,
-    )(part, edges, far, gain, output_projection, state)
+    )(part, edges, near, far, gain, output_projection, state)
     sent = jnp.broadcast_to(field.astype(jnp.float16)[None], (members, variables, points))
     every = lax.all_to_all(sent, MEMBER, 0, 0, tiled=True).astype(F32)
     fore_grad, parts = call(
@@ -343,33 +337,35 @@
         moved=4_000_000,
     )(every, field, target, weight_map, output_projection, scaled, gain)
 
+    parts = lax.all_to_all(parts, PLANE, 0, 0, tiled=True)
+    (mine,) = call(fold_kernel, [((CHUNK, channels), F32)])(parts)
+    met = lax.ppermute(mine, "c", swap)
+    depth = lax.axis_size("z")
+    (parts,) = call(
+        functools.partial(pair_kernel, variables), [((depth, CHUNK, channels), BF16)]
+    )(mine, met)
     own, near_grad, far_grad = call(
         back_kernel,
         [((mesh_count, channels), F32), ((rim, channels), BF16), ((rim, channels), BF16)],
         flops=2 * points * channels * (extent + variables),
         moved=6_000_000,
-    )(neighbours, edge_weight, fore_grad, output_projection, scaled, gain, rscale)
+        spaces="a",
+    )(met, neighbours, edge_weight, fore_grad, output_projection, scaled, gain, rscale)
     far_grad = lax.ppermute(far_grad, GRID, links)
     near_grad = lax.ppermute(near_grad, "c", swap)
     (latent_grad,) = call(finish_latent_kernel, [((1, mesh_count, channels), BF16)])(
         own, near_grad, far_grad
     )
-    parts = lax.all_to_all(parts, PLANE, 0, 0, tiled=True)
-    (mine,) = call(fold_kernel, [((CHUNK, channels), F32)], "va")(parts, own)
-    met = lax.ppermute(mine, "c", swap)
-    depth = lax.axis_size("z")
-    (parts,) = call(
-        functools.partial(pair_kernel, variables), [((depth, CHUNK, channels), BF16)]
-    )(mine, met)
     parts = lax.all_to_all(parts, "z", 0, 0, tiled=True)
     (parts,) = call(
-        functools.partial(spread_kernel, variables), [((plane, CHUNK, channels), BF16)], "vh"
-    )(parts, latent_grad)
+        functools.partial(spread_kernel, variables), [((plane, CHUNK, channels), BF16)], "va"
+    )(parts, own)
     parts = lax.all_to_all(parts, PLANE, 0, 0, tiled=True)
     wout, gain_grad, crps = call(
         functools.partial(finish_weights_kernel, points * slabs * variables),
         [((variables, channels), F32), ((1, channels), F32), ((1, 1), F32)],
-    )(parts)
+        "vh",
+    )(parts, latent_grad)
     return (crps[0, 0], latent_grad, wout, gain_grad[0])
 
 

time: 76.4 us -> 76.1 us (level)
  starting transfers between devices: 28.6 us -> 21.9 us
  blocking collectives: 23.1 us -> 28.2 us
  waiting for transfers between devices: 10.6 us -> 12 us
    all_to_all x1, waiting for transfers between devices: 0.01 us -> 6.44 us  [per_device(): parts = lax.all_to_all(parts, PLANE, 0, 0, tiled=True)]
    ppermute x1, starting transfers between devices: 6.74 us -> 0.71 us  [per_device(): near_grad = lax.ppermute(near_grad, 'c', swap)]
    all_to_all x1, blocking collectives: 12.7 us -> 17.1 us  [per_device(): every = lax.all_to_all(sent, MEMBER, 0, 0, tiled=True).astype(F32)]
    ppermute x1, starting transfers between devices: 7.01 us -> 3.12 us  [per_device(): met = lax.ppermute(mine, 'c', swap)]
    all_to_all x1, waiting for transfers between devices: 6.95 us -> 3.58 us  [per_device(): parts = lax.all_to_all(parts, 'z', 0, 0, tiled=True)]
    all_to_all x1, starting transfers between devices: 6.58 us -> 3.41 us  [per_device(): parts = lax.all_to_all(parts, 'z', 0, 0, tiled=True)]
    ppermute x1, starting transfers between devices: 0.01 us -> 3.11 us  [per_device(): far = lax.ppermute(far_send, GRID, links)]
    ppermute x1, starting transfers between devices: 3.33 us -> 6.32 us  [per_device(): near = lax.ppermute(near_send, 'c', swap)]
where the time goes in v8:
time: 76.1 us; the launch traced here: 74.7 us
  blocking collectives  28.2 us (37%)
  starting transfers between devices  21.9 us (29%)
  waiting for transfers between devices  12 us (16%)
  Pallas kernels  11.4 us (15%)
  between operations  0.78 us (1%)
    all_to_all x1, blocking collectives, per_device(): every = lax.all_to_all(sent, MEMBER, 0, 0, tiled=True).astype(F32)  17.1 us
    pallas_call x10, Pallas kernels, run(): pl.pallas_call(kernel, out_shape=[jax.ShapeDtypeStruct(s, d) for s, d in...  11.4 us
    all_to_all x1, blocking collectives, per_device(): parts = lax.all_to_all(parts, PLANE, 0, 0, tiled=True)  11.1 us
    all_to_all x1, waiting for transfers between devices, per_device(): parts = lax.all_to_all(parts, PLANE, 0, 0, tiled=True)  6.44 us
    ppermute x1, starting transfers between devices, per_device(): near = lax.ppermute(near_send, 'c', swap)  6.32 us
    all_to_all x1, waiting for transfers between devices, per_device(): parts = lax.all_to_all(parts, 'z', 0, 0, tiled=True)  3.58 us
    all_to_all x1, starting transfers between devices, per_device(): parts = lax.all_to_all(parts, PLANE, 0, 0, tiled=True)  3.53 us
    all_to_all x1, starting transfers between devices, per_device(): parts = lax.all_to_all(parts, 'z', 0, 0, tiled=True)  3.41 us
  transfers between devices with their start and end apart: 7, of which 4 were waited for; matrix products, arithmetic and copies ran while one was open for 0% of the time, Pallas kernels for 9%

profile of v8, /device:TPU:1, one launch (start us, length us, event | category | flops | bytes accessed | tf_op | source)
XLA Modules:
  0.0 74.7 jit_solution(426404111471129235)
XLA Ops:
  0.6 0.0 copy-start
  0.6 0.0 copy-start.2
  0.7 1.0 %shard_map.129.earlier = bf16[128,1024]{1,0:T(8,128)(2,1)S(1)} custom-call(bf16[256,1024]{1,0:T(8,128)(2,1)} %bitcast.11), custom_call_target="tpu_custom_call" | custom-call | tf_op jit(solution)/shard_map/pallas_call | solution.py:36
  1.7 3.1 %collective-permute-start.1 = (bf16[128,1024]{1,0:T(8,128)(2,1)S(1)}, bf16[128,1024]{1,0:T(8,128)(2,1)S(1)}, u32[]{:S(2)}, u32[]{:S(2)}) collective-permute-start(bf16[128,1024]{1,0:T(8,128)(2,1)S(1)} %shard_map.129.earlier), channel_id=1, source_target_pairs={{1,2},{3,4},{5,6},{7,8},{9,10},{11,12},{13,14},{15,16},{17,18},{19... | collective-permute-start | bytes 786440 | tf_op jit(solution)/shard_map/ppermute | solution.py:293
  4.8 2.8 %shard_map.130 = (bf16[128,1024]{1,0:T(8,128)(2,1)S(1)}, bf16[512,512]{1,0:T(8,128)(2,1)S(1)}, f32[512,1024]{1,0:T(8,128)S(1)}, f32[100,512]{1,0:T(8,128)S(1)}, f32[100,512]{1,0:T(8,128)S(1)}) custom-call(s32[3,512]{1,0:T(4,128)} %nb.1, f32[3,512]{1,0:T(4,128)} %ew.1, f32[1,100]{1,0:T(1,128)} %bitcast.17, f32[1,512]{1,0:T(1,128)} %bitcast.16, ...), custom_call_target="tpu_custom_call" | custom-call | flops 805306368 | bytes 8000000 | tf_op jit(solution)/shard_map/pallas_call | solution.py:36
  7.6 6.3 %collective-permute-start = (bf16[128,1024]{1,0:T(8,128)(2,1)S(1)}, bf16[128,1024]{1,0:T(8,128)(2,1)S(1)}, u32[]{:S(2)}, u32[]{:S(2)}) collective-permute-start(bf16[128,1024]{1,0:T(8,128)(2,1)S(1)} %get-tuple-element.22), channel_id=1, source_target_pairs={{0,1},{1,0},{2,3},{3,2},{4,5},{5,4},{6,7},{7,6},{8,9},{9,8},{10,11... | collective-permute-start | bytes 786440 | tf_op jit(solution)/shard_map/ppermute | solution.py:320
  13.9 0.0 collective-permute-done.1.far
  13.9 1.2 %collective-permute-done.near = bf16[128,1024]{1,0:T(8,128)(2,1)S(1)} collective-permute-done((bf16[128,1024]{1,0:T(8,128)(2,1)S(1)}, bf16[128,1024]{1,0:T(8,128)(2,1)S(1)}, u32[]{:S(2)}, u32[]{:S(2)}) %collective-permute-start) | collective-permute-done | bytes 262176 | tf_op jit(solution)/shard_map/ppermute | solution.py:320
  15.1 1.6 %shard_map.131 = (f32[100,512]{1,0:T(8,128)S(1)}, bf16[512,1024]{1,0:T(8,128)(2,1)S(1)}, f32[512,1]{1,0:T(8,128)S(1)}) custom-call(f32[512,1024]{1,0:T(8,128)S(1)} %get-tuple-element.20.part, bf16[512,512]{1,0:T(8,128)(2,1)S(1)} %get-tuple-element.21.edges, bf16[128,1024]{1,0:T(8,128)(2,1)S(1)} %collective-permute-done.near, ...), custom_call_target="tpu_custom_call" | custom-call | flops 373293056 | bytes 5000000 | tf_op jit(solution)/shard_map/pallas_call | solution.py:36
  16.7 0.1 broadcast_in_dim.18
  16.8 0.0 copy-start.1
  16.8 17.1 %all_to_all.20 = f16[8,100,512]{2,1,0:T(8,128)(2,1)S(1)} all-to-all(f16[8,100,512]{2,1,0:T(8,128)(2,1)S(1)} %broadcast_in_dim.18), channel_id=1, replica_groups=mesh['xl'=2,'y'=4,'xh'=2,'z'=8,'c'=2] {'xl','y'}, dimensions={0} | all-to-all | bytes 1638400 | tf_op jit(solution)/shard_map/all_to_all | solution.py:332
  33.9 0.2 convert_element_type.7.every
  34.1 0.0 copy-start.3
  34.1 0.0 copy-start.4
  34.1 0.9 %shard_map.132 = (bf16[100,512]{1,0:T(8,128)(2,1)S(1)}, bf16[16,8,1024]{2,1,0:T(8,128)(2,1)S(1)}) custom-call(f32[8,100,512]{2,1,0:T(8,128)S(1)} %convert_element_type.7.every, f32[100,512]{1,0:T(8,128)S(1)} %get-tuple-element.24.field, f32[100,512]{1,0:T(8,128)S(1)} %copy-done.1, f32[100,512]{1,0:T(8,128)S(1)} %get-tuple-element.25.wm, ...), custom_call_target="tpu_custom_call" | custom-call | flops 209715200 | bytes 4000000 | tf_op jit(solution)/shard_map/pallas_call | solution.py:36
  35.0 11.1 %all_to_all.21.parts = bf16[16,8,1024]{2,1,0:T(8,128)(2,1)S(1)} all-to-all(bf16[16,8,1024]{2,1,0:T(8,128)(2,1)S(1)} %get-tuple-element.27), channel_id=1, replica_groups=mesh['xl'=2,'y'=4,'xh'=2,'z'=8,'c'=2] {'xl','y','xh'}, dimensions={0} | all-to-all | bytes 524288 | tf_op jit(solution)/shard_map/all_to_all | solution.py:340
  46.2 3.1 %collective-permute-start.2 = (f32[8,1024]{1,0:T(8,128)S(1)}, f32[8,1024]{1,0:T(8,128)S(1)}, u32[]{:S(2)}, u32[]{:S(2)}) collective-permute-start(f32[8,1024]{1,0:T(8,128)S(1)} %shard_map.133.mine), channel_id=1, source_target_pairs={{0,1},{1,0},{2,3},{3,2},{4,5},{5,4},{6,7},{7,6},{8,9},{9,8},{10,11... | collective-permute-start | bytes 98312 | tf_op jit(solution)/shard_map/ppermute | solution.py:342
  49.3 0.9 %collective-permute-done.2.met.earlier = f32[8,1024]{1,0:T(8,128)S(1)} collective-permute-done((f32[8,1024]{1,0:T(8,128)S(1)}, f32[8,1024]{1,0:T(8,128)S(1)}, u32[]{:S(2)}, u32[]{:S(2)}) %collective-permute-start.2) | collective-permute-done | bytes 32800 | tf_op jit(solution)/shard_map/ppermute | solution.py:342
  50.2 0.7 shard_map.134
  50.9 3.4 %all-to-all-start.2 = ((bf16[8,8,1024]{2,1,0:T(8,128)(2,1)}), bf16[8,8,1024]{2,1,0:T(8,128)(2,1)S(1)}, u32[]{:S(2)}, u32[]{:S(2)}) async-start(bf16[8,8,1024]{2,1,0:T(8,128)(2,1)} %shard_map.134), calls=%async_computation.2 | async-start | bytes 262144 | tf_op jit(solution)/shard_map/all_to_all | solution.py:359
  54.3 1.9 %shard_map.135 = (f32[256,1024]{1,0:T(8,128)S(1)}, bf16[128,1024]{1,0:T(8,128)(2,1)S(1)}, bf16[128,1024]{1,0:T(8,128)(2,1)S(1)}) custom-call(f32[8,1024]{1,0:T(8,128)S(1)} %collective-permute-done.2.met.earlier, s32[3,512]{1,0:T(4,128)S(1)} %copy-done.3, f32[3,512]{1,0:T(4,128)S(1)} %copy-done.4, bf16[100,512]{1,0:T(8,128)(2,1)S(1)} %get-tuple-element.28.fore_grad, ...), custom_call_target="tpu_custom_call" | custom-call | flops 641728512 | bytes 6000000 | tf_op jit(solution)/shard_map/pallas_call | solution.py:36
  56.2 0.7 collective-permute-start.3
  56.9 1.7 %collective-permute-start.4 = (bf16[128,1024]{1,0:T(8,128)(2,1)S(1)}, bf16[128,1024]{1,0:T(8,128)(2,1)S(1)}, u32[]{:S(2)}, u32[]{:S(2)}) collective-permute-start(bf16[128,1024]{1,0:T(8,128)(2,1)S(1)} %get-tuple-element.32), channel_id=1, source_target_pairs={{1,2},{3,4},{5,6},{7,8},{9,10},{11,12},{13,14},{15,16},{17,18},{19... | collective-permute-start | bytes 786440 | tf_op jit(solution)/shard_map/ppermute | solution.py:354
  58.6 3.6 %all-to-all-done.2.parts = bf16[8,8,1024]{2,1,0:T(8,128)(2,1)S(1)} async-done(((bf16[8,8,1024]{2,1,0:T(8,128)(2,1)}), bf16[8,8,1024]{2,1,0:T(8,128)(2,1)S(1)}, u32[]{:S(2)}, u32[]{:S(2)}) %all-to-all-start.2) | async-done | bytes 131104 | tf_op jit(solution)/shard_map/all_to_all | solution.py:359
  62.2 0.8 %shard_map.136 = bf16[16,8,1024]{2,1,0:T(8,128)(2,1)} custom-call(bf16[8,8,1024]{2,1,0:T(8,128)(2,1)S(1)} %all-to-all-done.2.parts, f32[256,1024]{1,0:T(8,128)S(1)} %get-tuple-element.30.earlier.own), custom_call_target="tpu_custom_call" | custom-call | tf_op jit(solution)/shard_map/pallas_call | solution.py:36
  62.9 3.5 %all-to-all-start.3 = ((bf16[16,8,1024]{2,1,0:T(8,128)(2,1)}), bf16[16,8,1024]{2,1,0:T(8,128)(2,1)S(1)}, u32[]{:S(2)}, u32[]{:S(2)}) async-start(bf16[16,8,1024]{2,1,0:T(8,128)(2,1)} %shard_map.136), calls=%async_computation.3 | async-start | bytes 524288 | tf_op jit(solution)/shard_map/all_to_all | solution.py:363
  66.5 0.0 collective-permute-done.3.near
  66.5 0.0 collective-permute-done.4.far
  66.5 1.0 %shard_map.137.earlier = bf16[1,256,1024]{2,1,0:T(8,128)(2,1)} custom-call(f32[256,1024]{1,0:T(8,128)S(1)} %get-tuple-element.30.earlier.own, bf16[128,1024]{1,0:T(8,128)(2,1)S(1)} %collective-permute-done.3.near, bf16[128,1024]{1,0:T(8,128)(2,1)S(1)} %collective-permute-done.4.far), custom_call_target="tpu_custom_call" | custom-call | tf_op jit(solution)/shard_map/pallas_call | solution.py:36
  67.5 6.4 %all-to-all-done.3.parts = bf16[16,8,1024]{2,1,0:T(8,128)(2,1)S(1)} async-done(((bf16[16,8,1024]{2,1,0:T(8,128)(2,1)}), bf16[16,8,1024]{2,1,0:T(8,128)(2,1)S(1)}, u32[]{:S(2)}, u32[]{:S(2)}) %all-to-all-start.3) | async-done | bytes 262176 | tf_op jit(solution)/shard_map/all_to_all | solution.py:363
  73.9 0.8 %shard_map.138 = (f32[100,1024]{1,0:T(8,128)}, f32[1,1024]{1,0:T(1,128)}, f32[1,1]{1,0:T(1,128)}) custom-call(bf16[16,8,1024]{2,1,0:T(8,128)(2,1)S(1)} %all-to-all-done.3.parts, bf16[1,256,1024]{2,1,0:T(8,128)(2,1)} %shard_map.137.earlier), custom_call_target="tpu_custom_call" | custom-call | tf_op jit(solution)/shard_map/pallas_call | solution.py:36
  (7 shorter events, 0.1 us)
Async XLA Ops:
  0.6 14.5 %copy-start = (bf16[100,1024]{1,0:T(8,128)(2,1)S(1)}, bf16[100,1024]{1,0:T(8,128)(2,1)}, u32[]{:S(2)}) copy-start(bf16[100,1024]{1,0:T(8,128)(2,1)} %proj.5) | copy-start | bytes 614404
  0.6 14.4 %copy-start.2 = (f32[1024]{0:T(1024)S(1)}, f32[1024]{0:T(1024)}, u32[]{:S(2)}) copy-start(f32[1024]{0:T(1024)} %param.19) | copy-start | bytes 12292
  1.7 12.3 %collective-permute-start.1 = (bf16[128,1024]{1,0:T(8,128)(2,1)S(1)}, bf16[128,1024]{1,0:T(8,128)(2,1)S(1)}, u32[]{:S(2)}, u32[]{:S(2)}) collective-permute-start(bf16[128,1024]{1,0:T(8,128)(2,1)S(1)} %shard_map.129.earlier), channel_id=1, source_target_pairs={{1,2},{3,4},{5,6},{7,8},{9,10},{11,12},{13,14},{15,16},{17,18},{19... | collective-permute-start | bytes 786440 | tf_op jit(solution)/shard_map/ppermute | solution.py:293
  7.6 7.5 %collective-permute-start = (bf16[128,1024]{1,0:T(8,128)(2,1)S(1)}, bf16[128,1024]{1,0:T(8,128)(2,1)S(1)}, u32[]{:S(2)}, u32[]{:S(2)}) collective-permute-start(bf16[128,1024]{1,0:T(8,128)(2,1)S(1)} %get-tuple-element.22), channel_id=1, source_target_pairs={{0,1},{1,0},{2,3},{3,2},{4,5},{5,4},{6,7},{7,6},{8,9},{9,8},{10,11... | collective-permute-start | bytes 786440 | tf_op jit(solution)/shard_map/ppermute | solution.py:320
  16.8 17.3 %copy-start.1 = (f32[100,512]{1,0:T(8,128)S(1)}, f32[100,512]{1,0:T(8,128)}, u32[]{:S(2)}) copy-start(f32[100,512]{1,0:T(8,128)} %target.1) | copy-start | bytes 614404
  34.1 20.1 %copy-start.3 = (s32[3,512]{1,0:T(4,128)S(1)}, s32[3,512]{1,0:T(4,128)}, u32[]{:S(2)}) copy-start(s32[3,512]{1,0:T(4,128)} %nb.1) | copy-start | bytes 18436
  34.1 20.1 %copy-start.4 = (f32[3,512]{1,0:T(4,128)S(1)}, f32[3,512]{1,0:T(4,128)}, u32[]{:S(2)}) copy-start(f32[3,512]{1,0:T(4,128)} %ew.1) | copy-start | bytes 18436
  46.2 4.0 %collective-permute-start.2 = (f32[8,1024]{1,0:T(8,128)S(1)}, f32[8,1024]{1,0:T(8,128)S(1)}, u32[]{:S(2)}, u32[]{:S(2)}) collective-permute-start(f32[8,1024]{1,0:T(8,128)S(1)} %shard_map.133.mine), channel_id=1, source_target_pairs={{0,1},{1,0},{2,3},{3,2},{4,5},{5,4},{6,7},{7,6},{8,9},{9,8},{10,11... | collective-permute-start | bytes 98312 | tf_op jit(solution)/shard_map/ppermute | solution.py:342
  50.9 11.3 %all-to-all-start.2 = ((bf16[8,8,1024]{2,1,0:T(8,128)(2,1)}), bf16[8,8,1024]{2,1,0:T(8,128)(2,1)S(1)}, u32[]{:S(2)}, u32[]{:S(2)}) async-start(bf16[8,8,1024]{2,1,0:T(8,128)(2,1)} %shard_map.134), calls=%async_computation.2 | async-start | bytes 262144 | tf_op jit(solution)/shard_map/all_to_all | solution.py:359
  56.2 10.3 %collective-permute-start.3 = (bf16[128,1024]{1,0:T(8,128)(2,1)S(1)}, bf16[128,1024]{1,0:T(8,128)(2,1)S(1)}, u32[]{:S(2)}, u32[]{:S(2)}) collective-permute-start(bf16[128,1024]{1,0:T(8,128)(2,1)S(1)} %get-tuple-element.31), channel_id=1, source_target_pairs={{0,1},{1,0},{2,3},{3,2},{4,5},{5,4},{6,7},{7,6},{8,9},{9,8},{10,11... | collective-permute-start | bytes 786440 | tf_op jit(solution)/shard_map/ppermute | solution.py:355
  56.9 9.6 %collective-permute-start.4 = (bf16[128,1024]{1,0:T(8,128)(2,1)S(1)}, bf16[128,1024]{1,0:T(8,128)(2,1)S(1)}, u32[]{:S(2)}, u32[]{:S(2)}) collective-permute-start(bf16[128,1024]{1,0:T(8,128)(2,1)S(1)} %get-tuple-element.32), channel_id=1, source_target_pairs={{1,2},{3,4},{5,6},{7,8},{9,10},{11,12},{13,14},{15,16},{17,18},{19... | collective-permute-start | bytes 786440 | tf_op jit(solution)/shard_map/ppermute | solution.py:354
  62.9 11.0 %all-to-all-start.3 = ((bf16[16,8,1024]{2,1,0:T(8,128)(2,1)}), bf16[16,8,1024]{2,1,0:T(8,128)(2,1)S(1)}, u32[]{:S(2)}, u32[]{:S(2)}) async-start(bf16[16,8,1024]{2,1,0:T(8,128)(2,1)} %shard_map.136), calls=%async_computation.3 | async-start | bytes 524288 | tf_op jit(solution)/shard_map/all_to_all | solution.py:363

commit v9 on v8

--- a/solution.py
+++ b/solution.py
@@ -13,8 +13,8 @@
 NORM_EPS = 1e-05
 MEMBER = ("xl", "y")
 GRID = ("xh", "z", "c")
-PLANE = ("xl", "y", "xh")
-CHUNK = 8
+NEAR = ("xh", "c")
+CHUNK = 16
 BF16 = jnp.bfloat16
 F32 = jnp.float32
 VMEM_LIMIT = 24 * 1024 * 1024
@@ -223,7 +223,7 @@
 
 
 def narrowed(total, variables):
-    here = lax.axis_index(PLANE) == variables // CHUNK
+    here = lax.axis_index(MEMBER) == variables // CHUNK
     first = variables % CHUNK + 1
     loss = total[first : first + 1] + total[first + 1 : first + 2]
     high = loss.astype(BF16).astype(F32)
@@ -232,12 +232,13 @@
     return jnp.where(here, split, total).astype(BF16)
 
 
-def fold_kernel(parts, out):
-    out[...] = jnp.sum(parts[...].astype(F32), axis=0)
-
-
-def pair_kernel(variables, mine, met, out):
-    total = narrowed(mine[...] + met[...], variables)
+def fold_kernel(variables, parts, out):
+    out[...] = narrowed(jnp.sum(parts[...].astype(F32), axis=0), variables)
+
+
+def quad_kernel(variables, mine, a, b, c, out):
+    pair = mine[...].astype(F32) + a[...].astype(F32)
+    total = narrowed(pair + (b[...].astype(F32) + c[...].astype(F32)), variables)
     for i in range(out.shape[0]):
         out[i] = total
 
@@ -281,7 +282,6 @@
     variables = output_projection.shape[0]
     members = lax.axis_size(MEMBER)
     slabs = lax.axis_size(GRID)
-    plane = lax.axis_size(PLANE)
     gain = layer_norm_gain[None]
     swap = [(0, 1), (1, 0)]
     links = [((i + 1) % slabs, (i + 2) % slabs) for i in range(0, slabs, 2)]
@@ -332,25 +332,27 @@
     every = lax.all_to_all(sent, MEMBER, 0, 0, tiled=True).astype(F32)
     fore_grad, parts = call(
         loss_kernel,
-        [((variables, points), BF16), ((plane, CHUNK, channels), BF16)],
+        [((variables, points), BF16), ((members, CHUNK, channels), BF16)],
         flops=4 * points * channels * variables,
         moved=4_000_000,
     )(every, field, target, weight_map, output_projection, scaled, gain)
 
-    parts = lax.all_to_all(parts, PLANE, 0, 0, tiled=True)
-    (mine,) = call(fold_kernel, [((CHUNK, channels), F32)])(parts)
+    parts = lax.all_to_all(parts, MEMBER, 0, 0, tiled=True)
+    (mine,) = call(functools.partial(fold_kernel, variables), [((CHUNK, channels), BF16)])(parts)
     met = lax.ppermute(mine, "c", swap)
+    across = lax.ppermute(mine, "xh", swap)
+    oblique = lax.ppermute(mine, NEAR, [(i, 3 - i) for i in range(4)])
     depth = lax.axis_size("z")
     (parts,) = call(
-        functools.partial(pair_kernel, variables), [((depth, CHUNK, channels), BF16)]
-    )(mine, met)
+        functools.partial(quad_kernel, variables), [((depth, CHUNK, channels), BF16)]
+    )(mine, met, across, oblique)
     own, near_grad, far_grad = call(
         back_kernel,
         [((mesh_count, channels), F32), ((rim, channels), BF16), ((rim, channels), BF16)],
         flops=2 * points * channels * (extent + variables),
         moved=6_000_000,
         spaces="a",
-    )(met, neighbours, edge_weight, fore_grad, output_projection, scaled, gain, rscale)
+    )(oblique, neighbours, edge_weight, fore_grad, output_projection, scaled, gain, rscale)
     far_grad = lax.ppermute(far_grad, GRID, links)
     near_grad = lax.ppermute(near_grad, "c", swap)
     (latent_grad,) = call(finish_latent_kernel, [((1, mesh_count, channels), BF16)])(
@@ -358,9 +360,9 @@
     )
     parts = lax.all_to_all(parts, "z", 0, 0, tiled=True)
     (parts,) = call(
-        functools.partial(spread_kernel, variables), [((plane, CHUNK, channels), BF16)], "va"
+        functools.partial(spread_kernel, variables), [((members, CHUNK, channels), BF16)], "va"
     )(parts, own)
-    parts = lax.all_to_all(parts, PLANE, 0, 0, tiled=True)
+    parts = lax.all_to_all(parts, MEMBER, 0, 0, tiled=True)
     wout, gain_grad, crps = call(
         functools.partial(finish_weights_kernel, points * slabs * variables),
         [((variables, channels), F32), ((1, channels), F32), ((1, 1), F32)],

time: 76.1 us -> 79.8 us (1.049); the launches traced: 74.7 us -> 79.4 us
  waiting for transfers between devices: 12 us -> 16.8 us
  blocking collectives: 28.2 us -> 26.1 us
  starting transfers between devices: 21.9 us -> 23.9 us
    ppermute x0 -> x2, starting transfers between devices: none -> 5.33 us  [the longest x1 4.09 us: per_device(): oblique = lax.ppermute(mine, NEAR, [(i, 3 - i) for i in range(4)])]
    all_to_all x1, waiting for transfers between devices: 3.58 us -> 7.57 us  [per_device(): parts = lax.all_to_all(parts, 'z', 0, 0, tiled=True)]
    ppermute x1, starting transfers between devices: 3.12 us -> 0.01 us  [per_device(): met = lax.ppermute(mine, 'c', swap)]
    ppermute x0 -> x2, waiting for transfers between devices: none -> 3.02 us  [the longest x1 2.67 us: per_device(): across = lax.ppermute(mine, 'xh', swap)]
    all_to_all x1, blocking collectives: 11.1 us -> 8.96 us  [per_device(): parts = lax.all_to_all(parts, MEMBER, 0, 0, tiled=True)]
    all_to_all x1, waiting for transfers between devices: 6.44 us -> 5.06 us  [per_device(): parts = lax.all_to_all(parts, MEMBER, 0, 0, tiled=True)]
    ppermute x1, waiting for transfers between devices: 0.86 us -> 0.01 us  [per_device(): met = lax.ppermute(mine, 'c', swap)]
  transfers between devices with their start and end apart: 7 -> 9, of which waited for: 4 -> 5; matrix products, arithmetic and copies ran while one was open for 0% -> 0% of each run, Pallas kernels for 9% -> 8%
where the time goes in v9:
time: 79.8 us; the launch traced here: 79.4 us
  blocking collectives  26.1 us (33%)
  starting transfers between devices  23.9 us (30%)
  waiting for transfers between devices  16.8 us (21%)
  Pallas kernels  11.5 us (14%)
  between operations  0.8 us (1%)
    all_to_all x1, blocking collectives, per_device(): every = lax.all_to_all(sent, MEMBER, 0, 0, tiled=True).astype(F32)  17.1 us
    pallas_call x10, Pallas kernels, run(): pl.pallas_call(kernel, out_shape=[jax.ShapeDtypeStruct(s, d) for s, d in...  11.5 us
    all_to_all x1, blocking collectives, per_device(): parts = lax.all_to_all(parts, MEMBER, 0, 0, tiled=True)  8.96 us
    all_to_all x1, waiting for transfers between devices, per_device(): parts = lax.all_to_all(parts, 'z', 0, 0, tiled=True)  7.57 us
    ppermute x1, starting transfers between devices, per_device(): near = lax.ppermute(near_send, 'c', swap)  6.32 us
    all_to_all x1, waiting for transfers between devices, per_device(): parts = lax.all_to_all(parts, MEMBER, 0, 0, tiled=True)  5.06 us
    ppermute x1, starting transfers between devices, per_device(): oblique = lax.ppermute(mine, NEAR, [(i, 3 - i) for i in range(4)])  4.09 us
    all_to_all x1, starting transfers between devices, per_device(): parts = lax.all_to_all(parts, 'z', 0, 0, tiled=True)  3.41 us
  transfers between devices with their start and end apart: 9, of which 5 were waited for; matrix products, arithmetic and copies ran while one was open for 0% of the time, Pallas kernels for 8%

profile of v9, /device:TPU:1, one launch (start us, length us, event | category | flops | bytes accessed | tf_op | source)
XLA Modules:
  0.0 79.4 jit_solution(12885802901745873787)
XLA Ops:
  0.7 1.0 %shard_map.129.earlier = bf16[128,1024]{1,0:T(8,128)(2,1)S(1)} custom-call(bf16[256,1024]{1,0:T(8,128)(2,1)} %bitcast.11), custom_call_target="tpu_custom_call" | custom-call | tf_op jit(solution)/shard_map/pallas_call | solution.py:36
  1.7 3.1 %collective-permute-start.1 = (bf16[128,1024]{1,0:T(8,128)(2,1)S(1)}, bf16[128,1024]{1,0:T(8,128)(2,1)S(1)}, u32[]{:S(2)}, u32[]{:S(2)}) collective-permute-start(bf16[128,1024]{1,0:T(8,128)(2,1)S(1)} %shard_map.129.earlier), channel_id=1, source_target_pairs={{1,2},{3,4},{5,6},{7,8},{9,10},{11,12},{13,14},{15,16},{17,18},{19... | collective-permute-start | bytes 786440 | tf_op jit(solution)/shard_map/ppermute | solution.py:293
  4.8 2.8 %shard_map.130 = (bf16[128,1024]{1,0:T(8,128)(2,1)S(1)}, bf16[512,512]{1,0:T(8,128)(2,1)S(1)}, f32[512,1024]{1,0:T(8,128)S(1)}, f32[100,512]{1,0:T(8,128)S(1)}, f32[100,512]{1,0:T(8,128)S(1)}) custom-call(s32[3,512]{1,0:T(4,128)} %nb.1, f32[3,512]{1,0:T(4,128)} %ew.1, f32[1,100]{1,0:T(1,128)} %bitcast.17, f32[1,512]{1,0:T(1,128)} %bitcast.16, ...), custom_call_target="tpu_custom_call" | custom-call | flops 805306368 | bytes 8000000 | tf_op jit(solution)/shard_map/pallas_call | solution.py:36
  7.6 6.3 %collective-permute-start = (bf16[128,1024]{1,0:T(8,128)(2,1)S(1)}, bf16[128,1024]{1,0:T(8,128)(2,1)S(1)}, u32[]{:S(2)}, u32[]{:S(2)}) collective-permute-start(bf16[128,1024]{1,0:T(8,128)(2,1)S(1)} %get-tuple-element.22), channel_id=1, source_target_pairs={{0,1},{1,0},{2,3},{3,2},{4,5},{5,4},{6,7},{7,6},{8,9},{9,8},{10,11... | collective-permute-start | bytes 786440 | tf_op jit(solution)/shard_map/ppermute | solution.py:320
  13.9 0.0 collective-permute-done.1.far
  13.9 1.2 %collective-permute-done.near = bf16[128,1024]{1,0:T(8,128)(2,1)S(1)} collective-permute-done((bf16[128,1024]{1,0:T(8,128)(2,1)S(1)}, bf16[128,1024]{1,0:T(8,128)(2,1)S(1)}, u32[]{:S(2)}, u32[]{:S(2)}) %collective-permute-start) | collective-permute-done | bytes 262176 | tf_op jit(solution)/shard_map/ppermute | solution.py:320
  15.1 1.6 %shard_map.131 = (f32[100,512]{1,0:T(8,128)S(1)}, bf16[512,1024]{1,0:T(8,128)(2,1)S(1)}, f32[512,1]{1,0:T(8,128)S(1)}) custom-call(f32[512,1024]{1,0:T(8,128)S(1)} %get-tuple-element.20.part, bf16[512,512]{1,0:T(8,128)(2,1)S(1)} %get-tuple-element.21.edges, bf16[128,1024]{1,0:T(8,128)(2,1)S(1)} %collective-permute-done.near, ...), custom_call_target="tpu_custom_call" | custom-call | flops 373293056 | bytes 5000000 | tf_op jit(solution)/shard_map/pallas_call | solution.py:36
  16.7 0.1 broadcast_in_dim.18
  16.8 0.0 copy-start.1
  16.8 17.1 %all_to_all.20 = f16[8,100,512]{2,1,0:T(8,128)(2,1)S(1)} all-to-all(f16[8,100,512]{2,1,0:T(8,128)(2,1)S(1)} %broadcast_in_dim.18), channel_id=1, replica_groups=mesh['xl'=2,'y'=4,'xh'=2,'z'=8,'c'=2] {'xl','y'}, dimensions={0} | all-to-all | bytes 1638400 | tf_op jit(solution)/shard_map/all_to_all | solution.py:332
  33.9 0.2 convert_element_type.7.every
  34.1 0.0 copy-start.3
  34.1 0.0 copy-start.4
  34.1 0.9 %shard_map.132 = (bf16[100,512]{1,0:T(8,128)(2,1)S(1)}, bf16[8,16,1024]{2,1,0:T(8,128)(2,1)S(1)}) custom-call(f32[8,100,512]{2,1,0:T(8,128)S(1)} %convert_element_type.7.every, f32[100,512]{1,0:T(8,128)S(1)} %get-tuple-element.24.field, f32[100,512]{1,0:T(8,128)S(1)} %copy-done.1, f32[100,512]{1,0:T(8,128)S(1)} %get-tuple-element.25.wm, ...), custom_call_target="tpu_custom_call" | custom-call | flops 209715200 | bytes 4000000 | tf_op jit(solution)/shard_map/pallas_call | solution.py:36
  35.0 9.0 %all_to_all.21.parts = bf16[8,16,1024]{2,1,0:T(8,128)(2,1)S(1)} all-to-all(bf16[8,16,1024]{2,1,0:T(8,128)(2,1)S(1)} %get-tuple-element.27), channel_id=1, replica_groups=mesh['xl'=2,'y'=4,'xh'=2,'z'=8,'c'=2] {'xl','y'}, dimensions={0} | all-to-all | bytes 524288 | tf_op jit(solution)/shard_map/all_to_all | solution.py:340
  44.0 0.1 shard_map.133.mine
  44.1 4.1 %collective-permute-start.4 = (bf16[16,1024]{1,0:T(8,128)(2,1)S(1)}, bf16[16,1024]{1,0:T(8,128)(2,1)S(1)}, u32[]{:S(2)}, u32[]{:S(2)}) collective-permute-start(bf16[16,1024]{1,0:T(8,128)(2,1)S(1)} %shard_map.133.mine), channel_id=1, source_target_pairs={{0,17},{1,16},{16,1},{17,0},{2,19},{3,18},{18,3},{19,2},{4,21},{5,... | collective-permute-start | bytes 98312 | tf_op jit(solution)/shard_map/ppermute | solution.py:344
  48.2 1.2 %collective-permute-start.3 = (bf16[16,1024]{1,0:T(8,128)(2,1)S(1)}, bf16[16,1024]{1,0:T(8,128)(2,1)S(1)}, u32[]{:S(2)}, u32[]{:S(2)}) collective-permute-start(bf16[16,1024]{1,0:T(8,128)(2,1)S(1)} %shard_map.133.mine), channel_id=1, source_target_pairs={{0,16},{16,0},{1,17},{17,1},{2,18},{18,2},{3,19},{19,3},{4,20},{20... | collective-permute-start | bytes 98312 | tf_op jit(solution)/shard_map/ppermute | solution.py:343
  49.4 0.0 collective-permute-start.2
  49.4 0.4 collective-permute-done.4.c.earlier
  49.8 2.7 %collective-permute-done.3.b = bf16[16,1024]{1,0:T(8,128)(2,1)S(1)} collective-permute-done((bf16[16,1024]{1,0:T(8,128)(2,1)S(1)}, bf16[16,1024]{1,0:T(8,128)(2,1)S(1)}, u32[]{:S(2)}, u32[]{:S(2)}) %collective-permute-start.3) | collective-permute-done | bytes 32800 | tf_op jit(solution)/shard_map/ppermute | solution.py:343
  52.4 0.7 shard_map.134
  53.2 3.4 %all-to-all-start.2 = ((bf16[8,16,1024]{2,1,0:T(8,128)(2,1)}), bf16[8,16,1024]{2,1,0:T(8,128)(2,1)S(1)}, u32[]{:S(2)}, u32[]{:S(2)}) async-start(bf16[8,16,1024]{2,1,0:T(8,128)(2,1)} %shard_map.134), calls=%async_computation.2 | async-start | bytes 524288 | tf_op jit(solution)/shard_map/all_to_all | solution.py:361
  56.6 1.9 %shard_map.135 = (f32[256,1024]{1,0:T(8,128)S(1)}, bf16[128,1024]{1,0:T(8,128)(2,1)S(1)}, bf16[128,1024]{1,0:T(8,128)(2,1)S(1)}) custom-call(bf16[16,1024]{1,0:T(8,128)(2,1)S(1)} %collective-permute-done.4.c.earlier, s32[3,512]{1,0:T(4,128)S(1)} %copy-done.3, f32[3,512]{1,0:T(4,128)S(1)} %copy-done.4, bf16[100,512]{1,0:T(8,128)(2,1)S(1)} %get-tuple-element.28.fore_grad, ...), custom_call_target="tpu_custom_call" | custom-call | flops 641728512 | bytes 6000000 | tf_op jit(solution)/shard_map/pallas_call | solution.py:36
  58.5 0.6 collective-permute-start.5
  59.1 1.7 %collective-permute-start.6 = (bf16[128,1024]{1,0:T(8,128)(2,1)S(1)}, bf16[128,1024]{1,0:T(8,128)(2,1)S(1)}, u32[]{:S(2)}, u32[]{:S(2)}) collective-permute-start(bf16[128,1024]{1,0:T(8,128)(2,1)S(1)} %get-tuple-element.32), channel_id=1, source_target_pairs={{1,2},{3,4},{5,6},{7,8},{9,10},{11,12},{13,14},{15,16},{17,18},{19... | collective-permute-start | bytes 786440 | tf_op jit(solution)/shard_map/ppermute | solution.py:356
  60.8 7.6 %all-to-all-done.2.parts = bf16[8,16,1024]{2,1,0:T(8,128)(2,1)S(1)} async-done(((bf16[8,16,1024]{2,1,0:T(8,128)(2,1)}), bf16[8,16,1024]{2,1,0:T(8,128)(2,1)S(1)}, u32[]{:S(2)}, u32[]{:S(2)}) %all-to-all-start.2) | async-done | bytes 262176 | tf_op jit(solution)/shard_map/all_to_all | solution.py:361
  68.4 0.8 shard_map.136
  69.2 3.4 %all-to-all-start.3 = ((bf16[8,16,1024]{2,1,0:T(8,128)(2,1)}), bf16[8,16,1024]{2,1,0:T(8,128)(2,1)S(1)}, u32[]{:S(2)}, u32[]{:S(2)}) async-start(bf16[8,16,1024]{2,1,0:T(8,128)(2,1)} %shard_map.136), calls=%async_computation.3 | async-start | bytes 524288 | tf_op jit(solution)/shard_map/all_to_all | solution.py:365
  72.6 1.0 %shard_map.137.earlier = bf16[1,256,1024]{2,1,0:T(8,128)(2,1)} custom-call(f32[256,1024]{1,0:T(8,128)S(1)} %get-tuple-element.30.earlier.own, bf16[128,1024]{1,0:T(8,128)(2,1)S(1)} %collective-permute-done.5.near, bf16[128,1024]{1,0:T(8,128)(2,1)S(1)} %collective-permute-done.6.far), custom_call_target="tpu_custom_call" | custom-call | tf_op jit(solution)/shard_map/pallas_call | solution.py:36
  73.6 5.1 %all-to-all-done.3.parts = bf16[8,16,1024]{2,1,0:T(8,128)(2,1)S(1)} async-done(((bf16[8,16,1024]{2,1,0:T(8,128)(2,1)}), bf16[8,16,1024]{2,1,0:T(8,128)(2,1)S(1)}, u32[]{:S(2)}, u32[]{:S(2)}) %all-to-all-start.3) | async-done | bytes 262176 | tf_op jit(solution)/shard_map/all_to_all | solution.py:365
  78.6 0.8 shard_map.138
  (11 shorter events, 0.0 us)
Async XLA Ops:
  0.6 14.5 %copy-start = (bf16[100,1024]{1,0:T(8,128)(2,1)S(1)}, bf16[100,1024]{1,0:T(8,128)(2,1)}, u32[]{:S(2)}) copy-start(bf16[100,1024]{1,0:T(8,128)(2,1)} %proj.5) | copy-start | bytes 614404
  0.6 14.4 %copy-start.2 = (f32[1024]{0:T(1024)S(1)}, f32[1024]{0:T(1024)}, u32[]{:S(2)}) copy-start(f32[1024]{0:T(1024)} %param.19) | copy-start | bytes 12292
  1.7 12.3 %collective-permute-start.1 = (bf16[128,1024]{1,0:T(8,128)(2,1)S(1)}, bf16[128,1024]{1,0:T(8,128)(2,1)S(1)}, u32[]{:S(2)}, u32[]{:S(2)}) collective-permute-start(bf16[128,1024]{1,0:T(8,128)(2,1)S(1)} %shard_map.129.earlier), channel_id=1, source_target_pairs={{1,2},{3,4},{5,6},{7,8},{9,10},{11,12},{13,14},{15,16},{17,18},{19... | collective-permute-start | bytes 786440 | tf_op jit(solution)/shard_map/ppermute | solution.py:293
  7.6 7.5 %collective-permute-start = (bf16[128,1024]{1,0:T(8,128)(2,1)S(1)}, bf16[128,1024]{1,0:T(8,128)(2,1)S(1)}, u32[]{:S(2)}, u32[]{:S(2)}) collective-permute-start(bf16[128,1024]{1,0:T(8,128)(2,1)S(1)} %get-tuple-element.22), channel_id=1, source_target_pairs={{0,1},{1,0},{2,3},{3,2},{4,5},{5,4},{6,7},{7,6},{8,9},{9,8},{10,11... | collective-permute-start | bytes 786440 | tf_op jit(solution)/shard_map/ppermute | solution.py:320
  16.8 17.3 %copy-start.1 = (f32[100,512]{1,0:T(8,128)S(1)}, f32[100,512]{1,0:T(8,128)}, u32[]{:S(2)}) copy-start(f32[100,512]{1,0:T(8,128)} %target.1) | copy-start | bytes 614404
  34.1 22.5 %copy-start.3 = (s32[3,512]{1,0:T(4,128)S(1)}, s32[3,512]{1,0:T(4,128)}, u32[]{:S(2)}) copy-start(s32[3,512]{1,0:T(4,128)} %nb.1) | copy-start | bytes 18436
  34.1 22.5 %copy-start.4 = (f32[3,512]{1,0:T(4,128)S(1)}, f32[3,512]{1,0:T(4,128)}, u32[]{:S(2)}) copy-start(f32[3,512]{1,0:T(4,128)} %ew.1) | copy-start | bytes 18436
  44.1 5.7 %collective-permute-start.4 = (bf16[16,1024]{1,0:T(8,128)(2,1)S(1)}, bf16[16,1024]{1,0:T(8,128)(2,1)S(1)}, u32[]{:S(2)}, u32[]{:S(2)}) collective-permute-start(bf16[16,1024]{1,0:T(8,128)(2,1)S(1)} %shard_map.133.mine), channel_id=1, source_target_pairs={{0,17},{1,16},{16,1},{17,0},{2,19},{3,18},{18,3},{19,2},{4,21},{5,... | collective-permute-start | bytes 98312 | tf_op jit(solution)/shard_map/ppermute | solution.py:344
  48.2 4.3 %collective-permute-start.3 = (bf16[16,1024]{1,0:T(8,128)(2,1)S(1)}, bf16[16,1024]{1,0:T(8,128)(2,1)S(1)}, u32[]{:S(2)}, u32[]{:S(2)}) collective-permute-start(bf16[16,1024]{1,0:T(8,128)(2,1)S(1)} %shard_map.133.mine), channel_id=1, source_target_pairs={{0,16},{16,0},{1,17},{17,1},{2,18},{18,2},{3,19},{19,3},{4,20},{20... | collective-permute-start | bytes 98312 | tf_op jit(solution)/shard_map/ppermute | solution.py:343
  49.4 3.0 %collective-permute-start.2 = (bf16[16,1024]{1,0:T(8,128)(2,1)S(1)}, bf16[16,1024]{1,0:T(8,128)(2,1)S(1)}, u32[]{:S(2)}, u32[]{:S(2)}) collective-permute-start(bf16[16,1024]{1,0:T(8,128)(2,1)S(1)} %shard_map.133.mine), channel_id=1, source_target_pairs={{0,1},{1,0},{2,3},{3,2},{4,5},{5,4},{6,7},{7,6},{8,9},{9,8},{10,11... | collective-permute-start | bytes 98312 | tf_op jit(solution)/shard_map/ppermute | solution.py:342
  53.2 15.2 %all-to-all-start.2 = ((bf16[8,16,1024]{2,1,0:T(8,128)(2,1)}), bf16[8,16,1024]{2,1,0:T(8,128)(2,1)S(1)}, u32[]{:S(2)}, u32[]{:S(2)}) async-start(bf16[8,16,1024]{2,1,0:T(8,128)(2,1)} %shard_map.134), calls=%async_computation.2 | async-start | bytes 524288 | tf_op jit(solution)/shard_map/all_to_all | solution.py:361
  58.5 14.1 %collective-permute-start.5 = (bf16[128,1024]{1,0:T(8,128)(2,1)S(1)}, bf16[128,1024]{1,0:T(8,128)(2,1)S(1)}, u32[]{:S(2)}, u32[]{:S(2)}) collective-permute-start(bf16[128,1024]{1,0:T(8,128)(2,1)S(1)} %get-tuple-element.31), channel_id=1, source_target_pairs={{0,1},{1,0},{2,3},{3,2},{4,5},{5,4},{6,7},{7,6},{8,9},{9,8},{10,11... | collective-permute-start | bytes 786440 | tf_op jit(solution)/shard_map/ppermute | solution.py:357
  59.1 13.5 %collective-permute-start.6 = (bf16[128,1024]{1,0:T(8,128)(2,1)S(1)}, bf16[128,1024]{1,0:T(8,128)(2,1)S(1)}, u32[]{:S(2)}, u32[]{:S(2)}) collective-permute-start(bf16[128,1024]{1,0:T(8,128)(2,1)S(1)} %get-tuple-element.32), channel_id=1, source_target_pairs={{1,2},{3,4},{5,6},{7,8},{9,10},{11,12},{13,14},{15,16},{17,18},{19... | collective-permute-start | bytes 786440 | tf_op jit(solution)/shard_map/ppermute | solution.py:356
  69.2 9.5 %all-to-all-start.3 = ((bf16[8,16,1024]{2,1,0:T(8,128)(2,1)}), bf16[8,16,1024]{2,1,0:T(8,128)(2,1)S(1)}, u32[]{:S(2)}, u32[]{:S(2)}) async-start(bf16[8,16,1024]{2,1,0:T(8,128)(2,1)} %shard_map.136), calls=%async_computation.3 | async-start | bytes 524288 | tf_op jit(solution)/shard_map/all_to_all | solution.py:365

commit v10 on v8

--- a/solution.py
+++ b/solution.py
@@ -15,6 +15,7 @@
 GRID = ("xh", "z", "c")
 PLANE = ("xl", "y", "xh")
 CHUNK = 8
+BLOCK = 128
 BF16 = jnp.bfloat16
 F32 = jnp.float32
 VMEM_LIMIT = 24 * 1024 * 1024
@@ -125,16 +126,23 @@
     copies[7].wait()
 
 
-def forward_kernel(part, edges, near, far, gain, proj, state, f_out, sc_out, rs_out):
-    close, distant = near[...], far[...]
-    twice = jnp.concatenate([close, close, distant, distant], axis=0)
-    mixed = part[...] + dot(edges[...], twice, ((1,), (0,)))
-    centred = mixed - jnp.mean(mixed, axis=1, keepdims=True)
-    rscale = lax.rsqrt(jnp.mean(centred * centred, axis=1, keepdims=True) + NORM_EPS)
-    scaled = (centred * rscale * gain[...]).astype(BF16)
-    sc_out[...] = scaled
-    rs_out[...] = rscale
-    f_out[...] = state[...] + dot(proj[...], scaled, ((1,), (1,)))
+def near_kernel(part, edges, near, out):
+    close = near[...]
+    twice = jnp.concatenate([close, close], axis=0)
+    out[...] = part[...] + dot(edges[:, : twice.shape[0]], twice, ((1,), (0,)))
+
+
+def forward_kernel(part, edges, far, gain, proj, state, f_out, sc_out, rs_out):
+    distant = far[...]
+    twice = jnp.concatenate([distant, distant], axis=0)
+    for r in range(0, part.shape[0], BLOCK):
+        at = slice(r, r + BLOCK)
+        mixed = part[at] + dot(edges[at, twice.shape[0] :], twice, ((1,), (0,)))
+        centred = mixed - jnp.mean(mixed, axis=1, keepdims=True)
+        rscale = lax.rsqrt(jnp.mean(centred * centred, axis=1, keepdims=True) + NORM_EPS)
+        sc_out[at] = (centred * rscale * gain[...]).astype(BF16)
+        rs_out[at] = rscale
+    f_out[...] = state[...] + dot(proj[...], sc_out[...], ((1,), (1,)))
 
 
 def loss_kernel(every, field, target, wm, proj, scaled, gain, fg_out, parts_out):
@@ -318,6 +326,12 @@
         state.reshape(variables, 1, points), far_send,
     )
     near = lax.ppermute(near_send, "c", swap)
+    (part,) = call(
+        near_kernel,
+        [((points, channels), F32)],
+        flops=4 * points * channels * rim,
+        moved=5_000_000,
+    )(part, edges, near)
     field, scaled, rscale = call(
         forward_kernel,
         [
@@ -327,7 +341,7 @@
         ],
         flops=2 * points * channels * (2 * rim + variables),
         moved=5_000_000,
-    )(part, edges, near, far, gain, output_projection, state)
+    )(part, edges, far, gain, output_projection, state)
     sent = jnp.broadcast_to(field.astype(jnp.float16)[None], (members, variables, points))
     every = lax.all_to_all(sent, MEMBER, 0, 0, tiled=True).astype(F32)
     fore_grad, parts = call(

time: 76.1 us -> 79.3 us (1.042)
  waiting for transfers between devices: 12 us -> 16.2 us
  blocking collectives: 28.2 us -> 24.6 us
  starting transfers between devices: 21.9 us -> 24.5 us
    ppermute x1, starting transfers between devices: 3.12 us -> 7.89 us  [per_device(): met = lax.ppermute(mine, 'c', swap)]
    all_to_all x1, blocking collectives: 17.1 us -> 12.7 us  [per_device(): every = lax.all_to_all(sent, MEMBER, 0, 0, tiled=True).astype(F32)]
    ppermute x1, waiting for transfers between devices: 0.01 us -> 4.17 us  [per_device(): far = lax.ppermute(far_send, GRID, links)]
    all_to_all x1, starting transfers between devices: 3.41 us -> 7.29 us  [per_device(): parts = lax.all_to_all(parts, 'z', 0, 0, tiled=True)]
    ppermute x1, starting transfers between devices: 3.11 us -> 0.01 us  [per_device(): far = lax.ppermute(far_send, GRID, links)]
    ppermute x1, starting transfers between devices: 6.32 us -> 3.33 us  [per_device(): near = lax.ppermute(near_send, 'c', swap)]
    pallas_call x10 -> x11, Pallas kernels: 11.4 us -> 11.5 us  [run(): pl.pallas_call(kernel, out_shape=[jax.ShapeDtypeStruct(s, d) for s, d in...]
  transfers between devices with their start and end apart: 7 -> 7, of which waited for: 4 -> 5; matrix products, arithmetic and copies ran while one was open for 0% -> 0% of each run, Pallas kernels for 9% -> 5%
where the time goes in v10:
time: 79.3 us; the launch traced here: 77.9 us
  blocking collectives  24.6 us (31%)
  starting transfers between devices  24.5 us (31%)
  waiting for transfers between devices  16.2 us (20%)
  Pallas kernels  11.5 us (15%)
    all_to_all x1, blocking collectives, per_device(): every = lax.all_to_all(sent, MEMBER, 0, 0, tiled=True).astype(F32)  12.7 us
    all_to_all x1, blocking collectives, per_device(): parts = lax.all_to_all(parts, PLANE, 0, 0, tiled=True)  11.8 us
    pallas_call x11, Pallas kernels, run(): pl.pallas_call(kernel, out_shape=[jax.ShapeDtypeStruct(s, d) for s, d in...  11.5 us
    ppermute x1, starting transfers between devices, per_device(): met = lax.ppermute(mine, 'c', swap)  7.89 us
    all_to_all x1, starting transfers between devices, per_device(): parts = lax.all_to_all(parts, 'z', 0, 0, tiled=True)  7.29 us
    all_to_all x1, waiting for transfers between devices, per_device(): parts = lax.all_to_all(parts, PLANE, 0, 0, tiled=True)  6.44 us
    ppermute x1, waiting for transfers between devices, per_device(): far = lax.ppermute(far_send, GRID, links)  4.17 us
    all_to_all x1, waiting for transfers between devices, per_device(): parts = lax.all_to_all(parts, 'z', 0, 0, tiled=True)  3.58 us
  transfers between devices with their start and end apart: 7, of which 5 were waited for; matrix products, arithmetic and copies ran while one was open for 0% of the time, Pallas kernels for 5%

profile of v10, /device:TPU:1, one launch (start us, length us, event | category | flops | bytes accessed | tf_op | source)
XLA Modules:
  0.0 77.9 jit_solution(14594157562831344380)
XLA Ops:
  0.6 1.0 %shard_map.129.earlier = bf16[128,1024]{1,0:T(8,128)(2,1)S(1)} custom-call(bf16[256,1024]{1,0:T(8,128)(2,1)} %bitcast.11), custom_call_target="tpu_custom_call" | custom-call | tf_op jit(solution)/shard_map/pallas_call | solution.py:37
  1.6 2.8 %shard_map.130 = (bf16[128,1024]{1,0:T(8,128)(2,1)S(1)}, bf16[512,512]{1,0:T(8,128)(2,1)S(1)}, f32[512,1024]{1,0:T(8,128)S(1)}, f32[100,512]{1,0:T(8,128)S(1)}, f32[100,512]{1,0:T(8,128)S(1)}) custom-call(s32[3,512]{1,0:T(4,128)} %nb.1, f32[3,512]{1,0:T(4,128)} %ew.1, f32[1,100]{1,0:T(1,128)} %bitcast.17, f32[1,512]{1,0:T(1,128)} %bitcast.16, ...), custom_call_target="tpu_custom_call" | custom-call | flops 805306368 | bytes 8000000 | tf_op jit(solution)/shard_map/pallas_call | solution.py:37
  4.4 3.3 %collective-permute-start = (bf16[128,1024]{1,0:T(8,128)(2,1)S(1)}, bf16[128,1024]{1,0:T(8,128)(2,1)S(1)}, u32[]{:S(2)}, u32[]{:S(2)}) collective-permute-start(bf16[128,1024]{1,0:T(8,128)(2,1)S(1)} %get-tuple-element.22), channel_id=1, source_target_pairs={{0,1},{1,0},{2,3},{3,2},{4,5},{5,4},{6,7},{7,6},{8,9},{9,8},{10,11... | collective-permute-start | bytes 786440 | tf_op jit(solution)/shard_map/ppermute | solution.py:328
  7.8 0.0 collective-permute-start.1
  7.8 1.2 %collective-permute-done.near = bf16[128,1024]{1,0:T(8,128)(2,1)S(1)} collective-permute-done((bf16[128,1024]{1,0:T(8,128)(2,1)S(1)}, bf16[128,1024]{1,0:T(8,128)(2,1)S(1)}, u32[]{:S(2)}, u32[]{:S(2)}) %collective-permute-start) | collective-permute-done | bytes 262176 | tf_op jit(solution)/shard_map/ppermute | solution.py:328
  8.9 0.5 shard_map.131.part
  9.4 4.2 %collective-permute-done.1.far = bf16[128,1024]{1,0:T(8,128)(2,1)S(1)} collective-permute-done((bf16[128,1024]{1,0:T(8,128)(2,1)S(1)}, bf16[128,1024]{1,0:T(8,128)(2,1)S(1)}, u32[]{:S(2)}, u32[]{:S(2)}) %collective-permute-start.1) | collective-permute-done | bytes 262176 | tf_op jit(solution)/shard_map/ppermute | solution.py:301
  13.6 1.3 %shard_map.132 = (f32[100,512]{1,0:T(8,128)S(1)}, bf16[512,1024]{1,0:T(8,128)(2,1)S(1)}, f32[512,1]{1,0:T(8,128)S(1)}) custom-call(f32[512,1024]{1,0:T(8,128)S(1)} %shard_map.131.part, bf16[512,512]{1,0:T(8,128)(2,1)S(1)} %get-tuple-element.21.edges, bf16[128,1024]{1,0:T(8,128)(2,1)S(1)} %collective-permute-done.1.far, f32[1,1024]{1,0:T(1,128)S(1)} %bitcast.8, ...), custom_call_target="tpu_custom_call" | custom-call | flops 373293056 | bytes 5000000 | tf_op jit(solution)/shard_map/pallas_call | solution.py:37
  14.9 0.1 broadcast_in_dim.18
  14.9 0.0 copy-start.1
  14.9 12.7 %all_to_all.20 = f16[8,100,512]{2,1,0:T(8,128)(2,1)S(1)} all-to-all(f16[8,100,512]{2,1,0:T(8,128)(2,1)S(1)} %broadcast_in_dim.18), channel_id=1, replica_groups=mesh['xl'=2,'y'=4,'xh'=2,'z'=8,'c'=2] {'xl','y'}, dimensions={0} | all-to-all | bytes 1638400 | tf_op jit(solution)/shard_map/all_to_all | solution.py:346
  27.7 0.2 convert_element_type.7.every
  27.9 0.0 copy-start.3
  27.9 0.0 copy-start.4
  27.9 0.9 %shard_map.133 = (bf16[100,512]{1,0:T(8,128)(2,1)S(1)}, bf16[16,8,1024]{2,1,0:T(8,128)(2,1)S(1)}) custom-call(f32[8,100,512]{2,1,0:T(8,128)S(1)} %convert_element_type.7.every, f32[100,512]{1,0:T(8,128)S(1)} %get-tuple-element.24.field, f32[100,512]{1,0:T(8,128)S(1)} %copy-done.1, f32[100,512]{1,0:T(8,128)S(1)} %get-tuple-element.25.wm, ...), custom_call_target="tpu_custom_call" | custom-call | flops 209715200 | bytes 4000000 | tf_op jit(solution)/shard_map/pallas_call | solution.py:37
  28.8 11.8 %all_to_all.21.parts = bf16[16,8,1024]{2,1,0:T(8,128)(2,1)S(1)} all-to-all(bf16[16,8,1024]{2,1,0:T(8,128)(2,1)S(1)} %get-tuple-element.27), channel_id=1, replica_groups=mesh['xl'=2,'y'=4,'xh'=2,'z'=8,'c'=2] {'xl','y','xh'}, dimensions={0} | all-to-all | bytes 524288 | tf_op jit(solution)/shard_map/all_to_all | solution.py:354
  40.7 7.9 %collective-permute-start.2 = (f32[8,1024]{1,0:T(8,128)S(1)}, f32[8,1024]{1,0:T(8,128)S(1)}, u32[]{:S(2)}, u32[]{:S(2)}) collective-permute-start(f32[8,1024]{1,0:T(8,128)S(1)} %shard_map.134.mine), channel_id=1, source_target_pairs={{0,1},{1,0},{2,3},{3,2},{4,5},{5,4},{6,7},{7,6},{8,9},{9,8},{10,11... | collective-permute-start | bytes 98312 | tf_op jit(solution)/shard_map/ppermute | solution.py:356
  48.6 0.9 %collective-permute-done.2.met.earlier = f32[8,1024]{1,0:T(8,128)S(1)} collective-permute-done((f32[8,1024]{1,0:T(8,128)S(1)}, f32[8,1024]{1,0:T(8,128)S(1)}, u32[]{:S(2)}, u32[]{:S(2)}) %collective-permute-start.2) | collective-permute-done | bytes 32800 | tf_op jit(solution)/shard_map/ppermute | solution.py:356
  49.4 0.7 shard_map.135
  50.1 7.3 %all-to-all-start.2 = ((bf16[8,8,1024]{2,1,0:T(8,128)(2,1)}), bf16[8,8,1024]{2,1,0:T(8,128)(2,1)S(1)}, u32[]{:S(2)}, u32[]{:S(2)}) async-start(bf16[8,8,1024]{2,1,0:T(8,128)(2,1)} %shard_map.135), calls=%async_computation.2 | async-start | bytes 262144 | tf_op jit(solution)/shard_map/all_to_all | solution.py:373
  57.4 0.0 copy-done.4
  57.4 1.9 %shard_map.136 = (f32[256,1024]{1,0:T(8,128)S(1)}, bf16[128,1024]{1,0:T(8,128)(2,1)S(1)}, bf16[128,1024]{1,0:T(8,128)(2,1)S(1)}) custom-call(f32[8,1024]{1,0:T(8,128)S(1)} %collective-permute-done.2.met.earlier, s32[3,512]{1,0:T(4,128)S(1)} %copy-done.3, f32[3,512]{1,0:T(4,128)S(1)} %copy-done.4, bf16[100,512]{1,0:T(8,128)(2,1)S(1)} %get-tuple-element.28.fore_grad, ...), custom_call_target="tpu_custom_call" | custom-call | flops 641728512 | bytes 6000000 | tf_op jit(solution)/shard_map/pallas_call | solution.py:37
  59.3 0.7 collective-permute-start.3
  60.0 1.7 %collective-permute-start.4 = (bf16[128,1024]{1,0:T(8,128)(2,1)S(1)}, bf16[128,1024]{1,0:T(8,128)(2,1)S(1)}, u32[]{:S(2)}, u32[]{:S(2)}) collective-permute-start(bf16[128,1024]{1,0:T(8,128)(2,1)S(1)} %get-tuple-element.32), channel_id=1, source_target_pairs={{1,2},{3,4},{5,6},{7,8},{9,10},{11,12},{13,14},{15,16},{17,18},{19... | collective-permute-start | bytes 786440 | tf_op jit(solution)/shard_map/ppermute | solution.py:368
  61.8 3.6 %all-to-all-done.2.parts = bf16[8,8,1024]{2,1,0:T(8,128)(2,1)S(1)} async-done(((bf16[8,8,1024]{2,1,0:T(8,128)(2,1)}), bf16[8,8,1024]{2,1,0:T(8,128)(2,1)S(1)}, u32[]{:S(2)}, u32[]{:S(2)}) %all-to-all-start.2) | async-done | bytes 131104 | tf_op jit(solution)/shard_map/all_to_all | solution.py:373
  65.4 0.8 shard_map.137
  66.1 3.5 %all-to-all-start.3 = ((bf16[16,8,1024]{2,1,0:T(8,128)(2,1)}), bf16[16,8,1024]{2,1,0:T(8,128)(2,1)S(1)}, u32[]{:S(2)}, u32[]{:S(2)}) async-start(bf16[16,8,1024]{2,1,0:T(8,128)(2,1)} %shard_map.137), calls=%async_computation.3 | async-start | bytes 524288 | tf_op jit(solution)/shard_map/all_to_all | solution.py:377
  69.6 0.0 collective-permute-done.3.near
  69.7 0.0 collective-permute-done.4.far
  69.7 1.0 %shard_map.138.earlier = bf16[1,256,1024]{2,1,0:T(8,128)(2,1)} custom-call(f32[256,1024]{1,0:T(8,128)S(1)} %get-tuple-element.30.earlier.own, bf16[128,1024]{1,0:T(8,128)(2,1)S(1)} %collective-permute-done.3.near, bf16[128,1024]{1,0:T(8,128)(2,1)S(1)} %collective-permute-done.4.far), custom_call_target="tpu_custom_call" | custom-call | tf_op jit(solution)/shard_map/pallas_call | solution.py:37
  70.6 6.4 %all-to-all-done.3.parts = bf16[16,8,1024]{2,1,0:T(8,128)(2,1)S(1)} async-done(((bf16[16,8,1024]{2,1,0:T(8,128)(2,1)}), bf16[16,8,1024]{2,1,0:T(8,128)(2,1)S(1)}, u32[]{:S(2)}, u32[]{:S(2)}) %all-to-all-start.3) | async-done | bytes 262176 | tf_op jit(solution)/shard_map/all_to_all | solution.py:377
  77.1 0.8 %shard_map.139 = (f32[100,1024]{1,0:T(8,128)}, f32[1,1024]{1,0:T(1,128)}, f32[1,1]{1,0:T(1,128)}) custom-call(bf16[16,8,1024]{2,1,0:T(8,128)(2,1)S(1)} %all-to-all-done.3.parts, bf16[1,256,1024]{2,1,0:T(8,128)(2,1)} %shard_map.138.earlier), custom_call_target="tpu_custom_call" | custom-call | tf_op jit(solution)/shard_map/pallas_call | solution.py:37
  (8 shorter events, 0.1 us)
Async XLA Ops:
  4.4 4.5 %collective-permute-start = (bf16[128,1024]{1,0:T(8,128)(2,1)S(1)}, bf16[128,1024]{1,0:T(8,128)(2,1)S(1)}, u32[]{:S(2)}, u32[]{:S(2)}) collective-permute-start(bf16[128,1024]{1,0:T(8,128)(2,1)S(1)} %get-tuple-element.22), channel_id=1, source_target_pairs={{0,1},{1,0},{2,3},{3,2},{4,5},{5,4},{6,7},{7,6},{8,9},{9,8},{10,11... | collective-permute-start | bytes 786440 | tf_op jit(solution)/shard_map/ppermute | solution.py:328
  7.8 5.8 %collective-permute-start.1 = (bf16[128,1024]{1,0:T(8,128)(2,1)S(1)}, bf16[128,1024]{1,0:T(8,128)(2,1)S(1)}, u32[]{:S(2)}, u32[]{:S(2)}) collective-permute-start(bf16[128,1024]{1,0:T(8,128)(2,1)S(1)} %shard_map.129.earlier), channel_id=1, source_target_pairs={{1,2},{3,4},{5,6},{7,8},{9,10},{11,12},{13,14},{15,16},{17,18},{19... | collective-permute-start | bytes 786440 | tf_op jit(solution)/shard_map/ppermute | solution.py:301
  8.9 4.6 %copy-start = (bf16[100,1024]{1,0:T(8,128)(2,1)S(1)}, bf16[100,1024]{1,0:T(8,128)(2,1)}, u32[]{:S(2)}) copy-start(bf16[100,1024]{1,0:T(8,128)(2,1)} %proj.5) | copy-start | bytes 614404
  8.9 4.6 %copy-start.2 = (f32[1024]{0:T(1024)S(1)}, f32[1024]{0:T(1024)}, u32[]{:S(2)}) copy-start(f32[1024]{0:T(1024)} %param.19) | copy-start | bytes 12292
  14.9 13.0 %copy-start.1 = (f32[100,512]{1,0:T(8,128)S(1)}, f32[100,512]{1,0:T(8,128)}, u32[]{:S(2)}) copy-start(f32[100,512]{1,0:T(8,128)} %target.1) | copy-start | bytes 614404
  27.9 29.5 %copy-start.3 = (s32[3,512]{1,0:T(4,128)S(1)}, s32[3,512]{1,0:T(4,128)}, u32[]{:S(2)}) copy-start(s32[3,512]{1,0:T(4,128)} %nb.1) | copy-start | bytes 18436
  27.9 29.5 %copy-start.4 = (f32[3,512]{1,0:T(4,128)S(1)}, f32[3,512]{1,0:T(4,128)}, u32[]{:S(2)}) copy-start(f32[3,512]{1,0:T(4,128)} %ew.1) | copy-start | bytes 18436
  40.7 8.7 %collective-permute-start.2 = (f32[8,1024]{1,0:T(8,128)S(1)}, f32[8,1024]{1,0:T(8,128)S(1)}, u32[]{:S(2)}, u32[]{:S(2)}) collective-permute-start(f32[8,1024]{1,0:T(8,128)S(1)} %shard_map.134.mine), channel_id=1, source_target_pairs={{0,1},{1,0},{2,3},{3,2},{4,5},{5,4},{6,7},{7,6},{8,9},{9,8},{10,11... | collective-permute-start | bytes 98312 | tf_op jit(solution)/shard_map/ppermute | solution.py:356
  50.1 15.2 %all-to-all-start.2 = ((bf16[8,8,1024]{2,1,0:T(8,128)(2,1)}), bf16[8,8,1024]{2,1,0:T(8,128)(2,1)S(1)}, u32[]{:S(2)}, u32[]{:S(2)}) async-start(bf16[8,8,1024]{2,1,0:T(8,128)(2,1)} %shard_map.135), calls=%async_computation.2 | async-start | bytes 262144 | tf_op jit(solution)/shard_map/all_to_all | solution.py:373
  59.3 10.3 %collective-permute-start.3 = (bf16[128,1024]{1,0:T(8,128)(2,1)S(1)}, bf16[128,1024]{1,0:T(8,128)(2,1)S(1)}, u32[]{:S(2)}, u32[]{:S(2)}) collective-permute-start(bf16[128,1024]{1,0:T(8,128)(2,1)S(1)} %get-tuple-element.31), channel_id=1, source_target_pairs={{0,1},{1,0},{2,3},{3,2},{4,5},{5,4},{6,7},{7,6},{8,9},{9,8},{10,11... | collective-permute-start | bytes 786440 | tf_op jit(solution)/shard_map/ppermute | solution.py:369
  60.0 9.6 %collective-permute-start.4 = (bf16[128,1024]{1,0:T(8,128)(2,1)S(1)}, bf16[128,1024]{1,0:T(8,128)(2,1)S(1)}, u32[]{:S(2)}, u32[]{:S(2)}) collective-permute-start(bf16[128,1024]{1,0:T(8,128)(2,1)S(1)} %get-tuple-element.32), channel_id=1, source_target_pairs={{1,2},{3,4},{5,6},{7,8},{9,10},{11,12},{13,14},{15,16},{17,18},{19... | collective-permute-start | bytes 786440 | tf_op jit(solution)/shard_map/ppermute | solution.py:368
  66.1 11.0 %all-to-all-start.3 = ((bf16[16,8,1024]{2,1,0:T(8,128)(2,1)}), bf16[16,8,1024]{2,1,0:T(8,128)(2,1)S(1)}, u32[]{:S(2)}, u32[]{:S(2)}) async-start(bf16[16,8,1024]{2,1,0:T(8,128)(2,1)} %shard_map.137), calls=%async_computation.3 | async-start | bytes 524288 | tf_op jit(solution)/shard_map/all_to_all | solution.py:377

commit v11 on v7

--- a/solution.py
+++ b/solution.py
@@ -15,6 +15,7 @@
 GRID = ("xh", "z", "c")
 PLANE = ("xl", "y", "xh")
 CHUNK = 8
+BLOCK = 128
 BF16 = jnp.bfloat16
 F32 = jnp.float32
 VMEM_LIMIT = 24 * 1024 * 1024
@@ -130,15 +131,16 @@
 
 
 def forward_kernel(part, edges, far, gain, proj, state, f_out, sc_out, rs_out):
-    borrowed = far[...]
-    twice = jnp.concatenate([borrowed, borrowed], axis=0)
-    mixed = part[...] + dot(edges[...], twice, ((1,), (0,)))
-    centred = mixed - jnp.mean(mixed, axis=1, keepdims=True)
-    rscale = lax.rsqrt(jnp.mean(centred * centred, axis=1, keepdims=True) + NORM_EPS)
-    scaled = (centred * rscale * gain[...]).astype(BF16)
-    sc_out[...] = scaled
-    rs_out[...] = rscale
-    f_out[...] = state[...] + dot(proj[...], scaled, ((1,), (1,)))
+    distant = far[...]
+    twice = jnp.concatenate([distant, distant], axis=0)
+    for r in range(0, part.shape[0], BLOCK):
+        at = slice(r, r + BLOCK)
+        mixed = part[at] + dot(edges[at], twice, ((1,), (0,)))
+        centred = mixed - jnp.mean(mixed, axis=1, keepdims=True)
+        rscale = lax.rsqrt(jnp.mean(centred * centred, axis=1, keepdims=True) + NORM_EPS)
+        sc_out[at] = (centred * rscale * gain[...]).astype(BF16)
+        rs_out[at] = rscale
+    f_out[...] = state[...] + dot(proj[...], sc_out[...], ((1,), (1,)))
 
 
 def loss_kernel(every, field, target, wm, proj, scaled, gain, fg_out, parts_out):
@@ -188,7 +190,7 @@
         parts_out[i] = jnp.zeros((CHUNK, channels), BF16)
 
 
-def back_kernel(nb, ew, fore_grad, proj, scaled, gain, rscale, own_out, near_out, far_out):
+def back_kernel(earlier, nb, ew, fore_grad, proj, scaled, gain, rscale, own_out, near_out, far_out):
     channels = scaled.shape[1]
     rim = near_out.shape[0]
     mesh_count = own_out.shape[0]
@@ -236,7 +238,7 @@
     return jnp.where(here, split, total).astype(BF16)
 
 
-def fold_kernel(parts, earlier, out):
+def fold_kernel(parts, out):
     out[...] = jnp.sum(parts[...].astype(F32), axis=0)
 
 
@@ -252,7 +254,7 @@
         out[i] = total
 
 
-def finish_weights_kernel(count, parts, wout_out, gain_out, loss_out):
+def finish_weights_kernel(count, parts, earlier, wout_out, gain_out, loss_out):
     variables = wout_out.shape[0]
     last = variables // CHUNK
     for i in range(last):
@@ -343,33 +345,35 @@
         moved=4_000_000,
     )(every, field, target, weight_map, output_projection, scaled, gain)
 
+    parts = lax.all_to_all(parts, PLANE, 0, 0, tiled=True)
+    (mine,) = call(fold_kernel, [((CHUNK, channels), F32)])(parts)
+    met = lax.ppermute(mine, "c", swap)
+    depth = lax.axis_size("z")
+    (parts,) = call(
+        functools.partial(pair_kernel, variables), [((depth, CHUNK, channels), BF16)]
+    )(mine, met)
     own, near_grad, far_grad = call(
         back_kernel,
         [((mesh_count, channels), F32), ((rim, channels), BF16), ((rim, channels), BF16)],
         flops=2 * points * channels * (extent + variables),
         moved=6_000_000,
-    )(neighbours, edge_weight, fore_grad, output_projection, scaled, gain, rscale)
+        spaces="a",
+    )(met, neighbours, edge_weight, fore_grad, output_projection, scaled, gain, rscale)
     far_grad = lax.ppermute(far_grad, GRID, links)
     near_grad = lax.ppermute(near_grad, "c", swap)
     (latent_grad,) = call(finish_latent_kernel, [((1, mesh_count, channels), BF16)])(
         own, near_grad, far_grad
     )
-    parts = lax.all_to_all(parts, PLANE, 0, 0, tiled=True)
-    (mine,) = call(fold_kernel, [((CHUNK, channels), F32)], "va")(parts, own)
-    met = lax.ppermute(mine, "c", swap)
-    depth = lax.axis_size("z")
-    (parts,) = call(
-        functools.partial(pair_kernel, variables), [((depth, CHUNK, channels), BF16)]
-    )(mine, met)
     parts = lax.all_to_all(parts, "z", 0, 0, tiled=True)
     (parts,) = call(
-        functools.partial(spread_kernel, variables), [((plane, CHUNK, channels), BF16)], "vh"
-    )(parts, latent_grad)
+        functools.partial(spread_kernel, variables), [((plane, CHUNK, channels), BF16)], "va"
+    )(parts, own)
     parts = lax.all_to_all(parts, PLANE, 0, 0, tiled=True)
     wout, gain_grad, crps = call(
         functools.partial(finish_weights_kernel, points * slabs * variables),
         [((variables, channels), F32), ((1, channels), F32), ((1, 1), F32)],
-    )(parts)
+        "vh",
+    )(parts, latent_grad)
     return (crps[0, 0], latent_grad, wout, gain_grad[0])
 
 

time: 76.4 us -> 76.6 us (level)
  starting transfers between devices: 28.6 us -> 24.5 us
  waiting for transfers between devices: 10.6 us -> 13.6 us
  blocking collectives: 23.1 us -> 24.6 us
    all_to_all x1, waiting for transfers between devices: 0.01 us -> 6.44 us  [per_device(): parts = lax.all_to_all(parts, PLANE, 0, 0, tiled=True)]
    ppermute x1, starting transfers between devices: 6.74 us -> 0.71 us  [per_device(): near_grad = lax.ppermute(near_grad, 'c', swap)]
    all_to_all x1, waiting for transfers between devices: 6.95 us -> 3.58 us  [per_device(): parts = lax.all_to_all(parts, 'z', 0, 0, tiled=True)]
    all_to_all x1, blocking collectives: 10.4 us -> 11.8 us  [per_device(): parts = lax.all_to_all(parts, PLANE, 0, 0, tiled=True)]
    ppermute x1, starting transfers between devices: 0.4 us -> 1.72 us  [per_device(): far_grad = lax.ppermute(far_grad, GRID, links)]
    all_to_all x1, starting transfers between devices: 4.56 us -> 3.53 us  [per_device(): parts = lax.all_to_all(parts, PLANE, 0, 0, tiled=True)]
    ppermute x1, starting transfers between devices: 7.01 us -> 7.89 us  [per_device(): met = lax.ppermute(mine, 'c', swap)]
  transfers between devices with their start and end apart: 7 -> 7, of which waited for: 4 -> 5; matrix products, arithmetic and copies ran while one was open for 0% -> 0% of each run, Pallas kernels for 9% -> 9%
where the time goes in v11:
time: 76.6 us; the launch traced here: 75.2 us
  blocking collectives  24.6 us (32%)
  starting transfers between devices  24.5 us (32%)
  waiting for transfers between devices  13.6 us (18%)
  Pallas kernels  11.4 us (15%)
  between operations  0.79 us (1%)
    all_to_all x1, blocking collectives, per_device(): every = lax.all_to_all(sent, MEMBER, 0, 0, tiled=True).astype(F32)  12.7 us
    all_to_all x1, blocking collectives, per_device(): parts = lax.all_to_all(parts, PLANE, 0, 0, tiled=True)  11.8 us
    pallas_call x10, Pallas kernels, run(): pl.pallas_call(kernel, out_shape=[jax.ShapeDtypeStruct(s, d) for s, d in...  11.4 us
    ppermute x1, starting transfers between devices, per_device(): met = lax.ppermute(mine, 'c', swap)  7.89 us
    all_to_all x1, starting transfers between devices, per_device(): parts = lax.all_to_all(parts, 'z', 0, 0, tiled=True)  7.28 us
    all_to_all x1, waiting for transfers between devices, per_device(): parts = lax.all_to_all(parts, PLANE, 0, 0, tiled=True)  6.44 us
    all_to_all x1, waiting for transfers between devices, per_device(): parts = lax.all_to_all(parts, 'z', 0, 0, tiled=True)  3.58 us
    all_to_all x1, starting transfers between devices, per_device(): parts = lax.all_to_all(parts, PLANE, 0, 0, tiled=True)  3.53 us
  transfers between devices with their start and end apart: 7, of which 5 were waited for; matrix products, arithmetic and copies ran while one was open for 0% of the time, Pallas kernels for 9%

profile of v11, /device:TPU:1, one launch (start us, length us, event | category | flops | bytes accessed | tf_op | source)
XLA Modules:
  0.0 75.2 jit_solution(11207608929656521628)
XLA Ops:
  0.7 1.1 %shard_map.129 = (bf16[128,1024]{1,0:T(8,128)(2,1)S(1)}, bf16[128,1024]{1,0:T(8,128)(2,1)S(1)}) custom-call(bf16[256,1024]{1,0:T(8,128)(2,1)} %bitcast.11), custom_call_target="tpu_custom_call" | custom-call | tf_op jit(solution)/shard_map/pallas_call | solution.py:37
  1.8 3.3 %collective-permute-start = (bf16[128,1024]{1,0:T(8,128)(2,1)S(1)}, bf16[128,1024]{1,0:T(8,128)(2,1)S(1)}, u32[]{:S(2)}, u32[]{:S(2)}) collective-permute-start(bf16[128,1024]{1,0:T(8,128)(2,1)S(1)} %get-tuple-element.21), channel_id=1, source_target_pairs={{0,1},{1,0},{2,3},{3,2},{4,5},{5,4},{6,7},{7,6},{8,9},{9,8},{10,11... | collective-permute-start | bytes 786440 | tf_op jit(solution)/shard_map/ppermute | solution.py:303
  5.1 0.0 collective-permute-start.1
  5.1 1.2 %collective-permute-done.near = bf16[128,1024]{1,0:T(8,128)(2,1)S(1)} collective-permute-done((bf16[128,1024]{1,0:T(8,128)(2,1)S(1)}, bf16[128,1024]{1,0:T(8,128)(2,1)S(1)}, u32[]{:S(2)}, u32[]{:S(2)}) %collective-permute-start) | collective-permute-done | bytes 262176 | tf_op jit(solution)/shard_map/ppermute | solution.py:303
  6.2 3.0 %shard_map.130 = (bf16[512,256]{1,0:T(8,128)(2,1)S(1)}, f32[512,1024]{1,0:T(8,128)S(1)}, f32[100,512]{1,0:T(8,128)S(1)}, f32[100,512]{1,0:T(8,128)S(1)}) custom-call(s32[3,512]{1,0:T(4,128)} %nb.1, f32[3,512]{1,0:T(4,128)} %ew.1, f32[1,100]{1,0:T(1,128)} %bitcast.17, f32[1,512]{1,0:T(1,128)} %bitcast.16, bf16[256,1024]{1,0:T(8,128)(2,1)} %bitcast.12, ...), custom_call_target="tpu_custom_call" | custom-call | flops 805306368 | bytes 8000000 | tf_op jit(solution)/shard_map/pallas_call | solution.py:37
  9.3 1.6 %collective-permute-done.1.far = bf16[128,1024]{1,0:T(8,128)(2,1)S(1)} collective-permute-done((bf16[128,1024]{1,0:T(8,128)(2,1)S(1)}, bf16[128,1024]{1,0:T(8,128)(2,1)S(1)}, u32[]{:S(2)}, u32[]{:S(2)}) %collective-permute-start.1) | collective-permute-done | bytes 262176 | tf_op jit(solution)/shard_map/ppermute | solution.py:302
  10.9 0.0 copy-done.2
  10.9 1.3 %shard_map.131 = (f32[100,512]{1,0:T(8,128)S(1)}, bf16[512,1024]{1,0:T(8,128)(2,1)S(1)}, f32[512,1]{1,0:T(8,128)S(1)}) custom-call(f32[512,1024]{1,0:T(8,128)S(1)} %get-tuple-element.22.part, bf16[512,256]{1,0:T(8,128)(2,1)S(1)} %get-tuple-element.23.edges, bf16[128,1024]{1,0:T(8,128)(2,1)S(1)} %collective-permute-done.1.far, f32[1,1024]{1,0:T(1,128)S(1)} %bitcast.8, ...), custom_call_target="tpu_custom_call" | custom-call | flops 373293056 | bytes 5000000 | tf_op jit(solution)/shard_map/pallas_call | solution.py:37
  12.2 0.1 broadcast_in_dim.18
  12.3 0.0 copy-start.1
  12.3 12.7 %all_to_all.20 = f16[8,100,512]{2,1,0:T(8,128)(2,1)S(1)} all-to-all(f16[8,100,512]{2,1,0:T(8,128)(2,1)S(1)} %broadcast_in_dim.18), channel_id=1, replica_groups=mesh['xl'=2,'y'=4,'xh'=2,'z'=8,'c'=2] {'xl','y'}, dimensions={0} | all-to-all | bytes 1638400 | tf_op jit(solution)/shard_map/all_to_all | solution.py:340
  25.0 0.2 convert_element_type.7.every
  25.2 0.0 copy-start.3
  25.2 0.0 copy-start.4
  25.2 0.9 %shard_map.132 = (bf16[100,512]{1,0:T(8,128)(2,1)S(1)}, bf16[16,8,1024]{2,1,0:T(8,128)(2,1)S(1)}) custom-call(f32[8,100,512]{2,1,0:T(8,128)S(1)} %convert_element_type.7.every, f32[100,512]{1,0:T(8,128)S(1)} %get-tuple-element.26.field, f32[100,512]{1,0:T(8,128)S(1)} %copy-done.1, f32[100,512]{1,0:T(8,128)S(1)} %get-tuple-element.27.wm, ...), custom_call_target="tpu_custom_call" | custom-call | flops 209715200 | bytes 4000000 | tf_op jit(solution)/shard_map/pallas_call | solution.py:37
  26.2 11.8 %all_to_all.21.parts = bf16[16,8,1024]{2,1,0:T(8,128)(2,1)S(1)} all-to-all(bf16[16,8,1024]{2,1,0:T(8,128)(2,1)S(1)} %get-tuple-element.29), channel_id=1, replica_groups=mesh['xl'=2,'y'=4,'xh'=2,'z'=8,'c'=2] {'xl','y','xh'}, dimensions={0} | all-to-all | bytes 524288 | tf_op jit(solution)/shard_map/all_to_all | solution.py:348
  38.0 7.9 %collective-permute-start.2 = (f32[8,1024]{1,0:T(8,128)S(1)}, f32[8,1024]{1,0:T(8,128)S(1)}, u32[]{:S(2)}, u32[]{:S(2)}) collective-permute-start(f32[8,1024]{1,0:T(8,128)S(1)} %shard_map.133.mine), channel_id=1, source_target_pairs={{0,1},{1,0},{2,3},{3,2},{4,5},{5,4},{6,7},{7,6},{8,9},{9,8},{10,11... | collective-permute-start | bytes 98312 | tf_op jit(solution)/shard_map/ppermute | solution.py:350
  45.9 0.9 %collective-permute-done.2.met.earlier = f32[8,1024]{1,0:T(8,128)S(1)} collective-permute-done((f32[8,1024]{1,0:T(8,128)S(1)}, f32[8,1024]{1,0:T(8,128)S(1)}, u32[]{:S(2)}, u32[]{:S(2)}) %collective-permute-start.2) | collective-permute-done | bytes 32800 | tf_op jit(solution)/shard_map/ppermute | solution.py:350
  46.8 0.7 shard_map.134
  47.5 7.3 %all-to-all-start.2 = ((bf16[8,8,1024]{2,1,0:T(8,128)(2,1)}), bf16[8,8,1024]{2,1,0:T(8,128)(2,1)S(1)}, u32[]{:S(2)}, u32[]{:S(2)}) async-start(bf16[8,8,1024]{2,1,0:T(8,128)(2,1)} %shard_map.134), calls=%async_computation.2 | async-start | bytes 262144 | tf_op jit(solution)/shard_map/all_to_all | solution.py:367
  54.8 0.0 copy-done.4
  54.8 1.9 %shard_map.135 = (f32[256,1024]{1,0:T(8,128)S(1)}, bf16[128,1024]{1,0:T(8,128)(2,1)S(1)}, bf16[128,1024]{1,0:T(8,128)(2,1)S(1)}) custom-call(f32[8,1024]{1,0:T(8,128)S(1)} %collective-permute-done.2.met.earlier, s32[3,512]{1,0:T(4,128)S(1)} %copy-done.3, f32[3,512]{1,0:T(4,128)S(1)} %copy-done.4, bf16[100,512]{1,0:T(8,128)(2,1)S(1)} %get-tuple-element.30.fore_grad, ...), custom_call_target="tpu_custom_call" | custom-call | flops 641728512 | bytes 6000000 | tf_op jit(solution)/shard_map/pallas_call | solution.py:37
  56.7 0.7 collective-permute-start.3
  57.4 1.7 %collective-permute-start.4 = (bf16[128,1024]{1,0:T(8,128)(2,1)S(1)}, bf16[128,1024]{1,0:T(8,128)(2,1)S(1)}, u32[]{:S(2)}, u32[]{:S(2)}) collective-permute-start(bf16[128,1024]{1,0:T(8,128)(2,1)S(1)} %get-tuple-element.34), channel_id=1, source_target_pairs={{1,2},{3,4},{5,6},{7,8},{9,10},{11,12},{13,14},{15,16},{17,18},{19... | collective-permute-start | bytes 786440 | tf_op jit(solution)/shard_map/ppermute | solution.py:362
  59.1 3.6 %all-to-all-done.2.parts = bf16[8,8,1024]{2,1,0:T(8,128)(2,1)S(1)} async-done(((bf16[8,8,1024]{2,1,0:T(8,128)(2,1)}), bf16[8,8,1024]{2,1,0:T(8,128)(2,1)S(1)}, u32[]{:S(2)}, u32[]{:S(2)}) %all-to-all-start.2) | async-done | bytes 131104 | tf_op jit(solution)/shard_map/all_to_all | solution.py:367
  62.7 0.8 %shard_map.136 = bf16[16,8,1024]{2,1,0:T(8,128)(2,1)} custom-call(bf16[8,8,1024]{2,1,0:T(8,128)(2,1)S(1)} %all-to-all-done.2.parts, f32[256,1024]{1,0:T(8,128)S(1)} %get-tuple-element.32.earlier.own), custom_call_target="tpu_custom_call" | custom-call | tf_op jit(solution)/shard_map/pallas_call | solution.py:37
  63.4 3.5 %all-to-all-start.3 = ((bf16[16,8,1024]{2,1,0:T(8,128)(2,1)}), bf16[16,8,1024]{2,1,0:T(8,128)(2,1)S(1)}, u32[]{:S(2)}, u32[]{:S(2)}) async-start(bf16[16,8,1024]{2,1,0:T(8,128)(2,1)} %shard_map.136), calls=%async_computation.3 | async-start | bytes 524288 | tf_op jit(solution)/shard_map/all_to_all | solution.py:371
  67.0 0.0 collective-permute-done.3.near
  67.0 0.0 collective-permute-done.4.far
  67.0 1.0 %shard_map.137.earlier = bf16[1,256,1024]{2,1,0:T(8,128)(2,1)} custom-call(f32[256,1024]{1,0:T(8,128)S(1)} %get-tuple-element.32.earlier.own, bf16[128,1024]{1,0:T(8,128)(2,1)S(1)} %collective-permute-done.3.near, bf16[128,1024]{1,0:T(8,128)(2,1)S(1)} %collective-permute-done.4.far), custom_call_target="tpu_custom_call" | custom-call | tf_op jit(solution)/shard_map/pallas_call | solution.py:37
  68.0 6.4 %all-to-all-done.3.parts = bf16[16,8,1024]{2,1,0:T(8,128)(2,1)S(1)} async-done(((bf16[16,8,1024]{2,1,0:T(8,128)(2,1)}), bf16[16,8,1024]{2,1,0:T(8,128)(2,1)S(1)}, u32[]{:S(2)}, u32[]{:S(2)}) %all-to-all-start.3) | async-done | bytes 262176 | tf_op jit(solution)/shard_map/all_to_all | solution.py:371
  74.4 0.8 %shard_map.138 = (f32[100,1024]{1,0:T(8,128)}, f32[1,1024]{1,0:T(1,128)}, f32[1,1]{1,0:T(1,128)}) custom-call(bf16[16,8,1024]{2,1,0:T(8,128)(2,1)S(1)} %all-to-all-done.3.parts, bf16[1,256,1024]{2,1,0:T(8,128)(2,1)} %shard_map.137.earlier), custom_call_target="tpu_custom_call" | custom-call | tf_op jit(solution)/shard_map/pallas_call | solution.py:37
  (7 shorter events, 0.1 us)
Async XLA Ops:
  0.6 10.3 %copy-start = (bf16[100,1024]{1,0:T(8,128)(2,1)S(1)}, bf16[100,1024]{1,0:T(8,128)(2,1)}, u32[]{:S(2)}) copy-start(bf16[100,1024]{1,0:T(8,128)(2,1)} %proj.5) | copy-start | bytes 614404
  0.6 10.2 %copy-start.2 = (f32[1024]{0:T(1024)S(1)}, f32[1024]{0:T(1024)}, u32[]{:S(2)}) copy-start(f32[1024]{0:T(1024)} %param.19) | copy-start | bytes 12292
  1.8 4.5 %collective-permute-start = (bf16[128,1024]{1,0:T(8,128)(2,1)S(1)}, bf16[128,1024]{1,0:T(8,128)(2,1)S(1)}, u32[]{:S(2)}, u32[]{:S(2)}) collective-permute-start(bf16[128,1024]{1,0:T(8,128)(2,1)S(1)} %get-tuple-element.21), channel_id=1, source_target_pairs={{0,1},{1,0},{2,3},{3,2},{4,5},{5,4},{6,7},{7,6},{8,9},{9,8},{10,11... | collective-permute-start | bytes 786440 | tf_op jit(solution)/shard_map/ppermute | solution.py:303
  5.1 5.8 %collective-permute-start.1 = (bf16[128,1024]{1,0:T(8,128)(2,1)S(1)}, bf16[128,1024]{1,0:T(8,128)(2,1)S(1)}, u32[]{:S(2)}, u32[]{:S(2)}) collective-permute-start(bf16[128,1024]{1,0:T(8,128)(2,1)S(1)} %get-tuple-element.24), channel_id=1, source_target_pairs={{1,2},{3,4},{5,6},{7,8},{9,10},{11,12},{13,14},{15,16},{17,18},{19... | collective-permute-start | bytes 786440 | tf_op jit(solution)/shard_map/ppermute | solution.py:302
  12.3 13.0 %copy-start.1 = (f32[100,512]{1,0:T(8,128)S(1)}, f32[100,512]{1,0:T(8,128)}, u32[]{:S(2)}) copy-start(f32[100,512]{1,0:T(8,128)} %target.1) | copy-start | bytes 614404
  25.2 29.5 %copy-start.3 = (s32[3,512]{1,0:T(4,128)S(1)}, s32[3,512]{1,0:T(4,128)}, u32[]{:S(2)}) copy-start(s32[3,512]{1,0:T(4,128)} %nb.1) | copy-start | bytes 18436
  25.2 29.5 %copy-start.4 = (f32[3,512]{1,0:T(4,128)S(1)}, f32[3,512]{1,0:T(4,128)}, u32[]{:S(2)}) copy-start(f32[3,512]{1,0:T(4,128)} %ew.1) | copy-start | bytes 18436
  38.0 8.7 %collective-permute-start.2 = (f32[8,1024]{1,0:T(8,128)S(1)}, f32[8,1024]{1,0:T(8,128)S(1)}, u32[]{:S(2)}, u32[]{:S(2)}) collective-permute-start(f32[8,1024]{1,0:T(8,128)S(1)} %shard_map.133.mine), channel_id=1, source_target_pairs={{0,1},{1,0},{2,3},{3,2},{4,5},{5,4},{6,7},{7,6},{8,9},{9,8},{10,11... | collective-permute-start | bytes 98312 | tf_op jit(solution)/shard_map/ppermute | solution.py:350
  47.5 15.2 %all-to-all-start.2 = ((bf16[8,8,1024]{2,1,0:T(8,128)(2,1)}), bf16[8,8,1024]{2,1,0:T(8,128)(2,1)S(1)}, u32[]{:S(2)}, u32[]{:S(2)}) async-start(bf16[8,8,1024]{2,1,0:T(8,128)(2,1)} %shard_map.134), calls=%async_computation.2 | async-start | bytes 262144 | tf_op jit(solution)/shard_map/all_to_all | solution.py:367
  56.7 10.3 %collective-permute-start.3 = (bf16[128,1024]{1,0:T(8,128)(2,1)S(1)}, bf16[128,1024]{1,0:T(8,128)(2,1)S(1)}, u32[]{:S(2)}, u32[]{:S(2)}) collective-permute-start(bf16[128,1024]{1,0:T(8,128)(2,1)S(1)} %get-tuple-element.33), channel_id=1, source_target_pairs={{0,1},{1,0},{2,3},{3,2},{4,5},{5,4},{6,7},{7,6},{8,9},{9,8},{10,11... | collective-permute-start | bytes 786440 | tf_op jit(solution)/shard_map/ppermute | solution.py:363
  57.4 9.6 %collective-permute-start.4 = (bf16[128,1024]{1,0:T(8,128)(2,1)S(1)}, bf16[128,1024]{1,0:T(8,128)(2,1)S(1)}, u32[]{:S(2)}, u32[]{:S(2)}) collective-permute-start(bf16[128,1024]{1,0:T(8,128)(2,1)S(1)} %get-tuple-element.34), channel_id=1, source_target_pairs={{1,2},{3,4},{5,6},{7,8},{9,10},{11,12},{13,14},{15,16},{17,18},{19... | collective-permute-start | bytes 786440 | tf_op jit(solution)/shard_map/ppermute | solution.py:362
  63.4 11.0 %all-to-all-start.3 = ((bf16[16,8,1024]{2,1,0:T(8,128)(2,1)}), bf16[16,8,1024]{2,1,0:T(8,128)(2,1)S(1)}, u32[]{:S(2)}, u32[]{:S(2)}) async-start(bf16[16,8,1024]{2,1,0:T(8,128)(2,1)} %shard_map.136), calls=%async_computation.3 | async-start | bytes 524288 | tf_op jit(solution)/shard_map/all_to_all | solution.py:371

commit v12 on v8

--- a/solution.py
+++ b/solution.py
@@ -15,6 +15,7 @@
 GRID = ("xh", "z", "c")
 PLANE = ("xl", "y", "xh")
 CHUNK = 8
+BLOCK = 128
 BF16 = jnp.bfloat16
 F32 = jnp.float32
 VMEM_LIMIT = 24 * 1024 * 1024
@@ -128,13 +129,14 @@
 def forward_kernel(part, edges, near, far, gain, proj, state, f_out, sc_out, rs_out):
     close, distant = near[...], far[...]
     twice = jnp.concatenate([close, close, distant, distant], axis=0)
-    mixed = part[...] + dot(edges[...], twice, ((1,), (0,)))
-    centred = mixed - jnp.mean(mixed, axis=1, keepdims=True)
-    rscale = lax.rsqrt(jnp.mean(centred * centred, axis=1, keepdims=True) + NORM_EPS)
-    scaled = (centred * rscale * gain[...]).astype(BF16)
-    sc_out[...] = scaled
-    rs_out[...] = rscale
-    f_out[...] = state[...] + dot(proj[...], scaled, ((1,), (1,)))
+    for r in range(0, part.shape[0], BLOCK):
+        at = slice(r, r + BLOCK)
+        mixed = part[at] + dot(edges[at], twice, ((1,), (0,)))
+        centred = mixed - jnp.mean(mixed, axis=1, keepdims=True)
+        rscale = lax.rsqrt(jnp.mean(centred * centred, axis=1, keepdims=True) + NORM_EPS)
+        sc_out[at] = (centred * rscale * gain[...]).astype(BF16)
+        rs_out[at] = rscale
+    f_out[...] = state[...] + dot(proj[...], sc_out[...], ((1,), (1,)))
 
 
 def loss_kernel(every, field, target, wm, proj, scaled, gain, fg_out, parts_out):
@@ -284,8 +286,8 @@
     plane = lax.axis_size(PLANE)
     gain = layer_norm_gain[None]
     swap = [(0, 1), (1, 0)]
-    links = [((i + 1) % slabs, (i + 2) % slabs) for i in range(0, slabs, 2)]
-    links = links + [(j, i) for i, j in links]
+    links = [(i, i + 1) for i in range(1, slabs - 1, 2)]
+    links = links + [(j, i) for i, j in links] + [(0, 0), (slabs - 1, slabs - 1)]
 
     (far_send,) = call(
         cut_kernel, [((rim, channels), BF16)], "h", [pltpu.SemaphoreType.DMA]

time: 76.1 us -> 78 us (1.025)
  blocking collectives: 28.2 us -> 34.1 us
  starting transfers between devices: 21.9 us -> 19.3 us
  waiting for transfers between devices: 12 us -> 10.6 us
    ppermute x1, starting transfers between devices: 6.32 us -> 0.09 us  [per_device(): near = lax.ppermute(near_send, 'c', swap)]
    all_to_all x1, blocking collectives: 11.1 us -> 15.8 us  [per_device(): parts = lax.all_to_all(parts, PLANE, 0, 0, tiled=True)]
    all_to_all x1, waiting for transfers between devices: 3.58 us -> 1.75 us  [per_device(): parts = lax.all_to_all(parts, 'z', 0, 0, tiled=True)]
    ppermute x1, starting transfers between devices: 3.11 us -> 4.94 us  [per_device(): far = lax.ppermute(far_send, GRID, links)]
    ppermute x1, starting transfers between devices: 1.72 us -> 3.54 us  [per_device(): far_grad = lax.ppermute(far_grad, GRID, links)]
    all_to_all x1, blocking collectives: 17.1 us -> 18.3 us  [per_device(): every = lax.all_to_all(sent, MEMBER, 0, 0, tiled=True).astype(F32)]
    ppermute x1, waiting for transfers between devices: 0.01 us -> 1.11 us  [per_device(): far = lax.ppermute(far_send, GRID, links)]
  transfers between devices with their start and end apart: 7 -> 7, of which waited for: 4 -> 5; matrix products, arithmetic and copies ran while one was open for 0% -> 0% of each run, Pallas kernels for 9% -> 8%
where the time goes in v12:
time: 78 us; the launch traced here: 76.5 us
  blocking collectives  34.1 us (44%)
  starting transfers between devices  19.3 us (25%)
  Pallas kernels  11.4 us (15%)
  waiting for transfers between devices  10.6 us (14%)
  between operations  0.82 us (1%)
    all_to_all x1, blocking collectives, per_device(): every = lax.all_to_all(sent, MEMBER, 0, 0, tiled=True).astype(F32)  18.3 us
    all_to_all x1, blocking collectives, per_device(): parts = lax.all_to_all(parts, PLANE, 0, 0, tiled=True)  15.8 us
    pallas_call x10, Pallas kernels, run(): pl.pallas_call(kernel, out_shape=[jax.ShapeDtypeStruct(s, d) for s, d in...  11.4 us
    all_to_all x1, waiting for transfers between devices, per_device(): parts = lax.all_to_all(parts, PLANE, 0, 0, tiled=True)  6.44 us
    ppermute x1, starting transfers between devices, per_device(): far = lax.ppermute(far_send, GRID, links)  4.94 us
    ppermute x1, starting transfers between devices, per_device(): far_grad = lax.ppermute(far_grad, GRID, links)  3.54 us
    all_to_all x1, starting transfers between devices, per_device(): parts = lax.all_to_all(parts, PLANE, 0, 0, tiled=True)  3.53 us
    all_to_all x1, starting transfers between devices, per_device(): parts = lax.all_to_all(parts, 'z', 0, 0, tiled=True)  3.37 us
  transfers between devices with their start and end apart: 7, of which 5 were waited for; matrix products, arithmetic and copies ran while one was open for 0% of the time, Pallas kernels for 8%

profile of v12, /device:TPU:1, one launch (start us, length us, event | category | flops | bytes accessed | tf_op | source)
XLA Modules:
  0.0 76.5 jit_solution(15397448601312629647)
XLA Ops:
  0.6 0.0 copy-start
  0.6 0.0 copy-start.2
  0.7 1.0 %shard_map.129.earlier = bf16[128,1024]{1,0:T(8,128)(2,1)S(1)} custom-call(bf16[256,1024]{1,0:T(8,128)(2,1)} %bitcast.11), custom_call_target="tpu_custom_call" | custom-call | tf_op jit(solution)/shard_map/pallas_call | solution.py:37
  1.7 4.9 %collective-permute-start.1 = (bf16[128,1024]{1,0:T(8,128)(2,1)S(1)}, bf16[128,1024]{1,0:T(8,128)(2,1)S(1)}, u32[]{:S(2)}, u32[]{:S(2)}) collective-permute-start(bf16[128,1024]{1,0:T(8,128)(2,1)S(1)} %shard_map.129.earlier), channel_id=1, source_target_pairs={{1,2},{3,4},{5,6},{7,8},{9,10},{11,12},{13,14},{15,16},{17,18},{19... | collective-permute-start | bytes 786440 | tf_op jit(solution)/shard_map/ppermute | solution.py:295
  6.6 2.8 %shard_map.130 = (bf16[128,1024]{1,0:T(8,128)(2,1)S(1)}, bf16[512,512]{1,0:T(8,128)(2,1)S(1)}, f32[512,1024]{1,0:T(8,128)S(1)}, f32[100,512]{1,0:T(8,128)S(1)}, f32[100,512]{1,0:T(8,128)S(1)}) custom-call(s32[3,512]{1,0:T(4,128)} %nb.1, f32[3,512]{1,0:T(4,128)} %ew.1, f32[1,100]{1,0:T(1,128)} %bitcast.17, f32[1,512]{1,0:T(1,128)} %bitcast.16, ...), custom_call_target="tpu_custom_call" | custom-call | flops 805306368 | bytes 8000000 | tf_op jit(solution)/shard_map/pallas_call | solution.py:37
  9.4 0.1 collective-permute-start
  9.5 1.1 %collective-permute-done.1.far = bf16[128,1024]{1,0:T(8,128)(2,1)S(1)} collective-permute-done((bf16[128,1024]{1,0:T(8,128)(2,1)S(1)}, bf16[128,1024]{1,0:T(8,128)(2,1)S(1)}, u32[]{:S(2)}, u32[]{:S(2)}) %collective-permute-start.1) | collective-permute-done | bytes 262176 | tf_op jit(solution)/shard_map/ppermute | solution.py:295
  10.7 0.4 collective-permute-done.near
  11.1 1.6 %shard_map.131 = (f32[100,512]{1,0:T(8,128)S(1)}, bf16[512,1024]{1,0:T(8,128)(2,1)S(1)}, f32[512,1]{1,0:T(8,128)S(1)}) custom-call(f32[512,1024]{1,0:T(8,128)S(1)} %get-tuple-element.20.part, bf16[512,512]{1,0:T(8,128)(2,1)S(1)} %get-tuple-element.21.edges, bf16[128,1024]{1,0:T(8,128)(2,1)S(1)} %collective-permute-done.near, ...), custom_call_target="tpu_custom_call" | custom-call | flops 373293056 | bytes 5000000 | tf_op jit(solution)/shard_map/pallas_call | solution.py:37
  12.7 0.1 broadcast_in_dim.18
  12.7 0.0 copy-start.1
  12.8 18.3 %all_to_all.20 = f16[8,100,512]{2,1,0:T(8,128)(2,1)S(1)} all-to-all(f16[8,100,512]{2,1,0:T(8,128)(2,1)S(1)} %broadcast_in_dim.18), channel_id=1, replica_groups=mesh['xl'=2,'y'=4,'xh'=2,'z'=8,'c'=2] {'xl','y'}, dimensions={0} | all-to-all | bytes 1638400 | tf_op jit(solution)/shard_map/all_to_all | solution.py:334
  31.0 0.2 convert_element_type.7.every
  31.2 0.0 copy-start.3
  31.3 0.0 copy-start.4
  31.3 0.9 %shard_map.132 = (bf16[100,512]{1,0:T(8,128)(2,1)S(1)}, bf16[16,8,1024]{2,1,0:T(8,128)(2,1)S(1)}) custom-call(f32[8,100,512]{2,1,0:T(8,128)S(1)} %convert_element_type.7.every, f32[100,512]{1,0:T(8,128)S(1)} %get-tuple-element.24.field, f32[100,512]{1,0:T(8,128)S(1)} %copy-done.1, f32[100,512]{1,0:T(8,128)S(1)} %get-tuple-element.25.wm, ...), custom_call_target="tpu_custom_call" | custom-call | flops 209715200 | bytes 4000000 | tf_op jit(solution)/shard_map/pallas_call | solution.py:37
  32.2 15.8 %all_to_all.21.parts = bf16[16,8,1024]{2,1,0:T(8,128)(2,1)S(1)} all-to-all(bf16[16,8,1024]{2,1,0:T(8,128)(2,1)S(1)} %get-tuple-element.27), channel_id=1, replica_groups=mesh['xl'=2,'y'=4,'xh'=2,'z'=8,'c'=2] {'xl','y','xh'}, dimensions={0} | all-to-all | bytes 524288 | tf_op jit(solution)/shard_map/all_to_all | solution.py:342
  48.0 3.1 %collective-permute-start.2 = (f32[8,1024]{1,0:T(8,128)S(1)}, f32[8,1024]{1,0:T(8,128)S(1)}, u32[]{:S(2)}, u32[]{:S(2)}) collective-permute-start(f32[8,1024]{1,0:T(8,128)S(1)} %shard_map.133.mine), channel_id=1, source_target_pairs={{0,1},{1,0},{2,3},{3,2},{4,5},{5,4},{6,7},{7,6},{8,9},{9,8},{10,11... | collective-permute-start | bytes 98312 | tf_op jit(solution)/shard_map/ppermute | solution.py:344
  51.1 0.9 %collective-permute-done.2.met.earlier = f32[8,1024]{1,0:T(8,128)S(1)} collective-permute-done((f32[8,1024]{1,0:T(8,128)S(1)}, f32[8,1024]{1,0:T(8,128)S(1)}, u32[]{:S(2)}, u32[]{:S(2)}) %collective-permute-start.2) | collective-permute-done | bytes 32800 | tf_op jit(solution)/shard_map/ppermute | solution.py:344
  52.0 0.7 shard_map.134
  52.7 3.4 %all-to-all-start.2 = ((bf16[8,8,1024]{2,1,0:T(8,128)(2,1)}), bf16[8,8,1024]{2,1,0:T(8,128)(2,1)S(1)}, u32[]{:S(2)}, u32[]{:S(2)}) async-start(bf16[8,8,1024]{2,1,0:T(8,128)(2,1)} %shard_map.134), calls=%async_computation.2 | async-start | bytes 262144 | tf_op jit(solution)/shard_map/all_to_all | solution.py:361
  56.1 1.9 %shard_map.135 = (f32[256,1024]{1,0:T(8,128)S(1)}, bf16[128,1024]{1,0:T(8,128)(2,1)S(1)}, bf16[128,1024]{1,0:T(8,128)(2,1)S(1)}) custom-call(f32[8,1024]{1,0:T(8,128)S(1)} %collective-permute-done.2.met.earlier, s32[3,512]{1,0:T(4,128)S(1)} %copy-done.3, f32[3,512]{1,0:T(4,128)S(1)} %copy-done.4, bf16[100,512]{1,0:T(8,128)(2,1)S(1)} %get-tuple-element.28.fore_grad, ...), custom_call_target="tpu_custom_call" | custom-call | flops 641728512 | bytes 6000000 | tf_op jit(solution)/shard_map/pallas_call | solution.py:37
  58.0 0.7 collective-permute-start.3
  58.7 3.5 %collective-permute-start.4 = (bf16[128,1024]{1,0:T(8,128)(2,1)S(1)}, bf16[128,1024]{1,0:T(8,128)(2,1)S(1)}, u32[]{:S(2)}, u32[]{:S(2)}) collective-permute-start(bf16[128,1024]{1,0:T(8,128)(2,1)S(1)} %get-tuple-element.32), channel_id=1, source_target_pairs={{1,2},{3,4},{5,6},{7,8},{9,10},{11,12},{13,14},{15,16},{17,18},{19... | collective-permute-start | bytes 786440 | tf_op jit(solution)/shard_map/ppermute | solution.py:356
  62.2 1.8 %all-to-all-done.2.parts = bf16[8,8,1024]{2,1,0:T(8,128)(2,1)S(1)} async-done(((bf16[8,8,1024]{2,1,0:T(8,128)(2,1)}), bf16[8,8,1024]{2,1,0:T(8,128)(2,1)S(1)}, u32[]{:S(2)}, u32[]{:S(2)}) %all-to-all-start.2) | async-done | bytes 131104 | tf_op jit(solution)/shard_map/all_to_all | solution.py:361
  64.0 0.8 shard_map.136
  64.7 3.5 %all-to-all-start.3 = ((bf16[16,8,1024]{2,1,0:T(8,128)(2,1)}), bf16[16,8,1024]{2,1,0:T(8,128)(2,1)S(1)}, u32[]{:S(2)}, u32[]{:S(2)}) async-start(bf16[16,8,1024]{2,1,0:T(8,128)(2,1)} %shard_map.136), calls=%async_computation.3 | async-start | bytes 524288 | tf_op jit(solution)/shard_map/all_to_all | solution.py:365
  68.3 0.0 collective-permute-done.3.near
  68.3 0.0 collective-permute-done.4.far
  68.3 1.0 %shard_map.137.earlier = bf16[1,256,1024]{2,1,0:T(8,128)(2,1)} custom-call(f32[256,1024]{1,0:T(8,128)S(1)} %get-tuple-element.30.earlier.own, bf16[128,1024]{1,0:T(8,128)(2,1)S(1)} %collective-permute-done.3.near, bf16[128,1024]{1,0:T(8,128)(2,1)S(1)} %collective-permute-done.4.far), custom_call_target="tpu_custom_call" | custom-call | tf_op jit(solution)/shard_map/pallas_call | solution.py:37
  69.3 6.4 %all-to-all-done.3.parts = bf16[16,8,1024]{2,1,0:T(8,128)(2,1)S(1)} async-done(((bf16[16,8,1024]{2,1,0:T(8,128)(2,1)}), bf16[16,8,1024]{2,1,0:T(8,128)(2,1)S(1)}, u32[]{:S(2)}, u32[]{:S(2)}) %all-to-all-start.3) | async-done | bytes 262176 | tf_op jit(solution)/shard_map/all_to_all | solution.py:365
  75.7 0.8 %shard_map.138 = (f32[100,1024]{1,0:T(8,128)}, f32[1,1024]{1,0:T(1,128)}, f32[1,1]{1,0:T(1,128)}) custom-call(bf16[16,8,1024]{2,1,0:T(8,128)(2,1)S(1)} %all-to-all-done.3.parts, bf16[1,256,1024]{2,1,0:T(8,128)(2,1)} %shard_map.137.earlier), custom_call_target="tpu_custom_call" | custom-call | tf_op jit(solution)/shard_map/pallas_call | solution.py:37
  (7 shorter events, 0.1 us)
Async XLA Ops:
  0.6 10.4 %copy-start = (bf16[100,1024]{1,0:T(8,128)(2,1)S(1)}, bf16[100,1024]{1,0:T(8,128)(2,1)}, u32[]{:S(2)}) copy-start(bf16[100,1024]{1,0:T(8,128)(2,1)} %proj.5) | copy-start | bytes 614404
  0.6 10.4 %copy-start.2 = (f32[1024]{0:T(1024)S(1)}, f32[1024]{0:T(1024)}, u32[]{:S(2)}) copy-start(f32[1024]{0:T(1024)} %param.19) | copy-start | bytes 12292
  1.7 9.0 %collective-permute-start.1 = (bf16[128,1024]{1,0:T(8,128)(2,1)S(1)}, bf16[128,1024]{1,0:T(8,128)(2,1)S(1)}, u32[]{:S(2)}, u32[]{:S(2)}) collective-permute-start(bf16[128,1024]{1,0:T(8,128)(2,1)S(1)} %shard_map.129.earlier), channel_id=1, source_target_pairs={{1,2},{3,4},{5,6},{7,8},{9,10},{11,12},{13,14},{15,16},{17,18},{19... | collective-permute-start | bytes 786440 | tf_op jit(solution)/shard_map/ppermute | solution.py:295
  9.4 1.6 %collective-permute-start = (bf16[128,1024]{1,0:T(8,128)(2,1)S(1)}, bf16[128,1024]{1,0:T(8,128)(2,1)S(1)}, u32[]{:S(2)}, u32[]{:S(2)}) collective-permute-start(bf16[128,1024]{1,0:T(8,128)(2,1)S(1)} %get-tuple-element.22), channel_id=1, source_target_pairs={{0,1},{1,0},{2,3},{3,2},{4,5},{5,4},{6,7},{7,6},{8,9},{9,8},{10,11... | collective-permute-start | bytes 786440 | tf_op jit(solution)/shard_map/ppermute | solution.py:322
  12.7 18.5 %copy-start.1 = (f32[100,512]{1,0:T(8,128)S(1)}, f32[100,512]{1,0:T(8,128)}, u32[]{:S(2)}) copy-start(f32[100,512]{1,0:T(8,128)} %target.1) | copy-start | bytes 614404
  31.2 24.8 %copy-start.3 = (s32[3,512]{1,0:T(4,128)S(1)}, s32[3,512]{1,0:T(4,128)}, u32[]{:S(2)}) copy-start(s32[3,512]{1,0:T(4,128)} %nb.1) | copy-start | bytes 18436
  31.3 24.8 %copy-start.4 = (f32[3,512]{1,0:T(4,128)S(1)}, f32[3,512]{1,0:T(4,128)}, u32[]{:S(2)}) copy-start(f32[3,512]{1,0:T(4,128)} %ew.1) | copy-start | bytes 18436
  48.0 4.0 %collective-permute-start.2 = (f32[8,1024]{1,0:T(8,128)S(1)}, f32[8,1024]{1,0:T(8,128)S(1)}, u32[]{:S(2)}, u32[]{:S(2)}) collective-permute-start(f32[8,1024]{1,0:T(8,128)S(1)} %shard_map.133.mine), channel_id=1, source_target_pairs={{0,1},{1,0},{2,3},{3,2},{4,5},{5,4},{6,7},{7,6},{8,9},{9,8},{10,11... | collective-permute-start | bytes 98312 | tf_op jit(solution)/shard_map/ppermute | solution.py:344
  52.7 11.3 %all-to-all-start.2 = ((bf16[8,8,1024]{2,1,0:T(8,128)(2,1)}), bf16[8,8,1024]{2,1,0:T(8,128)(2,1)S(1)}, u32[]{:S(2)}, u32[]{:S(2)}) async-start(bf16[8,8,1024]{2,1,0:T(8,128)(2,1)} %shard_map.134), calls=%async_computation.2 | async-start | bytes 262144 | tf_op jit(solution)/shard_map/all_to_all | solution.py:361
  58.0 10.3 %collective-permute-start.3 = (bf16[128,1024]{1,0:T(8,128)(2,1)S(1)}, bf16[128,1024]{1,0:T(8,128)(2,1)S(1)}, u32[]{:S(2)}, u32[]{:S(2)}) collective-permute-start(bf16[128,1024]{1,0:T(8,128)(2,1)S(1)} %get-tuple-element.31), channel_id=1, source_target_pairs={{0,1},{1,0},{2,3},{3,2},{4,5},{5,4},{6,7},{7,6},{8,9},{9,8},{10,11... | collective-permute-start | bytes 786440 | tf_op jit(solution)/shard_map/ppermute | solution.py:357
  58.7 9.6 %collective-permute-start.4 = (bf16[128,1024]{1,0:T(8,128)(2,1)S(1)}, bf16[128,1024]{1,0:T(8,128)(2,1)S(1)}, u32[]{:S(2)}, u32[]{:S(2)}) collective-permute-start(bf16[128,1024]{1,0:T(8,128)(2,1)S(1)} %get-tuple-element.32), channel_id=1, source_target_pairs={{1,2},{3,4},{5,6},{7,8},{9,10},{11,12},{13,14},{15,16},{17,18},{19... | collective-permute-start | bytes 786440 | tf_op jit(solution)/shard_map/ppermute | solution.py:356
  64.7 11.0 %all-to-all-start.3 = ((bf16[16,8,1024]{2,1,0:T(8,128)(2,1)}), bf16[16,8,1024]{2,1,0:T(8,128)(2,1)S(1)}, u32[]{:S(2)}, u32[]{:S(2)}) async-start(bf16[16,8,1024]{2,1,0:T(8,128)(2,1)} %shard_map.136), calls=%async_computation.3 | async-start | bytes 524288 | tf_op jit(solution)/shard_map/all_to_all | solution.py:365

commit v13 on v12

--- a/solution.py
+++ b/solution.py
@@ -286,13 +286,19 @@
     plane = lax.axis_size(PLANE)
     gain = layer_norm_gain[None]
     swap = [(0, 1), (1, 0)]
-    links = [(i, i + 1) for i in range(1, slabs - 1, 2)]
-    links = links + [(j, i) for i, j in links] + [(0, 0), (slabs - 1, slabs - 1)]
+    links = [
+        (m * slabs + i, (m * slabs + i + 1) if i < slabs - 1 and i > 0 else ((m ^ 1) * slabs + i))
+        for m in range(members)
+        for i in range(slabs)
+        if i % 2 == 1 or i == 0
+    ]
+    links = [p for p in links if p[0] < p[1]]
+    links = links + [(j, i) for i, j in links]
 
     (far_send,) = call(
         cut_kernel, [((rim, channels), BF16)], "h", [pltpu.SemaphoreType.DMA]
     )(latent)
-    far = lax.ppermute(far_send, GRID, links)
+    far = lax.ppermute(far_send, MEMBER + GRID, links)
     near_send, edges, part, weight_map, state = call(
         prepare_kernel,
         [
@@ -353,7 +359,7 @@
         moved=6_000_000,
         spaces="a",
     )(met, neighbours, edge_weight, fore_grad, output_projection, scaled, gain, rscale)
-    far_grad = lax.ppermute(far_grad, GRID, links)
+    far_grad = lax.ppermute(far_grad, MEMBER + GRID, links)
     near_grad = lax.ppermute(near_grad, "c", swap)
     (latent_grad,) = call(finish_latent_kernel, [((1, mesh_count, channels), BF16)])(
         own, near_grad, far_grad

time: 78 us -> 76.1 us (0.976)
  starting transfers between devices: 19.3 us -> 15.9 us
  waiting for transfers between devices: 10.6 us -> 12.2 us
    ppermute x2, starting transfers between devices: 8.48 us -> 4.83 us  [the longest x1 3.11 us: per_device(): far = lax.ppermute(far_send, MEMBER + GRID, links)]
    all_to_all x1, waiting for transfers between devices: 1.75 us -> 3.58 us  [per_device(): parts = lax.all_to_all(parts, 'z', 0, 0, tiled=True)]
  transfers between devices with their start and end apart: 7 -> 7, of which waited for: 5 -> 5; matrix products, arithmetic and copies ran while one was open for 0% -> 0% of each run, Pallas kernels for 8% -> 9%
where the time goes in v13:
time: 76.1 us; the launch traced here: 74.7 us
  blocking collectives  34 us (45%)
  starting transfers between devices  15.9 us (21%)
  waiting for transfers between devices  12.2 us (16%)
  Pallas kernels  11.4 us (15%)
  between operations  0.79 us (1%)
    all_to_all x1, blocking collectives, per_device(): every = lax.all_to_all(sent, MEMBER, 0, 0, tiled=True).astype(F32)  18 us
    all_to_all x1, blocking collectives, per_device(): parts = lax.all_to_all(parts, PLANE, 0, 0, tiled=True)  16 us
    pallas_call x10, Pallas kernels, run(): pl.pallas_call(kernel, out_shape=[jax.ShapeDtypeStruct(s, d) for s, d in...  11.4 us
    all_to_all x1, waiting for transfers between devices, per_device(): parts = lax.all_to_all(parts, PLANE, 0, 0, tiled=True)  6.44 us
    all_to_all x1, waiting for transfers between devices, per_device(): parts = lax.all_to_all(parts, 'z', 0, 0, tiled=True)  3.58 us
    all_to_all x1, starting transfers between devices, per_device(): parts = lax.all_to_all(parts, PLANE, 0, 0, tiled=True)  3.53 us
    all_to_all x1, starting transfers between devices, per_device(): parts = lax.all_to_all(parts, 'z', 0, 0, tiled=True)  3.42 us
    ppermute x1, starting transfers between devices, per_device(): met = lax.ppermute(mine, 'c', swap)  3.13 us
  transfers between devices with their start and end apart: 7, of which 5 were waited for; matrix products, arithmetic and copies ran while one was open for 0% of the time, Pallas kernels for 9%

profile of v13, /device:TPU:1, one launch (start us, length us, event | category | flops | bytes accessed | tf_op | source)
XLA Modules:
  0.0 74.7 jit_solution(10960749538294326144)
XLA Ops:
  0.6 0.0 copy-start
  0.6 0.0 copy-start.2
  0.7 1.0 %shard_map.129.earlier = bf16[128,1024]{1,0:T(8,128)(2,1)S(1)} custom-call(bf16[256,1024]{1,0:T(8,128)(2,1)} %bitcast.11), custom_call_target="tpu_custom_call" | custom-call | tf_op jit(solution)/shard_map/pallas_call | solution.py:37
  1.7 3.1 %collective-permute-start.1 = (bf16[128,1024]{1,0:T(8,128)(2,1)S(1)}, bf16[128,1024]{1,0:T(8,128)(2,1)S(1)}, u32[]{:S(2)}, u32[]{:S(2)}) collective-permute-start(bf16[128,1024]{1,0:T(8,128)(2,1)S(1)} %shard_map.129.earlier), channel_id=1, source_target_pairs={{0,32},{1,2},{3,4},{5,6},{7,8},{9,10},{11,12},{13,14},{15,16},{17,... | collective-permute-start | bytes 786440 | tf_op jit(solution)/shard_map/ppermute | solution.py:301
  4.8 2.8 %shard_map.130 = (bf16[128,1024]{1,0:T(8,128)(2,1)S(1)}, bf16[512,512]{1,0:T(8,128)(2,1)S(1)}, f32[512,1024]{1,0:T(8,128)S(1)}, f32[100,512]{1,0:T(8,128)S(1)}, f32[100,512]{1,0:T(8,128)S(1)}) custom-call(s32[3,512]{1,0:T(4,128)} %nb.1, f32[3,512]{1,0:T(4,128)} %ew.1, f32[1,100]{1,0:T(1,128)} %bitcast.17, f32[1,512]{1,0:T(1,128)} %bitcast.16, ...), custom_call_target="tpu_custom_call" | custom-call | flops 805306368 | bytes 8000000 | tf_op jit(solution)/shard_map/pallas_call | solution.py:37
  7.6 0.3 collective-permute-start
  7.9 1.2 %collective-permute-done.1.far = bf16[128,1024]{1,0:T(8,128)(2,1)S(1)} collective-permute-done((bf16[128,1024]{1,0:T(8,128)(2,1)S(1)}, bf16[128,1024]{1,0:T(8,128)(2,1)S(1)}, u32[]{:S(2)}, u32[]{:S(2)}) %collective-permute-start.1) | collective-permute-done | bytes 262176 | tf_op jit(solution)/shard_map/ppermute | solution.py:301
  9.1 0.1 collective-permute-done.near
  9.2 1.6 %shard_map.131 = (f32[100,512]{1,0:T(8,128)S(1)}, bf16[512,1024]{1,0:T(8,128)(2,1)S(1)}, f32[512,1]{1,0:T(8,128)S(1)}) custom-call(f32[512,1024]{1,0:T(8,128)S(1)} %get-tuple-element.20.part, bf16[512,512]{1,0:T(8,128)(2,1)S(1)} %get-tuple-element.21.edges, bf16[128,1024]{1,0:T(8,128)(2,1)S(1)} %collective-permute-done.near, ...), custom_call_target="tpu_custom_call" | custom-call | flops 373293056 | bytes 5000000 | tf_op jit(solution)/shard_map/pallas_call | solution.py:37
  10.8 0.1 broadcast_in_dim.18
  10.9 0.0 copy-start.1
  10.9 18.0 %all_to_all.20 = f16[8,100,512]{2,1,0:T(8,128)(2,1)S(1)} all-to-all(f16[8,100,512]{2,1,0:T(8,128)(2,1)S(1)} %broadcast_in_dim.18), channel_id=1, replica_groups=mesh['xl'=2,'y'=4,'xh'=2,'z'=8,'c'=2] {'xl','y'}, dimensions={0} | all-to-all | bytes 1638400 | tf_op jit(solution)/shard_map/all_to_all | solution.py:340
  28.9 0.2 convert_element_type.7.every
  29.2 0.0 copy-start.3
  29.2 0.0 copy-start.4
  29.2 0.9 %shard_map.132 = (bf16[100,512]{1,0:T(8,128)(2,1)S(1)}, bf16[16,8,1024]{2,1,0:T(8,128)(2,1)S(1)}) custom-call(f32[8,100,512]{2,1,0:T(8,128)S(1)} %convert_element_type.7.every, f32[100,512]{1,0:T(8,128)S(1)} %get-tuple-element.24.field, f32[100,512]{1,0:T(8,128)S(1)} %copy-done.1, f32[100,512]{1,0:T(8,128)S(1)} %get-tuple-element.25.wm, ...), custom_call_target="tpu_custom_call" | custom-call | flops 209715200 | bytes 4000000 | tf_op jit(solution)/shard_map/pallas_call | solution.py:37
  30.1 16.0 %all_to_all.21.parts = bf16[16,8,1024]{2,1,0:T(8,128)(2,1)S(1)} all-to-all(bf16[16,8,1024]{2,1,0:T(8,128)(2,1)S(1)} %get-tuple-element.27), channel_id=1, replica_groups=mesh['xl'=2,'y'=4,'xh'=2,'z'=8,'c'=2] {'xl','y','xh'}, dimensions={0} | all-to-all | bytes 524288 | tf_op jit(solution)/shard_map/all_to_all | solution.py:348
  46.2 3.1 %collective-permute-start.2 = (f32[8,1024]{1,0:T(8,128)S(1)}, f32[8,1024]{1,0:T(8,128)S(1)}, u32[]{:S(2)}, u32[]{:S(2)}) collective-permute-start(f32[8,1024]{1,0:T(8,128)S(1)} %shard_map.133.mine), channel_id=1, source_target_pairs={{0,1},{1,0},{2,3},{3,2},{4,5},{5,4},{6,7},{7,6},{8,9},{9,8},{10,11... | collective-permute-start | bytes 98312 | tf_op jit(solution)/shard_map/ppermute | solution.py:350
  49.3 0.9 %collective-permute-done.2.met.earlier = f32[8,1024]{1,0:T(8,128)S(1)} collective-permute-done((f32[8,1024]{1,0:T(8,128)S(1)}, f32[8,1024]{1,0:T(8,128)S(1)}, u32[]{:S(2)}, u32[]{:S(2)}) %collective-permute-start.2) | collective-permute-done | bytes 32800 | tf_op jit(solution)/shard_map/ppermute | solution.py:350
  50.2 0.7 shard_map.134
  50.8 3.4 %all-to-all-start.2 = ((bf16[8,8,1024]{2,1,0:T(8,128)(2,1)}), bf16[8,8,1024]{2,1,0:T(8,128)(2,1)S(1)}, u32[]{:S(2)}, u32[]{:S(2)}) async-start(bf16[8,8,1024]{2,1,0:T(8,128)(2,1)} %shard_map.134), calls=%async_computation.2 | async-start | bytes 262144 | tf_op jit(solution)/shard_map/all_to_all | solution.py:367
  54.3 1.9 %shard_map.135 = (f32[256,1024]{1,0:T(8,128)S(1)}, bf16[128,1024]{1,0:T(8,128)(2,1)S(1)}, bf16[128,1024]{1,0:T(8,128)(2,1)S(1)}) custom-call(f32[8,1024]{1,0:T(8,128)S(1)} %collective-permute-done.2.met.earlier, s32[3,512]{1,0:T(4,128)S(1)} %copy-done.3, f32[3,512]{1,0:T(4,128)S(1)} %copy-done.4, bf16[100,512]{1,0:T(8,128)(2,1)S(1)} %get-tuple-element.28.fore_grad, ...), custom_call_target="tpu_custom_call" | custom-call | flops 641728512 | bytes 6000000 | tf_op jit(solution)/shard_map/pallas_call | solution.py:37
  56.2 0.7 collective-permute-start.3
  56.9 1.7 %collective-permute-start.4 = (bf16[128,1024]{1,0:T(8,128)(2,1)S(1)}, bf16[128,1024]{1,0:T(8,128)(2,1)S(1)}, u32[]{:S(2)}, u32[]{:S(2)}) collective-permute-start(bf16[128,1024]{1,0:T(8,128)(2,1)S(1)} %get-tuple-element.32), channel_id=1, source_target_pairs={{0,32},{1,2},{3,4},{5,6},{7,8},{9,10},{11,12},{13,14},{15,16},{17,... | collective-permute-start | bytes 786440 | tf_op jit(solution)/shard_map/ppermute | solution.py:362
  58.6 3.6 %all-to-all-done.2.parts = bf16[8,8,1024]{2,1,0:T(8,128)(2,1)S(1)} async-done(((bf16[8,8,1024]{2,1,0:T(8,128)(2,1)}), bf16[8,8,1024]{2,1,0:T(8,128)(2,1)S(1)}, u32[]{:S(2)}, u32[]{:S(2)}) %all-to-all-start.2) | async-done | bytes 131104 | tf_op jit(solution)/shard_map/all_to_all | solution.py:367
  62.2 0.8 %shard_map.136 = bf16[16,8,1024]{2,1,0:T(8,128)(2,1)} custom-call(bf16[8,8,1024]{2,1,0:T(8,128)(2,1)S(1)} %all-to-all-done.2.parts, f32[256,1024]{1,0:T(8,128)S(1)} %get-tuple-element.30.earlier.own), custom_call_target="tpu_custom_call" | custom-call | tf_op jit(solution)/shard_map/pallas_call | solution.py:37
  62.9 3.5 %all-to-all-start.3 = ((bf16[16,8,1024]{2,1,0:T(8,128)(2,1)}), bf16[16,8,1024]{2,1,0:T(8,128)(2,1)S(1)}, u32[]{:S(2)}, u32[]{:S(2)}) async-start(bf16[16,8,1024]{2,1,0:T(8,128)(2,1)} %shard_map.136), calls=%async_computation.3 | async-start | bytes 524288 | tf_op jit(solution)/shard_map/all_to_all | solution.py:371
  66.5 0.0 collective-permute-done.3.near
  66.5 0.0 collective-permute-done.4.far
  66.5 1.0 %shard_map.137.earlier = bf16[1,256,1024]{2,1,0:T(8,128)(2,1)} custom-call(f32[256,1024]{1,0:T(8,128)S(1)} %get-tuple-element.30.earlier.own, bf16[128,1024]{1,0:T(8,128)(2,1)S(1)} %collective-permute-done.3.near, bf16[128,1024]{1,0:T(8,128)(2,1)S(1)} %collective-permute-done.4.far), custom_call_target="tpu_custom_call" | custom-call | tf_op jit(solution)/shard_map/pallas_call | solution.py:37
  67.5 6.4 %all-to-all-done.3.parts = bf16[16,8,1024]{2,1,0:T(8,128)(2,1)S(1)} async-done(((bf16[16,8,1024]{2,1,0:T(8,128)(2,1)}), bf16[16,8,1024]{2,1,0:T(8,128)(2,1)S(1)}, u32[]{:S(2)}, u32[]{:S(2)}) %all-to-all-start.3) | async-done | bytes 262176 | tf_op jit(solution)/shard_map/all_to_all | solution.py:371
  73.9 0.8 %shard_map.138 = (f32[100,1024]{1,0:T(8,128)}, f32[1,1024]{1,0:T(1,128)}, f32[1,1]{1,0:T(1,128)}) custom-call(bf16[16,8,1024]{2,1,0:T(8,128)(2,1)S(1)} %all-to-all-done.3.parts, bf16[1,256,1024]{2,1,0:T(8,128)(2,1)} %shard_map.137.earlier), custom_call_target="tpu_custom_call" | custom-call | tf_op jit(solution)/shard_map/pallas_call | solution.py:37
  (7 shorter events, 0.1 us)
Async XLA Ops:
  0.6 8.6 %copy-start = (bf16[100,1024]{1,0:T(8,128)(2,1)S(1)}, bf16[100,1024]{1,0:T(8,128)(2,1)}, u32[]{:S(2)}) copy-start(bf16[100,1024]{1,0:T(8,128)(2,1)} %proj.5) | copy-start | bytes 614404
  0.6 8.6 %copy-start.2 = (f32[1024]{0:T(1024)S(1)}, f32[1024]{0:T(1024)}, u32[]{:S(2)}) copy-start(f32[1024]{0:T(1024)} %param.19) | copy-start | bytes 12292
  1.7 7.5 %collective-permute-start.1 = (bf16[128,1024]{1,0:T(8,128)(2,1)S(1)}, bf16[128,1024]{1,0:T(8,128)(2,1)S(1)}, u32[]{:S(2)}, u32[]{:S(2)}) collective-permute-start(bf16[128,1024]{1,0:T(8,128)(2,1)S(1)} %shard_map.129.earlier), channel_id=1, source_target_pairs={{0,32},{1,2},{3,4},{5,6},{7,8},{9,10},{11,12},{13,14},{15,16},{17,... | collective-permute-start | bytes 786440 | tf_op jit(solution)/shard_map/ppermute | solution.py:301
  7.6 1.6 %collective-permute-start = (bf16[128,1024]{1,0:T(8,128)(2,1)S(1)}, bf16[128,1024]{1,0:T(8,128)(2,1)S(1)}, u32[]{:S(2)}, u32[]{:S(2)}) collective-permute-start(bf16[128,1024]{1,0:T(8,128)(2,1)S(1)} %get-tuple-element.22), channel_id=1, source_target_pairs={{0,1},{1,0},{2,3},{3,2},{4,5},{5,4},{6,7},{7,6},{8,9},{9,8},{10,11... | collective-permute-start | bytes 786440 | tf_op jit(solution)/shard_map/ppermute | solution.py:328
  10.9 18.2 %copy-start.1 = (f32[100,512]{1,0:T(8,128)S(1)}, f32[100,512]{1,0:T(8,128)}, u32[]{:S(2)}) copy-start(f32[100,512]{1,0:T(8,128)} %target.1) | copy-start | bytes 614404
  29.2 25.1 %copy-start.3 = (s32[3,512]{1,0:T(4,128)S(1)}, s32[3,512]{1,0:T(4,128)}, u32[]{:S(2)}) copy-start(s32[3,512]{1,0:T(4,128)} %nb.1) | copy-start | bytes 18436
  29.2 25.1 %copy-start.4 = (f32[3,512]{1,0:T(4,128)S(1)}, f32[3,512]{1,0:T(4,128)}, u32[]{:S(2)}) copy-start(f32[3,512]{1,0:T(4,128)} %ew.1) | copy-start | bytes 18436
  46.2 4.0 %collective-permute-start.2 = (f32[8,1024]{1,0:T(8,128)S(1)}, f32[8,1024]{1,0:T(8,128)S(1)}, u32[]{:S(2)}, u32[]{:S(2)}) collective-permute-start(f32[8,1024]{1,0:T(8,128)S(1)} %shard_map.133.mine), channel_id=1, source_target_pairs={{0,1},{1,0},{2,3},{3,2},{4,5},{5,4},{6,7},{7,6},{8,9},{9,8},{10,11... | collective-permute-start | bytes 98312 | tf_op jit(solution)/shard_map/ppermute | solution.py:350
  50.8 11.3 %all-to-all-start.2 = ((bf16[8,8,1024]{2,1,0:T(8,128)(2,1)}), bf16[8,8,1024]{2,1,0:T(8,128)(2,1)S(1)}, u32[]{:S(2)}, u32[]{:S(2)}) async-start(bf16[8,8,1024]{2,1,0:T(8,128)(2,1)} %shard_map.134), calls=%async_computation.2 | async-start | bytes 262144 | tf_op jit(solution)/shard_map/all_to_all | solution.py:367
  56.2 10.3 %collective-permute-start.3 = (bf16[128,1024]{1,0:T(8,128)(2,1)S(1)}, bf16[128,1024]{1,0:T(8,128)(2,1)S(1)}, u32[]{:S(2)}, u32[]{:S(2)}) collective-permute-start(bf16[128,1024]{1,0:T(8,128)(2,1)S(1)} %get-tuple-element.31), channel_id=1, source_target_pairs={{0,1},{1,0},{2,3},{3,2},{4,5},{5,4},{6,7},{7,6},{8,9},{9,8},{10,11... | collective-permute-start | bytes 786440 | tf_op jit(solution)/shard_map/ppermute | solution.py:363
  56.9 9.6 %collective-permute-start.4 = (bf16[128,1024]{1,0:T(8,128)(2,1)S(1)}, bf16[128,1024]{1,0:T(8,128)(2,1)S(1)}, u32[]{:S(2)}, u32[]{:S(2)}) collective-permute-start(bf16[128,1024]{1,0:T(8,128)(2,1)S(1)} %get-tuple-element.32), channel_id=1, source_target_pairs={{0,32},{1,2},{3,4},{5,6},{7,8},{9,10},{11,12},{13,14},{15,16},{17,... | collective-permute-start | bytes 786440 | tf_op jit(solution)/shard_map/ppermute | solution.py:362
  62.9 11.0 %all-to-all-start.3 = ((bf16[16,8,1024]{2,1,0:T(8,128)(2,1)}), bf16[16,8,1024]{2,1,0:T(8,128)(2,1)S(1)}, u32[]{:S(2)}, u32[]{:S(2)}) async-start(bf16[16,8,1024]{2,1,0:T(8,128)(2,1)} %shard_map.136), calls=%async_computation.3 | async-start | bytes 524288 | tf_op jit(solution)/shard_map/all_to_all | solution.py:371

commit v14 on v13

--- a/solution.py
+++ b/solution.py
@@ -186,10 +186,20 @@
         parts_out[i] = jnp.zeros((CHUNK, channels), BF16)
 
 
-def back_kernel(earlier, nb, ew, fore_grad, proj, scaled, gain, rscale, own_out, near_out, far_out):
+def turned_edges(nb, ew, start, count):
+    weights = ew[...]
+    weights = weights / jnp.sum(weights, axis=0, keepdims=True)
+    rows = nb[...]
+    row = lax.broadcasted_iota(jnp.int32, (count, nb.shape[1]), 0) + start
+    edges = jnp.zeros(row.shape, F32)
+    for k in range(nb.shape[0]):
+        edges = edges + jnp.where(row == rows[k : k + 1], weights[k : k + 1], 0.0)
+    return edges
+
+
+def back_kernel(earlier, nb, ew, fore_grad, proj, scaled, gain, rscale, mg_out, near_out, far_out):
     channels = scaled.shape[1]
     rim = near_out.shape[0]
-    mesh_count = own_out.shape[0]
     scaled_grad = dot(fore_grad[...], proj[...], ((0,), (0,)))
     values = scaled[...].astype(F32)
     norm_grad = scaled_grad * gain[...]
@@ -197,27 +207,18 @@
     second = jnp.sum(scaled_grad * values, axis=1, keepdims=True) / channels
     mixed_grad = rscale[...] * (norm_grad - first - values * (1.0 / gain[...]) * second)
     mixed_grad = mixed_grad.astype(BF16)
-    weights = ew[...]
-    weights = weights / jnp.sum(weights, axis=0, keepdims=True)
-    rows = nb[...]
-    near_start, far_start, far_there = borrowed_rows(rim + mesh_count)
-
-    def back(start, count, there=None):
-        row = lax.broadcasted_iota(jnp.int32, (count, nb.shape[1]), 0) + start
-        edges = jnp.zeros(row.shape, F32)
-        for k in range(nb.shape[0]):
-            edges = edges + jnp.where(row == rows[k : k + 1], weights[k : k + 1], 0.0)
-        if there is not None:
-            edges = jnp.where(there, edges, 0.0)
-        return dot(edges.astype(BF16), mixed_grad, ((1,), (0,)))
-
-    far_out[...] = back(far_start, rim, far_there).astype(BF16)
-    near_out[...] = back(near_start, rim).astype(BF16)
-    own_out[...] = back(rim, mesh_count)
-
-
-def finish_latent_kernel(own, near, far, out):
+    mg_out[...] = mixed_grad
+    near_start, far_start, far_there = borrowed_rows(3 * rim)
+    far = jnp.where(far_there, turned_edges(nb, ew, far_start, rim), 0.0).astype(BF16)
+    far_out[...] = dot(far, mixed_grad, ((1,), (0,))).astype(BF16)
+    near = turned_edges(nb, ew, near_start, rim).astype(BF16)
+    near_out[...] = dot(near, mixed_grad, ((1,), (0,))).astype(BF16)
+
+
+def finish_latent_kernel(nb, ew, mixed_grad, near, far, out):
     rim = near.shape[0]
+    edges = turned_edges(nb, ew, rim, 2 * rim).astype(BF16)
+    own = dot(edges, mixed_grad[...], ((1,), (0,)))
     a, b = near[...].astype(F32), far[...].astype(F32)
     second = lax.axis_index("c") == 1
     out[0, :rim] = (own[:rim] + jnp.where(second, a, b)).astype(BF16)
@@ -352,22 +353,25 @@
     (parts,) = call(
         functools.partial(pair_kernel, variables), [((depth, CHUNK, channels), BF16)]
     )(mine, met)
-    own, near_grad, far_grad = call(
+    mixed_grad, near_grad, far_grad = call(
         back_kernel,
-        [((mesh_count, channels), F32), ((rim, channels), BF16), ((rim, channels), BF16)],
+        [((points, channels), BF16), ((rim, channels), BF16), ((rim, channels), BF16)],
         flops=2 * points * channels * (extent + variables),
         moved=6_000_000,
         spaces="a",
     )(met, neighbours, edge_weight, fore_grad, output_projection, scaled, gain, rscale)
     far_grad = lax.ppermute(far_grad, MEMBER + GRID, links)
     near_grad = lax.ppermute(near_grad, "c", swap)
-    (latent_grad,) = call(finish_latent_kernel, [((1, mesh_count, channels), BF16)])(
-        own, near_grad, far_grad
-    )
+    (latent_grad,) = call(
+        finish_latent_kernel,
+        [((1, mesh_count, channels), BF16)],
+        flops=2 * points * channels * mesh_count,
+        moved=3_000_000,
+    )(neighbours, edge_weight, mixed_grad, near_grad, far_grad)
     parts = lax.all_to_all(parts, "z", 0, 0, tiled=True)
     (parts,) = call(
         functools.partial(spread_kernel, variables), [((plane, CHUNK, channels), BF16)], "va"
-    )(parts, own)
+    )(parts, mixed_grad)
     parts = lax.all_to_all(parts, PLANE, 0, 0, tiled=True)
     wout, gain_grad, crps = call(
         functools.partial(finish_weights_kernel, points * slabs * variables),

time: 76.1 us -> 76.1 us (level)
  no operation moved by 1% of the time
where the time goes in v14:
time: 76.1 us; the launch traced here: 74.7 us
  blocking collectives  34 us (45%)
  starting transfers between devices  15.9 us (21%)
  waiting for transfers between devices  12 us (16%)
  Pallas kernels  11.6 us (15%)
  between operations  0.79 us (1%)
    all_to_all x1, blocking collectives, per_device(): every = lax.all_to_all(sent, MEMBER, 0, 0, tiled=True).astype(F32)  18 us
    all_to_all x1, blocking collectives, per_device(): parts = lax.all_to_all(parts, PLANE, 0, 0, tiled=True)  16 us
    pallas_call x10, Pallas kernels, run(): pl.pallas_call(kernel, out_shape=[jax.ShapeDtypeStruct(s, d) for s, d in...  11.6 us
    all_to_all x1, waiting for transfers between devices, per_device(): parts = lax.all_to_all(parts, PLANE, 0, 0, tiled=True)  6.06 us
    all_to_all x1, waiting for transfers between devices, per_device(): parts = lax.all_to_all(parts, 'z', 0, 0, tiled=True)  3.73 us
    all_to_all x1, starting transfers between devices, per_device(): parts = lax.all_to_all(parts, PLANE, 0, 0, tiled=True)  3.53 us
    all_to_all x1, starting transfers between devices, per_device(): parts = lax.all_to_all(parts, 'z', 0, 0, tiled=True)  3.42 us
    ppermute x1, starting transfers between devices, per_device(): met = lax.ppermute(mine, 'c', swap)  3.13 us
  transfers between devices with their start and end apart: 7, of which 5 were waited for; matrix products, arithmetic and copies ran while one was open for 0% of the time, Pallas kernels for 9%

profile of v14, /device:TPU:1, one launch (start us, length us, event | category | flops | bytes accessed | tf_op | source)
XLA Modules:
  0.0 74.7 jit_solution(2637560076811418048)
XLA Ops:
  0.6 0.0 copy-start
  0.6 0.0 copy-start.2
  0.7 1.0 %shard_map.129.earlier = bf16[128,1024]{1,0:T(8,128)(2,1)S(1)} custom-call(bf16[256,1024]{1,0:T(8,128)(2,1)} %bitcast.11), custom_call_target="tpu_custom_call" | custom-call | tf_op jit(solution)/shard_map/pallas_call | solution.py:37
  1.7 3.1 %collective-permute-start.1 = (bf16[128,1024]{1,0:T(8,128)(2,1)S(1)}, bf16[128,1024]{1,0:T(8,128)(2,1)S(1)}, u32[]{:S(2)}, u32[]{:S(2)}) collective-permute-start(bf16[128,1024]{1,0:T(8,128)(2,1)S(1)} %shard_map.129.earlier), channel_id=1, source_target_pairs={{0,32},{1,2},{3,4},{5,6},{7,8},{9,10},{11,12},{13,14},{15,16},{17,... | collective-permute-start | bytes 786440 | tf_op jit(solution)/shard_map/ppermute | solution.py:302
  4.8 2.8 %shard_map.130 = (bf16[128,1024]{1,0:T(8,128)(2,1)S(1)}, bf16[512,512]{1,0:T(8,128)(2,1)S(1)}, f32[512,1024]{1,0:T(8,128)S(1)}, f32[100,512]{1,0:T(8,128)S(1)}, f32[100,512]{1,0:T(8,128)S(1)}) custom-call(s32[3,512]{1,0:T(4,128)} %nb.3, f32[3,512]{1,0:T(4,128)} %ew.3, f32[1,100]{1,0:T(1,128)} %bitcast.17, f32[1,512]{1,0:T(1,128)} %bitcast.16, ...), custom_call_target="tpu_custom_call" | custom-call | flops 805306368 | bytes 8000000 | tf_op jit(solution)/shard_map/pallas_call | solution.py:37
  7.6 0.3 collective-permute-start
  7.9 1.2 %collective-permute-done.1.far = bf16[128,1024]{1,0:T(8,128)(2,1)S(1)} collective-permute-done((bf16[128,1024]{1,0:T(8,128)(2,1)S(1)}, bf16[128,1024]{1,0:T(8,128)(2,1)S(1)}, u32[]{:S(2)}, u32[]{:S(2)}) %collective-permute-start.1) | collective-permute-done | bytes 262176 | tf_op jit(solution)/shard_map/ppermute | solution.py:302
  9.1 0.1 collective-permute-done.near
  9.2 1.6 %shard_map.131 = (f32[100,512]{1,0:T(8,128)S(1)}, bf16[512,1024]{1,0:T(8,128)(2,1)S(1)}, f32[512,1]{1,0:T(8,128)S(1)}) custom-call(f32[512,1024]{1,0:T(8,128)S(1)} %get-tuple-element.20.part, bf16[512,512]{1,0:T(8,128)(2,1)S(1)} %get-tuple-element.21.edges, bf16[128,1024]{1,0:T(8,128)(2,1)S(1)} %collective-permute-done.near, ...), custom_call_target="tpu_custom_call" | custom-call | flops 373293056 | bytes 5000000 | tf_op jit(solution)/shard_map/pallas_call | solution.py:37
  10.8 0.1 broadcast_in_dim.18
  10.9 0.0 copy-start.1
  10.9 18.0 %all_to_all.20 = f16[8,100,512]{2,1,0:T(8,128)(2,1)S(1)} all-to-all(f16[8,100,512]{2,1,0:T(8,128)(2,1)S(1)} %broadcast_in_dim.18), channel_id=1, replica_groups=mesh['xl'=2,'y'=4,'xh'=2,'z'=8,'c'=2] {'xl','y'}, dimensions={0} | all-to-all | bytes 1638400 | tf_op jit(solution)/shard_map/all_to_all | solution.py:341
  28.9 0.2 convert_element_type.7.every
  29.2 0.0 copy-start.3
  29.2 0.0 copy-start.4
  29.2 0.9 %shard_map.132 = (bf16[100,512]{1,0:T(8,128)(2,1)S(1)}, bf16[16,8,1024]{2,1,0:T(8,128)(2,1)S(1)}) custom-call(f32[8,100,512]{2,1,0:T(8,128)S(1)} %convert_element_type.7.every, f32[100,512]{1,0:T(8,128)S(1)} %get-tuple-element.24.field, f32[100,512]{1,0:T(8,128)S(1)} %copy-done.1, f32[100,512]{1,0:T(8,128)S(1)} %get-tuple-element.25.wm, ...), custom_call_target="tpu_custom_call" | custom-call | flops 209715200 | bytes 4000000 | tf_op jit(solution)/shard_map/pallas_call | solution.py:37
  30.1 16.0 %all_to_all.21.parts = bf16[16,8,1024]{2,1,0:T(8,128)(2,1)S(1)} all-to-all(bf16[16,8,1024]{2,1,0:T(8,128)(2,1)S(1)} %get-tuple-element.27), channel_id=1, replica_groups=mesh['xl'=2,'y'=4,'xh'=2,'z'=8,'c'=2] {'xl','y','xh'}, dimensions={0} | all-to-all | bytes 524288 | tf_op jit(solution)/shard_map/all_to_all | solution.py:349
  46.2 3.1 %collective-permute-start.2 = (f32[8,1024]{1,0:T(8,128)S(1)}, f32[8,1024]{1,0:T(8,128)S(1)}, u32[]{:S(2)}, u32[]{:S(2)}) collective-permute-start(f32[8,1024]{1,0:T(8,128)S(1)} %shard_map.133.mine), channel_id=1, source_target_pairs={{0,1},{1,0},{2,3},{3,2},{4,5},{5,4},{6,7},{7,6},{8,9},{9,8},{10,11... | collective-permute-start | bytes 98312 | tf_op jit(solution)/shard_map/ppermute | solution.py:351
  49.3 0.9 %collective-permute-done.2.met.earlier = f32[8,1024]{1,0:T(8,128)S(1)} collective-permute-done((f32[8,1024]{1,0:T(8,128)S(1)}, f32[8,1024]{1,0:T(8,128)S(1)}, u32[]{:S(2)}, u32[]{:S(2)}) %collective-permute-start.2) | collective-permute-done | bytes 32800 | tf_op jit(solution)/shard_map/ppermute | solution.py:351
  50.2 0.7 shard_map.134
  50.8 3.4 %all-to-all-start.2 = ((bf16[8,8,1024]{2,1,0:T(8,128)(2,1)}), bf16[8,8,1024]{2,1,0:T(8,128)(2,1)S(1)}, u32[]{:S(2)}, u32[]{:S(2)}) async-start(bf16[8,8,1024]{2,1,0:T(8,128)(2,1)} %shard_map.134), calls=%async_computation.2 | async-start | bytes 262144 | tf_op jit(solution)/shard_map/all_to_all | solution.py:371
  54.3 1.8 %shard_map.135 = (bf16[512,1024]{1,0:T(8,128)(2,1)S(1)}, bf16[128,1024]{1,0:T(8,128)(2,1)S(1)}, bf16[128,1024]{1,0:T(8,128)(2,1)S(1)}) custom-call(f32[8,1024]{1,0:T(8,128)S(1)} %collective-permute-done.2.met.earlier, s32[3,512]{1,0:T(4,128)S(1)} %copy-done.3, f32[3,512]{1,0:T(4,128)S(1)} %copy-done.4, bf16[100,512]{1,0:T(8,128)(2,1)S(1)} %get-tuple-element.28.fore_grad, ...), custom_call_target="tpu_custom_call" | custom-call | flops 641728512 | bytes 6000000 | tf_op jit(solution)/shard_map/pallas_call | solution.py:37
  56.0 0.7 collective-permute-start.3
  56.7 1.7 %collective-permute-start.4 = (bf16[128,1024]{1,0:T(8,128)(2,1)S(1)}, bf16[128,1024]{1,0:T(8,128)(2,1)S(1)}, u32[]{:S(2)}, u32[]{:S(2)}) collective-permute-start(bf16[128,1024]{1,0:T(8,128)(2,1)S(1)} %get-tuple-element.32), channel_id=1, source_target_pairs={{0,32},{1,2},{3,4},{5,6},{7,8},{9,10},{11,12},{13,14},{15,16},{17,... | collective-permute-start | bytes 786440 | tf_op jit(solution)/shard_map/ppermute | solution.py:363
  58.5 3.7 %all-to-all-done.2.parts = bf16[8,8,1024]{2,1,0:T(8,128)(2,1)S(1)} async-done(((bf16[8,8,1024]{2,1,0:T(8,128)(2,1)}), bf16[8,8,1024]{2,1,0:T(8,128)(2,1)S(1)}, u32[]{:S(2)}, u32[]{:S(2)}) %all-to-all-start.2) | async-done | bytes 131104 | tf_op jit(solution)/shard_map/all_to_all | solution.py:371
  62.2 0.8 %shard_map.136 = bf16[16,8,1024]{2,1,0:T(8,128)(2,1)} custom-call(bf16[8,8,1024]{2,1,0:T(8,128)(2,1)S(1)} %all-to-all-done.2.parts, bf16[512,1024]{1,0:T(8,128)(2,1)S(1)} %get-tuple-element.30.earlier.mixed_grad), custom_call_target="tpu_custom_call" | custom-call | tf_op jit(solution)/shard_map/pallas_call | solution.py:37
  62.9 3.5 %all-to-all-start.3 = ((bf16[16,8,1024]{2,1,0:T(8,128)(2,1)}), bf16[16,8,1024]{2,1,0:T(8,128)(2,1)S(1)}, u32[]{:S(2)}, u32[]{:S(2)}) async-start(bf16[16,8,1024]{2,1,0:T(8,128)(2,1)} %shard_map.136), calls=%async_computation.3 | async-start | bytes 524288 | tf_op jit(solution)/shard_map/all_to_all | solution.py:375
  66.5 0.0 collective-permute-done.3.near
  66.5 0.0 collective-permute-done.4.far
  66.5 1.3 %shard_map.137.earlier = bf16[1,256,1024]{2,1,0:T(8,128)(2,1)} custom-call(s32[3,512]{1,0:T(4,128)S(1)} %copy-done.3, f32[3,512]{1,0:T(4,128)S(1)} %copy-done.4, bf16[512,1024]{1,0:T(8,128)(2,1)S(1)} %get-tuple-element.30.earlier.mixed_grad, bf16[128,1024]{1,0:T(8,128)(2,1)S(1)} %collective-permute-done.3.near, bf16[128,1024]{1,0:T(8,128)(2,1)S(1)} %collective-permute-done.4.far), custom_call_target="tpu_custom_call" | custom-call | flops 268435456 | bytes 3000000 | tf_op jit(solution)/shard_map/pallas_call | solution.py:37
  67.9 6.1 %all-to-all-done.3.parts = bf16[16,8,1024]{2,1,0:T(8,128)(2,1)S(1)} async-done(((bf16[16,8,1024]{2,1,0:T(8,128)(2,1)}), bf16[16,8,1024]{2,1,0:T(8,128)(2,1)S(1)}, u32[]{:S(2)}, u32[]{:S(2)}) %all-to-all-start.3) | async-done | bytes 262176 | tf_op jit(solution)/shard_map/all_to_all | solution.py:375
  73.9 0.8 %shard_map.138 = (f32[100,1024]{1,0:T(8,128)}, f32[1,1024]{1,0:T(1,128)}, f32[1,1]{1,0:T(1,128)}) custom-call(bf16[16,8,1024]{2,1,0:T(8,128)(2,1)S(1)} %all-to-all-done.3.parts, bf16[1,256,1024]{2,1,0:T(8,128)(2,1)} %shard_map.137.earlier), custom_call_target="tpu_custom_call" | custom-call | tf_op jit(solution)/shard_map/pallas_call | solution.py:37
  (7 shorter events, 0.1 us)
Async XLA Ops:
  0.6 8.6 %copy-start = (bf16[100,1024]{1,0:T(8,128)(2,1)S(1)}, bf16[100,1024]{1,0:T(8,128)(2,1)}, u32[]{:S(2)}) copy-start(bf16[100,1024]{1,0:T(8,128)(2,1)} %proj.5) | copy-start | bytes 614404
  0.6 8.6 %copy-start.2 = (f32[1024]{0:T(1024)S(1)}, f32[1024]{0:T(1024)}, u32[]{:S(2)}) copy-start(f32[1024]{0:T(1024)} %param.19) | copy-start | bytes 12292
  1.7 7.5 %collective-permute-start.1 = (bf16[128,1024]{1,0:T(8,128)(2,1)S(1)}, bf16[128,1024]{1,0:T(8,128)(2,1)S(1)}, u32[]{:S(2)}, u32[]{:S(2)}) collective-permute-start(bf16[128,1024]{1,0:T(8,128)(2,1)S(1)} %shard_map.129.earlier), channel_id=1, source_target_pairs={{0,32},{1,2},{3,4},{5,6},{7,8},{9,10},{11,12},{13,14},{15,16},{17,... | collective-permute-start | bytes 786440 | tf_op jit(solution)/shard_map/ppermute | solution.py:302
  7.6 1.6 %collective-permute-start = (bf16[128,1024]{1,0:T(8,128)(2,1)S(1)}, bf16[128,1024]{1,0:T(8,128)(2,1)S(1)}, u32[]{:S(2)}, u32[]{:S(2)}) collective-permute-start(bf16[128,1024]{1,0:T(8,128)(2,1)S(1)} %get-tuple-element.22), channel_id=1, source_target_pairs={{0,1},{1,0},{2,3},{3,2},{4,5},{5,4},{6,7},{7,6},{8,9},{9,8},{10,11... | collective-permute-start | bytes 786440 | tf_op jit(solution)/shard_map/ppermute | solution.py:329
  10.9 18.2 %copy-start.1 = (f32[100,512]{1,0:T(8,128)S(1)}, f32[100,512]{1,0:T(8,128)}, u32[]{:S(2)}) copy-start(f32[100,512]{1,0:T(8,128)} %target.1) | copy-start | bytes 614404
  29.2 25.1 %copy-start.3 = (s32[3,512]{1,0:T(4,128)S(1)}, s32[3,512]{1,0:T(4,128)}, u32[]{:S(2)}) copy-start(s32[3,512]{1,0:T(4,128)} %nb.3) | copy-start | bytes 18436
  29.2 25.1 %copy-start.4 = (f32[3,512]{1,0:T(4,128)S(1)}, f32[3,512]{1,0:T(4,128)}, u32[]{:S(2)}) copy-start(f32[3,512]{1,0:T(4,128)} %ew.3) | copy-start | bytes 18436
  46.2 4.0 %collective-permute-start.2 = (f32[8,1024]{1,0:T(8,128)S(1)}, f32[8,1024]{1,0:T(8,128)S(1)}, u32[]{:S(2)}, u32[]{:S(2)}) collective-permute-start(f32[8,1024]{1,0:T(8,128)S(1)} %shard_map.133.mine), channel_id=1, source_target_pairs={{0,1},{1,0},{2,3},{3,2},{4,5},{5,4},{6,7},{7,6},{8,9},{9,8},{10,11... | collective-permute-start | bytes 98312 | tf_op jit(solution)/shard_map/ppermute | solution.py:351
  50.8 11.3 %all-to-all-start.2 = ((bf16[8,8,1024]{2,1,0:T(8,128)(2,1)}), bf16[8,8,1024]{2,1,0:T(8,128)(2,1)S(1)}, u32[]{:S(2)}, u32[]{:S(2)}) async-start(bf16[8,8,1024]{2,1,0:T(8,128)(2,1)} %shard_map.134), calls=%async_computation.2 | async-start | bytes 262144 | tf_op jit(solution)/shard_map/all_to_all | solution.py:371
  56.0 10.5 %collective-permute-start.3 = (bf16[128,1024]{1,0:T(8,128)(2,1)S(1)}, bf16[128,1024]{1,0:T(8,128)(2,1)S(1)}, u32[]{:S(2)}, u32[]{:S(2)}) collective-permute-start(bf16[128,1024]{1,0:T(8,128)(2,1)S(1)} %get-tuple-element.31), channel_id=1, source_target_pairs={{0,1},{1,0},{2,3},{3,2},{4,5},{5,4},{6,7},{7,6},{8,9},{9,8},{10,11... | collective-permute-start | bytes 786440 | tf_op jit(solution)/shard_map/ppermute | solution.py:364
  56.7 9.8 %collective-permute-start.4 = (bf16[128,1024]{1,0:T(8,128)(2,1)S(1)}, bf16[128,1024]{1,0:T(8,128)(2,1)S(1)}, u32[]{:S(2)}, u32[]{:S(2)}) collective-permute-start(bf16[128,1024]{1,0:T(8,128)(2,1)S(1)} %get-tuple-element.32), channel_id=1, source_target_pairs={{0,32},{1,2},{3,4},{5,6},{7,8},{9,10},{11,12},{13,14},{15,16},{17,... | collective-permute-start | bytes 786440 | tf_op jit(solution)/shard_map/ppermute | solution.py:363
  62.9 11.0 %all-to-all-start.3 = ((bf16[16,8,1024]{2,1,0:T(8,128)(2,1)}), bf16[16,8,1024]{2,1,0:T(8,128)(2,1)S(1)}, u32[]{:S(2)}, u32[]{:S(2)}) async-start(bf16[16,8,1024]{2,1,0:T(8,128)(2,1)} %shard_map.136), calls=%async_computation.3 | async-start | bytes 524288 | tf_op jit(solution)/shard_map/all_to_all | solution.py:375

commit v15 on v13

--- a/solution.py
+++ b/solution.py
@@ -186,7 +186,7 @@
         parts_out[i] = jnp.zeros((CHUNK, channels), BF16)
 
 
-def back_kernel(earlier, nb, ew, fore_grad, proj, scaled, gain, rscale, own_out, near_out, far_out):
+def back_kernel(nb, ew, fore_grad, proj, scaled, gain, rscale, own_out, near_out, far_out):
     channels = scaled.shape[1]
     rim = near_out.shape[0]
     mesh_count = own_out.shape[0]
@@ -234,7 +234,7 @@
     return jnp.where(here, split, total).astype(BF16)
 
 
-def fold_kernel(parts, out):
+def fold_kernel(parts, earlier, out):
     out[...] = jnp.sum(parts[...].astype(F32), axis=0)
 
 
@@ -250,7 +250,7 @@
         out[i] = total
 
 
-def finish_weights_kernel(count, parts, earlier, wout_out, gain_out, loss_out):
+def finish_weights_kernel(count, parts, wout_out, gain_out, loss_out):
     variables = wout_out.shape[0]
     last = variables // CHUNK
     for i in range(last):
@@ -345,35 +345,33 @@
         moved=4_000_000,
     )(every, field, target, weight_map, output_projection, scaled, gain)
 
+    own, near_grad, far_grad = call(
+        back_kernel,
+        [((mesh_count, channels), F32), ((rim, channels), BF16), ((rim, channels), BF16)],
+        flops=2 * points * channels * (extent + variables),
+        moved=6_000_000,
+    )(neighbours, edge_weight, fore_grad, output_projection, scaled, gain, rscale)
+    far_grad = lax.ppermute(far_grad, MEMBER + GRID, links)
+    near_grad = lax.ppermute(near_grad, "c", swap)
+    (latent_grad,) = call(finish_latent_kernel, [((1, mesh_count, channels), BF16)])(
+        own, near_grad, far_grad
+    )
     parts = lax.all_to_all(parts, PLANE, 0, 0, tiled=True)
-    (mine,) = call(fold_kernel, [((CHUNK, channels), F32)])(parts)
+    (mine,) = call(fold_kernel, [((CHUNK, channels), F32)], "va")(parts, own)
     met = lax.ppermute(mine, "c", swap)
     depth = lax.axis_size("z")
     (parts,) = call(
         functools.partial(pair_kernel, variables), [((depth, CHUNK, channels), BF16)]
     )(mine, met)
-    own, near_grad, far_grad = call(
-        back_kernel,
-        [((mesh_count, channels), F32), ((rim, channels), BF16), ((rim, channels), BF16)],
-        flops=2 * points * channels * (extent + variables),
-        moved=6_000_000,
-        spaces="a",
-    )(met, neighbours, edge_weight, fore_grad, output_projection, scaled, gain, rscale)
-    far_grad = lax.ppermute(far_grad, MEMBER + GRID, links)
-    near_grad = lax.ppermute(near_grad, "c", swap)
-    (latent_grad,) = call(finish_latent_kernel, [((1, mesh_count, channels), BF16)])(
-        own, near_grad, far_grad
-    )
     parts = lax.all_to_all(parts, "z", 0, 0, tiled=True)
     (parts,) = call(
-        functools.partial(spread_kernel, variables), [((plane, CHUNK, channels), BF16)], "va"
-    )(parts, own)
+        functools.partial(spread_kernel, variables), [((plane, CHUNK, channels), BF16)], "vh"
+    )(parts, latent_grad)
     parts = lax.all_to_all(parts, PLANE, 0, 0, tiled=True)
     wout, gain_grad, crps = call(
         functools.partial(finish_weights_kernel, points * slabs * variables),
         [((variables, channels), F32), ((1, channels), F32), ((1, 1), F32)],
-        "vh",
-    )(parts, latent_grad)
+    )(parts)
     return (crps[0, 0], latent_grad, wout, gain_grad[0])
 
 

time: 76.1 us -> 75.8 us (level)
  blocking collectives: 34 us -> 28.4 us
  starting transfers between devices: 15.9 us -> 20.8 us
    all_to_all x1, blocking collectives: 16 us -> 10.4 us  [per_device(): parts = lax.all_to_all(parts, PLANE, 0, 0, tiled=True)]
    all_to_all x1, starting transfers between devices: 3.53 us -> 8.66 us  [per_device(): parts = lax.all_to_all(parts, PLANE, 0, 0, tiled=True)]
    all_to_all x1, waiting for transfers between devices: 3.58 us -> 6.89 us  [per_device(): parts = lax.all_to_all(parts, 'z', 0, 0, tiled=True)]
    all_to_all x1, waiting for transfers between devices: 6.44 us -> 3.58 us  [per_device(): parts = lax.all_to_all(parts, PLANE, 0, 0, tiled=True)]
    ppermute x1, starting transfers between devices: 1.72 us -> 0.01 us  [per_device(): far_grad = lax.ppermute(far_grad, MEMBER + GRID, links)]
    ppermute x1, starting transfers between devices: 0.71 us -> 2.07 us  [per_device(): near_grad = lax.ppermute(near_grad, 'c', swap)]
where the time goes in v15:
time: 75.8 us; the launch traced here: 74.3 us
  blocking collectives  28.4 us (37%)
  starting transfers between devices  20.8 us (27%)
  waiting for transfers between devices  12.6 us (17%)
  Pallas kernels  11.4 us (15%)
  between operations  0.8 us (1%)
    all_to_all x1, blocking collectives, per_device(): every = lax.all_to_all(sent, MEMBER, 0, 0, tiled=True).astype(F32)  18 us
    pallas_call x10, Pallas kernels, run(): pl.pallas_call(kernel, out_shape=[jax.ShapeDtypeStruct(s, d) for s, d in...  11.4 us
    all_to_all x1, blocking collectives, per_device(): parts = lax.all_to_all(parts, PLANE, 0, 0, tiled=True)  10.4 us
    all_to_all x1, starting transfers between devices, per_device(): parts = lax.all_to_all(parts, PLANE, 0, 0, tiled=True)  8.66 us
    all_to_all x1, waiting for transfers between devices, per_device(): parts = lax.all_to_all(parts, 'z', 0, 0, tiled=True)  6.89 us
    all_to_all x1, waiting for transfers between devices, per_device(): parts = lax.all_to_all(parts, PLANE, 0, 0, tiled=True)  3.58 us
    all_to_all x1, starting transfers between devices, per_device(): parts = lax.all_to_all(parts, 'z', 0, 0, tiled=True)  3.37 us
    ppermute x1, starting transfers between devices, per_device(): met = lax.ppermute(mine, 'c', swap)  3.22 us
  transfers between devices with their start and end apart: 7, of which 5 were waited for; matrix products, arithmetic and copies ran while one was open for 0% of the time, Pallas kernels for 9%

profile of v15, /device:TPU:1, one launch (start us, length us, event | category | flops | bytes accessed | tf_op | source)
XLA Modules:
  0.0 74.3 jit_solution(11264584321916259020)
XLA Ops:
  0.6 0.0 copy-start
  0.7 1.0 %shard_map.129.earlier = bf16[128,1024]{1,0:T(8,128)(2,1)S(1)} custom-call(bf16[256,1024]{1,0:T(8,128)(2,1)} %bitcast.11), custom_call_target="tpu_custom_call" | custom-call | tf_op jit(solution)/shard_map/pallas_call | solution.py:37
  1.7 3.1 %collective-permute-start.1 = (bf16[128,1024]{1,0:T(8,128)(2,1)S(1)}, bf16[128,1024]{1,0:T(8,128)(2,1)S(1)}, u32[]{:S(2)}, u32[]{:S(2)}) collective-permute-start(bf16[128,1024]{1,0:T(8,128)(2,1)S(1)} %shard_map.129.earlier), channel_id=1, source_target_pairs={{0,32},{1,2},{3,4},{5,6},{7,8},{9,10},{11,12},{13,14},{15,16},{17,... | collective-permute-start | bytes 786440 | tf_op jit(solution)/shard_map/ppermute | solution.py:301
  4.8 2.8 %shard_map.130 = (bf16[128,1024]{1,0:T(8,128)(2,1)S(1)}, bf16[512,512]{1,0:T(8,128)(2,1)S(1)}, f32[512,1024]{1,0:T(8,128)S(1)}, f32[100,512]{1,0:T(8,128)S(1)}, f32[100,512]{1,0:T(8,128)S(1)}) custom-call(s32[3,512]{1,0:T(4,128)} %nb.1, f32[3,512]{1,0:T(4,128)} %ew.1, f32[1,100]{1,0:T(1,128)} %bitcast.17, f32[1,512]{1,0:T(1,128)} %bitcast.16, ...), custom_call_target="tpu_custom_call" | custom-call | flops 805306368 | bytes 8000000 | tf_op jit(solution)/shard_map/pallas_call | solution.py:37
  7.6 0.3 collective-permute-start
  7.9 1.2 %collective-permute-done.1.far = bf16[128,1024]{1,0:T(8,128)(2,1)S(1)} collective-permute-done((bf16[128,1024]{1,0:T(8,128)(2,1)S(1)}, bf16[128,1024]{1,0:T(8,128)(2,1)S(1)}, u32[]{:S(2)}, u32[]{:S(2)}) %collective-permute-start.1) | collective-permute-done | bytes 262176 | tf_op jit(solution)/shard_map/ppermute | solution.py:301
  9.1 0.1 collective-permute-done.near
  9.2 1.6 %shard_map.131 = (f32[100,512]{1,0:T(8,128)S(1)}, bf16[512,1024]{1,0:T(8,128)(2,1)S(1)}, f32[512,1]{1,0:T(8,128)S(1)}) custom-call(f32[512,1024]{1,0:T(8,128)S(1)} %get-tuple-element.20.part, bf16[512,512]{1,0:T(8,128)(2,1)S(1)} %get-tuple-element.21.edges, bf16[128,1024]{1,0:T(8,128)(2,1)S(1)} %collective-permute-done.near, ...), custom_call_target="tpu_custom_call" | custom-call | flops 373293056 | bytes 5000000 | tf_op jit(solution)/shard_map/pallas_call | solution.py:37
  10.8 0.1 broadcast_in_dim.18
  10.9 0.0 copy-start.1
  10.9 18.0 %all_to_all.20 = f16[8,100,512]{2,1,0:T(8,128)(2,1)S(1)} all-to-all(f16[8,100,512]{2,1,0:T(8,128)(2,1)S(1)} %broadcast_in_dim.18), channel_id=1, replica_groups=mesh['xl'=2,'y'=4,'xh'=2,'z'=8,'c'=2] {'xl','y'}, dimensions={0} | all-to-all | bytes 1638400 | tf_op jit(solution)/shard_map/all_to_all | solution.py:340
  28.9 0.2 convert_element_type.7.every
  29.2 0.0 copy-start.3
  29.2 0.0 copy-start.4
  29.2 1.6 %shard_map.132 = (bf16[100,512]{1,0:T(8,128)(2,1)S(1)}, bf16[16,8,1024]{2,1,0:T(8,128)(2,1)}) custom-call(f32[8,100,512]{2,1,0:T(8,128)S(1)} %convert_element_type.7.every, f32[100,512]{1,0:T(8,128)S(1)} %get-tuple-element.24.field, f32[100,512]{1,0:T(8,128)S(1)} %copy-done.1, f32[100,512]{1,0:T(8,128)S(1)} %get-tuple-element.25.wm, ...), custom_call_target="tpu_custom_call" | custom-call | flops 209715200 | bytes 4000000 | tf_op jit(solution)/shard_map/pallas_call | solution.py:37
  30.8 8.7 %all-to-all-start.1 = ((bf16[16,8,1024]{2,1,0:T(8,128)(2,1)}), bf16[16,8,1024]{2,1,0:T(8,128)(2,1)S(1)}, u32[]{:S(2)}, u32[]{:S(2)}) async-start(bf16[16,8,1024]{2,1,0:T(8,128)(2,1)} %get-tuple-element.27), calls=%async_computation.1 | async-start | bytes 524288 | tf_op jit(solution)/shard_map/all_to_all | solution.py:359
  39.5 0.0 copy-done.3
  39.5 0.0 copy-done.4
  39.5 1.9 %shard_map.133 = (f32[256,1024]{1,0:T(8,128)S(1)}, bf16[128,1024]{1,0:T(8,128)(2,1)S(1)}, bf16[128,1024]{1,0:T(8,128)(2,1)S(1)}) custom-call(s32[3,512]{1,0:T(4,128)S(1)} %copy-done.3, f32[3,512]{1,0:T(4,128)S(1)} %copy-done.4, bf16[100,512]{1,0:T(8,128)(2,1)S(1)} %get-tuple-element.28.fore_grad, bf16[100,1024]{1,0:T(8,128)(2,1)S(1)} %copy-done, ...), custom_call_target="tpu_custom_call" | custom-call | flops 641728512 | bytes 6000000 | tf_op jit(solution)/shard_map/pallas_call | solution.py:37
  41.4 2.1 %collective-permute-start.3 = (bf16[128,1024]{1,0:T(8,128)(2,1)S(1)}, bf16[128,1024]{1,0:T(8,128)(2,1)S(1)}, u32[]{:S(2)}, u32[]{:S(2)}) collective-permute-start(bf16[128,1024]{1,0:T(8,128)(2,1)S(1)} %get-tuple-element.31), channel_id=1, source_target_pairs={{0,1},{1,0},{2,3},{3,2},{4,5},{5,4},{6,7},{7,6},{8,9},{9,8},{10,11... | collective-permute-start | bytes 786440 | tf_op jit(solution)/shard_map/ppermute | solution.py:355
  43.5 0.0 collective-permute-start.4
  43.5 3.6 %all-to-all-done.1.parts = bf16[16,8,1024]{2,1,0:T(8,128)(2,1)S(1)} async-done(((bf16[16,8,1024]{2,1,0:T(8,128)(2,1)}), bf16[16,8,1024]{2,1,0:T(8,128)(2,1)S(1)}, u32[]{:S(2)}, u32[]{:S(2)}) %all-to-all-start.1) | async-done | bytes 262176 | tf_op jit(solution)/shard_map/all_to_all | solution.py:359
  47.1 3.2 %collective-permute-start.2 = (f32[8,1024]{1,0:T(8,128)S(1)}, f32[8,1024]{1,0:T(8,128)S(1)}, u32[]{:S(2)}, u32[]{:S(2)}) collective-permute-start(f32[8,1024]{1,0:T(8,128)S(1)} %shard_map.134.mine), channel_id=1, source_target_pairs={{0,1},{1,0},{2,3},{3,2},{4,5},{5,4},{6,7},{7,6},{8,9},{9,8},{10,11... | collective-permute-start | bytes 98312 | tf_op jit(solution)/shard_map/ppermute | solution.py:361
  50.3 0.9 %collective-permute-done.2.met = f32[8,1024]{1,0:T(8,128)S(1)} collective-permute-done((f32[8,1024]{1,0:T(8,128)S(1)}, f32[8,1024]{1,0:T(8,128)S(1)}, u32[]{:S(2)}, u32[]{:S(2)}) %collective-permute-start.2) | collective-permute-done | bytes 32800 | tf_op jit(solution)/shard_map/ppermute | solution.py:361
  51.2 0.7 shard_map.135
  51.8 3.4 %all-to-all-start.2 = ((bf16[8,8,1024]{2,1,0:T(8,128)(2,1)}), bf16[8,8,1024]{2,1,0:T(8,128)(2,1)S(1)}, u32[]{:S(2)}, u32[]{:S(2)}) async-start(bf16[8,8,1024]{2,1,0:T(8,128)(2,1)} %shard_map.135), calls=%async_computation.2 | async-start | bytes 262144 | tf_op jit(solution)/shard_map/all_to_all | solution.py:366
  55.2 0.0 collective-permute-done.3.near
  55.2 0.0 collective-permute-done.4.far
  55.2 1.0 %shard_map.136.earlier = bf16[1,256,1024]{2,1,0:T(8,128)(2,1)} custom-call(f32[256,1024]{1,0:T(8,128)S(1)} %get-tuple-element.30.earlier.own, bf16[128,1024]{1,0:T(8,128)(2,1)S(1)} %collective-permute-done.3.near, bf16[128,1024]{1,0:T(8,128)(2,1)S(1)} %collective-permute-done.4.far), custom_call_target="tpu_custom_call" | custom-call | tf_op jit(solution)/shard_map/pallas_call | solution.py:37
  56.2 6.9 %all-to-all-done.2.parts = bf16[8,8,1024]{2,1,0:T(8,128)(2,1)S(1)} async-done(((bf16[8,8,1024]{2,1,0:T(8,128)(2,1)}), bf16[8,8,1024]{2,1,0:T(8,128)(2,1)S(1)}, u32[]{:S(2)}, u32[]{:S(2)}) %all-to-all-start.2) | async-done | bytes 131104 | tf_op jit(solution)/shard_map/all_to_all | solution.py:366
  63.1 10.4 %all_to_all.21.parts = bf16[16,8,1024]{2,1,0:T(8,128)(2,1)S(1)} all-to-all(bf16[16,8,1024]{2,1,0:T(8,128)(2,1)S(1)} %shard_map.137), channel_id=1, replica_groups=mesh['xl'=2,'y'=4,'xh'=2,'z'=8,'c'=2] {'xl','y','xh'}, dimensions={0} | all-to-all | bytes 524288 | tf_op jit(solution)/shard_map/all_to_all | solution.py:370
  73.6 0.8 %shard_map.138 = (f32[100,1024]{1,0:T(8,128)}, f32[1,1024]{1,0:T(1,128)}, f32[1,1]{1,0:T(1,128)}) custom-call(bf16[16,8,1024]{2,1,0:T(8,128)(2,1)S(1)} %all_to_all.21.parts), custom_call_target="tpu_custom_call" | custom-call | tf_op jit(solution)/shard_map/pallas_call | solution.py:37
  (7 shorter events, 0.1 us)
Async XLA Ops:
  0.6 8.6 %copy-start = (bf16[100,1024]{1,0:T(8,128)(2,1)S(1)}, bf16[100,1024]{1,0:T(8,128)(2,1)}, u32[]{:S(2)}) copy-start(bf16[100,1024]{1,0:T(8,128)(2,1)} %proj.5) | copy-start | bytes 614404
  0.6 8.6 %copy-start.2 = (f32[1024]{0:T(1024)S(1)}, f32[1024]{0:T(1024)}, u32[]{:S(2)}) copy-start(f32[1024]{0:T(1024)} %param.19) | copy-start | bytes 12292
  1.7 7.5 %collective-permute-start.1 = (bf16[128,1024]{1,0:T(8,128)(2,1)S(1)}, bf16[128,1024]{1,0:T(8,128)(2,1)S(1)}, u32[]{:S(2)}, u32[]{:S(2)}) collective-permute-start(bf16[128,1024]{1,0:T(8,128)(2,1)S(1)} %shard_map.129.earlier), channel_id=1, source_target_pairs={{0,32},{1,2},{3,4},{5,6},{7,8},{9,10},{11,12},{13,14},{15,16},{17,... | collective-permute-start | bytes 786440 | tf_op jit(solution)/shard_map/ppermute | solution.py:301
  7.6 1.6 %collective-permute-start = (bf16[128,1024]{1,0:T(8,128)(2,1)S(1)}, bf16[128,1024]{1,0:T(8,128)(2,1)S(1)}, u32[]{:S(2)}, u32[]{:S(2)}) collective-permute-start(bf16[128,1024]{1,0:T(8,128)(2,1)S(1)} %get-tuple-element.22), channel_id=1, source_target_pairs={{0,1},{1,0},{2,3},{3,2},{4,5},{5,4},{6,7},{7,6},{8,9},{9,8},{10,11... | collective-permute-start | bytes 786440 | tf_op jit(solution)/shard_map/ppermute | solution.py:328
  10.9 18.3 %copy-start.1 = (f32[100,512]{1,0:T(8,128)S(1)}, f32[100,512]{1,0:T(8,128)}, u32[]{:S(2)}) copy-start(f32[100,512]{1,0:T(8,128)} %target.1) | copy-start | bytes 614404
  29.2 10.3 %copy-start.3 = (s32[3,512]{1,0:T(4,128)S(1)}, s32[3,512]{1,0:T(4,128)}, u32[]{:S(2)}) copy-start(s32[3,512]{1,0:T(4,128)} %nb.1) | copy-start | bytes 18436
  29.2 10.3 %copy-start.4 = (f32[3,512]{1,0:T(4,128)S(1)}, f32[3,512]{1,0:T(4,128)}, u32[]{:S(2)}) copy-start(f32[3,512]{1,0:T(4,128)} %ew.1) | copy-start | bytes 18436
  30.8 16.3 %all-to-all-start.1 = ((bf16[16,8,1024]{2,1,0:T(8,128)(2,1)}), bf16[16,8,1024]{2,1,0:T(8,128)(2,1)S(1)}, u32[]{:S(2)}, u32[]{:S(2)}) async-start(bf16[16,8,1024]{2,1,0:T(8,128)(2,1)} %get-tuple-element.27), calls=%async_computation.1 | async-start | bytes 524288 | tf_op jit(solution)/shard_map/all_to_all | solution.py:359
  41.4 13.9 %collective-permute-start.3 = (bf16[128,1024]{1,0:T(8,128)(2,1)S(1)}, bf16[128,1024]{1,0:T(8,128)(2,1)S(1)}, u32[]{:S(2)}, u32[]{:S(2)}) collective-permute-start(bf16[128,1024]{1,0:T(8,128)(2,1)S(1)} %get-tuple-element.31), channel_id=1, source_target_pairs={{0,1},{1,0},{2,3},{3,2},{4,5},{5,4},{6,7},{7,6},{8,9},{9,8},{10,11... | collective-permute-start | bytes 786440 | tf_op jit(solution)/shard_map/ppermute | solution.py:355
  43.5 11.8 %collective-permute-start.4 = (bf16[128,1024]{1,0:T(8,128)(2,1)S(1)}, bf16[128,1024]{1,0:T(8,128)(2,1)S(1)}, u32[]{:S(2)}, u32[]{:S(2)}) collective-permute-start(bf16[128,1024]{1,0:T(8,128)(2,1)S(1)} %get-tuple-element.32), channel_id=1, source_target_pairs={{0,32},{1,2},{3,4},{5,6},{7,8},{9,10},{11,12},{13,14},{15,16},{17,... | collective-permute-start | bytes 786440 | tf_op jit(solution)/shard_map/ppermute | solution.py:354
  47.1 4.1 %collective-permute-start.2 = (f32[8,1024]{1,0:T(8,128)S(1)}, f32[8,1024]{1,0:T(8,128)S(1)}, u32[]{:S(2)}, u32[]{:S(2)}) collective-permute-start(f32[8,1024]{1,0:T(8,128)S(1)} %shard_map.134.mine), channel_id=1, source_target_pairs={{0,1},{1,0},{2,3},{3,2},{4,5},{5,4},{6,7},{7,6},{8,9},{9,8},{10,11... | collective-permute-start | bytes 98312 | tf_op jit(solution)/shard_map/ppermute | solution.py:361
  51.8 11.3 %all-to-all-start.2 = ((bf16[8,8,1024]{2,1,0:T(8,128)(2,1)}), bf16[8,8,1024]{2,1,0:T(8,128)(2,1)S(1)}, u32[]{:S(2)}, u32[]{:S(2)}) async-start(bf16[8,8,1024]{2,1,0:T(8,128)(2,1)} %shard_map.135), calls=%async_computation.2 | async-start | bytes 262144 | tf_op jit(solution)/shard_map/all_to_all | solution.py:366
